TPU v7x, 32 devices: a whole 2x2x4 slice. The times are simulated.
32 devices in a mesh: group: 2 (over y), expert: 4 (over z), query: 2 (over x), dp: 2 (over core).
Axes of the slice: x: 2, y: 2, z: 4, core: 2. Of those that a mesh axis runs over, the one named last changes fastest.
Arguments:
- tokens: bfloat16 [4096, 2048], P(('group', 'expert', 'query', 'dp')), parts along dimension 0, may hold values from -6 to 6
- route_ids: int32 [4096, 4], P(('group', 'expert', 'query', 'dp')), parts along dimension 0, may hold values from 0 to 7, all different within a row; in each aligned block of 128 rows (0 to 127, 128 to 255, ...) at most 128 rows name the same one
- gate_values: float32 [4096, 4], P(('group', 'expert', 'query', 'dp')), parts along dimension 0, may hold values from 0.1 to 1
- passage_lengths: int32 [64], P(('group', 'expert', 'query', 'dp')), parts along dimension 0, may hold values from 16 to 64
- gate_weight: bfloat16 [8, 2048, 384], P(('expert', 'query'), None, 'dp'), may hold values from -0.125 to 0.125
- up_weight: bfloat16 [8, 2048, 384], P(('expert', 'query'), None, 'dp'), may hold values from -0.125 to 0.125
- down_weight: bfloat16 [8, 2048, 384], P(('expert', 'query'), None, 'dp'), may hold values from -0.3125 to 0.3125
- proj_weight: bfloat16 [2048, 128], replicated, may hold values from -0.125 to 0.125
- queries: bfloat16 [128, 32, 128], P(('group', 'query')), parts along dimension 0, may hold values from -0.59765625 to 0.59765625
Outputs:
- scores: float32 [64, 64], P(('group', 'expert', 'query', 'dp')), parts along dimension 0
There are 2 independent parts, one for each index of `group`. A program takes and returns all parts, laid end to end along the dimension named above; an argument that names none is the same for every part. Nothing has to cross between parts.
Inputs may be any that keep to these rules, and one draw needn't show every extreme that they name: `route_ids`: in the rows of one device no expert is named more than 128 times, a bound that some block reaches.
All inputs are finite; a program needn't handle non-finite values.
Results may differ from a plain program's by a relative error of at most 0.0006.
Values may be sent and summed in bfloat16 or wider, within the bound.
No kernel may reach another device: no remote copies, remote signals or barrier semaphores. Data moves between devices by JAX's collectives and lax.ppermute only.
A program may use at most 64 MiB of HBM per device.

v0:
```python
import jax
import jax.numpy as jnp
from jax import lax
from jax.sharding import PartitionSpec as P

PLEN = 64


def passage_scores(embedding, live_mask, block_queries):
    query_rows = block_queries.reshape(-1, block_queries.shape[-1])
    raw_scores = jnp.dot(embedding, query_rows.T, preferred_element_type=jnp.float32)
    raw_scores = jnp.where(live_mask[:, None], raw_scores, -jnp.inf)
    best_match = jnp.max(raw_scores.reshape(-1, PLEN, raw_scores.shape[-1]), axis=1)
    return jnp.sum(best_match.reshape(best_match.shape[0], -1, block_queries.shape[1]), axis=-1)


def on_device(
    tokens,
    route_ids,
    gate_values,
    passage_lengths,
    gate_weight,
    up_weight,
    down_weight,
    proj_weight,
    queries,
):
    tok_rows, model_width = tokens.shape
    top_count = route_ids.shape[1]
    experts = lax.axis_size("expert") * lax.axis_size("query")
    capacity = max(2, 2 * tok_rows * top_count // experts)
    assignments = tok_rows * top_count
    flat_routes = route_ids.reshape(-1)
    one_hot = (flat_routes[:, None] == jnp.arange(experts, dtype=jnp.int32)[None, :]).astype(
        jnp.int32
    )
    earlier = jnp.cumsum(one_hot, axis=0) - one_hot
    slot_index = jnp.sum(earlier * one_hot, axis=1)
    slot_target = flat_routes * capacity + slot_index
    slot_owner = (
        jnp.full((experts * capacity,), assignments, jnp.int32)
        .at[slot_target]
        .set(jnp.arange(assignments, dtype=jnp.int32))
    )
    padded = jnp.concatenate([tokens, jnp.zeros((1, model_width), tokens.dtype)], axis=0)
    source_row = jnp.where(slot_owner < assignments, slot_owner // top_count, tok_rows)
    outgoing = padded[source_row].reshape(experts, capacity, model_width)
    arrived = lax.all_to_all(outgoing, ("expert", "query"), split_axis=0, concat_axis=0, tiled=True)
    expert_rows = arrived.reshape(experts * capacity, model_width)
    gate_act = jnp.dot(
        expert_rows,
        lax.all_gather(gate_weight[0], "dp", axis=1, tiled=True),
        preferred_element_type=jnp.float32,
    )
    up_act = jnp.dot(
        expert_rows,
        lax.all_gather(up_weight[0], "dp", axis=1, tiled=True),
        preferred_element_type=jnp.float32,
    )
    hidden = (jax.nn.silu(gate_act) * up_act).astype(jnp.bfloat16)
    accumulated = lax.dot_general(
        hidden,
        lax.all_gather(down_weight[0], "dp", axis=1, tiled=True),
        (((1,), (1,)), ((), ())),
        preferred_element_type=jnp.float32,
    )
    results = accumulated.astype(jnp.bfloat16)
    weights = gate_values.reshape(assignments, 1)
    folded = jnp.dot(results, proj_weight, preferred_element_type=jnp.float32)
    returned_rows = lax.all_to_all(
        folded.reshape(experts, capacity, folded.shape[-1]),
        ("expert", "query"),
        split_axis=0,
        concat_axis=0,
        tiled=True,
    )
    picked = returned_rows.reshape(experts * capacity, folded.shape[-1])[slot_target]
    projected = jnp.dot(tokens, proj_weight, preferred_element_type=jnp.float32) + jnp.sum(
        (picked * weights).reshape(tok_rows, top_count, folded.shape[-1]), axis=1
    )
    lengths_norm = jnp.sqrt(jnp.sum(projected * projected, axis=-1, keepdims=True) + 1e-06)
    embedding = (projected / lengths_norm).astype(jnp.bfloat16)
    position = jnp.arange(tok_rows, dtype=jnp.int32) % PLEN
    live_mask = position < jnp.repeat(passage_lengths, PLEN)
    return passage_scores(
        embedding, live_mask, lax.all_gather(queries, "query", axis=0, tiled=True)
    )


def solution(mesh):
    in_specs = (
        P(("group", "expert", "query", "dp"), None),
        P(("group", "expert", "query", "dp"), None),
        P(("group", "expert", "query", "dp"), None),
        P(("group", "expert", "query", "dp")),
        P(("expert", "query"), None, "dp"),
        P(("expert", "query"), None, "dp"),
        P(("expert", "query"), None, "dp"),
        P(),
        P(("group", "query"), None, None),
    )
    out_specs = P(("group", "expert", "query", "dp"), None)
    return jax.shard_map(
        on_device, mesh=mesh, in_specs=in_specs, out_specs=out_specs, check_vma=False
    )
```

profile of v0, /device:TPU:0, one launch (start us, length us, event | category | flops | bytes accessed | tf_op | source)
XLA Modules:
  0.0 163.8 jit_solution(16316723009276893319)
XLA Ops:
  6.5 0.8 copy.16
  7.6 0.7 broadcast_multiply_fusion
  8.3 1.1 reduce-window.6
  9.4 0.2 slice_reduce_fusion
  10.0 2.4 %scatter_custom_fusion = s32[1024]{0:T(1024)S(1)} fusion(s32[512]{0:T(512)S(1)} %bitcast.41, s32[512]{0:T(512)S(1)} %iota.17, s32[]{:T(128)} %constant.46.clone.1), kind=kCustom, calls=%fused_computation.38 | custom fusion | bytes 4100 | tf_op jit(solution)/shard_map/scatter | solution.py:43
  12.5 1.1 concatenate.3
  13.6 6.0 %gather_fusion = bf16[1024,2048]{1,0:T(8,128)(2,1)} fusion(bf16[129,2048]{1,0:T(8,128)(2,1)S(1)} %concatenate.3, s32[1024]{0:T(1024)S(1)} %fusion.18), kind=kCustom, calls=%fused_computation | custom fusion | bytes 8392704 | tf_op jit(solution)/shard_map/gather | solution.py:47
  19.6 7.3 %all-to-all-start = ((bf16[8,128,2048]{2,1,0:T(8,128)(2,1)}), bf16[8,128,2048]{2,1,0:T(8,128)(2,1)}, u32[]{:S(2)}, u32[]{:S(2)}) async-start(bf16[8,128,2048]{2,1,0:T(8,128)(2,1)} %bitcast.37), calls=%async_computation | async-start | bytes 8388608 | tf_op jit(solution)/shard_map/all_to_all | solution.py:48
  26.9 0.7 all-gather.7.cloned.1.call-update
  27.6 0.7 all-gather.9.cloned.1.call-update
  28.4 0.7 all-gather.11.cloned.1.call-update
  29.1 11.4 %all-gather.7.cloned.1.call-done = bf16[1,2048,384]{1,2,0:T(8,128)(2,1)} async-done(((bf16[1,2048,192]{1,2,0:T(8,128)(2,1)}), bf16[1,2048,384]{1,2,0:T(8,128)(2,1)}) %all-gather.7.cloned.1.call-update) | async-done | bytes 1572880 | tf_op jit(solution)/shard_map/all_gather | solution.py:52
  40.5 79.6 %all-to-all-done = bf16[8,128,2048]{2,1,0:T(8,128)(2,1)} async-done(((bf16[8,128,2048]{2,1,0:T(8,128)(2,1)}), bf16[8,128,2048]{2,1,0:T(8,128)(2,1)}, u32[]{:S(2)}, u32[]{:S(2)}) %all-to-all-start) | async-done | bytes 4194336 | tf_op jit(solution)/shard_map/all_to_all | solution.py:48
  120.1 5.0 %fusion.8 = f32[1024,384]{1,0:T(8,128)S(1)} fusion(bf16[1024,2048]{1,0:T(8,128)(2,1)} %bitcast.5, bf16[1,2048,384]{1,2,0:T(8,128)(2,1)} %all-gather.7.cloned.1.call-done), kind=kOutput, calls=%fused_computation.10 | convolution fusion | flops 1610612736 | bytes 7340032 | tf_op jit(solution)/shard_map/dot_general | solution.py:50
  125.2 5.1 %multiply_convert_fusion = bf16[1024,384]{1,0:T(8,128)(2,1)S(1)} fusion(f32[1024,384]{1,0:T(8,128)S(1)} %fusion.8, bf16[1024,2048]{1,0:T(8,128)(2,1)} %bitcast.5, bf16[1,2048,384]{1,2,0:T(8,128)(2,1)} %all-gather.9.cloned.1.call-done), kind=kOutput, calls=%fused_computation.12 | convolution fusion | flops 1612972032 | bytes 8126464 | tf_op jit(solution)/shard_map/dot_general | solution.py:55
  130.4 5.7 %fusion = f32[1024,128]{1,0:T(8,128)} fusion(bf16[2048,128]{1,0:T(8,128)(2,1)S(1)} %copy-done, bf16[1024,384]{1,0:T(8,128)(2,1)S(1)} %multiply_convert_fusion, bf16[1,2048,384]{1,2,0:T(8,128)(2,1)} %all-gather.11.cloned.1.call-done), kind=kOutput, calls=%fused_computation.3 | convolution fusion | flops 2149580800 | bytes 3407872 | tf_op jit(solution)/shard_map/dot_general | solution.py:69
  136.1 3.6 %all-to-all-start.1 = ((f32[8,128,128]{2,1,0:T(8,128)}), f32[8,128,128]{2,1,0:T(8,128)S(1)}, u32[]{:S(2)}, u32[]{:S(2)}) async-start(f32[8,128,128]{2,1,0:T(8,128)} %bitcast.9), calls=%async_computation.1 | async-start | bytes 1048576 | tf_op jit(solution)/shard_map/all_to_all | solution.py:70
  140.0 13.5 %all_gather.15 = bf16[64,32,128]{2,1,0:T(8,128)(2,1)S(1)} all-gather(bf16[32,32,128]{2,1,0:T(8,128)(2,1)S(1)} %copy-done.2), channel_id=1, replica_groups=mesh['group'=2,'expert'=4,'query'=2,'dp'=2] {'query'}, dimensions={0}, use_global_device_ids=true | all-gather | bytes 786432 | tf_op jit(solution)/shard_map/all_gather | solution.py:86
  153.6 0.8 all-to-all-done.1
  154.4 1.0 gather_fusion.1
  155.4 0.2 multiply_reduce_fusion
  155.8 0.4 multiply_reduce_fusion.1
  156.2 0.4 bitcast_reduce_fusion
  156.6 0.7 reduce_sum.42
  (34 shorter events, 1.2 us)
Async XLA Ops:
  6.5 123.9 %copy-start = (bf16[2048,128]{1,0:T(8,128)(2,1)S(1)}, bf16[2048,128]{1,0:T(8,128)(2,1)}, u32[]{:S(2)}) copy-start(bf16[2048,128]{1,0:T(8,128)(2,1)} %param.16) | copy-start | bytes 1572868
  19.6 100.5 %all-to-all-start = ((bf16[8,128,2048]{2,1,0:T(8,128)(2,1)}), bf16[8,128,2048]{2,1,0:T(8,128)(2,1)}, u32[]{:S(2)}, u32[]{:S(2)}) async-start(bf16[8,128,2048]{2,1,0:T(8,128)(2,1)} %bitcast.37), calls=%async_computation | async-start | bytes 8388608 | tf_op jit(solution)/shard_map/all_to_all | solution.py:48
  26.9 13.6 %all-gather.7.cloned.1.call-start = ((), (), s32[]{:S(2)}) async-start(), calls=%async_computation.2 | async-start | bytes 2359296 | tf_op jit(solution)/shard_map/all_gather | solution.py:52
  27.6 97.6 %all-gather.9.cloned.1.call-start = ((), (), s32[]{:S(2)}) async-start(), calls=%async_computation.3 | async-start | bytes 2359296 | tf_op jit(solution)/shard_map/all_gather | solution.py:57
  28.3 102.0 %all-gather.11.cloned.1.call-start = ((), (), s32[]{:S(2)}) async-start(), calls=%async_computation.4 | async-start | bytes 2359296 | tf_op jit(solution)/shard_map/all_gather | solution.py:63
  130.3 9.4 %copy-start.3 = (f32[128,4]{0,1:T(4,128)S(1)}, f32[128,4]{0,1:T(4,128)}, u32[]{:S(2)}) copy-start(f32[128,4]{0,1:T(4,128)} %param.11) | copy-start | bytes 6148
  130.3 9.5 %copy-start.4 = (s32[2]{0:T(128)S(1)}, s32[2]{0:T(128)}, u32[]{:S(2)}) copy-start(s32[2]{0:T(128)} %param.12) | copy-start | bytes 28
  130.3 9.7 %copy-start.2 = (bf16[32,32,128]{2,1,0:T(8,128)(2,1)S(1)}, bf16[32,32,128]{2,1,0:T(8,128)(2,1)}, u32[]{:S(2)}) copy-start(bf16[32,32,128]{2,1,0:T(8,128)(2,1)} %param.17) | copy-start | bytes 786436
  136.1 18.3 %all-to-all-start.1 = ((f32[8,128,128]{2,1,0:T(8,128)}), f32[8,128,128]{2,1,0:T(8,128)S(1)}, u32[]{:S(2)}, u32[]{:S(2)}) async-start(f32[8,128,128]{2,1,0:T(8,128)} %bitcast.9), calls=%async_computation.1 | async-start | bytes 1048576 | tf_op jit(solution)/shard_map/all_to_all | solution.py:70
  153.6 2.2 %copy-start.1 = (bf16[128,2048]{1,0:T(8,128)(2,1)S(1)}, bf16[128,2048]{1,0:T(8,128)(2,1)}, u32[]{:S(2)}) copy-start(bf16[128,2048]{1,0:T(8,128)(2,1)} %param.9) | copy-start | bytes 1572868
Sparse Core Ops, SparseCore 0:
  29.2 11.2 all-gather.6
  42.0 10.9 all-gather.8
  54.6 10.9 all-gather.10
where the time goes:
time: 164 us
  waiting for transfers between devices  94 us (57%)
  matrix products  16.6 us (10%)
  blocking collectives  13.5 us (8%)
  between operations  13.3 us (8%)
  local copies, waits for them, and re-layouts  12.6 us (8%)
  starting transfers between devices  11 us (7%)
  other arithmetic  2.88 us (2%)
    all_to_all x1, waiting for transfers between devices, on_device(): lax.all_to_all(outgoing, ('expert', 'query'), split_axis=0, concat_axis=0...  79.6 us
    all_gather x1, blocking collectives, on_device(): lax.all_gather(queries, 'query', axis=0, tiled=True)  13.5 us
    all_gather x1, waiting for transfers between devices, on_device(): lax.all_gather(gate_weight[0], 'dp', axis=1, tiled=True)  11.4 us
    all_to_all x1, starting transfers between devices, on_device(): lax.all_to_all(outgoing, ('expert', 'query'), split_axis=0, concat_axis=0...  7.25 us
    gather x1, local copies, waits for them, and re-layouts, on_device(): outgoing = padded[source_row].reshape(experts, capacity, model_width)  6.03 us
    dot_general x1, matrix products, on_device(): folded = jnp.dot(results, proj_weight, preferred_element_type=jnp.float32)  5.7 us
    dot_general x1, matrix products, on_device(): jnp.dot(expert_rows, lax.all_gather(up_weight[0], 'dp', axis=1, tiled=Tru...  5.12 us
    dot_general x1, matrix products, on_device(): jnp.dot(expert_rows, lax.all_gather(gate_weight[0], 'dp', axis=1, tiled=T...  5.02 us
  transfers between devices with their start and end apart: 5, of which 3 were waited for; matrix products, arithmetic and copies ran while one was open for 6% of the time, Pallas kernels for 0%

commit v1 on v0

v1 whole, which is shorter than its diff:
```python
import jax
import jax.numpy as jnp
from jax import lax
from jax.sharding import PartitionSpec as P

PLEN = 64
G, E, Q, D = "group", "expert", "query", "dp"


def matched(embedding, live_mask, block_queries):
    query_rows = block_queries.reshape(-1, block_queries.shape[-1])
    raw_scores = jnp.dot(embedding, query_rows.T, preferred_element_type=jnp.float32)
    raw_scores = jnp.where(live_mask[:, None], raw_scores, -jnp.inf)
    best_match = jnp.max(raw_scores.reshape(-1, PLEN, raw_scores.shape[-1]), axis=1)
    return jnp.sum(best_match.reshape(best_match.shape[0], -1, block_queries.shape[1]), axis=-1)


def embedded(projected):
    lengths_norm = jnp.sqrt(jnp.sum(projected * projected, axis=-1, keepdims=True) + 1e-06)
    return (projected / lengths_norm).astype(jnp.bfloat16)


def live_tokens(passage_lengths, tok_rows):
    position = jnp.arange(tok_rows, dtype=jnp.int32) % PLEN
    return position < jnp.repeat(passage_lengths, PLEN)


def by_dispatch(
    tokens, route_ids, gate_values, passage_lengths, gate_weight, up_weight, down_weight, proj_weight, queries
):
    tok_rows, model_width = tokens.shape
    top_count = route_ids.shape[1]
    experts = lax.axis_size(E) * lax.axis_size(Q)
    capacity = max(2, 2 * tok_rows * top_count // experts)
    assignments = tok_rows * top_count
    flat_routes = route_ids.reshape(-1)
    one_hot = flat_routes[:, None] == jnp.arange(experts, dtype=jnp.int32)[None, :]
    order = jnp.arange(assignments, dtype=jnp.int32)
    before = (order[None, :] < order[:, None]).astype(jnp.bfloat16)
    earlier = jnp.dot(before, one_hot.astype(jnp.bfloat16), preferred_element_type=jnp.float32)
    slot_index = jnp.sum(jnp.where(one_hot, earlier, 0.0), axis=1).astype(jnp.int32)
    slot_target = flat_routes * capacity + slot_index
    slot_owner = jnp.full((experts * capacity,), assignments, jnp.int32).at[slot_target].set(order)
    padded = jnp.concatenate([tokens, jnp.zeros((1, model_width), tokens.dtype)], axis=0)
    source_row = jnp.where(slot_owner < assignments, slot_owner // top_count, tok_rows)
    outgoing = padded[source_row].reshape(experts, capacity, model_width)
    arrived = lax.all_to_all(outgoing, (E, Q), split_axis=0, concat_axis=0, tiled=True)
    expert_rows = arrived.reshape(experts * capacity, model_width)
    gate_act = jnp.dot(
        expert_rows, lax.all_gather(gate_weight[0], D, axis=1, tiled=True), preferred_element_type=jnp.float32
    )
    up_act = jnp.dot(
        expert_rows, lax.all_gather(up_weight[0], D, axis=1, tiled=True), preferred_element_type=jnp.float32
    )
    hidden = (jax.nn.silu(gate_act) * up_act).astype(jnp.bfloat16)
    results = lax.dot_general(
        hidden,
        lax.all_gather(down_weight[0], D, axis=1, tiled=True),
        (((1,), (1,)), ((), ())),
        preferred_element_type=jnp.float32,
    ).astype(jnp.bfloat16)
    folded = jnp.dot(results, proj_weight, preferred_element_type=jnp.float32)
    returned_rows = lax.all_to_all(
        folded.reshape(experts, capacity, folded.shape[-1]), (E, Q), split_axis=0, concat_axis=0, tiled=True
    )
    picked = returned_rows.reshape(experts * capacity, folded.shape[-1])[slot_target]
    weights = gate_values.reshape(assignments, 1)
    projected = jnp.dot(tokens, proj_weight, preferred_element_type=jnp.float32) + jnp.sum(
        (picked * weights).reshape(tok_rows, top_count, folded.shape[-1]), axis=1
    )
    live_mask = live_tokens(passage_lengths, tok_rows)
    return matched(embedded(projected), live_mask, lax.all_gather(queries, Q, axis=0, tiled=True))


def hi_lo(values):
    high = values.astype(jnp.bfloat16)
    return high, (values - high.astype(jnp.float32)).astype(jnp.bfloat16)


def by_column(
    tokens, route_ids, gate_values, passage_lengths, gate_weight, up_weight, down_weight, proj_weight, queries
):
    tok_rows, model_width = tokens.shape
    hidden_part = gate_weight.shape[2]
    proj_width = proj_weight.shape[1]
    z, x, y, core = (lax.axis_index(a) for a in (E, Q, G, D))
    swap = [(0, 1), (1, 0)]
    ends, middle = [(1, 0), (2, 3)], [(1, 2), (2, 1)]

    near = lax.ppermute(tokens, E, [(i, i ^ 1) for i in range(4)])
    across = lax.ppermute(tokens, E, middle)
    far_inner = lax.ppermute(near, E, middle)
    end_two = lax.ppermute(across, E, ends)
    end_three = lax.ppermute(far_inner, E, ends)
    at_end = (z == 0) | (z == 3)

    folded = lax.dot_general(
        proj_weight, down_weight[0], (((0,), (0,)), ((), ())), preferred_element_type=jnp.float32
    )
    own = jnp.concatenate(
        [jnp.concatenate([gate_weight[0], up_weight[0]], axis=1), jnp.concatenate(hi_lo(folded), axis=1)], axis=0
    )
    half = own.shape[0] // 2
    mine = lax.dynamic_slice_in_dim(own, y * half, half, 0)
    half_x = lax.ppermute(mine, Q, swap)
    half_y = lax.ppermute(half_x, G, swap)
    own_pair = lax.ppermute(own, D, swap)
    pair_x = lax.ppermute(half_x, D, swap)
    pair_y = lax.ppermute(half_y, D, swap)

    def joined(here, there):
        return jnp.concatenate([jnp.where(y == 0, here, there), jnp.where(y == 0, there, here)], axis=0)

    other, other_pair = joined(half_x, half_y), joined(pair_x, pair_y)

    def through(rows, weights):
        act = jnp.dot(rows, weights[:model_width], preferred_element_type=jnp.float32)
        gate_act, up_act = act[:, :hidden_part], act[:, hidden_part:]
        hidden = (jax.nn.silu(gate_act) * up_act).astype(jnp.bfloat16)
        back = weights[model_width:]
        return sum(
            lax.dot_general(hidden, part, (((1,), (1,)), ((), ())), preferred_element_type=jnp.float32)
            for part in (back[:, :hidden_part], back[:, hidden_part:])
        )

    def results(rows):
        return jnp.concatenate(
            [through(rows, own) + through(rows, own_pair), through(rows, other) + through(rows, other_pair)], axis=1
        )

    blocks = [tokens, near, jnp.where(at_end, end_two, far_inner), jnp.where(at_end, end_three, across)]
    total = jnp.dot(tokens, proj_weight, preferred_element_type=jnp.float32)
    for k, rows in enumerate(blocks):
        got = results(rows)
        if k:
            got = lax.ppermute(got.astype(jnp.bfloat16), E, [(i, i ^ k) for i in range(4)]).astype(jnp.float32)
        for which in (0, 1):
            expert = (z ^ k) * 2 + (x ^ which)
            weight = jnp.sum(jnp.where(route_ids == expert, gate_values, 0.0), axis=1, keepdims=True)
            total = total + weight * got[:, which * proj_width : (which + 1) * proj_width]
    embedding = embedded(total)
    live_mask = live_tokens(passage_lengths, tok_rows)
    here = matched(embedding, live_mask, queries)
    there = matched(embedding, live_mask, lax.ppermute(queries, Q, swap))
    return jnp.where(x == 0, jnp.concatenate([here, there], axis=1), jnp.concatenate([there, here], axis=1))


def solution(mesh):
    in_specs = (
        P((G, E, Q, D), None),
        P((G, E, Q, D), None),
        P((G, E, Q, D), None),
        P((G, E, Q, D)),
        P((E, Q), None, D),
        P((E, Q), None, D),
        P((E, Q), None, D),
        P(),
        P((G, Q), None, None),
    )
    sizes = [mesh.shape[a] for a in (G, E, Q, D)]
    return jax.shard_map(
        by_column if sizes == [2, 4, 2, 2] else by_dispatch,
        mesh=mesh,
        in_specs=in_specs,
        out_specs=P((G, E, Q, D), None),
        check_vma=False,
    )
```

time: 164 us -> 104 us (0.63)
  waiting for transfers between devices: 94 us -> 29.2 us
  matrix products: 16.6 us -> 41.8 us
  blocking collectives: 13.5 us -> 0 us
  between operations: 13.3 us -> 0.79 us
  local copies, waits for them, and re-layouts: 12.6 us -> 4.59 us
  starting transfers between devices: 11 us -> 18.4 us
  other arithmetic: 2.88 us -> 7.7 us
    all_to_all x2 -> x0, waiting for transfers between devices: 80.5 us -> none  [the longest x1 79.6 us: on_device(): lax.all_to_all(outgoing, ('expert', 'query'), split_axis=0, concat_axis=0...]
    ppermute x0 -> x14, waiting for transfers between devices: none -> 29.2 us  [the longest x1 12.9 us: by_column(): end_three = lax.ppermute(far_inner, E, ends)]
    dot_general x5 -> x52, matrix products: 16.6 us -> 41.8 us  [the longest x16 23.2 us: through(): jnp.dot(rows, weights[:model_width], preferred_element_type=jnp.float32)]
    ppermute x0 -> x14, starting transfers between devices: none -> 18.4 us  [the longest x1 5.08 us: by_column(): near = lax.ppermute(tokens, E, [(i, i ^ 1) for i in range(4)])]
    all_gather x1 -> x0, blocking collectives: 13.5 us -> none  [on_device(): lax.all_gather(queries, 'query', axis=0, tiled=True)]
    all_gather x3 -> x0, waiting for transfers between devices: 11.5 us -> none  [the longest x1 11.4 us: on_device(): lax.all_gather(gate_weight[0], 'dp', axis=1, tiled=True)]
    all_to_all x2 -> x0, starting transfers between devices: 10.9 us -> none  [the longest x1 7.25 us: on_device(): lax.all_to_all(outgoing, ('expert', 'query'), split_axis=0, concat_axis=0...]
    gather x2 -> x0, local copies, waits for them, and re-layouts: 7.05 us -> none  [the longest x1 6.03 us: on_device(): outgoing = padded[source_row].reshape(experts, capacity, model_width)]
  transfers between devices with their start and end apart: 5 -> 14, of which waited for: 3 -> 6; matrix products, arithmetic and copies ran while one was open for 6% -> 50% of each run, Pallas kernels for 0% -> 0%
where the time goes in v1:
time: 104 us; the launch traced here: 102 us
  matrix products  41.8 us (40%)
  waiting for transfers between devices  29.2 us (28%)
  starting transfers between devices  18.4 us (18%)
  other arithmetic  7.7 us (7%)
  local copies, waits for them, and re-layouts  4.59 us (4%)
    dot_general x16, matrix products, through(): jnp.dot(rows, weights[:model_width], preferred_element_type=jnp.float32)  23.2 us
    dot_general x32, matrix products, through(): lax.dot_general(hidden, part, (((1,), (1,)), ((), ())), preferred_element...  14.2 us
    ppermute x1, waiting for transfers between devices, by_column(): end_three = lax.ppermute(far_inner, E, ends)  12.9 us
    ppermute x1, waiting for transfers between devices, by_column(): half_x = lax.ppermute(mine, Q, swap)  7.14 us
    ppermute x1, starting transfers between devices, by_column(): near = lax.ppermute(tokens, E, [(i, i ^ 1) for i in range(4)])  5.08 us
    ppermute x3, starting transfers between devices, by_column(): lax.ppermute(got.astype(jnp.bfloat16), E, [(i, i ^ k) for i in range(4)])  4.58 us
    ppermute x1, waiting for transfers between devices, by_column(): end_two = lax.ppermute(across, E, ends)  4.46 us
    ppermute x3, waiting for transfers between devices, by_column(): lax.ppermute(got.astype(jnp.bfloat16), E, [(i, i ^ k) for i in range(4)])  4.03 us
  transfers between devices with their start and end apart: 14, of which 6 were waited for; matrix products, arithmetic and copies ran while one was open for 50% of the time, Pallas kernels for 0%

profile of v1, /device:TPU:0, one launch (start us, length us, event | category | flops | bytes accessed | tf_op | source)
XLA Modules:
  0.0 102.4 jit_solution(3102159386927789002)
XLA Ops:
  0.0 1.6 %collective-permute-start.7 = (bf16[128,2048]{1,0:T(8,128)(2,1)}, bf16[128,2048]{1,0:T(8,128)(2,1)}, u32[]{:S(2)}, u32[]{:S(2)}) collective-permute-start(bf16[128,2048]{1,0:T(8,128)(2,1)} %param.9), channel_id=1, source_target_pairs={{4,8},{8,4},{5,9},{9,5},{6,10},{10,6},{7,11},{11,7},{20,24},{24,20... | collective-permute-start | bytes 1572872 | tf_op jit(solution)/shard_map/ppermute | solution.py:91
  1.6 5.1 %collective-permute-start.5 = (bf16[128,2048]{1,0:T(8,128)(2,1)}, bf16[128,2048]{1,0:T(8,128)(2,1)}, u32[]{:S(2)}, u32[]{:S(2)}) collective-permute-start(bf16[128,2048]{1,0:T(8,128)(2,1)} %param.9), channel_id=1, source_target_pairs={{0,4},{4,0},{8,12},{12,8},{1,5},{5,1},{9,13},{13,9},{2,6},{6,2},{1... | collective-permute-start | bytes 1572872 | tf_op jit(solution)/shard_map/ppermute | solution.py:90
  6.7 1.5 %collective-permute-start.13 = (bf16[32,32,128]{2,1,0:T(8,128)(2,1)}, bf16[32,32,128]{2,1,0:T(8,128)(2,1)}, u32[]{:S(2)}, u32[]{:S(2)}) collective-permute-start(bf16[32,32,128]{2,1,0:T(8,128)(2,1)} %param.17), channel_id=1, source_target_pairs={{0,2},{2,0},{1,3},{3,1},{4,6},{6,4},{5,7},{7,5},{8,10},{10,8},{9,1... | collective-permute-start | bytes 786440 | tf_op jit(solution)/shard_map/ppermute | solution.py:144
  8.2 1.4 %subtract_convert_fusion = (bf16[128,192]{0,1:T(8,128)(2,1)S(1)}, bf16[128,192]{0,1:T(8,128)(2,1)S(1)}) fusion(bf16[2048,128]{1,0:T(8,128)(2,1)} %param.16, bf16[1,2048,192]{1,2,0:T(8,128)(2,1)S(1)} %copy-done), kind=kOutput, calls=%fused_computation.103 | convolution fusion | flops 100761600 | bytes 1409024 | tf_op jit(solution)/shard_map/dot_general | solution.py:97
  10.3 1.4 %copy.46 = bf16[1,2048,192]{2,1,0:T(8,128)(2,1)S(1)} copy(bf16[1,2048,192]{1,2,0:T(8,128)(2,1)} %param.14) | data formatting | bytes 1572864 | tf_op args[5]
  11.7 1.8 %pad_maximum_fusion = bf16[2176,384]{1,0:T(8,128)(2,1)} fusion(bf16[128,384]{1,0:T(8,128)(2,1)S(1)} %copy.47, bf16[2048,192]{1,0:T(8,128)(2,1)S(1)} %bitcast.95, bf16[2048,192]{1,0:T(8,128)(2,1)S(1)} %bitcast.90), kind=kLoop, calls=%fused_computation | loop fusion | flops 5013504 | bytes 3342336 | tf_op jit(solution)/shard_map/concatenate | solution.py:100
  13.5 2.1 %constant_dynamic-slice_fusion = bf16[1088,384]{1,0:T(8,128)(2,1)} fusion(bf16[2176,384]{1,0:T(8,128)(2,1)} %pad_maximum_fusion, s32[]{:T(128)S(6)} %select_n.91), kind=kLoop, calls=%fused_computation.163 | loop fusion | bytes 1671172 | tf_op jit(solution)/shard_map/dynamic_slice | solution.py:104
  16.2 2.8 %convolution_bitcast_fusion.7 = f32[128,384]{0,1:T(8,128)} fusion(bf16[128,2048]{1,0:T(8,128)(2,1)} %param.9, bf16[2048,192]{1,0:T(8,128)(2,1)S(1)} %bitcast.96, bf16[2048,192]{1,0:T(8,128)(2,1)S(1)} %bitcast.91), kind=kOutput, calls=%fused_computation.13 | convolution fusion | flops 204472320 | bytes 2293760 | tf_op jit(solution)/shard_map/dot_general | solution.py:117
  27.3 2.1 %convolution_bitcast_fusion.3 = f32[128,384]{0,1:T(8,128)S(1)} fusion(bf16[128,2048]{1,0:T(8,128)(2,1)} %collective-permute-done.5, bf16[2048,192]{1,0:T(8,128)(2,1)S(1)} %bitcast.97, bf16[2048,192]{1,0:T(8,128)(2,1)S(1)} %bitcast.92), kind=kOutput, calls=%fused_computation.9 | convolution fusion | flops 204472320 | bytes 2293760 | tf_op jit(solution)/shard_map/dot_general | solution.py:117
  29.8 7.1 %collective-permute-done.1 = bf16[1088,384]{1,0:T(8,128)(2,1)} collective-permute-done((bf16[1088,384]{1,0:T(8,128)(2,1)}, bf16[1088,384]{1,0:T(8,128)(2,1)}, u32[]{:S(2)}, u32[]{:S(2)}) %collective-permute-start.1) | collective-permute-done | bytes 835616 | tf_op jit(solution)/shard_map/ppermute | solution.py:105
  37.0 4.5 %collective-permute-done.8 = bf16[128,2048]{1,0:T(8,128)(2,1)S(1)} collective-permute-done((bf16[128,2048]{1,0:T(8,128)(2,1)}, bf16[128,2048]{1,0:T(8,128)(2,1)S(1)}, u32[]{:S(2)}, u32[]{:S(2)}) %collective-permute-start.8) | collective-permute-done | bytes 524320 | tf_op jit(solution)/shard_map/ppermute | solution.py:93
  41.4 1.5 %collective-permute-start.2 = (bf16[1088,384]{1,0:T(8,128)(2,1)}, bf16[1088,384]{1,0:T(8,128)(2,1)S(1)}, u32[]{:S(2)}, u32[]{:S(2)}) collective-permute-start(bf16[1088,384]{1,0:T(8,128)(2,1)} %collective-permute-done.1), channel_id=1, source_target_pairs={{0,16},{16,0},{1,17},{17,1},{2,18},{18,2},{3,19},{19,3},{4,20},{20... | collective-permute-start | bytes 2506760 | tf_op jit(solution)/shard_map/ppermute | solution.py:106
  44.3 1.5 %collective-permute-start.11 = (bf16[128,2048]{1,0:T(8,128)(2,1)S(1)}, bf16[128,2048]{1,0:T(8,128)(2,1)S(1)}, u32[]{:S(2)}, u32[]{:S(2)}) collective-permute-start(bf16[128,2048]{1,0:T(8,128)(2,1)S(1)} %collective-permute-done.9), channel_id=1, source_target_pairs={{4,0},{8,12},{5,1},{9,13},{6,2},{10,14},{7,3},{11,15},{20,16},{24,... | collective-permute-start | bytes 1572872 | tf_op jit(solution)/shard_map/ppermute | solution.py:94
  46.2 12.9 %collective-permute-done.11 = bf16[128,2048]{1,0:T(8,128)(2,1)S(1)} collective-permute-done((bf16[128,2048]{1,0:T(8,128)(2,1)S(1)}, bf16[128,2048]{1,0:T(8,128)(2,1)S(1)}, u32[]{:S(2)}, u32[]{:S(2)}) %collective-permute-start.11) | collective-permute-done | bytes 524320 | tf_op jit(solution)/shard_map/ppermute | solution.py:94
  65.2 1.7 %convolution_bitcast_fusion.1 = f32[128,384]{0,1:T(8,128)S(1)} fusion(bf16[128,2048]{1,0:T(8,128)(2,1)} %collective-permute-done.5, bf16[1088,384]{1,0:T(8,128)(2,1)S(1)} %get-tuple-element.18, bf16[1088,384]{1,0:T(8,128)(2,1)S(1)} %get-tuple-element.17), kind=kOutput, calls=%fused_computation.7 | convolution fusion | flops 204472320 | bytes 2392064 | tf_op jit(solution)/shard_map/dot_general | solution.py:117
  68.3 2.1 %fusion.24 = f32[128,384]{0,1:T(8,128)S(1)} fusion(bf16[128,2048]{1,0:T(8,128)(2,1)S(1)} %broadcast_select_fusion.4, bf16[2176,384]{1,0:T(8,128)(2,1)} %collective-permute-done), kind=kOutput, calls=%fused_computation.54 | convolution fusion | flops 201326592 | bytes 2293760 | tf_op jit(solution)/shard_map/dot_general | solution.py:117
  70.5 2.1 %fusion.26 = f32[128,384]{0,1:T(8,128)S(1)} fusion(bf16[128,2048]{1,0:T(8,128)(2,1)S(1)} %broadcast_select_fusion.5, bf16[2176,384]{1,0:T(8,128)(2,1)} %collective-permute-done), kind=kOutput, calls=%fused_computation.56 | convolution fusion | flops 201326592 | bytes 2293760 | tf_op jit(solution)/shard_map/dot_general | solution.py:117
  72.7 2.1 %convolution_bitcast_fusion.2 = f32[128,384]{0,1:T(8,128)S(1)} fusion(bf16[128,2048]{1,0:T(8,128)(2,1)} %collective-permute-done.5, bf16[2176,384]{1,0:T(8,128)(2,1)} %collective-permute-done), kind=kOutput, calls=%fused_computation.8 | convolution fusion | flops 201326592 | bytes 2293760 | tf_op jit(solution)/shard_map/dot_general | solution.py:117
  74.9 2.0 %convolution_bitcast_fusion.6 = f32[128,384]{0,1:T(8,128)S(1)} fusion(bf16[128,2048]{1,0:T(8,128)(2,1)S(1)} %copy-done.3, bf16[2176,384]{1,0:T(8,128)(2,1)} %collective-permute-done), kind=kOutput, calls=%fused_computation.12 | convolution fusion | flops 201326592 | bytes 2293760 | tf_op jit(solution)/shard_map/dot_general | solution.py:117
  87.6 1.7 %convolution_bitcast_fusion = f32[128,384]{0,1:T(8,128)S(1)} fusion(bf16[128,2048]{1,0:T(8,128)(2,1)} %collective-permute-done.5, bf16[1088,384]{1,0:T(8,128)(2,1)S(1)} %get-tuple-element.16, bf16[1088,384]{1,0:T(8,128)(2,1)S(1)} %get-tuple-element.15), kind=kOutput, calls=%fused_computation.6 | convolution fusion | flops 204472320 | bytes 2392064 | tf_op jit(solution)/shard_map/dot_general | solution.py:117
  90.3 1.4 %collective-permute-start.12 = (bf16[128,256]{0,1:T(8,128)(2,1)S(1)}, bf16[128,256]{0,1:T(8,128)(2,1)S(1)}, u32[]{:S(2)}, u32[]{:S(2)}) collective-permute-start(bf16[128,256]{0,1:T(8,128)(2,1)S(1)} %pad_maximum_fusion.7), channel_id=1, source_target_pairs={{0,12},{4,8},{8,4},{12,0},{1,13},{5,9},{9,5},{13,1},{2,14},{6,10},... | collective-permute-start | bytes 196616 | tf_op jit(solution)/shard_map/ppermute | solution.py:136
  92.3 3.0 %collective-permute-start.6 = (bf16[128,256]{0,1:T(8,128)(2,1)S(1)}, bf16[128,256]{0,1:T(8,128)(2,1)S(1)}, u32[]{:S(2)}, u32[]{:S(2)}) collective-permute-start(bf16[128,256]{0,1:T(8,128)(2,1)S(1)} %pad_maximum_fusion.5), channel_id=1, source_target_pairs={{0,4},{4,0},{8,12},{12,8},{1,5},{5,1},{9,13},{13,9},{2,6},{6,2},{1... | collective-permute-start | bytes 196616 | tf_op jit(solution)/shard_map/ppermute | solution.py:136
  95.4 1.7 %collective-permute-done.12 = bf16[128,256]{0,1:T(8,128)(2,1)S(1)} collective-permute-done((bf16[128,256]{0,1:T(8,128)(2,1)S(1)}, bf16[128,256]{0,1:T(8,128)(2,1)S(1)}, u32[]{:S(2)}, u32[]{:S(2)}) %collective-permute-start.12) | collective-permute-done | bytes 65568 | tf_op jit(solution)/shard_map/ppermute | solution.py:136
  97.2 2.3 %collective-permute-done.10 = bf16[128,256]{0,1:T(8,128)(2,1)S(1)} collective-permute-done((bf16[128,256]{0,1:T(8,128)(2,1)S(1)}, bf16[128,256]{0,1:T(8,128)(2,1)S(1)}, u32[]{:S(2)}, u32[]{:S(2)}) %collective-permute-start.10) | collective-permute-done | bytes 65568 | tf_op jit(solution)/shard_map/ppermute | solution.py:136
  (128 shorter events, 34.1 us)
Async XLA Ops:
  0.0 9.7 %copy-start.2 = (bf16[1,2048,192]{1,2,0:T(8,128)(2,1)S(1)}, bf16[1,2048,192]{1,2,0:T(8,128)(2,1)}, u32[]{:S(2)}) copy-start(bf16[1,2048,192]{1,2,0:T(8,128)(2,1)} %param.13) | copy-start | bytes 2359300
  0.0 25.3 %collective-permute-start.7 = (bf16[128,2048]{1,0:T(8,128)(2,1)}, bf16[128,2048]{1,0:T(8,128)(2,1)}, u32[]{:S(2)}, u32[]{:S(2)}) collective-permute-start(bf16[128,2048]{1,0:T(8,128)(2,1)} %param.9), channel_id=1, source_target_pairs={{4,8},{8,4},{5,9},{9,5},{6,10},{10,6},{7,11},{11,7},{20,24},{24,20... | collective-permute-start | bytes 1572872 | tf_op jit(solution)/shard_map/ppermute | solution.py:91
  1.6 25.0 %collective-permute-start.5 = (bf16[128,2048]{1,0:T(8,128)(2,1)}, bf16[128,2048]{1,0:T(8,128)(2,1)}, u32[]{:S(2)}, u32[]{:S(2)}) collective-permute-start(bf16[128,2048]{1,0:T(8,128)(2,1)} %param.9), channel_id=1, source_target_pairs={{0,4},{4,0},{8,12},{12,8},{1,5},{5,1},{9,13},{13,9},{2,6},{6,2},{1... | collective-permute-start | bytes 1572872 | tf_op jit(solution)/shard_map/ppermute | solution.py:90
  6.7 93.1 %collective-permute-start.13 = (bf16[32,32,128]{2,1,0:T(8,128)(2,1)}, bf16[32,32,128]{2,1,0:T(8,128)(2,1)}, u32[]{:S(2)}, u32[]{:S(2)}) collective-permute-start(bf16[32,32,128]{2,1,0:T(8,128)(2,1)} %param.17), channel_id=1, source_target_pairs={{0,2},{2,0},{1,3},{3,1},{4,6},{6,4},{5,7},{7,5},{8,10},{10,8},{9,1... | collective-permute-start | bytes 786440 | tf_op jit(solution)/shard_map/ppermute | solution.py:144
  13.5 54.8 %collective-permute-start = (bf16[2176,384]{1,0:T(8,128)(2,1)}, bf16[2176,384]{1,0:T(8,128)(2,1)}, u32[]{:S(2)}, u32[]{:S(2)}) collective-permute-start(bf16[2176,384]{1,0:T(8,128)(2,1)} %pad_maximum_fusion), channel_id=1, source_target_pairs={{0,1},{1,0},{2,3},{3,2},{4,5},{5,4},{6,7},{7,6},{8,9},{9,8},{10,11... | collective-permute-start | bytes 5013512 | tf_op jit(solution)/shard_map/ppermute | solution.py:107
  15.7 21.3 %collective-permute-start.1 = (bf16[1088,384]{1,0:T(8,128)(2,1)}, bf16[1088,384]{1,0:T(8,128)(2,1)}, u32[]{:S(2)}, u32[]{:S(2)}) collective-permute-start(bf16[1088,384]{1,0:T(8,128)(2,1)} %constant_dynamic-slice_fusion), channel_id=1, source_target_pairs={{0,2},{2,0},{1,3},{3,1},{4,6},{6,4},{5,7},{7,5},{8,10},{10,8},{9,1... | collective-permute-start | bytes 2506760 | tf_op jit(solution)/shard_map/ppermute | solution.py:105
  25.3 16.2 %collective-permute-start.8 = (bf16[128,2048]{1,0:T(8,128)(2,1)}, bf16[128,2048]{1,0:T(8,128)(2,1)S(1)}, u32[]{:S(2)}, u32[]{:S(2)}) collective-permute-start(bf16[128,2048]{1,0:T(8,128)(2,1)} %collective-permute-done.7), channel_id=1, source_target_pairs={{4,0},{8,12},{5,1},{9,13},{6,2},{10,14},{7,3},{11,15},{20,16},{24,... | collective-permute-start | bytes 1572872 | tf_op jit(solution)/shard_map/ppermute | solution.py:93
  26.6 16.4 %collective-permute-start.9 = (bf16[128,2048]{1,0:T(8,128)(2,1)}, bf16[128,2048]{1,0:T(8,128)(2,1)S(1)}, u32[]{:S(2)}, u32[]{:S(2)}) collective-permute-start(bf16[128,2048]{1,0:T(8,128)(2,1)} %collective-permute-done.5), channel_id=1, source_target_pairs={{4,8},{8,4},{5,9},{9,5},{6,10},{10,6},{7,11},{11,7},{20,24},{24,20... | collective-permute-start | bytes 1572872 | tf_op jit(solution)/shard_map/ppermute | solution.py:92
  37.0 48.3 %collective-permute-start.3 = (bf16[1088,384]{1,0:T(8,128)(2,1)}, bf16[1088,384]{1,0:T(8,128)(2,1)S(1)}, u32[]{:S(2)}, u32[]{:S(2)}) collective-permute-start(bf16[1088,384]{1,0:T(8,128)(2,1)} %collective-permute-done.1), channel_id=1, source_target_pairs={{0,1},{1,0},{2,3},{3,2},{4,5},{5,4},{6,7},{7,6},{8,9},{9,8},{10,11... | collective-permute-start | bytes 2506760 | tf_op jit(solution)/shard_map/ppermute | solution.py:108
  41.4 20.1 %collective-permute-start.2 = (bf16[1088,384]{1,0:T(8,128)(2,1)}, bf16[1088,384]{1,0:T(8,128)(2,1)S(1)}, u32[]{:S(2)}, u32[]{:S(2)}) collective-permute-start(bf16[1088,384]{1,0:T(8,128)(2,1)} %collective-permute-done.1), channel_id=1, source_target_pairs={{0,16},{16,0},{1,17},{17,1},{2,18},{18,2},{3,19},{19,3},{4,20},{20... | collective-permute-start | bytes 2506760 | tf_op jit(solution)/shard_map/ppermute | solution.py:106
  44.3 14.8 %collective-permute-start.11 = (bf16[128,2048]{1,0:T(8,128)(2,1)S(1)}, bf16[128,2048]{1,0:T(8,128)(2,1)S(1)}, u32[]{:S(2)}, u32[]{:S(2)}) collective-permute-start(bf16[128,2048]{1,0:T(8,128)(2,1)S(1)} %collective-permute-done.9), channel_id=1, source_target_pairs={{4,0},{8,12},{5,1},{9,13},{6,2},{10,14},{7,3},{11,15},{20,16},{24,... | collective-permute-start | bytes 1572872 | tf_op jit(solution)/shard_map/ppermute | solution.py:94
  77.0 8.3 %collective-permute-start.4 = (bf16[1088,384]{1,0:T(8,128)(2,1)S(1)}, bf16[1088,384]{1,0:T(8,128)(2,1)S(1)}, u32[]{:S(2)}, u32[]{:S(2)}) collective-permute-start(bf16[1088,384]{1,0:T(8,128)(2,1)S(1)} %collective-permute-done.2), channel_id=1, source_target_pairs={{0,1},{1,0},{2,3},{3,2},{4,5},{5,4},{6,7},{7,6},{8,9},{9,8},{10,11... | collective-permute-start | bytes 2506760 | tf_op jit(solution)/shard_map/ppermute | solution.py:109
  89.3 10.3 %copy-start.4 = (f32[128]{0:T(128)S(1)}, f32[128]{0:T(128)}, u32[]{:S(2)}) copy-start(f32[128]{0:T(128)} %get-tuple-element.5) | copy-start | bytes 1540
  89.3 10.3 %copy-start.5 = (f32[128]{0:T(128)S(1)}, f32[128]{0:T(128)}, u32[]{:S(2)}) copy-start(f32[128]{0:T(128)} %get-tuple-element.6) | copy-start | bytes 1540
  89.3 10.3 %copy-start.6 = (f32[128]{0:T(128)S(1)}, f32[128]{0:T(128)}, u32[]{:S(2)}) copy-start(f32[128]{0:T(128)} %get-tuple-element.7) | copy-start | bytes 1540
  89.3 10.3 %copy-start.7 = (f32[128]{0:T(128)S(1)}, f32[128]{0:T(128)}, u32[]{:S(2)}) copy-start(f32[128]{0:T(128)} %get-tuple-element.8) | copy-start | bytes 1540
  89.3 10.3 %copy-start.8 = (f32[128]{0:T(128)S(1)}, f32[128]{0:T(128)}, u32[]{:S(2)}) copy-start(f32[128]{0:T(128)} %get-tuple-element.9) | copy-start | bytes 1540
  89.3 10.3 %copy-start.9 = (f32[128]{0:T(128)S(1)}, f32[128]{0:T(128)}, u32[]{:S(2)}) copy-start(f32[128]{0:T(128)} %get-tuple-element.11) | copy-start | bytes 1540
  89.3 10.3 %copy-start.10 = (f32[128]{0:T(128)S(1)}, f32[128]{0:T(128)}, u32[]{:S(2)}) copy-start(f32[128]{0:T(128)} %get-tuple-element.12) | copy-start | bytes 1540
  89.6 10.2 %copy-start.14 = (pred[128]{0:T(512)(128)(4,1)S(1)}, pred[128]{0:T(512)(128)(4,1)}, u32[]{:S(2)}) copy-start(pred[128]{0:T(512)(128)(4,1)} %fusion.84) | copy-start | bytes 388
  90.1 10.9 %copy-start.12 = (bf16[32,32,128]{2,1,0:T(8,128)(2,1)S(1)}, bf16[32,32,128]{2,1,0:T(8,128)(2,1)}, u32[]{:S(2)}) copy-start(bf16[32,32,128]{2,1,0:T(8,128)(2,1)} %param.17) | copy-start | bytes 786436
  90.3 6.9 %collective-permute-start.12 = (bf16[128,256]{0,1:T(8,128)(2,1)S(1)}, bf16[128,256]{0,1:T(8,128)(2,1)S(1)}, u32[]{:S(2)}, u32[]{:S(2)}) collective-permute-start(bf16[128,256]{0,1:T(8,128)(2,1)S(1)} %pad_maximum_fusion.7), channel_id=1, source_target_pairs={{0,12},{4,8},{8,4},{12,0},{1,13},{5,9},{9,5},{13,1},{2,14},{6,10},... | collective-permute-start | bytes 196616 | tf_op jit(solution)/shard_map/ppermute | solution.py:136
  91.9 7.6 %collective-permute-start.10 = (bf16[128,256]{0,1:T(8,128)(2,1)S(1)}, bf16[128,256]{0,1:T(8,128)(2,1)S(1)}, u32[]{:S(2)}, u32[]{:S(2)}) collective-permute-start(bf16[128,256]{0,1:T(8,128)(2,1)S(1)} %pad_maximum_fusion.6), channel_id=1, source_target_pairs={{0,8},{4,12},{8,0},{12,4},{1,9},{5,13},{9,1},{13,5},{2,10},{6,14},... | collective-permute-start | bytes 196616 | tf_op jit(solution)/shard_map/ppermute | solution.py:136
  92.3 7.2 %collective-permute-start.6 = (bf16[128,256]{0,1:T(8,128)(2,1)S(1)}, bf16[128,256]{0,1:T(8,128)(2,1)S(1)}, u32[]{:S(2)}, u32[]{:S(2)}) collective-permute-start(bf16[128,256]{0,1:T(8,128)(2,1)S(1)} %pad_maximum_fusion.5), channel_id=1, source_target_pairs={{0,4},{4,0},{8,12},{12,8},{1,5},{5,1},{9,13},{13,9},{2,6},{6,2},{1... | collective-permute-start | bytes 196616 | tf_op jit(solution)/shard_map/ppermute | solution.py:136
  (5 other events, 30.0 us)

commit v2 on v1

--- a/solution.py
+++ b/solution.py
@@ -1,6 +1,8 @@
 import jax
 import jax.numpy as jnp
 from jax import lax
+from jax.experimental import pallas as pl
+from jax.experimental.pallas import tpu as pltpu
 from jax.sharding import PartitionSpec as P
 
 PLEN = 64
@@ -72,77 +74,218 @@
     return matched(embedded(projected), live_mask, lax.all_gather(queries, Q, axis=0, tiled=True))
 
 
-def hi_lo(values):
-    high = values.astype(jnp.bfloat16)
-    return high, (values - high.astype(jnp.float32)).astype(jnp.bfloat16)
+VMEM = pl.BlockSpec(memory_space=pltpu.VMEM)
+SMEM = pl.BlockSpec(memory_space=pltpu.SMEM)
+NT, TN = (((1,), (1,)), ((), ())), (((0,), (0,)), ((), ()))
+
+
+def dot(a, b, dims=(((1,), (0,)), ((), ()))):
+    return lax.dot_general(a, b, dims, preferred_element_type=jnp.float32)
+
+
+def kernel(body, operands, outs, flops, smem=()):
+    moved = sum(a.size * a.dtype.itemsize for a in operands)
+    return pl.pallas_call(
+        body,
+        out_shape=[jax.ShapeDtypeStruct(shape, dtype) for shape, dtype in outs],
+        in_specs=[SMEM if i in smem else VMEM for i in range(len(operands))],
+        out_specs=[VMEM] * len(outs),
+        compiler_params=pltpu.CompilerParams(vmem_limit_bytes=24 * 2**20),
+        cost_estimate=pl.CostEstimate(flops=int(flops), bytes_accessed=int(moved), transcendentals=0),
+    )(*operands)
+
+
+FOLD = 16
+
+
+def pack_body(tokens, gate, up, down, proj, pack, half, base):
+    rows = gate.shape[0]
+    width = proj.shape[1]
+    pack[:rows, :] = gate[...]
+    pack[rows : 2 * rows, :] = up[...]
+    folded = dot(down[...], proj[...])
+    high = folded.astype(jnp.bfloat16)
+    low = (folded - high.astype(jnp.float32)).astype(jnp.bfloat16)
+    pack[2 * rows :, :] = jnp.zeros((2 * FOLD, pack.shape[1]), jnp.bfloat16)
+    for i in range(rows // FOLD):
+        pack[2 * rows : 2 * rows + FOLD, i * width : (i + 1) * width] = high[i * FOLD : (i + 1) * FOLD]
+        pack[2 * rows + FOLD :, i * width : (i + 1) * width] = low[i * FOLD : (i + 1) * FOLD]
+    part = half.shape[0]
+    for y in range(2):
+
+        @pl.when(lax.axis_index(G) == y)
+        def _():
+            half[...] = pack[y * part : (y + 1) * part, :]
+
+    base[...] = dot(tokens[...], proj[...]).T
+
+
+def folded_parts(tile, rows, width):
+    return [
+        jnp.concatenate([tile[k * FOLD : (k + 1) * FOLD, i * width : (i + 1) * width] for i in range(rows // FOLD)], axis=0)
+        for k in range(2)
+    ]
+
+
+def finish(act, tile, width):
+    rows = act.shape[0] // 2
+    gate_act, up_act = act[:rows], act[rows:]
+    hidden = (gate_act / (1.0 + jnp.exp(-gate_act)) * up_act).astype(jnp.bfloat16)
+    return sum(dot(part, hidden, TN) for part in folded_parts(tile, rows, width))
+
+
+def through_whole(x, packs, width):
+    total = None
+    for pack in packs:
+        rows = pack.shape[0] - 2 * FOLD
+        part = finish(dot(pack[:rows, :], x, NT), pack[rows:, :], width)
+        total = part if total is None else total + part
+    return total
+
+
+def through_halves(x, halves, width):
+    first = lax.axis_index(G) == 0
+    total = None
+    for mine, others in halves:
+        a, b = dot(mine[...], x, NT), dot(others[...], x, NT)
+        rows = mine.shape[0]
+        act = jnp.concatenate([jnp.where(first, a, b), jnp.where(first, b, a)[: rows - 2 * FOLD]], axis=0)
+        tile = jnp.where(first, others[rows - 2 * FOLD :, :], mine[rows - 2 * FOLD :, :])
+        part = finish(act, tile, width)
+        total = part if total is None else total + part
+    return total
+
+
+def at_end():
+    z = lax.axis_index(E)
+    return (z == 0) | (z == lax.axis_size(E) - 1)
+
+
+def first_body(tokens, near, own, pair, here, back):
+    width = here.shape[0]
+    x = jnp.concatenate([tokens[...], near[...]], axis=0)
+    got = through_whole(x, (own, pair), width)
+    here[...] = got[:, : tokens.shape[0]]
+    back[...] = got[:, tokens.shape[0] :].astype(back.dtype)
+
+
+def second_body(tokens, near, end_two, far_inner, own, pair, ox, oy, px, py, here, back_near, back_two):
+    width = here.shape[0]
+    n = tokens.shape[0]
+    two = jnp.where(at_end(), end_two[...], far_inner[...])
+    back_two[:width, :] = through_whole(two, (own, pair), width).astype(back_two.dtype)
+    x = jnp.concatenate([tokens[...], near[...], two], axis=0)
+    got = through_halves(x, ((ox, oy), (px, py)), width)
+    here[...] = got[:, :n]
+    back_near[...] = got[:, n : 2 * n].astype(back_near.dtype)
+    back_two[width:, :] = got[:, 2 * n :].astype(back_two.dtype)
+
+
+def third_body(end_three, across, own, pair, ox, oy, px, py, back_three):
+    width = back_three.shape[0] // 2
+    three = jnp.where(at_end(), end_three[...], across[...])
+    back_three[:width, :] = through_whole(three, (own, pair), width).astype(back_three.dtype)
+    back_three[width:, :] = through_halves(three, ((ox, oy), (px, py)), width).astype(back_three.dtype)
+
+
+def score_body(lengths, base, here, here_other, near, near_other, two, three, routes, gates, queries, others, scores):
+    z, x = lax.axis_index(E), lax.axis_index(Q)
+    width, tokens = base.shape
+    total = base[...]
+    route, gate = routes[...], gates[...]
+    sent = [
+        (here[...], here_other[...]),
+        (near[...], near_other[...]),
+        (two[:width, :], two[width:, :]),
+        (three[:width, :], three[width:, :]),
+    ]
+    for k, pair in enumerate(sent):
+        for which in (0, 1):
+            expert = (z ^ k) * 2 + (x ^ which)
+            weight = jnp.sum(jnp.where(route == expert, gate, 0.0), axis=0, keepdims=True)
+            total = total + weight * pair[which].astype(jnp.float32)
+    norm = jnp.sqrt(jnp.sum(total * total, axis=0, keepdims=True) + 1e-06)
+    embedding = (total / norm).T.astype(jnp.bfloat16)
+    count, span = queries.shape[0], queries.shape[0] * 2 // scores.shape[1]
+    query_at = lax.broadcasted_iota(jnp.int32, (count, scores.shape[1]), 0) // span
+    column = lax.broadcasted_iota(jnp.int32, (count, scores.shape[1]), 1)
+    result = jnp.zeros(scores.shape, jnp.float32)
+    for which, block in ((0, queries), (1, others)):
+        raw = dot(embedding, block[...], NT)
+        best = []
+        for p in range(tokens // PLEN):
+            live = lax.broadcasted_iota(jnp.int32, (PLEN, count), 0) < lengths[p]
+            best.append(
+                jnp.max(jnp.where(live, raw[p * PLEN : (p + 1) * PLEN], -jnp.inf), axis=0, keepdims=True)
+            )
+        chosen = (column == query_at + (x ^ which) * (count // span)).astype(jnp.float32)
+        result = result + lax.dot_general(
+            jnp.concatenate(best, axis=0), chosen, (((1,), (0,)), ((), ())),
+            precision=lax.Precision.HIGHEST, preferred_element_type=jnp.float32,
+        )
+    scores[...] = result
 
 
 def by_column(
     tokens, route_ids, gate_values, passage_lengths, gate_weight, up_weight, down_weight, proj_weight, queries
 ):
-    tok_rows, model_width = tokens.shape
+    n, model_width = tokens.shape
     hidden_part = gate_weight.shape[2]
-    proj_width = proj_weight.shape[1]
-    z, x, y, core = (lax.axis_index(a) for a in (E, Q, G, D))
+    width = proj_weight.shape[1]
     swap = [(0, 1), (1, 0)]
     ends, middle = [(1, 0), (2, 3)], [(1, 2), (2, 1)]
+    f32, bf16 = jnp.float32, jnp.bfloat16
 
     near = lax.ppermute(tokens, E, [(i, i ^ 1) for i in range(4)])
     across = lax.ppermute(tokens, E, middle)
     far_inner = lax.ppermute(near, E, middle)
     end_two = lax.ppermute(across, E, ends)
     end_three = lax.ppermute(far_inner, E, ends)
-    at_end = (z == 0) | (z == 3)
-
-    folded = lax.dot_general(
-        proj_weight, down_weight[0], (((0,), (0,)), ((), ())), preferred_element_type=jnp.float32
-    )
-    own = jnp.concatenate(
-        [jnp.concatenate([gate_weight[0], up_weight[0]], axis=1), jnp.concatenate(hi_lo(folded), axis=1)], axis=0
-    )
-    half = own.shape[0] // 2
-    mine = lax.dynamic_slice_in_dim(own, y * half, half, 0)
-    half_x = lax.ppermute(mine, Q, swap)
+
+    pack_rows = 2 * hidden_part + 2 * FOLD
+    own, half, base = kernel(
+        pack_body,
+        [tokens, gate_weight[0].T, up_weight[0].T, down_weight[0].T, proj_weight],
+        [((pack_rows, model_width), bf16), ((pack_rows // 2, model_width), bf16), ((width, n), f32)],
+        2 * (hidden_part + n) * model_width * width,
+    )
+    pair = lax.ppermute(own, D, swap)
+    half_x = lax.ppermute(half, Q, swap)
     half_y = lax.ppermute(half_x, G, swap)
-    own_pair = lax.ppermute(own, D, swap)
     pair_x = lax.ppermute(half_x, D, swap)
     pair_y = lax.ppermute(half_y, D, swap)
-
-    def joined(here, there):
-        return jnp.concatenate([jnp.where(y == 0, here, there), jnp.where(y == 0, there, here)], axis=0)
-
-    other, other_pair = joined(half_x, half_y), joined(pair_x, pair_y)
-
-    def through(rows, weights):
-        act = jnp.dot(rows, weights[:model_width], preferred_element_type=jnp.float32)
-        gate_act, up_act = act[:, :hidden_part], act[:, hidden_part:]
-        hidden = (jax.nn.silu(gate_act) * up_act).astype(jnp.bfloat16)
-        back = weights[model_width:]
-        return sum(
-            lax.dot_general(hidden, part, (((1,), (1,)), ((), ())), preferred_element_type=jnp.float32)
-            for part in (back[:, :hidden_part], back[:, hidden_part:])
-        )
-
-    def results(rows):
-        return jnp.concatenate(
-            [through(rows, own) + through(rows, own_pair), through(rows, other) + through(rows, other_pair)], axis=1
-        )
-
-    blocks = [tokens, near, jnp.where(at_end, end_two, far_inner), jnp.where(at_end, end_three, across)]
-    total = jnp.dot(tokens, proj_weight, preferred_element_type=jnp.float32)
-    for k, rows in enumerate(blocks):
-        got = results(rows)
-        if k:
-            got = lax.ppermute(got.astype(jnp.bfloat16), E, [(i, i ^ k) for i in range(4)]).astype(jnp.float32)
-        for which in (0, 1):
-            expert = (z ^ k) * 2 + (x ^ which)
-            weight = jnp.sum(jnp.where(route_ids == expert, gate_values, 0.0), axis=1, keepdims=True)
-            total = total + weight * got[:, which * proj_width : (which + 1) * proj_width]
-    embedding = embedded(total)
-    live_mask = live_tokens(passage_lengths, tok_rows)
-    here = matched(embedding, live_mask, queries)
-    there = matched(embedding, live_mask, lax.ppermute(queries, Q, swap))
-    return jnp.where(x == 0, jnp.concatenate([here, there], axis=1), jnp.concatenate([there, here], axis=1))
+    other_queries = lax.ppermute(queries, Q, swap)
+
+    work = 2 * n * model_width * 4 * hidden_part
+    here, back_near = kernel(
+        first_body, [tokens, near, own, pair], [((width, n), f32), ((width, n), bf16)], 2 * work
+    )
+    other = [half_x, half_y, pair_x, pair_y]
+    here_other, back_near_other, back_two = kernel(
+        second_body,
+        [tokens, near, end_two, far_inner, own, pair, *other],
+        [((width, n), f32), ((width, n), bf16), ((2 * width, n), bf16)],
+        4 * work,
+    )
+    (back_three,) = kernel(
+        third_body, [end_three, across, own, pair, *other], [((2 * width, n), bf16)], 2 * work
+    )
+    from_near, from_near_other, two, three = (
+        lax.ppermute(a, E, [(i, i ^ k) for i in range(4)])
+        for a, k in ((back_near, 1), (back_near_other, 1), (back_two, 2), (back_three, 3))
+    )
+    rows = queries.shape[0] * queries.shape[1]
+    (scores,) = kernel(
+        score_body,
+        [
+            passage_lengths, base, here, here_other, from_near, from_near_other, two, three,
+            route_ids.T, gate_values.T, queries.reshape(rows, width), other_queries.reshape(rows, width),
+        ],
+        [((n // PLEN, 2 * queries.shape[0]), f32)],
+        4 * n * width * rows,
+        smem=(0,),
+    )
+    return scores
 
 
 def solution(mesh):

time: 104 us -> 93.4 us (0.90); the launches traced: 102 us -> 93 us
  matrix products: 41.8 us -> 0 us
  waiting for transfers between devices: 29.2 us -> 55.1 us
  Pallas kernels: 0 us -> 13 us
  other arithmetic: 7.7 us -> 0 us
    dot_general x52 -> x0, matrix products: 41.8 us -> none  [the longest x16 23.2 us: through(): jnp.dot(rows, weights[:model_width], preferred_element_type=jnp.float32)]
    pallas_call x0 -> x5, Pallas kernels: none -> 13 us  [kernel(): pl.pallas_call(body, out_shape=[jax.ShapeDtypeStruct(shape, dtype) for sh...]
    ppermute x1, waiting for transfers between devices: 0.01 us -> 10.2 us  [by_column(): near = lax.ppermute(tokens, E, [(i, i ^ 1) for i in range(4)])]
    ppermute x6 -> x7, waiting for transfers between devices: 11.2 us -> 21.2 us  [the longest x1 18.9 us: by_column(): half_x = lax.ppermute(half, Q, swap)]
    ppermute x1, waiting for transfers between devices: 4.46 us -> 14 us  [by_column(): end_two = lax.ppermute(across, E, ends)]
    ppermute x1, waiting for transfers between devices: 12.9 us -> 4.6 us  [by_column(): end_three = lax.ppermute(far_inner, E, ends)]
    ppermute x6 -> x7, starting transfers between devices: 6.62 us -> 11.9 us  [the longest x4 7.45 us: by_column(): lax.ppermute(a, E, [(i, i ^ k) for i in range(4)])]
    ppermute x1, waiting for transfers between devices: 0.64 us -> 5.06 us  [by_column(): half_y = lax.ppermute(half_x, G, swap)]
  transfers between devices with their start and end apart: 14 -> 15, of which waited for: 6 -> 7; matrix products, arithmetic and copies ran while one was open for 50% -> 0% of each run, Pallas kernels for 0% -> 11%
where the time goes in v2:
time: 93.4 us; the launch traced here: 93 us
  waiting for transfers between devices  55.1 us (59%)
  starting transfers between devices  19.2 us (21%)
  Pallas kernels  13 us (14%)
  local copies, waits for them, and re-layouts  5.5 us (6%)
    ppermute x1, waiting for transfers between devices, by_column(): half_x = lax.ppermute(half, Q, swap)  18.9 us
    ppermute x1, waiting for transfers between devices, by_column(): end_two = lax.ppermute(across, E, ends)  14 us
    pallas_call x5, Pallas kernels, kernel(): pl.pallas_call(body, out_shape=[jax.ShapeDtypeStruct(shape, dtype) for sh...  13 us
    ppermute x1, waiting for transfers between devices, by_column(): near = lax.ppermute(tokens, E, [(i, i ^ 1) for i in range(4)])  10.2 us
    ppermute x4, starting transfers between devices, by_column(): lax.ppermute(a, E, [(i, i ^ k) for i in range(4)])  7.45 us
    unnamed x18, local copies, waits for them, and re-layouts  5.5 us
    ppermute x1, waiting for transfers between devices, by_column(): half_y = lax.ppermute(half_x, G, swap)  5.06 us
    ppermute x1, waiting for transfers between devices, by_column(): end_three = lax.ppermute(far_inner, E, ends)  4.6 us
  transfers between devices with their start and end apart: 15, of which 7 were waited for; matrix products, arithmetic and copies ran while one was open for 0% of the time, Pallas kernels for 11%

profile of v2, /device:TPU:0, one launch (start us, length us, event | category | flops | bytes accessed | tf_op | source)
XLA Modules:
  0.0 93.0 jit_solution(15149946534258717450)
XLA Ops:
  0.0 1.0 %copy-done = bf16[128,2048]{1,0:T(8,128)(2,1)S(1)} copy-done((bf16[128,2048]{1,0:T(8,128)(2,1)S(1)}, bf16[128,2048]{1,0:T(8,128)(2,1)}, u32[]{:S(2)}) %copy-start) | copy-done | bytes 524312
  1.0 1.1 %copy-done.1 = bf16[1,2048,192]{1,2,0:T(8,128)(2,1)S(1)} copy-done((bf16[1,2048,192]{1,2,0:T(8,128)(2,1)S(1)}, bf16[1,2048,192]{1,2,0:T(8,128)(2,1)}, u32[]{:S(2)}) %copy-start.1) | copy-done | bytes 786456
  2.2 1.1 %copy-done.2 = bf16[1,2048,192]{1,2,0:T(8,128)(2,1)S(1)} copy-done((bf16[1,2048,192]{1,2,0:T(8,128)(2,1)S(1)}, bf16[1,2048,192]{1,2,0:T(8,128)(2,1)}, u32[]{:S(2)}) %copy-start.2) | copy-done | bytes 786456
  3.3 1.1 %copy-done.3 = bf16[1,2048,192]{1,2,0:T(8,128)(2,1)S(1)} copy-done((bf16[1,2048,192]{1,2,0:T(8,128)(2,1)S(1)}, bf16[1,2048,192]{1,2,0:T(8,128)(2,1)}, u32[]{:S(2)}) %copy-start.3) | copy-done | bytes 786456
  4.4 1.0 %copy-done.4 = bf16[2048,128]{1,0:T(8,128)(2,1)S(1)} copy-done((bf16[2048,128]{1,0:T(8,128)(2,1)S(1)}, bf16[2048,128]{1,0:T(8,128)(2,1)}, u32[]{:S(2)}) %copy-start.4) | copy-done | bytes 524312
  6.3 3.0 %collective-permute-start.5 = (bf16[208,2048]{1,0:T(8,128)(2,1)S(1)}, bf16[208,2048]{1,0:T(8,128)(2,1)S(1)}, u32[]{:S(2)}, u32[]{:S(2)}) collective-permute-start(bf16[208,2048]{1,0:T(8,128)(2,1)S(1)} %get-tuple-element.16), channel_id=1, source_target_pairs={{0,2},{2,0},{1,3},{3,1},{4,6},{6,4},{5,7},{7,5},{8,10},{10,8},{9,1... | collective-permute-start | bytes 2555912 | tf_op jit(solution)/shard_map/ppermute | solution.py:253
  9.4 18.9 %collective-permute-done.5.ox = bf16[208,2048]{1,0:T(8,128)(2,1)S(1)} collective-permute-done((bf16[208,2048]{1,0:T(8,128)(2,1)S(1)}, bf16[208,2048]{1,0:T(8,128)(2,1)S(1)}, u32[]{:S(2)}, u32[]{:S(2)}) %collective-permute-start.5) | collective-permute-done | bytes 852000 | tf_op jit(solution)/shard_map/ppermute | solution.py:253
  28.3 1.8 %collective-permute-start.6 = (bf16[208,2048]{1,0:T(8,128)(2,1)S(1)}, bf16[208,2048]{1,0:T(8,128)(2,1)S(1)}, u32[]{:S(2)}, u32[]{:S(2)}) collective-permute-start(bf16[208,2048]{1,0:T(8,128)(2,1)S(1)} %collective-permute-done.5.ox), channel_id=1, source_target_pairs={{0,16},{16,0},{1,17},{17,1},{2,18},{18,2},{3,19},{19,3},{4,20},{20... | collective-permute-start | bytes 2555912 | tf_op jit(solution)/shard_map/ppermute | solution.py:254
  30.1 1.6 %collective-permute-start = (bf16[128,2048]{1,0:T(8,128)(2,1)S(1)}, bf16[128,2048]{1,0:T(8,128)(2,1)S(1)}, u32[]{:S(2)}, u32[]{:S(2)}) collective-permute-start(bf16[128,2048]{1,0:T(8,128)(2,1)S(1)} %copy-done), channel_id=1, source_target_pairs={{0,4},{4,0},{8,12},{12,8},{1,5},{5,1},{9,13},{13,9},{2,6},{6,2},{1... | collective-permute-start | bytes 1572872 | tf_op jit(solution)/shard_map/ppermute | solution.py:239
  32.3 10.2 %collective-permute-done.near = bf16[128,2048]{1,0:T(8,128)(2,1)S(1)} collective-permute-done((bf16[128,2048]{1,0:T(8,128)(2,1)S(1)}, bf16[128,2048]{1,0:T(8,128)(2,1)S(1)}, u32[]{:S(2)}, u32[]{:S(2)}) %collective-permute-start) | collective-permute-done | bytes 524320 | tf_op jit(solution)/shard_map/ppermute | solution.py:239
  43.4 5.1 %collective-permute-done.6.oy = bf16[208,2048]{1,0:T(8,128)(2,1)S(1)} collective-permute-done((bf16[208,2048]{1,0:T(8,128)(2,1)S(1)}, bf16[208,2048]{1,0:T(8,128)(2,1)S(1)}, u32[]{:S(2)}, u32[]{:S(2)}) %collective-permute-start.6) | collective-permute-done | bytes 852000 | tf_op jit(solution)/shard_map/ppermute | solution.py:254
  48.4 1.3 %collective-permute-start.3 = (bf16[128,2048]{1,0:T(8,128)(2,1)S(1)}, bf16[128,2048]{1,0:T(8,128)(2,1)S(1)}, u32[]{:S(2)}, u32[]{:S(2)}) collective-permute-start(bf16[128,2048]{1,0:T(8,128)(2,1)S(1)} %collective-permute-done.2.across), channel_id=1, source_target_pairs={{4,0},{8,12},{5,1},{9,13},{6,2},{10,14},{7,3},{11,15},{20,16},{24,... | collective-permute-start | bytes 1572872 | tf_op jit(solution)/shard_map/ppermute | solution.py:242
  49.7 1.3 %collective-permute-start.12 = (bf16[128,2048]{1,0:T(8,128)(2,1)S(1)}, bf16[128,2048]{1,0:T(8,128)(2,1)S(1)}, u32[]{:S(2)}, u32[]{:S(2)}) collective-permute-start(bf16[128,2048]{1,0:T(8,128)(2,1)S(1)} %collective-permute-done.4.far_inner), channel_id=1, source_target_pairs={{4,0},{8,12},{5,1},{9,13},{6,2},{10,14},{7,3},{11,15},{20,16},{24,... | collective-permute-start | bytes 1572872 | tf_op jit(solution)/shard_map/ppermute | solution.py:243
  51.0 14.0 %collective-permute-done.3.end_two = bf16[128,2048]{1,0:T(8,128)(2,1)S(1)} collective-permute-done((bf16[128,2048]{1,0:T(8,128)(2,1)S(1)}, bf16[128,2048]{1,0:T(8,128)(2,1)S(1)}, u32[]{:S(2)}, u32[]{:S(2)}) %collective-permute-start.3) | collective-permute-done | bytes 524320 | tf_op jit(solution)/shard_map/ppermute | solution.py:242
  65.0 1.4 %collective-permute-start.14 = (bf16[32,32,128]{2,1,0:T(8,128)(2,1)S(1)}, bf16[32,32,128]{2,1,0:T(8,128)(2,1)S(1)}, u32[]{:S(2)}, u32[]{:S(2)}) collective-permute-start(bf16[32,32,128]{2,1,0:T(8,128)(2,1)S(1)} %copy-done.5), channel_id=1, source_target_pairs={{0,2},{2,0},{1,3},{3,1},{4,6},{6,4},{5,7},{7,5},{8,10},{10,8},{9,1... | collective-permute-start | bytes 786440 | tf_op jit(solution)/shard_map/ppermute | solution.py:257
  66.5 4.5 %shard_map.93 = (f32[128,128]{1,0:T(8,128)S(1)}, bf16[128,128]{1,0:T(8,128)(2,1)S(1)}, bf16[256,128]{1,0:T(8,128)(2,1)S(1)}) custom-call(bf16[128,2048]{1,0:T(8,128)(2,1)S(1)} %copy-done, bf16[128,2048]{1,0:T(8,128)(2,1)S(1)} %collective-permute-done.near, bf16[128,2048]{1,0:T(8,128)(2,1)S(1)} %collective-permute-done.3.end_two, ...), custom_call_target="tpu_custom_call" | custom-call | flops 1610612736 | bytes 8912896 | tf_op jit(solution)/shard_map/pallas_call | solution.py:88
  70.9 1.8 %collective-permute-start.11 = (bf16[256,128]{1,0:T(8,128)(2,1)S(1)}, bf16[256,128]{1,0:T(8,128)(2,1)S(1)}, u32[]{:S(2)}, u32[]{:S(2)}) collective-permute-start(bf16[256,128]{1,0:T(8,128)(2,1)S(1)} %get-tuple-element.20), channel_id=1, source_target_pairs={{0,8},{4,12},{8,0},{12,4},{1,9},{5,13},{9,1},{13,5},{2,10},{6,14},... | collective-permute-start | bytes 196616 | tf_op jit(solution)/shard_map/ppermute | solution.py:274
  72.7 4.6 %collective-permute-done.12.end_three = bf16[128,2048]{1,0:T(8,128)(2,1)S(1)} collective-permute-done((bf16[128,2048]{1,0:T(8,128)(2,1)S(1)}, bf16[128,2048]{1,0:T(8,128)(2,1)S(1)}, u32[]{:S(2)}, u32[]{:S(2)}) %collective-permute-start.12) | collective-permute-done | bytes 524320 | tf_op jit(solution)/shard_map/ppermute | solution.py:243
  77.3 3.4 %shard_map.94 = bf16[256,128]{1,0:T(8,128)(2,1)S(1)} custom-call(bf16[128,2048]{1,0:T(8,128)(2,1)S(1)} %collective-permute-done.12.end_three, bf16[128,2048]{1,0:T(8,128)(2,1)S(1)} %collective-permute-done.2.across, bf16[416,2048]{1,0:T(8,128)(2,1)S(1)} %get-tuple-element.14.own, bf16[416,2048]{1,0:T(8,128)(2,1)S(1)} %collective-permute-done.1.pair, ...), custom_call_target="tpu_custom_call" | custom-call | flops 805306368 | bytes 7864320 | tf_op jit(solution)/shard_map/pallas_call | solution.py:88
  80.8 3.6 %collective-permute-start.13 = (bf16[256,128]{1,0:T(8,128)(2,1)S(1)}, bf16[256,128]{1,0:T(8,128)(2,1)S(1)}, u32[]{:S(2)}, u32[]{:S(2)}) collective-permute-start(bf16[256,128]{1,0:T(8,128)(2,1)S(1)} %shard_map.94), channel_id=1, source_target_pairs={{0,12},{4,8},{8,4},{12,0},{1,13},{5,9},{9,5},{13,1},{2,14},{6,10},... | collective-permute-start | bytes 196616 | tf_op jit(solution)/shard_map/ppermute | solution.py:274
  84.4 2.1 %shard_map.92 = (f32[128,128]{1,0:T(8,128)S(1)}, bf16[128,128]{1,0:T(8,128)(2,1)S(1)}) custom-call(bf16[128,2048]{1,0:T(8,128)(2,1)S(1)} %copy-done, bf16[128,2048]{1,0:T(8,128)(2,1)S(1)} %collective-permute-done.near, bf16[416,2048]{1,0:T(8,128)(2,1)S(1)} %get-tuple-element.14.own, bf16[416,2048]{1,0:T(8,128)(2,1)S(1)} %collective-permute-done.1.pair), custom_call_target="tpu_custom_call" | custom-call | flops 805306368 | bytes 4456448 | tf_op jit(solution)/shard_map/pallas_call | solution.py:88
  86.6 2.0 %collective-permute-start.10 = (bf16[128,128]{1,0:T(8,128)(2,1)S(1)}, bf16[128,128]{1,0:T(8,128)(2,1)S(1)}, u32[]{:S(2)}, u32[]{:S(2)}) collective-permute-start(bf16[128,128]{1,0:T(8,128)(2,1)S(1)} %get-tuple-element.19), channel_id=1, source_target_pairs={{0,4},{4,0},{8,12},{12,8},{1,5},{5,1},{9,13},{13,9},{2,6},{6,2},{1... | collective-permute-start | bytes 98312 | tf_op jit(solution)/shard_map/ppermute | solution.py:274
  88.6 1.9 %collective-permute-done.9.near = bf16[128,128]{1,0:T(8,128)(2,1)S(1)} collective-permute-done((bf16[128,128]{1,0:T(8,128)(2,1)S(1)}, bf16[128,128]{1,0:T(8,128)(2,1)S(1)}, u32[]{:S(2)}, u32[]{:S(2)}) %collective-permute-start.9) | collective-permute-done | bytes 32800 | tf_op jit(solution)/shard_map/ppermute | solution.py:274
  90.9 2.1 %shard_map.95 = f32[2,64]{1,0:T(2,128)} custom-call(s32[2]{0:T(128)S(1)} %copy-done.8, f32[128,128]{1,0:T(8,128)S(1)} %get-tuple-element.13.base, f32[128,128]{1,0:T(8,128)S(1)} %get-tuple-element.15.here, f32[128,128]{1,0:T(8,128)S(1)} %get-tuple-element.17.here_other, bf16[128,128]{1,0:T(8,128)(2,1)S(1)} %collective-permute-done.9.near, ...), custom_call_target="tpu_custom_call" | custom-call | flops 67108864 | bytes 921608 | tf_op jit(solution)/shard_map/pallas_call | solution.py:88
  (29 shorter events, 2.8 us)
Async XLA Ops:
  0.0 1.0 %copy-start = (bf16[128,2048]{1,0:T(8,128)(2,1)S(1)}, bf16[128,2048]{1,0:T(8,128)(2,1)}, u32[]{:S(2)}) copy-start(bf16[128,2048]{1,0:T(8,128)(2,1)} %tokens.5) | copy-start | bytes 1572868
  1.0 1.1 %copy-start.1 = (bf16[1,2048,192]{1,2,0:T(8,128)(2,1)S(1)}, bf16[1,2048,192]{1,2,0:T(8,128)(2,1)}, u32[]{:S(2)}) copy-start(bf16[1,2048,192]{1,2,0:T(8,128)(2,1)} %param.13) | copy-start | bytes 2359300
  2.2 1.1 %copy-start.2 = (bf16[1,2048,192]{1,2,0:T(8,128)(2,1)S(1)}, bf16[1,2048,192]{1,2,0:T(8,128)(2,1)}, u32[]{:S(2)}) copy-start(bf16[1,2048,192]{1,2,0:T(8,128)(2,1)} %param.14) | copy-start | bytes 2359300
  3.3 1.1 %copy-start.3 = (bf16[1,2048,192]{1,2,0:T(8,128)(2,1)S(1)}, bf16[1,2048,192]{1,2,0:T(8,128)(2,1)}, u32[]{:S(2)}) copy-start(bf16[1,2048,192]{1,2,0:T(8,128)(2,1)} %param.15) | copy-start | bytes 2359300
  4.4 1.0 %copy-start.4 = (bf16[2048,128]{1,0:T(8,128)(2,1)S(1)}, bf16[2048,128]{1,0:T(8,128)(2,1)}, u32[]{:S(2)}) copy-start(bf16[2048,128]{1,0:T(8,128)(2,1)} %proj.1) | copy-start | bytes 1572868
  5.5 59.5 %copy-start.5 = (bf16[32,32,128]{2,1,0:T(8,128)(2,1)S(1)}, bf16[32,32,128]{2,1,0:T(8,128)(2,1)}, u32[]{:S(2)}) copy-start(bf16[32,32,128]{2,1,0:T(8,128)(2,1)} %param.17) | copy-start | bytes 786436
  6.3 21.9 %collective-permute-start.5 = (bf16[208,2048]{1,0:T(8,128)(2,1)S(1)}, bf16[208,2048]{1,0:T(8,128)(2,1)S(1)}, u32[]{:S(2)}, u32[]{:S(2)}) collective-permute-start(bf16[208,2048]{1,0:T(8,128)(2,1)S(1)} %get-tuple-element.16), channel_id=1, source_target_pairs={{0,2},{2,0},{1,3},{3,1},{4,6},{6,4},{5,7},{7,5},{8,10},{10,8},{9,1... | collective-permute-start | bytes 2555912 | tf_op jit(solution)/shard_map/ppermute | solution.py:253
  9.4 57.1 %collective-permute-start.1 = (bf16[416,2048]{1,0:T(8,128)(2,1)S(1)}, bf16[416,2048]{1,0:T(8,128)(2,1)S(1)}, u32[]{:S(2)}, u32[]{:S(2)}) collective-permute-start(bf16[416,2048]{1,0:T(8,128)(2,1)S(1)} %get-tuple-element.14.own), channel_id=1, source_target_pairs={{0,1},{1,0},{2,3},{3,2},{4,5},{5,4},{6,7},{7,6},{8,9},{9,8},{10,11... | collective-permute-start | bytes 5111816 | tf_op jit(solution)/shard_map/ppermute | solution.py:252
  28.3 20.1 %collective-permute-start.6 = (bf16[208,2048]{1,0:T(8,128)(2,1)S(1)}, bf16[208,2048]{1,0:T(8,128)(2,1)S(1)}, u32[]{:S(2)}, u32[]{:S(2)}) collective-permute-start(bf16[208,2048]{1,0:T(8,128)(2,1)S(1)} %collective-permute-done.5.ox), channel_id=1, source_target_pairs={{0,16},{16,0},{1,17},{17,1},{2,18},{18,2},{3,19},{19,3},{4,20},{20... | collective-permute-start | bytes 2555912 | tf_op jit(solution)/shard_map/ppermute | solution.py:254
  30.1 12.5 %collective-permute-start = (bf16[128,2048]{1,0:T(8,128)(2,1)S(1)}, bf16[128,2048]{1,0:T(8,128)(2,1)S(1)}, u32[]{:S(2)}, u32[]{:S(2)}) collective-permute-start(bf16[128,2048]{1,0:T(8,128)(2,1)S(1)} %copy-done), channel_id=1, source_target_pairs={{0,4},{4,0},{8,12},{12,8},{1,5},{5,1},{9,13},{13,9},{2,6},{6,2},{1... | collective-permute-start | bytes 1572872 | tf_op jit(solution)/shard_map/ppermute | solution.py:239
  31.6 16.8 %collective-permute-start.2 = (bf16[128,2048]{1,0:T(8,128)(2,1)S(1)}, bf16[128,2048]{1,0:T(8,128)(2,1)S(1)}, u32[]{:S(2)}, u32[]{:S(2)}) collective-permute-start(bf16[128,2048]{1,0:T(8,128)(2,1)S(1)} %copy-done), channel_id=1, source_target_pairs={{4,8},{8,4},{5,9},{9,5},{6,10},{10,6},{7,11},{11,7},{20,24},{24,20... | collective-permute-start | bytes 1572872 | tf_op jit(solution)/shard_map/ppermute | solution.py:240
  42.6 7.1 %collective-permute-start.4 = (bf16[128,2048]{1,0:T(8,128)(2,1)S(1)}, bf16[128,2048]{1,0:T(8,128)(2,1)S(1)}, u32[]{:S(2)}, u32[]{:S(2)}) collective-permute-start(bf16[128,2048]{1,0:T(8,128)(2,1)S(1)} %collective-permute-done.near), channel_id=1, source_target_pairs={{4,8},{8,4},{5,9},{9,5},{6,10},{10,6},{7,11},{11,7},{20,24},{24,20... | collective-permute-start | bytes 1572872 | tf_op jit(solution)/shard_map/ppermute | solution.py:241
  43.3 23.2 %collective-permute-start.7 = (bf16[208,2048]{1,0:T(8,128)(2,1)S(1)}, bf16[208,2048]{1,0:T(8,128)(2,1)S(1)}, u32[]{:S(2)}, u32[]{:S(2)}) collective-permute-start(bf16[208,2048]{1,0:T(8,128)(2,1)S(1)} %collective-permute-done.5.ox), channel_id=1, source_target_pairs={{0,1},{1,0},{2,3},{3,2},{4,5},{5,4},{6,7},{7,6},{8,9},{9,8},{10,11... | collective-permute-start | bytes 2555912 | tf_op jit(solution)/shard_map/ppermute | solution.py:255
  48.4 18.0 %collective-permute-start.8 = (bf16[208,2048]{1,0:T(8,128)(2,1)S(1)}, bf16[208,2048]{1,0:T(8,128)(2,1)S(1)}, u32[]{:S(2)}, u32[]{:S(2)}) collective-permute-start(bf16[208,2048]{1,0:T(8,128)(2,1)S(1)} %collective-permute-done.6.oy), channel_id=1, source_target_pairs={{0,1},{1,0},{2,3},{3,2},{4,5},{5,4},{6,7},{7,6},{8,9},{9,8},{10,11... | collective-permute-start | bytes 2555912 | tf_op jit(solution)/shard_map/ppermute | solution.py:256
  48.4 16.6 %collective-permute-start.3 = (bf16[128,2048]{1,0:T(8,128)(2,1)S(1)}, bf16[128,2048]{1,0:T(8,128)(2,1)S(1)}, u32[]{:S(2)}, u32[]{:S(2)}) collective-permute-start(bf16[128,2048]{1,0:T(8,128)(2,1)S(1)} %collective-permute-done.2.across), channel_id=1, source_target_pairs={{4,0},{8,12},{5,1},{9,13},{6,2},{10,14},{7,3},{11,15},{20,16},{24,... | collective-permute-start | bytes 1572872 | tf_op jit(solution)/shard_map/ppermute | solution.py:242
  49.7 27.6 %collective-permute-start.12 = (bf16[128,2048]{1,0:T(8,128)(2,1)S(1)}, bf16[128,2048]{1,0:T(8,128)(2,1)S(1)}, u32[]{:S(2)}, u32[]{:S(2)}) collective-permute-start(bf16[128,2048]{1,0:T(8,128)(2,1)S(1)} %collective-permute-done.4.far_inner), channel_id=1, source_target_pairs={{4,0},{8,12},{5,1},{9,13},{6,2},{10,14},{7,3},{11,15},{20,16},{24,... | collective-permute-start | bytes 1572872 | tf_op jit(solution)/shard_map/ppermute | solution.py:243
  65.0 23.6 %collective-permute-start.14 = (bf16[32,32,128]{2,1,0:T(8,128)(2,1)S(1)}, bf16[32,32,128]{2,1,0:T(8,128)(2,1)S(1)}, u32[]{:S(2)}, u32[]{:S(2)}) collective-permute-start(bf16[32,32,128]{2,1,0:T(8,128)(2,1)S(1)} %copy-done.5), channel_id=1, source_target_pairs={{0,2},{2,0},{1,3},{3,1},{4,6},{6,4},{5,7},{7,5},{8,10},{10,8},{9,1... | collective-permute-start | bytes 786440 | tf_op jit(solution)/shard_map/ppermute | solution.py:257
  70.9 19.9 %collective-permute-start.11 = (bf16[256,128]{1,0:T(8,128)(2,1)S(1)}, bf16[256,128]{1,0:T(8,128)(2,1)S(1)}, u32[]{:S(2)}, u32[]{:S(2)}) collective-permute-start(bf16[256,128]{1,0:T(8,128)(2,1)S(1)} %get-tuple-element.20), channel_id=1, source_target_pairs={{0,8},{4,12},{8,0},{12,4},{1,9},{5,13},{9,1},{13,5},{2,10},{6,14},... | collective-permute-start | bytes 196616 | tf_op jit(solution)/shard_map/ppermute | solution.py:274
  80.7 10.1 %copy-start.6 = (s32[128,4]{0,1:T(4,128)S(1)}, s32[128,4]{0,1:T(4,128)}, u32[]{:S(2)}) copy-start(s32[128,4]{0,1:T(4,128)} %param.10) | copy-start | bytes 6148
  80.7 10.1 %copy-start.7 = (f32[128,4]{0,1:T(4,128)S(1)}, f32[128,4]{0,1:T(4,128)}, u32[]{:S(2)}) copy-start(f32[128,4]{0,1:T(4,128)} %param.11) | copy-start | bytes 6148
  80.8 10.1 %copy-start.8 = (s32[2]{0:T(128)S(1)}, s32[2]{0:T(128)}, u32[]{:S(2)}) copy-start(s32[2]{0:T(128)} %lengths.1) | copy-start | bytes 28
  80.8 10.1 %collective-permute-start.13 = (bf16[256,128]{1,0:T(8,128)(2,1)S(1)}, bf16[256,128]{1,0:T(8,128)(2,1)S(1)}, u32[]{:S(2)}, u32[]{:S(2)}) collective-permute-start(bf16[256,128]{1,0:T(8,128)(2,1)S(1)} %shard_map.94), channel_id=1, source_target_pairs={{0,12},{4,8},{8,4},{12,0},{1,13},{5,9},{9,5},{13,1},{2,14},{6,10},... | collective-permute-start | bytes 196616 | tf_op jit(solution)/shard_map/ppermute | solution.py:274
  86.5 4.0 %collective-permute-start.9 = (bf16[128,128]{1,0:T(8,128)(2,1)S(1)}, bf16[128,128]{1,0:T(8,128)(2,1)S(1)}, u32[]{:S(2)}, u32[]{:S(2)}) collective-permute-start(bf16[128,128]{1,0:T(8,128)(2,1)S(1)} %get-tuple-element.18), channel_id=1, source_target_pairs={{0,4},{4,0},{8,12},{12,8},{1,5},{5,1},{9,13},{13,9},{2,6},{6,2},{1... | collective-permute-start | bytes 98312 | tf_op jit(solution)/shard_map/ppermute | solution.py:274
  86.6 4.3 %collective-permute-start.10 = (bf16[128,128]{1,0:T(8,128)(2,1)S(1)}, bf16[128,128]{1,0:T(8,128)(2,1)S(1)}, u32[]{:S(2)}, u32[]{:S(2)}) collective-permute-start(bf16[128,128]{1,0:T(8,128)(2,1)S(1)} %get-tuple-element.19), channel_id=1, source_target_pairs={{0,4},{4,0},{8,12},{12,8},{1,5},{5,1},{9,13},{13,9},{2,6},{6,2},{1... | collective-permute-start | bytes 98312 | tf_op jit(solution)/shard_map/ppermute | solution.py:274

commit v3 on v2

--- a/solution.py
+++ b/solution.py
@@ -83,14 +83,34 @@
     return lax.dot_general(a, b, dims, preferred_element_type=jnp.float32)
 
 
-def kernel(body, operands, outs, flops, smem=()):
+def whole_block(a):
+    return pl.BlockSpec(a.shape, lambda *_: (0,) * a.ndim)
+
+
+def tied(values, after):
+    def body(*refs):
+        for i in range(len(values)):
+            refs[len(values) + len(after) + i][...] = refs[i][...]
+
+    return pl.pallas_call(
+        body,
+        out_shape=[jax.ShapeDtypeStruct(a.shape, a.dtype) for a in values],
+        in_specs=[VMEM] * len(values) + [pl.BlockSpec(memory_space=pl.ANY)] * len(after),
+        out_specs=[VMEM] * len(values),
+        compiler_params=pltpu.CompilerParams(vmem_limit_bytes=8 * 2**20),
+    )(*values, *after)
+
+
+def kernel(body, operands, outs, flops, smem=(), fetched=(), limit=24):
     moved = sum(a.size * a.dtype.itemsize for a in operands)
     return pl.pallas_call(
         body,
         out_shape=[jax.ShapeDtypeStruct(shape, dtype) for shape, dtype in outs],
-        in_specs=[SMEM if i in smem else VMEM for i in range(len(operands))],
+        in_specs=[
+            SMEM if i in smem else whole_block(a) if i in fetched else VMEM for i, a in enumerate(operands)
+        ],
         out_specs=[VMEM] * len(outs),
-        compiler_params=pltpu.CompilerParams(vmem_limit_bytes=24 * 2**20),
+        compiler_params=pltpu.CompilerParams(vmem_limit_bytes=limit * 2**20),
         cost_estimate=pl.CostEstimate(flops=int(flops), bytes_accessed=int(moved), transcendentals=0),
     )(*operands)
 
@@ -98,60 +118,51 @@
 FOLD = 16
 
 
-def pack_body(tokens, gate, up, down, proj, pack, half, base):
+def pack_body(tokens, gate, up, down, proj, pack, part, rest, base):
     rows = gate.shape[0]
     width = proj.shape[1]
     pack[:rows, :] = gate[...]
     pack[rows : 2 * rows, :] = up[...]
-    folded = dot(down[...], proj[...])
-    high = folded.astype(jnp.bfloat16)
-    low = (folded - high.astype(jnp.float32)).astype(jnp.bfloat16)
-    pack[2 * rows :, :] = jnp.zeros((2 * FOLD, pack.shape[1]), jnp.bfloat16)
+    folded = dot(down[...], proj[...]).astype(jnp.bfloat16)
+    pack[2 * rows :, :] = jnp.zeros((FOLD, pack.shape[1]), jnp.bfloat16)
     for i in range(rows // FOLD):
-        pack[2 * rows : 2 * rows + FOLD, i * width : (i + 1) * width] = high[i * FOLD : (i + 1) * FOLD]
-        pack[2 * rows + FOLD :, i * width : (i + 1) * width] = low[i * FOLD : (i + 1) * FOLD]
-    part = half.shape[0]
+        pack[2 * rows :, i * width : (i + 1) * width] = folded[i * FOLD : (i + 1) * FOLD]
+    size = part.shape[0]
     for y in range(2):
 
         @pl.when(lax.axis_index(G) == y)
         def _():
-            half[...] = pack[y * part : (y + 1) * part, :]
-
+            part[...] = pack[y * size : (y + 1) * size, :]
+
+    rest[...] = pack[2 * size :, :]
     base[...] = dot(tokens[...], proj[...]).T
-
-
-def folded_parts(tile, rows, width):
-    return [
-        jnp.concatenate([tile[k * FOLD : (k + 1) * FOLD, i * width : (i + 1) * width] for i in range(rows // FOLD)], axis=0)
-        for k in range(2)
-    ]
 
 
 def finish(act, tile, width):
     rows = act.shape[0] // 2
     gate_act, up_act = act[:rows], act[rows:]
     hidden = (gate_act / (1.0 + jnp.exp(-gate_act)) * up_act).astype(jnp.bfloat16)
-    return sum(dot(part, hidden, TN) for part in folded_parts(tile, rows, width))
+    folded = jnp.concatenate([tile[:, i * width : (i + 1) * width] for i in range(rows // FOLD)], axis=0)
+    return dot(folded, hidden, TN)
 
 
 def through_whole(x, packs, width):
     total = None
     for pack in packs:
-        rows = pack.shape[0] - 2 * FOLD
+        rows = pack.shape[0] - FOLD
         part = finish(dot(pack[:rows, :], x, NT), pack[rows:, :], width)
         total = part if total is None else total + part
     return total
 
 
-def through_halves(x, halves, width):
+def through_parts(x, packs, width):
     first = lax.axis_index(G) == 0
     total = None
-    for mine, others in halves:
+    for mine, others, rest in packs:
         a, b = dot(mine[...], x, NT), dot(others[...], x, NT)
-        rows = mine.shape[0]
-        act = jnp.concatenate([jnp.where(first, a, b), jnp.where(first, b, a)[: rows - 2 * FOLD]], axis=0)
-        tile = jnp.where(first, others[rows - 2 * FOLD :, :], mine[rows - 2 * FOLD :, :])
-        part = finish(act, tile, width)
+        rows = rest.shape[0] - FOLD
+        act = [jnp.where(first, a, b), jnp.where(first, b, a), dot(rest[:rows, :], x, NT)]
+        part = finish(jnp.concatenate(act, axis=0), rest[rows:, :], width)
         total = part if total is None else total + part
     return total
 
@@ -161,49 +172,41 @@
     return (z == 0) | (z == lax.axis_size(E) - 1)
 
 
-def first_body(tokens, near, own, pair, here, back):
-    width = here.shape[0]
+def first_body(tokens, near, own, pair, got):
     x = jnp.concatenate([tokens[...], near[...]], axis=0)
-    got = through_whole(x, (own, pair), width)
-    here[...] = got[:, : tokens.shape[0]]
-    back[...] = got[:, tokens.shape[0] :].astype(back.dtype)
-
-
-def second_body(tokens, near, end_two, far_inner, own, pair, ox, oy, px, py, here, back_near, back_two):
-    width = here.shape[0]
-    n = tokens.shape[0]
+    got[...] = through_whole(x, (own, pair), got.shape[0])
+
+
+def second_body(tokens, near, end_two, far_inner, own, pair, ox, oy, oz, px, py, pz, got_own, here, back_near, back_two):
+    n, width = tokens.shape[0], got_own.shape[0]
     two = jnp.where(at_end(), end_two[...], far_inner[...])
     back_two[:width, :] = through_whole(two, (own, pair), width).astype(back_two.dtype)
     x = jnp.concatenate([tokens[...], near[...], two], axis=0)
-    got = through_halves(x, ((ox, oy), (px, py)), width)
-    here[...] = got[:, :n]
-    back_near[...] = got[:, n : 2 * n].astype(back_near.dtype)
+    got = through_parts(x, ((ox, oy, oz), (px, py, pz)), width)
+    here[:width, :] = got_own[:, :n]
+    here[width:, :] = got[:, :n]
+    back_near[:width, :] = got_own[:, n:].astype(back_near.dtype)
+    back_near[width:, :] = got[:, n : 2 * n].astype(back_near.dtype)
     back_two[width:, :] = got[:, 2 * n :].astype(back_two.dtype)
 
 
-def third_body(end_three, across, own, pair, ox, oy, px, py, back_three):
+def third_body(end_three, across, own, pair, ox, oy, oz, px, py, pz, back_three):
     width = back_three.shape[0] // 2
     three = jnp.where(at_end(), end_three[...], across[...])
     back_three[:width, :] = through_whole(three, (own, pair), width).astype(back_three.dtype)
-    back_three[width:, :] = through_halves(three, ((ox, oy), (px, py)), width).astype(back_three.dtype)
-
-
-def score_body(lengths, base, here, here_other, near, near_other, two, three, routes, gates, queries, others, scores):
+    back_three[width:, :] = through_parts(three, ((ox, oy, oz), (px, py, pz)), width).astype(back_three.dtype)
+
+
+def score_body(lengths, base, here, near, two, three, routes, gates, queries, others, scores):
     z, x = lax.axis_index(E), lax.axis_index(Q)
     width, tokens = base.shape
     total = base[...]
     route, gate = routes[...], gates[...]
-    sent = [
-        (here[...], here_other[...]),
-        (near[...], near_other[...]),
-        (two[:width, :], two[width:, :]),
-        (three[:width, :], three[width:, :]),
-    ]
-    for k, pair in enumerate(sent):
+    for k, sent in enumerate((here, near, two, three)):
         for which in (0, 1):
             expert = (z ^ k) * 2 + (x ^ which)
             weight = jnp.sum(jnp.where(route == expert, gate, 0.0), axis=0, keepdims=True)
-            total = total + weight * pair[which].astype(jnp.float32)
+            total = total + weight * sent[which * width : (which + 1) * width, :].astype(jnp.float32)
     norm = jnp.sqrt(jnp.sum(total * total, axis=0, keepdims=True) + 1e-06)
     embedding = (total / norm).T.astype(jnp.bfloat16)
     count, span = queries.shape[0], queries.shape[0] * 2 // scores.shape[1]
@@ -236,50 +239,56 @@
     ends, middle = [(1, 0), (2, 3)], [(1, 2), (2, 1)]
     f32, bf16 = jnp.float32, jnp.bfloat16
 
+    pack_rows = 2 * hidden_part + FOLD
+    part_rows = pack_rows // 3 // 16 * 16
+    own, part, rest, base = kernel(
+        pack_body,
+        [tokens, gate_weight[0].T, up_weight[0].T, down_weight[0].T, proj_weight],
+        [((r, model_width), bf16) for r in (pack_rows, part_rows, pack_rows - 2 * part_rows)] + [((width, n), f32)],
+        2 * (hidden_part + n) * model_width * width,
+        fetched=(0, 1, 2, 3, 4),
+        limit=56,
+    )
     near = lax.ppermute(tokens, E, [(i, i ^ 1) for i in range(4)])
     across = lax.ppermute(tokens, E, middle)
+    part_x = lax.ppermute(part, Q, swap)
+    pair = lax.ppermute(own, D, swap)
+    part_x, rest = tied([part_x, rest], [near, across])
+
     far_inner = lax.ppermute(near, E, middle)
     end_two = lax.ppermute(across, E, ends)
+    rest_x = lax.ppermute(rest, Q, swap)
+    part_y = lax.ppermute(part_x, G, swap)
+    pair_part_x = lax.ppermute(part_x, D, swap)
+    work = 2 * n * model_width * 4 * hidden_part
+    (got_own,) = kernel(first_body, [tokens, near, own, pair], [((width, 2 * n), f32)], 2 * work, fetched=(0,))
+
     end_three = lax.ppermute(far_inner, E, ends)
-
-    pack_rows = 2 * hidden_part + 2 * FOLD
-    own, half, base = kernel(
-        pack_body,
-        [tokens, gate_weight[0].T, up_weight[0].T, down_weight[0].T, proj_weight],
-        [((pack_rows, model_width), bf16), ((pack_rows // 2, model_width), bf16), ((width, n), f32)],
-        2 * (hidden_part + n) * model_width * width,
-    )
-    pair = lax.ppermute(own, D, swap)
-    half_x = lax.ppermute(half, Q, swap)
-    half_y = lax.ppermute(half_x, G, swap)
-    pair_x = lax.ppermute(half_x, D, swap)
-    pair_y = lax.ppermute(half_y, D, swap)
+    rest_x, part_y = tied([rest_x, part_y], [far_inner, end_two, got_own])
+    pair_rest_x = lax.ppermute(rest_x, D, swap)
+    pair_part_y = lax.ppermute(part_y, D, swap)
     other_queries = lax.ppermute(queries, Q, swap)
 
-    work = 2 * n * model_width * 4 * hidden_part
-    here, back_near = kernel(
-        first_body, [tokens, near, own, pair], [((width, n), f32), ((width, n), bf16)], 2 * work
-    )
-    other = [half_x, half_y, pair_x, pair_y]
-    here_other, back_near_other, back_two = kernel(
+    other = [part_x, part_y, rest_x, pair_part_x, pair_part_y, pair_rest_x]
+    both = (2 * width, n)
+    here, back_near, back_two = kernel(
         second_body,
-        [tokens, near, end_two, far_inner, own, pair, *other],
-        [((width, n), f32), ((width, n), bf16), ((2 * width, n), bf16)],
+        [tokens, near, end_two, far_inner, own, pair, *other, got_own],
+        [(both, f32), (both, bf16), (both, bf16)],
         4 * work,
-    )
-    (back_three,) = kernel(
-        third_body, [end_three, across, own, pair, *other], [((2 * width, n), bf16)], 2 * work
-    )
-    from_near, from_near_other, two, three = (
+        fetched=(0,),
+    )
+    (back_three,) = kernel(third_body, [end_three, across, own, pair, *other], [(both, bf16)], 2 * work)
+    from_near, two, three = (
         lax.ppermute(a, E, [(i, i ^ k) for i in range(4)])
-        for a, k in ((back_near, 1), (back_near_other, 1), (back_two, 2), (back_three, 3))
+        for k, a in ((1, back_near), (2, back_two), (3, back_three))
     )
     rows = queries.shape[0] * queries.shape[1]
     (scores,) = kernel(
         score_body,
         [
-            passage_lengths, base, here, here_other, from_near, from_near_other, two, three,
-            route_ids.T, gate_values.T, queries.reshape(rows, width), other_queries.reshape(rows, width),
+            passage_lengths, base, here, from_near, two, three, route_ids.T, gate_values.T,
+            queries.reshape(rows, width), other_queries.reshape(rows, width),
         ],
         [((n // PLEN, 2 * queries.shape[0]), f32)],
         4 * n * width * rows,

time: 93.4 us -> 71.9 us (0.77)
  waiting for transfers between devices: 55.1 us -> 36.3 us
  local copies, waits for them, and re-layouts: 5.5 us -> 1.09 us
  starting transfers between devices: 19.2 us -> 20.5 us
    ppermute x4 -> x6, waiting for transfers between devices: 24 us -> 3.45 us  [the longest x1 2.43 us: by_column(): part_x = lax.ppermute(part, Q, swap)]
    unnamed x18 -> x16, local copies, waits for them, and re-layouts: 5.5 us -> 1.09 us
    ppermute x1, waiting for transfers between devices: 4.6 us -> 7.46 us  [by_column(): end_three = lax.ppermute(far_inner, E, ends)]
    ppermute x1, waiting for transfers between devices: 14 us -> 11.3 us  [by_column(): end_two = lax.ppermute(across, E, ends)]
    ppermute x4 -> x3, waiting for transfers between devices: 2.24 us -> 3.74 us  [by_column(): lax.ppermute(a, E, [(i, i ^ k) for i in range(4)])]
    ppermute x1, starting transfers between devices: 1.57 us -> 2.64 us  [by_column(): near = lax.ppermute(tokens, E, [(i, i ^ 1) for i in range(4)])]
    ppermute x4 -> x6, starting transfers between devices: 4.86 us -> 5.37 us  [the longest x1 1.6 us: by_column(): part_y = lax.ppermute(part_x, G, swap)]
    ppermute x4 -> x3, starting transfers between devices: 7.45 us -> 7.5 us  [by_column(): lax.ppermute(a, E, [(i, i ^ k) for i in range(4)])]
  transfers between devices with their start and end apart: 15 -> 16, of which waited for: 7 -> 7; matrix products, arithmetic and copies ran while one was open for 0% -> 0% of each run, Pallas kernels for 11% -> 10%
where the time goes in v3:
time: 71.9 us; the launch traced here: 71.7 us
  waiting for transfers between devices  36.3 us (50%)
  starting transfers between devices  20.5 us (29%)
  Pallas kernels  13.7 us (19%)
  local copies, waits for them, and re-layouts  1.09 us (2%)
    pallas_call x5, Pallas kernels, kernel(): pl.pallas_call(body, out_shape=[jax.ShapeDtypeStruct(shape, dtype) for sh...  13.5 us
    ppermute x1, waiting for transfers between devices, by_column(): end_two = lax.ppermute(across, E, ends)  11.3 us
    ppermute x1, waiting for transfers between devices, by_column(): near = lax.ppermute(tokens, E, [(i, i ^ 1) for i in range(4)])  10.3 us
    ppermute x3, starting transfers between devices, by_column(): lax.ppermute(a, E, [(i, i ^ k) for i in range(4)])  7.5 us
    ppermute x1, waiting for transfers between devices, by_column(): end_three = lax.ppermute(far_inner, E, ends)  7.46 us
    ppermute x3, waiting for transfers between devices, by_column(): lax.ppermute(a, E, [(i, i ^ k) for i in range(4)])  3.74 us
    ppermute x1, starting transfers between devices, by_column(): near = lax.ppermute(tokens, E, [(i, i ^ 1) for i in range(4)])  2.64 us
    ppermute x1, waiting for transfers between devices, by_column(): part_x = lax.ppermute(part, Q, swap)  2.43 us
  transfers between devices with their start and end apart: 16, of which 7 were waited for; matrix products, arithmetic and copies ran while one was open for 0% of the time, Pallas kernels for 10%

profile of v3, /device:TPU:0, one launch (start us, length us, event | category | flops | bytes accessed | tf_op | source)
XLA Modules:
  0.0 71.7 jit_solution(10933059064540283963)
XLA Ops:
  0.0 4.0 %shard_map.91 = (bf16[400,2048]{1,0:T(8,128)(2,1)}, bf16[128,2048]{1,0:T(8,128)(2,1)}, bf16[144,2048]{1,0:T(8,128)(2,1)}, f32[128,128]{1,0:T(8,128)}) custom-call(bf16[128,2048]{1,0:T(8,128)(2,1)} %tokens.5, bf16[192,2048]{1,0:T(8,128)(2,1)} %bitcast.17, bf16[192,2048]{1,0:T(8,128)(2,1)} %bitcast.18, bf16[192,2048]{1,0:T(8,128)(2,1)} %bitcast.19, ...), custom_call_target="tpu_custom_call" | custom-call | flops 167772160 | bytes 3407872 | tf_op jit(solution)/shard_map/pallas_call | solution.py:106
  4.5 2.6 %collective-permute-start = (bf16[128,2048]{1,0:T(8,128)(2,1)S(1)}, bf16[128,2048]{1,0:T(8,128)(2,1)S(1)}, u32[]{:S(2)}, u32[]{:S(2)}) collective-permute-start(bf16[128,2048]{1,0:T(8,128)(2,1)S(1)} %copy-done.1), channel_id=1, source_target_pairs={{0,4},{4,0},{8,12},{12,8},{1,5},{5,1},{9,13},{13,9},{2,6},{6,2},{1... | collective-permute-start | bytes 1572872 | tf_op jit(solution)/shard_map/ppermute | solution.py:252
  7.1 0.7 collective-permute-start.1
  7.8 1.6 %collective-permute-start.5 = (bf16[128,2048]{1,0:T(8,128)(2,1)}, bf16[128,2048]{1,0:T(8,128)(2,1)S(1)}, u32[]{:S(2)}, u32[]{:S(2)}) collective-permute-start(bf16[128,2048]{1,0:T(8,128)(2,1)} %get-tuple-element.18), channel_id=1, source_target_pairs={{0,2},{2,0},{1,3},{3,1},{4,6},{6,4},{5,7},{7,5},{8,10},{10,8},{9,1... | collective-permute-start | bytes 1572872 | tf_op jit(solution)/shard_map/ppermute | solution.py:254
  9.4 10.3 %collective-permute-done.refs_2_.near = bf16[128,2048]{1,0:T(8,128)(2,1)S(1)} collective-permute-done((bf16[128,2048]{1,0:T(8,128)(2,1)S(1)}, bf16[128,2048]{1,0:T(8,128)(2,1)S(1)}, u32[]{:S(2)}, u32[]{:S(2)}) %collective-permute-start) | collective-permute-done | bytes 524320 | tf_op jit(solution)/shard_map/ppermute | solution.py:252
  19.7 2.4 %collective-permute-done.5.refs_0_ = bf16[128,2048]{1,0:T(8,128)(2,1)S(1)} collective-permute-done((bf16[128,2048]{1,0:T(8,128)(2,1)}, bf16[128,2048]{1,0:T(8,128)(2,1)S(1)}, u32[]{:S(2)}, u32[]{:S(2)}) %collective-permute-start.5) | collective-permute-done | bytes 524320 | tf_op jit(solution)/shard_map/ppermute | solution.py:254
  22.1 1.1 %copy-done.2 = bf16[144,2048]{1,0:T(8,128)(2,1)S(1)} copy-done((bf16[144,2048]{1,0:T(8,128)(2,1)S(1)}, bf16[144,2048]{1,0:T(8,128)(2,1)}, u32[]{:S(2)}) %copy-start.2) | copy-done | bytes 589848
  23.2 1.6 %collective-permute-start.6 = (bf16[144,2048]{1,0:T(8,128)(2,1)S(1)}, bf16[144,2048]{1,0:T(8,128)(2,1)S(1)}, u32[]{:S(2)}, u32[]{:S(2)}) collective-permute-start(bf16[144,2048]{1,0:T(8,128)(2,1)S(1)} %get-tuple-element.21), channel_id=1, source_target_pairs={{0,2},{2,0},{1,3},{3,1},{4,6},{6,4},{5,7},{7,5},{8,10},{10,8},{9,1... | collective-permute-start | bytes 1769480 | tf_op jit(solution)/shard_map/ppermute | solution.py:260
  24.8 1.3 %collective-permute-start.2 = (bf16[128,2048]{1,0:T(8,128)(2,1)S(1)}, bf16[128,2048]{1,0:T(8,128)(2,1)S(1)}, u32[]{:S(2)}, u32[]{:S(2)}) collective-permute-start(bf16[128,2048]{1,0:T(8,128)(2,1)S(1)} %collective-permute-done.1.refs_3_.across), channel_id=1, source_target_pairs={{4,0},{8,12},{5,1},{9,13},{6,2},{10,14},{7,3},{11,15},{20,16},{24,... | collective-permute-start | bytes 1572872 | tf_op jit(solution)/shard_map/ppermute | solution.py:259
  26.1 0.7 collective-permute-start.3
  26.8 1.6 %collective-permute-start.7 = (bf16[128,2048]{1,0:T(8,128)(2,1)S(1)}, bf16[128,2048]{1,0:T(8,128)(2,1)S(1)}, u32[]{:S(2)}, u32[]{:S(2)}) collective-permute-start(bf16[128,2048]{1,0:T(8,128)(2,1)S(1)} %get-tuple-element.20.ox), channel_id=1, source_target_pairs={{0,16},{16,0},{1,17},{17,1},{2,18},{18,2},{3,19},{19,3},{4,20},{20... | collective-permute-start | bytes 1572872 | tf_op jit(solution)/shard_map/ppermute | solution.py:261
  28.4 1.2 %shard_map.93.refs_4_.got_own = f32[128,256]{1,0:T(8,128)S(1)} custom-call(bf16[128,2048]{1,0:T(8,128)(2,1)S(1)} %copy-done.1, bf16[128,2048]{1,0:T(8,128)(2,1)S(1)} %collective-permute-done.refs_2_.near, bf16[400,2048]{1,0:T(8,128)(2,1)S(1)} %copy-done, bf16[400,2048]{1,0:T(8,128)(2,1)S(1)} %collective-permute-done.4.pair), custom_call_target="tpu_custom_call" | custom-call | flops 805306368 | bytes 4325376 | tf_op jit(solution)/shard_map/pallas_call | solution.py:106
  29.6 11.3 %collective-permute-done.2.refs_3_.end_two = bf16[128,2048]{1,0:T(8,128)(2,1)S(1)} collective-permute-done((bf16[128,2048]{1,0:T(8,128)(2,1)S(1)}, bf16[128,2048]{1,0:T(8,128)(2,1)S(1)}, u32[]{:S(2)}, u32[]{:S(2)}) %collective-permute-start.2) | collective-permute-done | bytes 524320 | tf_op jit(solution)/shard_map/ppermute | solution.py:259
  41.7 1.3 %collective-permute-start.13 = (bf16[128,2048]{1,0:T(8,128)(2,1)S(1)}, bf16[128,2048]{1,0:T(8,128)(2,1)S(1)}, u32[]{:S(2)}, u32[]{:S(2)}) collective-permute-start(bf16[128,2048]{1,0:T(8,128)(2,1)S(1)} %collective-permute-done.3.refs_2_.far_inner), channel_id=1, source_target_pairs={{4,0},{8,12},{5,1},{9,13},{6,2},{10,14},{7,3},{11,15},{20,16},{24,... | collective-permute-start | bytes 1572872 | tf_op jit(solution)/shard_map/ppermute | solution.py:266
  43.0 0.6 collective-permute-start.15
  43.9 0.7 %collective-permute-done.9.py = bf16[128,2048]{1,0:T(8,128)(2,1)S(1)} collective-permute-done((bf16[128,2048]{1,0:T(8,128)(2,1)S(1)}, bf16[128,2048]{1,0:T(8,128)(2,1)S(1)}, u32[]{:S(2)}, u32[]{:S(2)}) %collective-permute-start.9) | collective-permute-done | bytes 524320 | tf_op jit(solution)/shard_map/ppermute | solution.py:269
  44.6 4.0 %shard_map.95 = (f32[256,128]{1,0:T(8,128)S(1)}, bf16[256,128]{1,0:T(8,128)(2,1)S(1)}, bf16[256,128]{1,0:T(8,128)(2,1)S(1)}) custom-call(bf16[128,2048]{1,0:T(8,128)(2,1)S(1)} %copy-done.1, bf16[128,2048]{1,0:T(8,128)(2,1)S(1)} %collective-permute-done.refs_2_.near, bf16[128,2048]{1,0:T(8,128)(2,1)S(1)} %collective-permute-done.2.refs_3_.end_two, ...), custom_call_target="tpu_custom_call" | custom-call | flops 1610612736 | bytes 8781824 | tf_op jit(solution)/shard_map/pallas_call | solution.py:106
  48.6 4.2 %collective-permute-start.11 = (bf16[256,128]{1,0:T(8,128)(2,1)S(1)}, bf16[256,128]{1,0:T(8,128)(2,1)S(1)}, u32[]{:S(2)}, u32[]{:S(2)}) collective-permute-start(bf16[256,128]{1,0:T(8,128)(2,1)S(1)} %get-tuple-element.25), channel_id=1, source_target_pairs={{0,4},{4,0},{8,12},{12,8},{1,5},{5,1},{9,13},{13,9},{2,6},{6,2},{1... | collective-permute-start | bytes 196616 | tf_op jit(solution)/shard_map/ppermute | solution.py:283
  52.8 1.0 %collective-permute-start.12 = (bf16[256,128]{1,0:T(8,128)(2,1)S(1)}, bf16[256,128]{1,0:T(8,128)(2,1)S(1)}, u32[]{:S(2)}, u32[]{:S(2)}) collective-permute-start(bf16[256,128]{1,0:T(8,128)(2,1)S(1)} %get-tuple-element.26), channel_id=1, source_target_pairs={{0,8},{4,12},{8,0},{12,4},{1,9},{5,13},{9,1},{13,5},{2,10},{6,14},... | collective-permute-start | bytes 196616 | tf_op jit(solution)/shard_map/ppermute | solution.py:283
  53.8 7.5 %collective-permute-done.13.end_three = bf16[128,2048]{1,0:T(8,128)(2,1)S(1)} collective-permute-done((bf16[128,2048]{1,0:T(8,128)(2,1)S(1)}, bf16[128,2048]{1,0:T(8,128)(2,1)S(1)}, u32[]{:S(2)}, u32[]{:S(2)}) %collective-permute-start.13) | collective-permute-done | bytes 524320 | tf_op jit(solution)/shard_map/ppermute | solution.py:266
  61.2 2.2 %shard_map.96 = bf16[256,128]{1,0:T(8,128)(2,1)S(1)} custom-call(bf16[128,2048]{1,0:T(8,128)(2,1)S(1)} %collective-permute-done.13.end_three, bf16[128,2048]{1,0:T(8,128)(2,1)S(1)} %collective-permute-done.1.refs_3_.across, bf16[400,2048]{1,0:T(8,128)(2,1)S(1)} %copy-done, bf16[400,2048]{1,0:T(8,128)(2,1)S(1)} %collective-permute-done.4.pair, ...), custom_call_target="tpu_custom_call" | custom-call | flops 805306368 | bytes 7602176 | tf_op jit(solution)/shard_map/pallas_call | solution.py:106
  63.4 2.4 %collective-permute-start.14 = (bf16[256,128]{1,0:T(8,128)(2,1)S(1)}, bf16[256,128]{1,0:T(8,128)(2,1)S(1)}, u32[]{:S(2)}, u32[]{:S(2)}) collective-permute-start(bf16[256,128]{1,0:T(8,128)(2,1)S(1)} %shard_map.96), channel_id=1, source_target_pairs={{0,12},{4,8},{8,4},{12,0},{1,13},{5,9},{9,5},{13,1},{2,14},{6,10},... | collective-permute-start | bytes 196616 | tf_op jit(solution)/shard_map/ppermute | solution.py:283
  65.8 3.7 %collective-permute-done.14.three = bf16[256,128]{1,0:T(8,128)(2,1)S(1)} collective-permute-done((bf16[256,128]{1,0:T(8,128)(2,1)S(1)}, bf16[256,128]{1,0:T(8,128)(2,1)S(1)}, u32[]{:S(2)}, u32[]{:S(2)}) %collective-permute-start.14) | collective-permute-done | bytes 65568 | tf_op jit(solution)/shard_map/ppermute | solution.py:283
  69.6 2.1 %shard_map.97 = f32[2,64]{1,0:T(2,128)} custom-call(s32[2]{0:T(128)S(1)} %copy-done.7, f32[128,128]{1,0:T(8,128)S(1)} %copy-done.4, f32[256,128]{1,0:T(8,128)S(1)} %get-tuple-element.24.here, bf16[256,128]{1,0:T(8,128)(2,1)S(1)} %collective-permute-done.11.near, bf16[256,128]{1,0:T(8,128)(2,1)S(1)} %collective-permute-done.12.two, ...), custom_call_target="tpu_custom_call" | custom-call | flops 67108864 | bytes 921608 | tf_op jit(solution)/shard_map/pallas_call | solution.py:106
  (31 shorter events, 1.6 us)
Async XLA Ops:
  0.0 4.5 %copy-start.1 = (bf16[128,2048]{1,0:T(8,128)(2,1)S(1)}, bf16[128,2048]{1,0:T(8,128)(2,1)}, u32[]{:S(2)}) copy-start(bf16[128,2048]{1,0:T(8,128)(2,1)} %tokens.5) | copy-start | bytes 1572868
  4.0 24.3 %copy-start = (bf16[400,2048]{1,0:T(8,128)(2,1)S(1)}, bf16[400,2048]{1,0:T(8,128)(2,1)}, u32[]{:S(2)}) copy-start(bf16[400,2048]{1,0:T(8,128)(2,1)} %get-tuple-element.17.own) | copy-start | bytes 4915204
  4.0 24.3 %collective-permute-start.4 = (bf16[400,2048]{1,0:T(8,128)(2,1)}, bf16[400,2048]{1,0:T(8,128)(2,1)S(1)}, u32[]{:S(2)}, u32[]{:S(2)}) collective-permute-start(bf16[400,2048]{1,0:T(8,128)(2,1)} %get-tuple-element.17.own), channel_id=1, source_target_pairs={{0,1},{1,0},{2,3},{3,2},{4,5},{5,4},{6,7},{7,6},{8,9},{9,8},{10,11... | collective-permute-start | bytes 4915208 | tf_op jit(solution)/shard_map/ppermute | solution.py:255
  4.5 15.2 %collective-permute-start = (bf16[128,2048]{1,0:T(8,128)(2,1)S(1)}, bf16[128,2048]{1,0:T(8,128)(2,1)S(1)}, u32[]{:S(2)}, u32[]{:S(2)}) collective-permute-start(bf16[128,2048]{1,0:T(8,128)(2,1)S(1)} %copy-done.1), channel_id=1, source_target_pairs={{0,4},{4,0},{8,12},{12,8},{1,5},{5,1},{9,13},{13,9},{2,6},{6,2},{1... | collective-permute-start | bytes 1572872 | tf_op jit(solution)/shard_map/ppermute | solution.py:252
  7.1 12.5 %collective-permute-start.1 = (bf16[128,2048]{1,0:T(8,128)(2,1)S(1)}, bf16[128,2048]{1,0:T(8,128)(2,1)S(1)}, u32[]{:S(2)}, u32[]{:S(2)}) collective-permute-start(bf16[128,2048]{1,0:T(8,128)(2,1)S(1)} %copy-done.1), channel_id=1, source_target_pairs={{4,8},{8,4},{5,9},{9,5},{6,10},{10,6},{7,11},{11,7},{20,24},{24,20... | collective-permute-start | bytes 1572872 | tf_op jit(solution)/shard_map/ppermute | solution.py:253
  7.8 14.3 %collective-permute-start.5 = (bf16[128,2048]{1,0:T(8,128)(2,1)}, bf16[128,2048]{1,0:T(8,128)(2,1)S(1)}, u32[]{:S(2)}, u32[]{:S(2)}) collective-permute-start(bf16[128,2048]{1,0:T(8,128)(2,1)} %get-tuple-element.18), channel_id=1, source_target_pairs={{0,2},{2,0},{1,3},{3,1},{4,6},{6,4},{5,7},{7,5},{8,10},{10,8},{9,1... | collective-permute-start | bytes 1572872 | tf_op jit(solution)/shard_map/ppermute | solution.py:254
  22.1 1.1 %copy-start.2 = (bf16[144,2048]{1,0:T(8,128)(2,1)S(1)}, bf16[144,2048]{1,0:T(8,128)(2,1)}, u32[]{:S(2)}) copy-start(bf16[144,2048]{1,0:T(8,128)(2,1)} %get-tuple-element.19.refs_1_) | copy-start | bytes 1769476
  23.2 17.7 %collective-permute-start.6 = (bf16[144,2048]{1,0:T(8,128)(2,1)S(1)}, bf16[144,2048]{1,0:T(8,128)(2,1)S(1)}, u32[]{:S(2)}, u32[]{:S(2)}) collective-permute-start(bf16[144,2048]{1,0:T(8,128)(2,1)S(1)} %get-tuple-element.21), channel_id=1, source_target_pairs={{0,2},{2,0},{1,3},{3,1},{4,6},{6,4},{5,7},{7,5},{8,10},{10,8},{9,1... | collective-permute-start | bytes 1769480 | tf_op jit(solution)/shard_map/ppermute | solution.py:260
  24.8 16.2 %collective-permute-start.2 = (bf16[128,2048]{1,0:T(8,128)(2,1)S(1)}, bf16[128,2048]{1,0:T(8,128)(2,1)S(1)}, u32[]{:S(2)}, u32[]{:S(2)}) collective-permute-start(bf16[128,2048]{1,0:T(8,128)(2,1)S(1)} %collective-permute-done.1.refs_3_.across), channel_id=1, source_target_pairs={{4,0},{8,12},{5,1},{9,13},{6,2},{10,14},{7,3},{11,15},{20,16},{24,... | collective-permute-start | bytes 1572872 | tf_op jit(solution)/shard_map/ppermute | solution.py:259
  26.1 14.9 %collective-permute-start.3 = (bf16[128,2048]{1,0:T(8,128)(2,1)S(1)}, bf16[128,2048]{1,0:T(8,128)(2,1)S(1)}, u32[]{:S(2)}, u32[]{:S(2)}) collective-permute-start(bf16[128,2048]{1,0:T(8,128)(2,1)S(1)} %collective-permute-done.refs_2_.near), channel_id=1, source_target_pairs={{4,8},{8,4},{5,9},{9,5},{6,10},{10,6},{7,11},{11,7},{20,24},{24,20... | collective-permute-start | bytes 1572872 | tf_op jit(solution)/shard_map/ppermute | solution.py:258
  26.8 14.2 %collective-permute-start.7 = (bf16[128,2048]{1,0:T(8,128)(2,1)S(1)}, bf16[128,2048]{1,0:T(8,128)(2,1)S(1)}, u32[]{:S(2)}, u32[]{:S(2)}) collective-permute-start(bf16[128,2048]{1,0:T(8,128)(2,1)S(1)} %get-tuple-element.20.ox), channel_id=1, source_target_pairs={{0,16},{16,0},{1,17},{17,1},{2,18},{18,2},{3,19},{19,3},{4,20},{20... | collective-permute-start | bytes 1572872 | tf_op jit(solution)/shard_map/ppermute | solution.py:261
  29.6 13.4 %copy-start.3 = (bf16[32,32,128]{2,1,0:T(8,128)(2,1)S(1)}, bf16[32,32,128]{2,1,0:T(8,128)(2,1)}, u32[]{:S(2)}) copy-start(bf16[32,32,128]{2,1,0:T(8,128)(2,1)} %param.17) | copy-start | bytes 786436
  41.0 3.6 %collective-permute-start.10 = (bf16[144,2048]{1,0:T(8,128)(2,1)S(1)}, bf16[144,2048]{1,0:T(8,128)(2,1)S(1)}, u32[]{:S(2)}, u32[]{:S(2)}) collective-permute-start(bf16[144,2048]{1,0:T(8,128)(2,1)S(1)} %get-tuple-element.23.oz), channel_id=1, source_target_pairs={{0,1},{1,0},{2,3},{3,2},{4,5},{5,4},{6,7},{7,6},{8,9},{9,8},{10,11... | collective-permute-start | bytes 1769480 | tf_op jit(solution)/shard_map/ppermute | solution.py:268
  41.1 2.7 %collective-permute-start.8 = (bf16[128,2048]{1,0:T(8,128)(2,1)S(1)}, bf16[128,2048]{1,0:T(8,128)(2,1)S(1)}, u32[]{:S(2)}, u32[]{:S(2)}) collective-permute-start(bf16[128,2048]{1,0:T(8,128)(2,1)S(1)} %get-tuple-element.20.ox), channel_id=1, source_target_pairs={{0,1},{1,0},{2,3},{3,2},{4,5},{5,4},{6,7},{7,6},{8,9},{9,8},{10,11... | collective-permute-start | bytes 1572872 | tf_op jit(solution)/shard_map/ppermute | solution.py:262
  41.6 3.0 %collective-permute-start.9 = (bf16[128,2048]{1,0:T(8,128)(2,1)S(1)}, bf16[128,2048]{1,0:T(8,128)(2,1)S(1)}, u32[]{:S(2)}, u32[]{:S(2)}) collective-permute-start(bf16[128,2048]{1,0:T(8,128)(2,1)S(1)} %get-tuple-element.22.oy), channel_id=1, source_target_pairs={{0,1},{1,0},{2,3},{3,2},{4,5},{5,4},{6,7},{7,6},{8,9},{9,8},{10,11... | collective-permute-start | bytes 1572872 | tf_op jit(solution)/shard_map/ppermute | solution.py:269
  41.7 19.5 %collective-permute-start.13 = (bf16[128,2048]{1,0:T(8,128)(2,1)S(1)}, bf16[128,2048]{1,0:T(8,128)(2,1)S(1)}, u32[]{:S(2)}, u32[]{:S(2)}) collective-permute-start(bf16[128,2048]{1,0:T(8,128)(2,1)S(1)} %collective-permute-done.3.refs_2_.far_inner), channel_id=1, source_target_pairs={{4,0},{8,12},{5,1},{9,13},{6,2},{10,14},{7,3},{11,15},{20,16},{24,... | collective-permute-start | bytes 1572872 | tf_op jit(solution)/shard_map/ppermute | solution.py:266
  43.0 22.8 %collective-permute-start.15 = (bf16[32,32,128]{2,1,0:T(8,128)(2,1)S(1)}, bf16[32,32,128]{2,1,0:T(8,128)(2,1)S(1)}, u32[]{:S(2)}, u32[]{:S(2)}) collective-permute-start(bf16[32,32,128]{2,1,0:T(8,128)(2,1)S(1)} %copy-done.3), channel_id=1, source_target_pairs={{0,2},{2,0},{1,3},{3,1},{4,6},{6,4},{5,7},{7,5},{8,10},{10,8},{9,1... | collective-permute-start | bytes 786440 | tf_op jit(solution)/shard_map/ppermute | solution.py:270
  48.6 17.2 %collective-permute-start.11 = (bf16[256,128]{1,0:T(8,128)(2,1)S(1)}, bf16[256,128]{1,0:T(8,128)(2,1)S(1)}, u32[]{:S(2)}, u32[]{:S(2)}) collective-permute-start(bf16[256,128]{1,0:T(8,128)(2,1)S(1)} %get-tuple-element.25), channel_id=1, source_target_pairs={{0,4},{4,0},{8,12},{12,8},{1,5},{5,1},{9,13},{13,9},{2,6},{6,2},{1... | collective-permute-start | bytes 196616 | tf_op jit(solution)/shard_map/ppermute | solution.py:283
  52.8 16.7 %copy-start.4 = (f32[128,128]{1,0:T(8,128)S(1)}, f32[128,128]{1,0:T(8,128)}, u32[]{:S(2)}) copy-start(f32[128,128]{1,0:T(8,128)} %get-tuple-element.16.base) | copy-start | bytes 196612
  52.8 16.7 %copy-start.5 = (s32[128,4]{0,1:T(4,128)S(1)}, s32[128,4]{0,1:T(4,128)}, u32[]{:S(2)}) copy-start(s32[128,4]{0,1:T(4,128)} %param.10) | copy-start | bytes 6148
  52.8 16.7 %copy-start.6 = (f32[128,4]{0,1:T(4,128)S(1)}, f32[128,4]{0,1:T(4,128)}, u32[]{:S(2)}) copy-start(f32[128,4]{0,1:T(4,128)} %param.11) | copy-start | bytes 6148
  52.8 16.7 %copy-start.7 = (s32[2]{0:T(128)S(1)}, s32[2]{0:T(128)}, u32[]{:S(2)}) copy-start(s32[2]{0:T(128)} %lengths.1) | copy-start | bytes 28
  52.8 13.0 %collective-permute-start.12 = (bf16[256,128]{1,0:T(8,128)(2,1)S(1)}, bf16[256,128]{1,0:T(8,128)(2,1)S(1)}, u32[]{:S(2)}, u32[]{:S(2)}) collective-permute-start(bf16[256,128]{1,0:T(8,128)(2,1)S(1)} %get-tuple-element.26), channel_id=1, source_target_pairs={{0,8},{4,12},{8,0},{12,4},{1,9},{5,13},{9,1},{13,5},{2,10},{6,14},... | collective-permute-start | bytes 196616 | tf_op jit(solution)/shard_map/ppermute | solution.py:283
  63.4 6.1 %collective-permute-start.14 = (bf16[256,128]{1,0:T(8,128)(2,1)S(1)}, bf16[256,128]{1,0:T(8,128)(2,1)S(1)}, u32[]{:S(2)}, u32[]{:S(2)}) collective-permute-start(bf16[256,128]{1,0:T(8,128)(2,1)S(1)} %shard_map.96), channel_id=1, source_target_pairs={{0,12},{4,8},{8,4},{12,0},{1,13},{5,9},{9,5},{13,1},{2,14},{6,10},... | collective-permute-start | bytes 196616 | tf_op jit(solution)/shard_map/ppermute | solution.py:283

commit v4 on v3

v4 whole, which is shorter than its diff:
```python
import jax
import jax.numpy as jnp
from jax import lax
from jax.experimental import pallas as pl
from jax.experimental.pallas import tpu as pltpu
from jax.sharding import PartitionSpec as P

PLEN = 64
G, E, Q, D = "group", "expert", "query", "dp"


def matched(embedding, live_mask, block_queries):
    query_rows = block_queries.reshape(-1, block_queries.shape[-1])
    raw_scores = jnp.dot(embedding, query_rows.T, preferred_element_type=jnp.float32)
    raw_scores = jnp.where(live_mask[:, None], raw_scores, -jnp.inf)
    best_match = jnp.max(raw_scores.reshape(-1, PLEN, raw_scores.shape[-1]), axis=1)
    return jnp.sum(best_match.reshape(best_match.shape[0], -1, block_queries.shape[1]), axis=-1)


def embedded(projected):
    lengths_norm = jnp.sqrt(jnp.sum(projected * projected, axis=-1, keepdims=True) + 1e-06)
    return (projected / lengths_norm).astype(jnp.bfloat16)


def live_tokens(passage_lengths, tok_rows):
    position = jnp.arange(tok_rows, dtype=jnp.int32) % PLEN
    return position < jnp.repeat(passage_lengths, PLEN)


def by_dispatch(
    tokens, route_ids, gate_values, passage_lengths, gate_weight, up_weight, down_weight, proj_weight, queries
):
    tok_rows, model_width = tokens.shape
    top_count = route_ids.shape[1]
    experts = lax.axis_size(E) * lax.axis_size(Q)
    capacity = max(2, 2 * tok_rows * top_count // experts)
    assignments = tok_rows * top_count
    flat_routes = route_ids.reshape(-1)
    one_hot = flat_routes[:, None] == jnp.arange(experts, dtype=jnp.int32)[None, :]
    order = jnp.arange(assignments, dtype=jnp.int32)
    before = (order[None, :] < order[:, None]).astype(jnp.bfloat16)
    earlier = jnp.dot(before, one_hot.astype(jnp.bfloat16), preferred_element_type=jnp.float32)
    slot_index = jnp.sum(jnp.where(one_hot, earlier, 0.0), axis=1).astype(jnp.int32)
    slot_target = flat_routes * capacity + slot_index
    slot_owner = jnp.full((experts * capacity,), assignments, jnp.int32).at[slot_target].set(order)
    padded = jnp.concatenate([tokens, jnp.zeros((1, model_width), tokens.dtype)], axis=0)
    source_row = jnp.where(slot_owner < assignments, slot_owner // top_count, tok_rows)
    outgoing = padded[source_row].reshape(experts, capacity, model_width)
    arrived = lax.all_to_all(outgoing, (E, Q), split_axis=0, concat_axis=0, tiled=True)
    expert_rows = arrived.reshape(experts * capacity, model_width)
    gate_act = jnp.dot(
        expert_rows, lax.all_gather(gate_weight[0], D, axis=1, tiled=True), preferred_element_type=jnp.float32
    )
    up_act = jnp.dot(
        expert_rows, lax.all_gather(up_weight[0], D, axis=1, tiled=True), preferred_element_type=jnp.float32
    )
    hidden = (jax.nn.silu(gate_act) * up_act).astype(jnp.bfloat16)
    results = lax.dot_general(
        hidden,
        lax.all_gather(down_weight[0], D, axis=1, tiled=True),
        (((1,), (1,)), ((), ())),
        preferred_element_type=jnp.float32,
    ).astype(jnp.bfloat16)
    folded = jnp.dot(results, proj_weight, preferred_element_type=jnp.float32)
    returned_rows = lax.all_to_all(
        folded.reshape(experts, capacity, folded.shape[-1]), (E, Q), split_axis=0, concat_axis=0, tiled=True
    )
    picked = returned_rows.reshape(experts * capacity, folded.shape[-1])[slot_target]
    weights = gate_values.reshape(assignments, 1)
    projected = jnp.dot(tokens, proj_weight, preferred_element_type=jnp.float32) + jnp.sum(
        (picked * weights).reshape(tok_rows, top_count, folded.shape[-1]), axis=1
    )
    live_mask = live_tokens(passage_lengths, tok_rows)
    return matched(embedded(projected), live_mask, lax.all_gather(queries, Q, axis=0, tiled=True))


VMEM = pl.BlockSpec(memory_space=pltpu.VMEM)
SMEM = pl.BlockSpec(memory_space=pltpu.SMEM)
NT, TN = (((1,), (1,)), ((), ())), (((0,), (0,)), ((), ()))


def dot(a, b, dims=(((1,), (0,)), ((), ()))):
    return lax.dot_general(a, b, dims, preferred_element_type=jnp.float32)


def whole_block(a):
    return pl.BlockSpec(a.shape, lambda *_: (0,) * a.ndim)


def tied(values, after, parts):
    def body(*refs):
        outs = refs[len(values) + len(after) :]
        for i in range(len(values)):
            rows = outs[parts * i].shape[0]
            for p in range(parts):
                outs[parts * i + p][...] = refs[i][p * rows : (p + 1) * rows, :]

    blocks = [jax.ShapeDtypeStruct((a.shape[0] // parts, a.shape[1]), a.dtype) for a in values for _ in range(parts)]

    return pl.pallas_call(
        body,
        out_shape=blocks,
        in_specs=[VMEM] * len(values) + [pl.BlockSpec(memory_space=pl.ANY)] * len(after),
        out_specs=[VMEM] * len(blocks),
        compiler_params=pltpu.CompilerParams(vmem_limit_bytes=8 * 2**20),
    )(*values, *after)


def kernel(body, operands, outs, smem=(), fetched=(), limit=24, flops=0):
    return pl.pallas_call(
        body,
        out_shape=[jax.ShapeDtypeStruct(shape, dtype) for shape, dtype in outs],
        in_specs=[
            SMEM if i in smem else whole_block(a) if i in fetched else VMEM for i, a in enumerate(operands)
        ],
        out_specs=[VMEM] * len(outs),
        compiler_params=pltpu.CompilerParams(vmem_limit_bytes=limit * 2**20),
        cost_estimate=pl.CostEstimate(flops=flops, bytes_accessed=0, transcendentals=0),
    )(*operands)


FOLD = 16


def part_body(gate, up, part):
    rows = part.shape[0]
    part[...] = jnp.where(lax.axis_index(G) == 0, gate[:rows, :], up[:rows, :])


def fold_body(
    lengths, tokens, gate, up, down, proj, routes, gates,
    fold, rest_gate, rest_up, base, weights, live, chosen,
):
    rows, width = down.shape[0], proj.shape[1]
    folded = dot(down[...], proj[...]).astype(jnp.bfloat16)
    fold[...] = jnp.zeros_like(fold)
    for i in range(rows // FOLD):
        fold[:, i * width : (i + 1) * width] = folded[i * FOLD : (i + 1) * FOLD]
    left = rest_up.shape[0]
    rest_gate[:left, :] = gate[rows - left :, :]
    rest_gate[left:, :] = fold[...]
    rest_up[...] = up[rows - left :, :]
    base[...] = dot(tokens[...], proj[...]).T
    z, x = lax.axis_index(E), lax.axis_index(Q)
    for i in range(weights.shape[0]):
        expert = (z ^ (i // 2)) * 2 + (x ^ (i % 2))
        weights[i : i + 1, :] = jnp.sum(jnp.where(routes[...] == expert, gates[...], 0.0), axis=0, keepdims=True)
    position = lax.broadcasted_iota(jnp.int32, (PLEN, live.shape[1]), 0)
    for p in range(live.shape[0] // PLEN):
        live[p * PLEN : (p + 1) * PLEN, :] = jnp.where(position < lengths[p], 0.0, -jnp.inf)
    count, span = chosen.shape[0] // 2, chosen.shape[0] // chosen.shape[1]
    query = lax.broadcasted_iota(jnp.int32, (count, chosen.shape[1]), 0) // span
    column = lax.broadcasted_iota(jnp.int32, (count, chosen.shape[1]), 1)
    for w in (0, 1):
        hit = jnp.where(column == query + (x ^ w) * (count // span), 1.0, 0.0)
        chosen[w * count : (w + 1) * count, :] = hit.astype(chosen.dtype)


def finish(act, tile, width):
    rows = act.shape[0] // 2
    gate_act, up_act = act[:rows], act[rows:]
    hidden = (gate_act / (1.0 + jnp.exp(-gate_act)) * up_act).astype(jnp.bfloat16)
    folded = jnp.concatenate([tile[:, i * width : (i + 1) * width] for i in range(rows // FOLD)], axis=0)
    return dot(folded, hidden, TN)


def through(x, cores, width):
    total = None
    for blocks, fold in cores:
        part = finish(dot(jnp.concatenate(blocks, axis=0), x, NT), fold, width)
        total = part if total is None else total + part
    return total


def own_cores(gate, up, fold, pair_gate, pair_up, pair_fold):
    return [([gate[...], up[...]], fold[...]), ([pair_gate[...], pair_up[...]], pair_fold[...])]


def other_cores(*refs):
    first = lax.axis_index(G) == 0
    cores = []
    for mine, others, rest_gate, rest_up in (refs[:4], refs[4:]):
        left = rest_up.shape[0]
        gate, up = jnp.where(first, mine[...], others[...]), jnp.where(first, others[...], mine[...])
        cores.append(([gate, rest_gate[:left, :], up, rest_up[...]], rest_gate[left:, :]))
    return cores


def at_end():
    z = lax.axis_index(E)
    return (z == 0) | (z == lax.axis_size(E) - 1)


def first_body(tokens, near, *refs):
    *own, got = refs
    x = jnp.concatenate([tokens[...], near[...]], axis=0)
    got[...] = through(x, own_cores(*own), got.shape[0])


def two_body(end_two, far_inner, *refs):
    *own, got = refs
    got[...] = through(jnp.where(at_end(), end_two[...], far_inner[...]), own_cores(*own), got.shape[0])


def second_body(tokens, near, end_two, far_inner, got_own, got_two, *refs):
    other, (here, back_near, back_two) = refs[:8], refs[8:]
    n, width = tokens.shape[0], got_own.shape[0]
    two = jnp.where(at_end(), end_two[...], far_inner[...])
    got = through(jnp.concatenate([tokens[...], near[...], two], axis=0), other_cores(*other), width)
    mine = [got_own[:, :n], got_own[:, n:], got_two[...]]
    for k, to in enumerate((here, back_near, back_two)):
        to[:width, :] = mine[k].astype(to.dtype)
        to[width:, :] = got[:, k * n : (k + 1) * n].astype(to.dtype)


def third_body(end_three, across, earlier, *refs):
    own, other, to = refs[:6], refs[6:14], refs[14]
    width = to.shape[0] // 2
    three = jnp.where(at_end(), end_three[...], across[...])
    to[:width, :] = through(three, own_cores(*own), width).astype(to.dtype)
    to[width:, :] = through(three, other_cores(*other), width).astype(to.dtype)


def score_body(base, here, near, two, three, weights, live, chosen, queries, others, scores):
    width, tokens = base.shape
    total = base[...]
    for k, sent in enumerate((here, near, two, three)):
        for w in (0, 1):
            part = sent[w * width : (w + 1) * width, :].astype(jnp.float32)
            total = total + weights[2 * k + w : 2 * k + w + 1, :] * part
    norm = jnp.sqrt(jnp.sum(total * total, axis=0, keepdims=True) + 1e-06)
    embedding = (total / norm).T.astype(jnp.bfloat16)
    best = [[] for _ in range(tokens // PLEN)]
    for block in (queries, others):
        raw = dot(embedding, block[...], NT) + live[:, :1]
        for p, found in enumerate(best):
            found.append(jnp.max(raw[p * PLEN : (p + 1) * PLEN], axis=0, keepdims=True))
    left = jnp.concatenate([jnp.concatenate(found, axis=1) for found in best], axis=0)
    thirds = []
    for _ in range(3):
        thirds.append(left.astype(jnp.bfloat16))
        left = left - thirds[-1].astype(jnp.float32)
    sums = [dot(third, chosen[...]) for third in thirds]
    scores[...] = sums[0] + (sums[1] + sums[2])


def by_column(
    tokens, route_ids, gate_values, passage_lengths, gate_weight, up_weight, down_weight, proj_weight, queries
):
    n, model_width = tokens.shape
    hidden_part = gate_weight.shape[2]
    width = proj_weight.shape[1]
    swap = [(0, 1), (1, 0)]
    ends, middle = [(1, 0), (2, 3)], [(1, 2), (2, 1)]
    f32, bf16 = jnp.float32, jnp.bfloat16

    rows = queries.shape[0] * queries.shape[1]
    both = (2 * width, n)
    near = lax.ppermute(tokens, E, [(i, i ^ 1) for i in range(4)])
    across = lax.ppermute(tokens, E, middle)
    gate, up, down = gate_weight[0].T, up_weight[0].T, down_weight[0].T
    part_rows = 2 * hidden_part // 3 // 16 * 16
    left = hidden_part - part_rows
    (part,) = kernel(part_body, [gate, up], [((part_rows, model_width), bf16)])
    part_x = lax.ppermute(part, Q, swap)
    fold, rest_gate, rest_up, base, weights, live, chosen = kernel(
        fold_body,
        [passage_lengths, tokens, gate, up, down, proj_weight, route_ids.T, gate_values.T],
        [((r, model_width), bf16) for r in (FOLD, left + FOLD, left)]
        + [((width, n), f32), ((8, n), f32), ((n, width), f32), ((2 * rows, 2 * queries.shape[0]), bf16)],
        smem=(0,),
        fetched=(1,),
    )
    pair_gate, pair_up = lax.ppermute(gate, D, swap), lax.ppermute(up, D, swap)
    pair_fold = lax.ppermute(tied([fold], [pair_gate], 1)[0], D, swap)
    own = [gate, up, fold, pair_gate, pair_up, pair_fold]
    (got_own,) = kernel(first_body, [tokens, near, *own], [((width, 2 * n), f32)], fetched=(0,))

    far_inner = lax.ppermute(near, E, middle)
    end_two = lax.ppermute(across, E, ends)
    rest_x = [lax.ppermute(a, Q, swap) for a in tied([rest_gate, rest_up], [near, across], 1)]
    (part_x,) = tied([part_x], [got_own], 1)
    part_y = lax.ppermute(part_x, G, swap)
    work = 8 * n * model_width * hidden_part
    (got_two,) = kernel(two_body, [end_two, far_inner, *own], [((width, n), f32)], flops=work)

    end_three = lax.ppermute(far_inner, E, ends)
    other = [part_x, part_y, *rest_x]
    other = other + [lax.ppermute(a, D, swap) for a in tied(other, [far_inner], 1)]
    other_queries = lax.ppermute(queries, Q, swap)
    here, *back = kernel(
        second_body,
        [tokens, near, end_two, far_inner, got_own, got_two, *other],
        [(both, f32), (both, bf16), (both, bf16)],
        fetched=(0,),
        flops=3 * work,
    )
    back += kernel(third_body, [end_three, across, here, *own, *other], [(both, bf16)])
    from_near, two, three = (
        lax.ppermute(a, E, [(i, i ^ k) for i in range(4)]) for k, a in enumerate(back, start=1)
    )
    (scores,) = kernel(
        score_body,
        [
            base, here, from_near, two, three, weights, live, chosen,
            queries.reshape(rows, width), other_queries.reshape(rows, width),
        ],
        [((n // PLEN, 2 * queries.shape[0]), f32)],
    )
    return scores


def solution(mesh):
    in_specs = (
        P((G, E, Q, D), None),
        P((G, E, Q, D), None),
        P((G, E, Q, D), None),
        P((G, E, Q, D)),
        P((E, Q), None, D),
        P((E, Q), None, D),
        P((E, Q), None, D),
        P(),
        P((G, Q), None, None),
    )
    sizes = [mesh.shape[a] for a in (G, E, Q, D)]
    return jax.shard_map(
        by_column if sizes == [2, 4, 2, 2] else by_dispatch,
        mesh=mesh,
        in_specs=in_specs,
        out_specs=P((G, E, Q, D), None),
        check_vma=False,
    )
```

time: 71.9 us -> 64.3 us (0.89)
  waiting for transfers between devices: 36.3 us -> 30.8 us
  Pallas kernels: 13.7 us -> 9.39 us
  local copies, waits for them, and re-layouts: 1.09 us -> 3.99 us
  starting transfers between devices: 20.5 us -> 19.5 us
    ppermute x1, waiting for transfers between devices: 11.3 us -> 0.37 us  [by_column(): end_two = lax.ppermute(across, E, ends)]
    ppermute x5 -> x9, waiting for transfers between devices: 1.02 us -> 11.4 us  [the longest x2 10.4 us: by_column(): lax.ppermute(a, Q, swap)]
    ppermute x1, waiting for transfers between devices: 10.3 us -> 4.54 us  [by_column(): near = lax.ppermute(tokens, E, [(i, i ^ 1) for i in range(4)])]
    pallas_call x5 -> x7, Pallas kernels: 13.5 us -> 9.2 us  [kernel(): pl.pallas_call(body, out_shape=[jax.ShapeDtypeStruct(shape, dtype) for sh...]
    ppermute x3, starting transfers between devices: 7.5 us -> 4.45 us  [by_column(): lax.ppermute(a, E, [(i, i ^ k) for i in range(4)])]
    unnamed x16 -> x22, local copies, waits for them, and re-layouts: 1.09 us -> 3.99 us
    ppermute x1, waiting for transfers between devices: 7.46 us -> 8.96 us  [by_column(): end_three = lax.ppermute(far_inner, E, ends)]
    ppermute x1, starting transfers between devices: 0.6 us -> 1.49 us  [by_column(): other_queries = lax.ppermute(queries, Q, swap)]
  transfers between devices with their start and end apart: 16 -> 20, of which waited for: 7 -> 8; matrix products, arithmetic and copies ran while one was open for 0% -> 0% of each run, Pallas kernels for 10% -> 13%
where the time goes in v4:
time: 64.3 us; the launch traced here: 64 us
  waiting for transfers between devices  30.8 us (48%)
  starting transfers between devices  19.5 us (30%)
  Pallas kernels  9.39 us (15%)
  local copies, waits for them, and re-layouts  3.99 us (6%)
    ppermute x2, waiting for transfers between devices, by_column(): lax.ppermute(a, Q, swap)  10.4 us
    pallas_call x7, Pallas kernels, kernel(): pl.pallas_call(body, out_shape=[jax.ShapeDtypeStruct(shape, dtype) for sh...  9.2 us
    ppermute x1, waiting for transfers between devices, by_column(): end_three = lax.ppermute(far_inner, E, ends)  8.96 us
    ppermute x1, waiting for transfers between devices, by_column(): near = lax.ppermute(tokens, E, [(i, i ^ 1) for i in range(4)])  4.54 us
    ppermute x3, starting transfers between devices, by_column(): lax.ppermute(a, E, [(i, i ^ k) for i in range(4)])  4.45 us
    unnamed x22, local copies, waits for them, and re-layouts  3.99 us
    ppermute x3, waiting for transfers between devices, by_column(): lax.ppermute(a, E, [(i, i ^ k) for i in range(4)])  3.76 us
    ppermute x1, starting transfers between devices, by_column(): near = lax.ppermute(tokens, E, [(i, i ^ 1) for i in range(4)])  3.02 us
  transfers between devices with their start and end apart: 20, of which 8 were waited for; matrix products, arithmetic and copies ran while one was open for 0% of the time, Pallas kernels for 13%

profile of v4, /device:TPU:0, one launch (start us, length us, event | category | flops | bytes accessed | tf_op | source)
XLA Modules:
  0.0 64.0 jit_solution(5983295235470490613)
XLA Ops:
  0.5 3.0 %collective-permute-start = (bf16[128,2048]{1,0:T(8,128)(2,1)}, bf16[128,2048]{1,0:T(8,128)(2,1)S(1)}, u32[]{:S(2)}, u32[]{:S(2)}) collective-permute-start(bf16[128,2048]{1,0:T(8,128)(2,1)} %tokens.5), channel_id=1, source_target_pairs={{0,4},{4,0},{8,12},{12,8},{1,5},{5,1},{9,13},{13,9},{2,6},{6,2},{1... | collective-permute-start | bytes 1572872 | tf_op jit(solution)/shard_map/ppermute | solution.py:259
  3.5 1.1 %copy-done = bf16[1,2048,192]{1,2,0:T(8,128)(2,1)S(1)} copy-done((bf16[1,2048,192]{1,2,0:T(8,128)(2,1)S(1)}, bf16[1,2048,192]{1,2,0:T(8,128)(2,1)}, u32[]{:S(2)}) %copy-start) | copy-done | bytes 786456
  4.7 1.1 %copy-done.2 = bf16[1,2048,192]{1,2,0:T(8,128)(2,1)S(1)} copy-done((bf16[1,2048,192]{1,2,0:T(8,128)(2,1)S(1)}, bf16[1,2048,192]{1,2,0:T(8,128)(2,1)}, u32[]{:S(2)}) %copy-start.2) | copy-done | bytes 786456
  5.9 1.6 %collective-permute-start.7 = (bf16[128,2048]{1,0:T(8,128)(2,1)S(1)}, bf16[128,2048]{1,0:T(8,128)(2,1)S(1)}, u32[]{:S(2)}, u32[]{:S(2)}) collective-permute-start(bf16[128,2048]{1,0:T(8,128)(2,1)S(1)} %shard_map.95), channel_id=1, source_target_pairs={{0,2},{2,0},{1,3},{3,1},{4,6},{6,4},{5,7},{7,5},{8,10},{10,8},{9,1... | collective-permute-start | bytes 1572872 | tf_op jit(solution)/shard_map/ppermute | solution.py:265
  8.8 1.0 %copy-done.6 = bf16[2048,128]{1,0:T(8,128)(2,1)S(1)} copy-done((bf16[2048,128]{1,0:T(8,128)(2,1)S(1)}, bf16[2048,128]{1,0:T(8,128)(2,1)}, u32[]{:S(2)}) %copy-start.6) | copy-done | bytes 524312
  9.9 1.3 %shard_map.91 = (bf16[16,2048]{1,0:T(8,128)(2,1)S(1)}, bf16[80,2048]{1,0:T(8,128)(2,1)S(1)}, bf16[64,2048]{1,0:T(8,128)(2,1)S(1)}, f32[128,128]{1,0:T(8,128)S(1)...) custom-call(s32[2]{0:T(128)S(1)} %copy-done.10, bf16[128,2048]{1,0:T(8,128)(2,1)S(1)} %copy-done.4, ...), custom_call_target="tpu_custom_call" | custom-call | tf_op jit(solution)/shard_map/pallas_call | solution.py:110
  11.3 4.5 %collective-permute-done.near.refs_2_ = bf16[128,2048]{1,0:T(8,128)(2,1)S(1)} collective-permute-done((bf16[128,2048]{1,0:T(8,128)(2,1)}, bf16[128,2048]{1,0:T(8,128)(2,1)S(1)}, u32[]{:S(2)}, u32[]{:S(2)}) %collective-permute-start) | collective-permute-done | bytes 524320 | tf_op jit(solution)/shard_map/ppermute | solution.py:259
  16.5 1.2 %shard_map.93.refs_1_.got_own = f32[128,256]{1,0:T(8,128)S(1)} custom-call(bf16[128,2048]{1,0:T(8,128)(2,1)S(1)} %copy-done.4, bf16[128,2048]{1,0:T(8,128)(2,1)S(1)} %collective-permute-done.near.refs_2_, bf16[192,2048]{1,0:T(8,128)(2,1)S(1)} %bitcast.16, bf16[192,2048]{1,0:T(8,128)(2,1)S(1)} %bitcast.22, ...), custom_call_target="tpu_custom_call" | custom-call | tf_op jit(solution)/shard_map/pallas_call | solution.py:110
  17.8 1.7 %collective-permute-done.7.refs_0_ = bf16[128,2048]{1,0:T(8,128)(2,1)S(1)} collective-permute-done((bf16[128,2048]{1,0:T(8,128)(2,1)S(1)}, bf16[128,2048]{1,0:T(8,128)(2,1)S(1)}, u32[]{:S(2)}, u32[]{:S(2)}) %collective-permute-start.7) | collective-permute-done | bytes 524320 | tf_op jit(solution)/shard_map/ppermute | solution.py:265
  19.5 1.6 %collective-permute-start.8 = (bf16[128,2048]{1,0:T(8,128)(2,1)S(1)}, bf16[128,2048]{1,0:T(8,128)(2,1)S(1)}, u32[]{:S(2)}, u32[]{:S(2)}) collective-permute-start(bf16[128,2048]{1,0:T(8,128)(2,1)S(1)} %shard_map.96.refs_0_.refs_6_), channel_id=1, source_target_pairs={{0,16},{16,0},{1,17},{17,1},{2,18},{18,2},{3,19},{19,3},{4,20},{20... | collective-permute-start | bytes 1572872 | tf_op jit(solution)/shard_map/ppermute | solution.py:283
  21.2 1.6 %collective-permute-start.9 = (bf16[80,2048]{1,0:T(8,128)(2,1)S(1)}, bf16[80,2048]{1,0:T(8,128)(2,1)S(1)}, u32[]{:S(2)}, u32[]{:S(2)}) collective-permute-start(bf16[80,2048]{1,0:T(8,128)(2,1)S(1)} %get-tuple-element.25), channel_id=1, source_target_pairs={{0,2},{2,0},{1,3},{3,1},{4,6},{6,4},{5,7},{7,5},{8,10},{10,8},{9,1... | collective-permute-start | bytes 983048 | tf_op jit(solution)/shard_map/ppermute | solution.py:281
  22.7 1.3 %collective-permute-start.2 = (bf16[128,2048]{1,0:T(8,128)(2,1)S(1)}, bf16[128,2048]{1,0:T(8,128)(2,1)S(1)}, u32[]{:S(2)}, u32[]{:S(2)}) collective-permute-start(bf16[128,2048]{1,0:T(8,128)(2,1)S(1)} %collective-permute-done.1.refs_3_.across), channel_id=1, source_target_pairs={{4,0},{8,12},{5,1},{9,13},{6,2},{10,14},{7,3},{11,15},{20,16},{24,... | collective-permute-start | bytes 1572872 | tf_op jit(solution)/shard_map/ppermute | solution.py:280
  24.6 10.4 %collective-permute-done.10.refs_3_.refs_9_ = bf16[64,2048]{1,0:T(8,128)(2,1)S(1)} collective-permute-done((bf16[64,2048]{1,0:T(8,128)(2,1)S(1)}, bf16[64,2048]{1,0:T(8,128)(2,1)S(1)}, u32[]{:S(2)}, u32[]{:S(2)}) %collective-permute-start.10) | collective-permute-done | bytes 262176 | tf_op jit(solution)/shard_map/ppermute | solution.py:281
  35.7 1.3 %collective-permute-start.17 = (bf16[128,2048]{1,0:T(8,128)(2,1)S(1)}, bf16[128,2048]{1,0:T(8,128)(2,1)S(1)}, u32[]{:S(2)}, u32[]{:S(2)}) collective-permute-start(bf16[128,2048]{1,0:T(8,128)(2,1)S(1)} %collective-permute-done.3.far_inner.refs_4_), channel_id=1, source_target_pairs={{4,0},{8,12},{5,1},{9,13},{6,2},{10,14},{7,3},{11,15},{20,16},{24,... | collective-permute-start | bytes 1572872 | tf_op jit(solution)/shard_map/ppermute | solution.py:287
  38.6 1.5 %collective-permute-start.19 = (bf16[32,32,128]{2,1,0:T(8,128)(2,1)S(1)}, bf16[32,32,128]{2,1,0:T(8,128)(2,1)S(1)}, u32[]{:S(2)}, u32[]{:S(2)}) collective-permute-start(bf16[32,32,128]{2,1,0:T(8,128)(2,1)S(1)} %copy-done.7), channel_id=1, source_target_pairs={{0,2},{2,0},{1,3},{3,1},{4,6},{6,4},{5,7},{7,5},{8,10},{10,8},{9,1... | collective-permute-start | bytes 786440 | tf_op jit(solution)/shard_map/ppermute | solution.py:290
  40.1 1.2 %shard_map.94.got_two = f32[128,128]{1,0:T(8,128)S(1)} custom-call(bf16[128,2048]{1,0:T(8,128)(2,1)S(1)} %collective-permute-done.2.end_two, bf16[128,2048]{1,0:T(8,128)(2,1)S(1)} %collective-permute-done.3.far_inner.refs_4_, bf16[192,2048]{1,0:T(8,128)(2,1)S(1)} %bitcast.17, bf16[192,2048]{1,0:T(8,128)(2,1)S(1)} %bitcast.23, ...), custom_call_target="tpu_custom_call" | custom-call | flops 402653184 | tf_op jit(solution)/shard_map/pallas_call | solution.py:110
  41.3 2.0 %shard_map.99 = (f32[256,128]{1,0:T(8,128)S(1)}, bf16[256,128]{1,0:T(8,128)(2,1)S(1)}, bf16[256,128]{1,0:T(8,128)(2,1)S(1)}) custom-call(bf16[128,2048]{1,0:T(8,128)(2,1)S(1)} %copy-done.4, bf16[128,2048]{1,0:T(8,128)(2,1)S(1)} %collective-permute-done.near.refs_2_, bf16[128,2048]{1,0:T(8,128)(2,1)S(1)} %collective-permute-done.2.end_two, ...), custom_call_target="tpu_custom_call" | custom-call | flops 1207959552 | tf_op jit(solution)/shard_map/pallas_call | solution.py:110
  43.4 9.0 %collective-permute-done.17.end_three = bf16[128,2048]{1,0:T(8,128)(2,1)S(1)} collective-permute-done((bf16[128,2048]{1,0:T(8,128)(2,1)S(1)}, bf16[128,2048]{1,0:T(8,128)(2,1)S(1)}, u32[]{:S(2)}, u32[]{:S(2)}) %collective-permute-start.17) | collective-permute-done | bytes 524320 | tf_op jit(solution)/shard_map/ppermute | solution.py:287
  52.3 2.2 %shard_map.100 = bf16[256,128]{1,0:T(8,128)(2,1)S(1)} custom-call(bf16[128,2048]{1,0:T(8,128)(2,1)S(1)} %collective-permute-done.17.end_three, bf16[128,2048]{1,0:T(8,128)(2,1)S(1)} %collective-permute-done.1.refs_3_.across, f32[256,128]{1,0:T(8,128)S(1)} %get-tuple-element.31.earlier.here, bf16[192,2048]{1,0:T(8,128)(2,1)S(1)} %bitcast.18, ...), custom_call_target="tpu_custom_call" | custom-call | tf_op jit(solution)/shard_map/pallas_call | solution.py:110
  54.5 2.4 %collective-permute-start.18 = (bf16[256,128]{1,0:T(8,128)(2,1)S(1)}, bf16[256,128]{1,0:T(8,128)(2,1)S(1)}, u32[]{:S(2)}, u32[]{:S(2)}) collective-permute-start(bf16[256,128]{1,0:T(8,128)(2,1)S(1)} %shard_map.100), channel_id=1, source_target_pairs={{0,12},{4,8},{8,4},{12,0},{1,13},{5,9},{9,5},{13,1},{2,14},{6,10},... | collective-permute-start | bytes 196616 | tf_op jit(solution)/shard_map/ppermute | solution.py:300
  56.9 2.1 %collective-permute-start.16 = (bf16[256,128]{1,0:T(8,128)(2,1)S(1)}, bf16[256,128]{1,0:T(8,128)(2,1)S(1)}, u32[]{:S(2)}, u32[]{:S(2)}) collective-permute-start(bf16[256,128]{1,0:T(8,128)(2,1)S(1)} %get-tuple-element.33), channel_id=1, source_target_pairs={{0,8},{4,12},{8,0},{12,4},{1,9},{5,13},{9,1},{13,5},{2,10},{6,14},... | collective-permute-start | bytes 196616 | tf_op jit(solution)/shard_map/ppermute | solution.py:300
  58.9 1.8 %collective-permute-done.18.three = bf16[256,128]{1,0:T(8,128)(2,1)S(1)} collective-permute-done((bf16[256,128]{1,0:T(8,128)(2,1)S(1)}, bf16[256,128]{1,0:T(8,128)(2,1)S(1)}, u32[]{:S(2)}, u32[]{:S(2)}) %collective-permute-start.18) | collective-permute-done | bytes 65568 | tf_op jit(solution)/shard_map/ppermute | solution.py:300
  60.8 1.9 %collective-permute-done.15.near = bf16[256,128]{1,0:T(8,128)(2,1)S(1)} collective-permute-done((bf16[256,128]{1,0:T(8,128)(2,1)S(1)}, bf16[256,128]{1,0:T(8,128)(2,1)S(1)}, u32[]{:S(2)}, u32[]{:S(2)}) %collective-permute-start.15) | collective-permute-done | bytes 65568 | tf_op jit(solution)/shard_map/ppermute | solution.py:300
  62.7 1.3 %shard_map.101 = f32[2,64]{1,0:T(2,128)} custom-call(f32[128,128]{1,0:T(8,128)S(1)} %get-tuple-element.21.base, f32[256,128]{1,0:T(8,128)S(1)} %get-tuple-element.31.earlier.here, bf16[256,128]{1,0:T(8,128)(2,1)S(1)} %collective-permute-done.15.near, bf16[256,128]{1,0:T(8,128)(2,1)S(1)} %collective-permute-done.16.two, ...), custom_call_target="tpu_custom_call" | custom-call | tf_op jit(solution)/shard_map/pallas_call | solution.py:110
  (49 shorter events, 5.7 us)
Async XLA Ops:
  0.0 11.2 %collective-permute-start.4 = (bf16[192,2048]{1,0:T(8,128)(2,1)}, bf16[192,2048]{1,0:T(8,128)(2,1)S(1)}, u32[]{:S(2)}, u32[]{:S(2)}) collective-permute-start(bf16[192,2048]{1,0:T(8,128)(2,1)} %bitcast.13), channel_id=1, source_target_pairs={{0,1},{1,0},{2,3},{3,2},{4,5},{5,4},{6,7},{7,6},{8,9},{9,8},{10,11... | collective-permute-start | bytes 2359304 | tf_op jit(solution)/shard_map/ppermute | solution.py:274
  0.5 16.1 %collective-permute-start.5 = (bf16[192,2048]{1,0:T(8,128)(2,1)}, bf16[192,2048]{1,0:T(8,128)(2,1)S(1)}, u32[]{:S(2)}, u32[]{:S(2)}) collective-permute-start(bf16[192,2048]{1,0:T(8,128)(2,1)} %bitcast.19), channel_id=1, source_target_pairs={{0,1},{1,0},{2,3},{3,2},{4,5},{5,4},{6,7},{7,6},{8,9},{9,8},{10,11... | collective-permute-start | bytes 2359304 | tf_op jit(solution)/shard_map/ppermute | solution.py:274
  0.5 15.3 %collective-permute-start = (bf16[128,2048]{1,0:T(8,128)(2,1)}, bf16[128,2048]{1,0:T(8,128)(2,1)S(1)}, u32[]{:S(2)}, u32[]{:S(2)}) collective-permute-start(bf16[128,2048]{1,0:T(8,128)(2,1)} %tokens.5), channel_id=1, source_target_pairs={{0,4},{4,0},{8,12},{12,8},{1,5},{5,1},{9,13},{13,9},{2,6},{6,2},{1... | collective-permute-start | bytes 1572872 | tf_op jit(solution)/shard_map/ppermute | solution.py:259
  5.8 2.4 %copy-start.1 = (bf16[1,2048,192]{1,2,0:T(8,128)(2,1)S(1)}, bf16[1,2048,192]{1,2,0:T(8,128)(2,1)}, u32[]{:S(2)}) copy-start(bf16[1,2048,192]{1,2,0:T(8,128)(2,1)} %param.13) | copy-start | bytes 2359300
  5.8 2.4 %copy-start.5 = (bf16[1,2048,192]{1,2,0:T(8,128)(2,1)S(1)}, bf16[1,2048,192]{1,2,0:T(8,128)(2,1)}, u32[]{:S(2)}) copy-start(bf16[1,2048,192]{1,2,0:T(8,128)(2,1)} %param.15) | copy-start | bytes 2359300
  5.9 13.6 %collective-permute-start.7 = (bf16[128,2048]{1,0:T(8,128)(2,1)S(1)}, bf16[128,2048]{1,0:T(8,128)(2,1)S(1)}, u32[]{:S(2)}, u32[]{:S(2)}) collective-permute-start(bf16[128,2048]{1,0:T(8,128)(2,1)S(1)} %shard_map.95), channel_id=1, source_target_pairs={{0,2},{2,0},{1,3},{3,1},{4,6},{6,4},{5,7},{7,5},{8,10},{10,8},{9,1... | collective-permute-start | bytes 1572872 | tf_op jit(solution)/shard_map/ppermute | solution.py:265
  7.4 13.7 %collective-permute-start.1 = (bf16[128,2048]{1,0:T(8,128)(2,1)S(1)}, bf16[128,2048]{1,0:T(8,128)(2,1)S(1)}, u32[]{:S(2)}, u32[]{:S(2)}) collective-permute-start(bf16[128,2048]{1,0:T(8,128)(2,1)S(1)} %copy-done.4), channel_id=1, source_target_pairs={{4,8},{8,4},{5,9},{9,5},{6,10},{10,6},{7,11},{11,7},{20,24},{24,20... | collective-permute-start | bytes 1572872 | tf_op jit(solution)/shard_map/ppermute | solution.py:260
  11.2 5.3 %collective-permute-start.6 = (bf16[16,2048]{1,0:T(8,128)(2,1)S(1)}, bf16[16,2048]{1,0:T(8,128)(2,1)S(1)}, u32[]{:S(2)}, u32[]{:S(2)}) collective-permute-start(bf16[16,2048]{1,0:T(8,128)(2,1)S(1)} %shard_map.92), channel_id=1, source_target_pairs={{0,1},{1,0},{2,3},{3,2},{4,5},{5,4},{6,7},{7,6},{8,9},{9,8},{10,11... | collective-permute-start | bytes 196616 | tf_op jit(solution)/shard_map/ppermute | solution.py:275
  15.8 19.2 %collective-permute-start.3 = (bf16[128,2048]{1,0:T(8,128)(2,1)S(1)}, bf16[128,2048]{1,0:T(8,128)(2,1)S(1)}, u32[]{:S(2)}, u32[]{:S(2)}) collective-permute-start(bf16[128,2048]{1,0:T(8,128)(2,1)S(1)} %collective-permute-done.near.refs_2_), channel_id=1, source_target_pairs={{4,8},{8,4},{5,9},{9,5},{6,10},{10,6},{7,11},{11,7},{20,24},{24,20... | collective-permute-start | bytes 1572872 | tf_op jit(solution)/shard_map/ppermute | solution.py:279
  19.5 15.5 %collective-permute-start.8 = (bf16[128,2048]{1,0:T(8,128)(2,1)S(1)}, bf16[128,2048]{1,0:T(8,128)(2,1)S(1)}, u32[]{:S(2)}, u32[]{:S(2)}) collective-permute-start(bf16[128,2048]{1,0:T(8,128)(2,1)S(1)} %shard_map.96.refs_0_.refs_6_), channel_id=1, source_target_pairs={{0,16},{16,0},{1,17},{17,1},{2,18},{18,2},{3,19},{19,3},{4,20},{20... | collective-permute-start | bytes 1572872 | tf_op jit(solution)/shard_map/ppermute | solution.py:283
  21.2 13.9 %collective-permute-start.9 = (bf16[80,2048]{1,0:T(8,128)(2,1)S(1)}, bf16[80,2048]{1,0:T(8,128)(2,1)S(1)}, u32[]{:S(2)}, u32[]{:S(2)}) collective-permute-start(bf16[80,2048]{1,0:T(8,128)(2,1)S(1)} %get-tuple-element.25), channel_id=1, source_target_pairs={{0,2},{2,0},{1,3},{3,1},{4,6},{6,4},{5,7},{7,5},{8,10},{10,8},{9,1... | collective-permute-start | bytes 983048 | tf_op jit(solution)/shard_map/ppermute | solution.py:281
  22.7 14.8 %collective-permute-start.2 = (bf16[128,2048]{1,0:T(8,128)(2,1)S(1)}, bf16[128,2048]{1,0:T(8,128)(2,1)S(1)}, u32[]{:S(2)}, u32[]{:S(2)}) collective-permute-start(bf16[128,2048]{1,0:T(8,128)(2,1)S(1)} %collective-permute-done.1.refs_3_.across), channel_id=1, source_target_pairs={{4,0},{8,12},{5,1},{9,13},{6,2},{10,14},{7,3},{11,15},{20,16},{24,... | collective-permute-start | bytes 1572872 | tf_op jit(solution)/shard_map/ppermute | solution.py:280
  24.0 14.6 %copy-start.7 = (bf16[32,32,128]{2,1,0:T(8,128)(2,1)S(1)}, bf16[32,32,128]{2,1,0:T(8,128)(2,1)}, u32[]{:S(2)}) copy-start(bf16[32,32,128]{2,1,0:T(8,128)(2,1)} %param.17) | copy-start | bytes 786436
  24.0 11.0 %collective-permute-start.10 = (bf16[64,2048]{1,0:T(8,128)(2,1)S(1)}, bf16[64,2048]{1,0:T(8,128)(2,1)S(1)}, u32[]{:S(2)}, u32[]{:S(2)}) collective-permute-start(bf16[64,2048]{1,0:T(8,128)(2,1)S(1)} %get-tuple-element.26), channel_id=1, source_target_pairs={{0,2},{2,0},{1,3},{3,1},{4,6},{6,4},{5,7},{7,5},{8,10},{10,8},{9,1... | collective-permute-start | bytes 786440 | tf_op jit(solution)/shard_map/ppermute | solution.py:281
  35.1 6.2 %collective-permute-start.11 = (bf16[128,2048]{1,0:T(8,128)(2,1)S(1)}, bf16[128,2048]{1,0:T(8,128)(2,1)S(1)}, u32[]{:S(2)}, u32[]{:S(2)}) collective-permute-start(bf16[128,2048]{1,0:T(8,128)(2,1)S(1)} %get-tuple-element.27), channel_id=1, source_target_pairs={{0,1},{1,0},{2,3},{3,2},{4,5},{5,4},{6,7},{7,6},{8,9},{9,8},{10,11... | collective-permute-start | bytes 1572872 | tf_op jit(solution)/shard_map/ppermute | solution.py:289
  35.2 6.1 %collective-permute-start.12 = (bf16[128,2048]{1,0:T(8,128)(2,1)S(1)}, bf16[128,2048]{1,0:T(8,128)(2,1)S(1)}, u32[]{:S(2)}, u32[]{:S(2)}) collective-permute-start(bf16[128,2048]{1,0:T(8,128)(2,1)S(1)} %get-tuple-element.28), channel_id=1, source_target_pairs={{0,1},{1,0},{2,3},{3,2},{4,5},{5,4},{6,7},{7,6},{8,9},{9,8},{10,11... | collective-permute-start | bytes 1572872 | tf_op jit(solution)/shard_map/ppermute | solution.py:289
  35.7 16.6 %collective-permute-start.17 = (bf16[128,2048]{1,0:T(8,128)(2,1)S(1)}, bf16[128,2048]{1,0:T(8,128)(2,1)S(1)}, u32[]{:S(2)}, u32[]{:S(2)}) collective-permute-start(bf16[128,2048]{1,0:T(8,128)(2,1)S(1)} %collective-permute-done.3.far_inner.refs_4_), channel_id=1, source_target_pairs={{4,0},{8,12},{5,1},{9,13},{6,2},{10,14},{7,3},{11,15},{20,16},{24,... | collective-permute-start | bytes 1572872 | tf_op jit(solution)/shard_map/ppermute | solution.py:287
  37.0 1.6 %collective-permute-start.14 = (bf16[64,2048]{1,0:T(8,128)(2,1)S(1)}, bf16[64,2048]{1,0:T(8,128)(2,1)S(1)}, u32[]{:S(2)}, u32[]{:S(2)}) collective-permute-start(bf16[64,2048]{1,0:T(8,128)(2,1)S(1)} %get-tuple-element.30), channel_id=1, source_target_pairs={{0,1},{1,0},{2,3},{3,2},{4,5},{5,4},{6,7},{7,6},{8,9},{9,8},{10,11... | collective-permute-start | bytes 786440 | tf_op jit(solution)/shard_map/ppermute | solution.py:289
  37.5 3.8 %collective-permute-start.13 = (bf16[80,2048]{1,0:T(8,128)(2,1)S(1)}, bf16[80,2048]{1,0:T(8,128)(2,1)S(1)}, u32[]{:S(2)}, u32[]{:S(2)}) collective-permute-start(bf16[80,2048]{1,0:T(8,128)(2,1)S(1)} %get-tuple-element.29), channel_id=1, source_target_pairs={{0,1},{1,0},{2,3},{3,2},{4,5},{5,4},{6,7},{7,6},{8,9},{9,8},{10,11... | collective-permute-start | bytes 983048 | tf_op jit(solution)/shard_map/ppermute | solution.py:289
  38.6 20.3 %collective-permute-start.19 = (bf16[32,32,128]{2,1,0:T(8,128)(2,1)S(1)}, bf16[32,32,128]{2,1,0:T(8,128)(2,1)S(1)}, u32[]{:S(2)}, u32[]{:S(2)}) collective-permute-start(bf16[32,32,128]{2,1,0:T(8,128)(2,1)S(1)} %copy-done.7), channel_id=1, source_target_pairs={{0,2},{2,0},{1,3},{3,1},{4,6},{6,4},{5,7},{7,5},{8,10},{10,8},{9,1... | collective-permute-start | bytes 786440 | tf_op jit(solution)/shard_map/ppermute | solution.py:290
  41.3 11.0 %copy-start.3 = (bf16[1,2048,192]{1,2,0:T(8,128)(2,1)S(1)}, bf16[1,2048,192]{1,2,0:T(8,128)(2,1)}, u32[]{:S(2)}) copy-start(bf16[1,2048,192]{1,2,0:T(8,128)(2,1)} %param.14) | copy-start | bytes 2359300
  54.5 6.3 %collective-permute-start.18 = (bf16[256,128]{1,0:T(8,128)(2,1)S(1)}, bf16[256,128]{1,0:T(8,128)(2,1)S(1)}, u32[]{:S(2)}, u32[]{:S(2)}) collective-permute-start(bf16[256,128]{1,0:T(8,128)(2,1)S(1)} %shard_map.100), channel_id=1, source_target_pairs={{0,12},{4,8},{8,4},{12,0},{1,13},{5,9},{9,5},{13,1},{2,14},{6,10},... | collective-permute-start | bytes 196616 | tf_op jit(solution)/shard_map/ppermute | solution.py:300
  56.9 5.8 %collective-permute-start.15 = (bf16[256,128]{1,0:T(8,128)(2,1)S(1)}, bf16[256,128]{1,0:T(8,128)(2,1)S(1)}, u32[]{:S(2)}, u32[]{:S(2)}) collective-permute-start(bf16[256,128]{1,0:T(8,128)(2,1)S(1)} %get-tuple-element.32), channel_id=1, source_target_pairs={{0,4},{4,0},{8,12},{12,8},{1,5},{5,1},{9,13},{13,9},{2,6},{6,2},{1... | collective-permute-start | bytes 196616 | tf_op jit(solution)/shard_map/ppermute | solution.py:300
  56.9 5.8 %collective-permute-start.16 = (bf16[256,128]{1,0:T(8,128)(2,1)S(1)}, bf16[256,128]{1,0:T(8,128)(2,1)S(1)}, u32[]{:S(2)}, u32[]{:S(2)}) collective-permute-start(bf16[256,128]{1,0:T(8,128)(2,1)S(1)} %get-tuple-element.33), channel_id=1, source_target_pairs={{0,8},{4,12},{8,0},{12,4},{1,9},{5,13},{9,1},{13,5},{2,10},{6,14},... | collective-permute-start | bytes 196616 | tf_op jit(solution)/shard_map/ppermute | solution.py:300
  (7 other events, 7.0 us)

commit v5 on v4

--- a/solution.py
+++ b/solution.py
@@ -259,7 +259,7 @@
     near = lax.ppermute(tokens, E, [(i, i ^ 1) for i in range(4)])
     across = lax.ppermute(tokens, E, middle)
     gate, up, down = gate_weight[0].T, up_weight[0].T, down_weight[0].T
-    part_rows = 2 * hidden_part // 3 // 16 * 16
+    part_rows = min(2 * hidden_part // 3, n - 1) // 16 * 16
     left = hidden_part - part_rows
     (part,) = kernel(part_body, [gate, up], [((part_rows, model_width), bf16)])
     part_x = lax.ppermute(part, Q, swap)
@@ -281,8 +281,7 @@
     rest_x = [lax.ppermute(a, Q, swap) for a in tied([rest_gate, rest_up], [near, across], 1)]
     (part_x,) = tied([part_x], [got_own], 1)
     part_y = lax.ppermute(part_x, G, swap)
-    work = 8 * n * model_width * hidden_part
-    (got_two,) = kernel(two_body, [end_two, far_inner, *own], [((width, n), f32)], flops=work)
+    (got_two,) = kernel(two_body, [end_two, far_inner, *own], [((width, n), f32)])
 
     end_three = lax.ppermute(far_inner, E, ends)
     other = [part_x, part_y, *rest_x]
@@ -293,7 +292,6 @@
         [tokens, near, end_two, far_inner, got_own, got_two, *other],
         [(both, f32), (both, bf16), (both, bf16)],
         fetched=(0,),
-        flops=3 * work,
     )
     back += kernel(third_body, [end_three, across, here, *own, *other], [(both, bf16)])
     from_near, two, three = (

time: 64.3 us -> 59.8 us (0.930)
  waiting for transfers between devices: 30.8 us -> 26 us
    ppermute x1, waiting for transfers between devices: 8.96 us -> 2.33 us  [by_column(): end_three = lax.ppermute(far_inner, E, ends)]
    ppermute x2, waiting for transfers between devices: 10.4 us -> 13.3 us  [by_column(): lax.ppermute(a, Q, swap)]
    ppermute x1, waiting for transfers between devices: 1.73 us -> 1.01 us  [by_column(): part_x = lax.ppermute(part, Q, swap)]
  transfers between devices with their start and end apart: 20 -> 20, of which waited for: 8 -> 7; matrix products, arithmetic and copies ran while one was open for 0% -> 0% of each run, Pallas kernels for 13% -> 14%
where the time goes in v5:
time: 59.8 us; the launch traced here: 59.5 us
  waiting for transfers between devices  26 us (43%)
  starting transfers between devices  19.8 us (33%)
  Pallas kernels  9.39 us (16%)
  local copies, waits for them, and re-layouts  4.09 us (7%)
    ppermute x2, waiting for transfers between devices, by_column(): lax.ppermute(a, Q, swap)  13.3 us
    pallas_call x7, Pallas kernels, kernel(): pl.pallas_call(body, out_shape=[jax.ShapeDtypeStruct(shape, dtype) for sh...  9.19 us
    ppermute x1, waiting for transfers between devices, by_column(): near = lax.ppermute(tokens, E, [(i, i ^ 1) for i in range(4)])  4.46 us
    ppermute x3, starting transfers between devices, by_column(): lax.ppermute(a, E, [(i, i ^ k) for i in range(4)])  4.45 us
    ppermute x3, waiting for transfers between devices, by_column(): lax.ppermute(a, E, [(i, i ^ k) for i in range(4)])  4.3 us
    unnamed x22, local copies, waits for them, and re-layouts  4.09 us
    ppermute x1, starting transfers between devices, by_column(): near = lax.ppermute(tokens, E, [(i, i ^ 1) for i in range(4)])  3.02 us
    ppermute x1, waiting for transfers between devices, by_column(): end_three = lax.ppermute(far_inner, E, ends)  2.33 us
  transfers between devices with their start and end apart: 20, of which 7 were waited for; matrix products, arithmetic and copies ran while one was open for 0% of the time, Pallas kernels for 14%

profile of v5, /device:TPU:0, one launch (start us, length us, event | category | flops | bytes accessed | tf_op | source)
XLA Modules:
  0.0 59.5 jit_solution(3435917685320760817)
XLA Ops:
  0.5 3.0 %collective-permute-start = (bf16[128,2048]{1,0:T(8,128)(2,1)}, bf16[128,2048]{1,0:T(8,128)(2,1)S(1)}, u32[]{:S(2)}, u32[]{:S(2)}) collective-permute-start(bf16[128,2048]{1,0:T(8,128)(2,1)} %tokens.5), channel_id=1, source_target_pairs={{0,4},{4,0},{8,12},{12,8},{1,5},{5,1},{9,13},{13,9},{2,6},{6,2},{1... | collective-permute-start | bytes 1572872 | tf_op jit(solution)/shard_map/ppermute | solution.py:259
  4.2 1.1 %copy-done = bf16[1,2048,192]{1,2,0:T(8,128)(2,1)S(1)} copy-done((bf16[1,2048,192]{1,2,0:T(8,128)(2,1)S(1)}, bf16[1,2048,192]{1,2,0:T(8,128)(2,1)}, u32[]{:S(2)}) %copy-start) | copy-done | bytes 786456
  5.4 1.1 %copy-done.2 = bf16[1,2048,192]{1,2,0:T(8,128)(2,1)S(1)} copy-done((bf16[1,2048,192]{1,2,0:T(8,128)(2,1)S(1)}, bf16[1,2048,192]{1,2,0:T(8,128)(2,1)}, u32[]{:S(2)}) %copy-start.2) | copy-done | bytes 786456
  6.6 1.6 %collective-permute-start.7 = (bf16[112,2048]{1,0:T(8,128)(2,1)S(1)}, bf16[112,2048]{1,0:T(8,128)(2,1)S(1)}, u32[]{:S(2)}, u32[]{:S(2)}) collective-permute-start(bf16[112,2048]{1,0:T(8,128)(2,1)S(1)} %shard_map.95), channel_id=1, source_target_pairs={{0,2},{2,0},{1,3},{3,1},{4,6},{6,4},{5,7},{7,5},{8,10},{10,8},{9,1... | collective-permute-start | bytes 1376264 | tf_op jit(solution)/shard_map/ppermute | solution.py:265
  8.8 1.1 %copy-done.5 = bf16[1,2048,192]{1,2,0:T(8,128)(2,1)S(1)} copy-done((bf16[1,2048,192]{1,2,0:T(8,128)(2,1)S(1)}, bf16[1,2048,192]{1,2,0:T(8,128)(2,1)}, u32[]{:S(2)}) %copy-start.5) | copy-done | bytes 786456
  9.9 1.3 %shard_map.91 = (bf16[16,2048]{1,0:T(8,128)(2,1)S(1)}, bf16[96,2048]{1,0:T(8,128)(2,1)S(1)}, bf16[80,2048]{1,0:T(8,128)(2,1)S(1)}, f32[128,128]{1,0:T(8,128)S(1)...) custom-call(s32[2]{0:T(128)S(1)} %copy-done.10, bf16[128,2048]{1,0:T(8,128)(2,1)S(1)} %copy-done.4, ...), custom_call_target="tpu_custom_call" | custom-call | tf_op jit(solution)/shard_map/pallas_call | solution.py:110
  11.4 4.5 %collective-permute-done.near.refs_2_ = bf16[128,2048]{1,0:T(8,128)(2,1)S(1)} collective-permute-done((bf16[128,2048]{1,0:T(8,128)(2,1)}, bf16[128,2048]{1,0:T(8,128)(2,1)S(1)}, u32[]{:S(2)}, u32[]{:S(2)}) %collective-permute-start) | collective-permute-done | bytes 524320 | tf_op jit(solution)/shard_map/ppermute | solution.py:259
  16.5 1.2 %shard_map.93.refs_1_.got_own = f32[128,256]{1,0:T(8,128)S(1)} custom-call(bf16[128,2048]{1,0:T(8,128)(2,1)S(1)} %copy-done.4, bf16[128,2048]{1,0:T(8,128)(2,1)S(1)} %collective-permute-done.near.refs_2_, bf16[192,2048]{1,0:T(8,128)(2,1)S(1)} %bitcast.16, bf16[192,2048]{1,0:T(8,128)(2,1)S(1)} %bitcast.22, ...), custom_call_target="tpu_custom_call" | custom-call | tf_op jit(solution)/shard_map/pallas_call | solution.py:110
  17.8 1.0 %collective-permute-done.7.refs_0_ = bf16[112,2048]{1,0:T(8,128)(2,1)S(1)} collective-permute-done((bf16[112,2048]{1,0:T(8,128)(2,1)S(1)}, bf16[112,2048]{1,0:T(8,128)(2,1)S(1)}, u32[]{:S(2)}, u32[]{:S(2)}) %collective-permute-start.7) | collective-permute-done | bytes 458784 | tf_op jit(solution)/shard_map/ppermute | solution.py:265
  18.8 1.6 %collective-permute-start.8 = (bf16[112,2048]{1,0:T(8,128)(2,1)S(1)}, bf16[112,2048]{1,0:T(8,128)(2,1)S(1)}, u32[]{:S(2)}, u32[]{:S(2)}) collective-permute-start(bf16[112,2048]{1,0:T(8,128)(2,1)S(1)} %shard_map.96.refs_0_.refs_6_), channel_id=1, source_target_pairs={{0,16},{16,0},{1,17},{17,1},{2,18},{18,2},{3,19},{19,3},{4,20},{20... | collective-permute-start | bytes 1376264 | tf_op jit(solution)/shard_map/ppermute | solution.py:283
  20.4 1.3 %collective-permute-start.2 = (bf16[128,2048]{1,0:T(8,128)(2,1)S(1)}, bf16[128,2048]{1,0:T(8,128)(2,1)S(1)}, u32[]{:S(2)}, u32[]{:S(2)}) collective-permute-start(bf16[128,2048]{1,0:T(8,128)(2,1)S(1)} %collective-permute-done.1.refs_3_.across), channel_id=1, source_target_pairs={{4,0},{8,12},{5,1},{9,13},{6,2},{10,14},{7,3},{11,15},{20,16},{24,... | collective-permute-start | bytes 1572872 | tf_op jit(solution)/shard_map/ppermute | solution.py:280
  21.7 1.6 %collective-permute-start.9 = (bf16[96,2048]{1,0:T(8,128)(2,1)S(1)}, bf16[96,2048]{1,0:T(8,128)(2,1)S(1)}, u32[]{:S(2)}, u32[]{:S(2)}) collective-permute-start(bf16[96,2048]{1,0:T(8,128)(2,1)S(1)} %get-tuple-element.25), channel_id=1, source_target_pairs={{0,2},{2,0},{1,3},{3,1},{4,6},{6,4},{5,7},{7,5},{8,10},{10,8},{9,1... | collective-permute-start | bytes 1179656 | tf_op jit(solution)/shard_map/ppermute | solution.py:281
  23.8 1.3 %collective-permute-start.17 = (bf16[128,2048]{1,0:T(8,128)(2,1)S(1)}, bf16[128,2048]{1,0:T(8,128)(2,1)S(1)}, u32[]{:S(2)}, u32[]{:S(2)}) collective-permute-start(bf16[128,2048]{1,0:T(8,128)(2,1)S(1)} %collective-permute-done.3.far_inner.refs_4_), channel_id=1, source_target_pairs={{4,0},{8,12},{5,1},{9,13},{6,2},{10,14},{7,3},{11,15},{20,16},{24,... | collective-permute-start | bytes 1572872 | tf_op jit(solution)/shard_map/ppermute | solution.py:286
  25.1 13.3 %collective-permute-done.10.refs_3_.refs_9_ = bf16[80,2048]{1,0:T(8,128)(2,1)S(1)} collective-permute-done((bf16[80,2048]{1,0:T(8,128)(2,1)S(1)}, bf16[80,2048]{1,0:T(8,128)(2,1)S(1)}, u32[]{:S(2)}, u32[]{:S(2)}) %collective-permute-start.10) | collective-permute-done | bytes 327712 | tf_op jit(solution)/shard_map/ppermute | solution.py:281
  40.2 1.5 %collective-permute-start.19 = (bf16[32,32,128]{2,1,0:T(8,128)(2,1)S(1)}, bf16[32,32,128]{2,1,0:T(8,128)(2,1)S(1)}, u32[]{:S(2)}, u32[]{:S(2)}) collective-permute-start(bf16[32,32,128]{2,1,0:T(8,128)(2,1)S(1)} %copy-done.7), channel_id=1, source_target_pairs={{0,2},{2,0},{1,3},{3,1},{4,6},{6,4},{5,7},{7,5},{8,10},{10,8},{9,1... | collective-permute-start | bytes 786440 | tf_op jit(solution)/shard_map/ppermute | solution.py:289
  41.7 1.2 %shard_map.94.got_two = f32[128,128]{1,0:T(8,128)S(1)} custom-call(bf16[128,2048]{1,0:T(8,128)(2,1)S(1)} %collective-permute-done.2.end_two, bf16[128,2048]{1,0:T(8,128)(2,1)S(1)} %collective-permute-done.3.far_inner.refs_4_, bf16[192,2048]{1,0:T(8,128)(2,1)S(1)} %bitcast.17, bf16[192,2048]{1,0:T(8,128)(2,1)S(1)} %bitcast.23, ...), custom_call_target="tpu_custom_call" | custom-call | tf_op jit(solution)/shard_map/pallas_call | solution.py:110
  43.0 2.0 %shard_map.99 = (f32[256,128]{1,0:T(8,128)S(1)}, bf16[256,128]{1,0:T(8,128)(2,1)S(1)}, bf16[256,128]{1,0:T(8,128)(2,1)S(1)}) custom-call(bf16[128,2048]{1,0:T(8,128)(2,1)S(1)} %copy-done.4, bf16[128,2048]{1,0:T(8,128)(2,1)S(1)} %collective-permute-done.near.refs_2_, bf16[128,2048]{1,0:T(8,128)(2,1)S(1)} %collective-permute-done.2.end_two, ...), custom_call_target="tpu_custom_call" | custom-call | tf_op jit(solution)/shard_map/pallas_call | solution.py:110
  45.0 2.3 %collective-permute-done.17.end_three = bf16[128,2048]{1,0:T(8,128)(2,1)S(1)} collective-permute-done((bf16[128,2048]{1,0:T(8,128)(2,1)S(1)}, bf16[128,2048]{1,0:T(8,128)(2,1)S(1)}, u32[]{:S(2)}, u32[]{:S(2)}) %collective-permute-start.17) | collective-permute-done | bytes 524320 | tf_op jit(solution)/shard_map/ppermute | solution.py:286
  47.3 2.2 %shard_map.100 = bf16[256,128]{1,0:T(8,128)(2,1)S(1)} custom-call(bf16[128,2048]{1,0:T(8,128)(2,1)S(1)} %collective-permute-done.17.end_three, bf16[128,2048]{1,0:T(8,128)(2,1)S(1)} %collective-permute-done.1.refs_3_.across, f32[256,128]{1,0:T(8,128)S(1)} %get-tuple-element.31.earlier.here, bf16[192,2048]{1,0:T(8,128)(2,1)S(1)} %bitcast.18, ...), custom_call_target="tpu_custom_call" | custom-call | tf_op jit(solution)/shard_map/pallas_call | solution.py:110
  49.5 1.8 %collective-permute-start.18 = (bf16[256,128]{1,0:T(8,128)(2,1)S(1)}, bf16[256,128]{1,0:T(8,128)(2,1)S(1)}, u32[]{:S(2)}, u32[]{:S(2)}) collective-permute-start(bf16[256,128]{1,0:T(8,128)(2,1)S(1)} %shard_map.100), channel_id=1, source_target_pairs={{0,12},{4,8},{8,4},{12,0},{1,13},{5,9},{9,5},{13,1},{2,14},{6,10},... | collective-permute-start | bytes 196616 | tf_op jit(solution)/shard_map/ppermute | solution.py:298
  51.8 2.1 %collective-permute-start.16 = (bf16[256,128]{1,0:T(8,128)(2,1)S(1)}, bf16[256,128]{1,0:T(8,128)(2,1)S(1)}, u32[]{:S(2)}, u32[]{:S(2)}) collective-permute-start(bf16[256,128]{1,0:T(8,128)(2,1)S(1)} %get-tuple-element.33), channel_id=1, source_target_pairs={{0,8},{4,12},{8,0},{12,4},{1,9},{5,13},{9,1},{13,5},{2,10},{6,14},... | collective-permute-start | bytes 196616 | tf_op jit(solution)/shard_map/ppermute | solution.py:298
  53.9 2.4 %collective-permute-done.18.three = bf16[256,128]{1,0:T(8,128)(2,1)S(1)} collective-permute-done((bf16[256,128]{1,0:T(8,128)(2,1)S(1)}, bf16[256,128]{1,0:T(8,128)(2,1)S(1)}, u32[]{:S(2)}, u32[]{:S(2)}) %collective-permute-start.18) | collective-permute-done | bytes 65568 | tf_op jit(solution)/shard_map/ppermute | solution.py:298
  56.3 1.9 %collective-permute-done.16.two = bf16[256,128]{1,0:T(8,128)(2,1)S(1)} collective-permute-done((bf16[256,128]{1,0:T(8,128)(2,1)S(1)}, bf16[256,128]{1,0:T(8,128)(2,1)S(1)}, u32[]{:S(2)}, u32[]{:S(2)}) %collective-permute-start.16) | collective-permute-done | bytes 65568 | tf_op jit(solution)/shard_map/ppermute | solution.py:298
  58.2 1.3 %shard_map.101 = f32[2,64]{1,0:T(2,128)} custom-call(f32[128,128]{1,0:T(8,128)S(1)} %get-tuple-element.21.base, f32[256,128]{1,0:T(8,128)S(1)} %get-tuple-element.31.earlier.here, bf16[256,128]{1,0:T(8,128)(2,1)S(1)} %collective-permute-done.15.near, bf16[256,128]{1,0:T(8,128)(2,1)S(1)} %collective-permute-done.16.two, ...), custom_call_target="tpu_custom_call" | custom-call | tf_op jit(solution)/shard_map/pallas_call | solution.py:110
  (49 shorter events, 5.7 us)
Async XLA Ops:
  0.0 11.3 %collective-permute-start.4 = (bf16[192,2048]{1,0:T(8,128)(2,1)}, bf16[192,2048]{1,0:T(8,128)(2,1)S(1)}, u32[]{:S(2)}, u32[]{:S(2)}) collective-permute-start(bf16[192,2048]{1,0:T(8,128)(2,1)} %bitcast.13), channel_id=1, source_target_pairs={{0,1},{1,0},{2,3},{3,2},{4,5},{5,4},{6,7},{7,6},{8,9},{9,8},{10,11... | collective-permute-start | bytes 2359304 | tf_op jit(solution)/shard_map/ppermute | solution.py:274
  0.5 16.1 %collective-permute-start.5 = (bf16[192,2048]{1,0:T(8,128)(2,1)}, bf16[192,2048]{1,0:T(8,128)(2,1)S(1)}, u32[]{:S(2)}, u32[]{:S(2)}) collective-permute-start(bf16[192,2048]{1,0:T(8,128)(2,1)} %bitcast.19), channel_id=1, source_target_pairs={{0,1},{1,0},{2,3},{3,2},{4,5},{5,4},{6,7},{7,6},{8,9},{9,8},{10,11... | collective-permute-start | bytes 2359304 | tf_op jit(solution)/shard_map/ppermute | solution.py:274
  0.5 15.3 %collective-permute-start = (bf16[128,2048]{1,0:T(8,128)(2,1)}, bf16[128,2048]{1,0:T(8,128)(2,1)S(1)}, u32[]{:S(2)}, u32[]{:S(2)}) collective-permute-start(bf16[128,2048]{1,0:T(8,128)(2,1)} %tokens.5), channel_id=1, source_target_pairs={{0,4},{4,0},{8,12},{12,8},{1,5},{5,1},{9,13},{13,9},{2,6},{6,2},{1... | collective-permute-start | bytes 1572872 | tf_op jit(solution)/shard_map/ppermute | solution.py:259
  3.5 16.9 %collective-permute-start.1 = (bf16[128,2048]{1,0:T(8,128)(2,1)}, bf16[128,2048]{1,0:T(8,128)(2,1)S(1)}, u32[]{:S(2)}, u32[]{:S(2)}) collective-permute-start(bf16[128,2048]{1,0:T(8,128)(2,1)} %tokens.5), channel_id=1, source_target_pairs={{4,8},{8,4},{5,9},{9,5},{6,10},{10,6},{7,11},{11,7},{20,24},{24,20... | collective-permute-start | bytes 1572872 | tf_op jit(solution)/shard_map/ppermute | solution.py:260
  6.5 1.6 %copy-start.4 = (bf16[128,2048]{1,0:T(8,128)(2,1)S(1)}, bf16[128,2048]{1,0:T(8,128)(2,1)}, u32[]{:S(2)}) copy-start(bf16[128,2048]{1,0:T(8,128)(2,1)} %tokens.5) | copy-start | bytes 1572868
  6.5 1.6 %copy-start.6 = (bf16[2048,128]{1,0:T(8,128)(2,1)S(1)}, bf16[2048,128]{1,0:T(8,128)(2,1)}, u32[]{:S(2)}) copy-start(bf16[2048,128]{1,0:T(8,128)(2,1)} %proj.1) | copy-start | bytes 1572868
  6.6 12.2 %collective-permute-start.7 = (bf16[112,2048]{1,0:T(8,128)(2,1)S(1)}, bf16[112,2048]{1,0:T(8,128)(2,1)S(1)}, u32[]{:S(2)}, u32[]{:S(2)}) collective-permute-start(bf16[112,2048]{1,0:T(8,128)(2,1)S(1)} %shard_map.95), channel_id=1, source_target_pairs={{0,2},{2,0},{1,3},{3,1},{4,6},{6,4},{5,7},{7,5},{8,10},{10,8},{9,1... | collective-permute-start | bytes 1376264 | tf_op jit(solution)/shard_map/ppermute | solution.py:265
  11.3 5.2 %collective-permute-start.6 = (bf16[16,2048]{1,0:T(8,128)(2,1)S(1)}, bf16[16,2048]{1,0:T(8,128)(2,1)S(1)}, u32[]{:S(2)}, u32[]{:S(2)}) collective-permute-start(bf16[16,2048]{1,0:T(8,128)(2,1)S(1)} %shard_map.92), channel_id=1, source_target_pairs={{0,1},{1,0},{2,3},{3,2},{4,5},{5,4},{6,7},{7,6},{8,9},{9,8},{10,11... | collective-permute-start | bytes 196616 | tf_op jit(solution)/shard_map/ppermute | solution.py:275
  15.8 8.0 %collective-permute-start.3 = (bf16[128,2048]{1,0:T(8,128)(2,1)S(1)}, bf16[128,2048]{1,0:T(8,128)(2,1)S(1)}, u32[]{:S(2)}, u32[]{:S(2)}) collective-permute-start(bf16[128,2048]{1,0:T(8,128)(2,1)S(1)} %collective-permute-done.near.refs_2_), channel_id=1, source_target_pairs={{4,8},{8,4},{5,9},{9,5},{6,10},{10,6},{7,11},{11,7},{20,24},{24,20... | collective-permute-start | bytes 1572872 | tf_op jit(solution)/shard_map/ppermute | solution.py:279
  18.8 19.6 %collective-permute-start.8 = (bf16[112,2048]{1,0:T(8,128)(2,1)S(1)}, bf16[112,2048]{1,0:T(8,128)(2,1)S(1)}, u32[]{:S(2)}, u32[]{:S(2)}) collective-permute-start(bf16[112,2048]{1,0:T(8,128)(2,1)S(1)} %shard_map.96.refs_0_.refs_6_), channel_id=1, source_target_pairs={{0,16},{16,0},{1,17},{17,1},{2,18},{18,2},{3,19},{19,3},{4,20},{20... | collective-permute-start | bytes 1376264 | tf_op jit(solution)/shard_map/ppermute | solution.py:283
  20.4 18.8 %collective-permute-start.2 = (bf16[128,2048]{1,0:T(8,128)(2,1)S(1)}, bf16[128,2048]{1,0:T(8,128)(2,1)S(1)}, u32[]{:S(2)}, u32[]{:S(2)}) collective-permute-start(bf16[128,2048]{1,0:T(8,128)(2,1)S(1)} %collective-permute-done.1.refs_3_.across), channel_id=1, source_target_pairs={{4,0},{8,12},{5,1},{9,13},{6,2},{10,14},{7,3},{11,15},{20,16},{24,... | collective-permute-start | bytes 1572872 | tf_op jit(solution)/shard_map/ppermute | solution.py:280
  21.7 16.7 %collective-permute-start.9 = (bf16[96,2048]{1,0:T(8,128)(2,1)S(1)}, bf16[96,2048]{1,0:T(8,128)(2,1)S(1)}, u32[]{:S(2)}, u32[]{:S(2)}) collective-permute-start(bf16[96,2048]{1,0:T(8,128)(2,1)S(1)} %get-tuple-element.25), channel_id=1, source_target_pairs={{0,2},{2,0},{1,3},{3,1},{4,6},{6,4},{5,7},{7,5},{8,10},{10,8},{9,1... | collective-permute-start | bytes 1179656 | tf_op jit(solution)/shard_map/ppermute | solution.py:281
  23.3 16.9 %copy-start.7 = (bf16[32,32,128]{2,1,0:T(8,128)(2,1)S(1)}, bf16[32,32,128]{2,1,0:T(8,128)(2,1)}, u32[]{:S(2)}) copy-start(bf16[32,32,128]{2,1,0:T(8,128)(2,1)} %param.17) | copy-start | bytes 786436
  23.3 15.1 %collective-permute-start.10 = (bf16[80,2048]{1,0:T(8,128)(2,1)S(1)}, bf16[80,2048]{1,0:T(8,128)(2,1)S(1)}, u32[]{:S(2)}, u32[]{:S(2)}) collective-permute-start(bf16[80,2048]{1,0:T(8,128)(2,1)S(1)} %get-tuple-element.26), channel_id=1, source_target_pairs={{0,2},{2,0},{1,3},{3,1},{4,6},{6,4},{5,7},{7,5},{8,10},{10,8},{9,1... | collective-permute-start | bytes 983048 | tf_op jit(solution)/shard_map/ppermute | solution.py:281
  23.8 23.5 %collective-permute-start.17 = (bf16[128,2048]{1,0:T(8,128)(2,1)S(1)}, bf16[128,2048]{1,0:T(8,128)(2,1)S(1)}, u32[]{:S(2)}, u32[]{:S(2)}) collective-permute-start(bf16[128,2048]{1,0:T(8,128)(2,1)S(1)} %collective-permute-done.3.far_inner.refs_4_), channel_id=1, source_target_pairs={{4,0},{8,12},{5,1},{9,13},{6,2},{10,14},{7,3},{11,15},{20,16},{24,... | collective-permute-start | bytes 1572872 | tf_op jit(solution)/shard_map/ppermute | solution.py:286
  38.5 1.7 %collective-permute-start.14 = (bf16[80,2048]{1,0:T(8,128)(2,1)S(1)}, bf16[80,2048]{1,0:T(8,128)(2,1)S(1)}, u32[]{:S(2)}, u32[]{:S(2)}) collective-permute-start(bf16[80,2048]{1,0:T(8,128)(2,1)S(1)} %get-tuple-element.30), channel_id=1, source_target_pairs={{0,1},{1,0},{2,3},{3,2},{4,5},{5,4},{6,7},{7,6},{8,9},{9,8},{10,11... | collective-permute-start | bytes 983048 | tf_op jit(solution)/shard_map/ppermute | solution.py:288
  38.6 4.3 %collective-permute-start.11 = (bf16[112,2048]{1,0:T(8,128)(2,1)S(1)}, bf16[112,2048]{1,0:T(8,128)(2,1)S(1)}, u32[]{:S(2)}, u32[]{:S(2)}) collective-permute-start(bf16[112,2048]{1,0:T(8,128)(2,1)S(1)} %get-tuple-element.27), channel_id=1, source_target_pairs={{0,1},{1,0},{2,3},{3,2},{4,5},{5,4},{6,7},{7,6},{8,9},{9,8},{10,11... | collective-permute-start | bytes 1376264 | tf_op jit(solution)/shard_map/ppermute | solution.py:288
  39.1 3.9 %collective-permute-start.12 = (bf16[112,2048]{1,0:T(8,128)(2,1)S(1)}, bf16[112,2048]{1,0:T(8,128)(2,1)S(1)}, u32[]{:S(2)}, u32[]{:S(2)}) collective-permute-start(bf16[112,2048]{1,0:T(8,128)(2,1)S(1)} %get-tuple-element.28), channel_id=1, source_target_pairs={{0,1},{1,0},{2,3},{3,2},{4,5},{5,4},{6,7},{7,6},{8,9},{9,8},{10,11... | collective-permute-start | bytes 1376264 | tf_op jit(solution)/shard_map/ppermute | solution.py:288
  39.2 3.8 %collective-permute-start.13 = (bf16[96,2048]{1,0:T(8,128)(2,1)S(1)}, bf16[96,2048]{1,0:T(8,128)(2,1)S(1)}, u32[]{:S(2)}, u32[]{:S(2)}) collective-permute-start(bf16[96,2048]{1,0:T(8,128)(2,1)S(1)} %get-tuple-element.29), channel_id=1, source_target_pairs={{0,1},{1,0},{2,3},{3,2},{4,5},{5,4},{6,7},{7,6},{8,9},{9,8},{10,11... | collective-permute-start | bytes 1179656 | tf_op jit(solution)/shard_map/ppermute | solution.py:288
  40.2 13.7 %collective-permute-start.19 = (bf16[32,32,128]{2,1,0:T(8,128)(2,1)S(1)}, bf16[32,32,128]{2,1,0:T(8,128)(2,1)S(1)}, u32[]{:S(2)}, u32[]{:S(2)}) collective-permute-start(bf16[32,32,128]{2,1,0:T(8,128)(2,1)S(1)} %copy-done.7), channel_id=1, source_target_pairs={{0,2},{2,0},{1,3},{3,1},{4,6},{6,4},{5,7},{7,5},{8,10},{10,8},{9,1... | collective-permute-start | bytes 786440 | tf_op jit(solution)/shard_map/ppermute | solution.py:289
  42.9 4.4 %copy-start.3 = (bf16[1,2048,192]{1,2,0:T(8,128)(2,1)S(1)}, bf16[1,2048,192]{1,2,0:T(8,128)(2,1)}, u32[]{:S(2)}) copy-start(bf16[1,2048,192]{1,2,0:T(8,128)(2,1)} %param.14) | copy-start | bytes 2359300
  49.5 6.8 %collective-permute-start.18 = (bf16[256,128]{1,0:T(8,128)(2,1)S(1)}, bf16[256,128]{1,0:T(8,128)(2,1)S(1)}, u32[]{:S(2)}, u32[]{:S(2)}) collective-permute-start(bf16[256,128]{1,0:T(8,128)(2,1)S(1)} %shard_map.100), channel_id=1, source_target_pairs={{0,12},{4,8},{8,4},{12,0},{1,13},{5,9},{9,5},{13,1},{2,14},{6,10},... | collective-permute-start | bytes 196616 | tf_op jit(solution)/shard_map/ppermute | solution.py:298
  51.2 5.1 %collective-permute-start.15 = (bf16[256,128]{1,0:T(8,128)(2,1)S(1)}, bf16[256,128]{1,0:T(8,128)(2,1)S(1)}, u32[]{:S(2)}, u32[]{:S(2)}) collective-permute-start(bf16[256,128]{1,0:T(8,128)(2,1)S(1)} %get-tuple-element.32), channel_id=1, source_target_pairs={{0,4},{4,0},{8,12},{12,8},{1,5},{5,1},{9,13},{13,9},{2,6},{6,2},{1... | collective-permute-start | bytes 196616 | tf_op jit(solution)/shard_map/ppermute | solution.py:298
  51.8 6.4 %collective-permute-start.16 = (bf16[256,128]{1,0:T(8,128)(2,1)S(1)}, bf16[256,128]{1,0:T(8,128)(2,1)S(1)}, u32[]{:S(2)}, u32[]{:S(2)}) collective-permute-start(bf16[256,128]{1,0:T(8,128)(2,1)S(1)} %get-tuple-element.33), channel_id=1, source_target_pairs={{0,8},{4,12},{8,0},{12,4},{1,9},{5,13},{9,1},{13,5},{2,10},{6,14},... | collective-permute-start | bytes 196616 | tf_op jit(solution)/shard_map/ppermute | solution.py:298
  (7 other events, 7.1 us)

commit v6 on v5

--- a/solution.py
+++ b/solution.py
@@ -129,7 +129,7 @@
 
 def fold_body(
     lengths, tokens, gate, up, down, proj, routes, gates,
-    fold, rest_gate, rest_up, base, weights, live, chosen,
+    fold, rest_gate, rest_up, held_gate, held_up, base, weights, live, chosen,
 ):
     rows, width = down.shape[0], proj.shape[1]
     folded = dot(down[...], proj[...]).astype(jnp.bfloat16)
@@ -140,6 +140,8 @@
     rest_gate[:left, :] = gate[rows - left :, :]
     rest_gate[left:, :] = fold[...]
     rest_up[...] = up[rows - left :, :]
+    held_gate[...] = gate[...]
+    held_up[...] = up[...]
     base[...] = dot(tokens[...], proj[...]).T
     z, x = lax.axis_index(E), lax.axis_index(Q)
     for i in range(weights.shape[0]):
@@ -263,29 +265,31 @@
     left = hidden_part - part_rows
     (part,) = kernel(part_body, [gate, up], [((part_rows, model_width), bf16)])
     part_x = lax.ppermute(part, Q, swap)
-    fold, rest_gate, rest_up, base, weights, live, chosen = kernel(
+    fold, rest_gate, rest_up, held_gate, held_up, base, weights, live, chosen = kernel(
         fold_body,
         [passage_lengths, tokens, gate, up, down, proj_weight, route_ids.T, gate_values.T],
-        [((r, model_width), bf16) for r in (FOLD, left + FOLD, left)]
+        [((r, model_width), bf16) for r in (FOLD, left + FOLD, left, hidden_part, hidden_part)]
         + [((width, n), f32), ((8, n), f32), ((n, width), f32), ((2 * rows, 2 * queries.shape[0]), bf16)],
         smem=(0,),
         fetched=(1,),
     )
     pair_gate, pair_up = lax.ppermute(gate, D, swap), lax.ppermute(up, D, swap)
     pair_fold = lax.ppermute(tied([fold], [pair_gate], 1)[0], D, swap)
-    own = [gate, up, fold, pair_gate, pair_up, pair_fold]
+    own = [held_gate, held_up, fold, pair_gate, pair_up, pair_fold]
     (got_own,) = kernel(first_body, [tokens, near, *own], [((width, 2 * n), f32)], fetched=(0,))
 
     far_inner = lax.ppermute(near, E, middle)
     end_two = lax.ppermute(across, E, ends)
-    rest_x = [lax.ppermute(a, Q, swap) for a in tied([rest_gate, rest_up], [near, across], 1)]
-    (part_x,) = tied([part_x], [got_own], 1)
+    rest_x = [lax.ppermute(a, Q, swap) for a in (rest_gate, *tied([rest_up], [near, across], 1))]
+    (part_x,) = tied([part_x], [near, across], 1)
     part_y = lax.ppermute(part_x, G, swap)
     (got_two,) = kernel(two_body, [end_two, far_inner, *own], [((width, n), f32)])
 
     end_three = lax.ppermute(far_inner, E, ends)
     other = [part_x, part_y, *rest_x]
-    other = other + [lax.ppermute(a, D, swap) for a in tied(other, [far_inner], 1)]
+    free = {i: lax.ppermute(other[i], D, swap) for i in (2,)}
+    held = dict(zip((0, 1, 3), tied([other[i] for i in (0, 1, 3)], [far_inner, got_own, got_two, free[2]], 1)))
+    other = other + [free[i] if i in free else lax.ppermute(held[i], D, swap) for i in range(4)]
     other_queries = lax.ppermute(queries, Q, swap)
     here, *back = kernel(
         second_body,

time: 59.8 us -> 58 us (0.970)
  local copies, waits for them, and re-layouts: 4.09 us -> 0.68 us
  waiting for transfers between devices: 26 us -> 23 us
  Pallas kernels: 9.39 us -> 11.8 us
  starting transfers between devices: 19.8 us -> 22.1 us
    ppermute x2, waiting for transfers between devices: 13.3 us -> 4.96 us  [by_column(): lax.ppermute(a, Q, swap)]
    ppermute x1, waiting for transfers between devices: 0.01 us -> 4.01 us  [by_column(): end_two = lax.ppermute(across, E, ends)]
    ppermute x1, waiting for transfers between devices: 1.01 us -> 4.78 us  [by_column(): part_x = lax.ppermute(part, Q, swap)]
    unnamed x22 -> x14, local copies, waits for them, and re-layouts: 4.09 us -> 0.68 us
    pallas_call x7, Pallas kernels: 9.19 us -> 11.6 us  [kernel(): pl.pallas_call(body, out_shape=[jax.ShapeDtypeStruct(shape, dtype) for sh...]
    ppermute x1, waiting for transfers between devices: 4.46 us -> 2.09 us  [by_column(): near = lax.ppermute(tokens, E, [(i, i ^ 1) for i in range(4)])]
    ppermute x1, waiting for transfers between devices: 2.33 us -> 0.4 us  [by_column(): end_three = lax.ppermute(far_inner, E, ends)]
    ppermute x1, starting transfers between devices: 1.56 us -> 3.01 us  [by_column(): part_x = lax.ppermute(part, Q, swap)]
  transfers between devices with their start and end apart: 20 -> 20, of which waited for: 7 -> 9; matrix products, arithmetic and copies ran while one was open for 0% -> 0% of each run, Pallas kernels for 14% -> 16%
where the time goes in v6:
time: 58 us; the launch traced here: 57.7 us
  waiting for transfers between devices  23 us (40%)
  starting transfers between devices  22.1 us (38%)
  Pallas kernels  11.8 us (20%)
  local copies, waits for them, and re-layouts  0.68 us (1%)
    pallas_call x7, Pallas kernels, kernel(): pl.pallas_call(body, out_shape=[jax.ShapeDtypeStruct(shape, dtype) for sh...  11.6 us
    ppermute x3, starting transfers between devices, by_column(): lax.ppermute(a, E, [(i, i ^ k) for i in range(4)])  5.7 us
    ppermute x2, waiting for transfers between devices, by_column(): lax.ppermute(a, Q, swap)  4.96 us
    ppermute x1, waiting for transfers between devices, by_column(): part_x = lax.ppermute(part, Q, swap)  4.78 us
    ppermute x3, waiting for transfers between devices, by_column(): lax.ppermute(a, E, [(i, i ^ k) for i in range(4)])  4.65 us
    ppermute x1, waiting for transfers between devices, by_column(): end_two = lax.ppermute(across, E, ends)  4.01 us
    ppermute x2, starting transfers between devices, by_column(): lax.ppermute(a, Q, swap)  3.23 us
    ppermute x1, starting transfers between devices, by_column(): part_x = lax.ppermute(part, Q, swap)  3.01 us
  transfers between devices with their start and end apart: 20, of which 9 were waited for; matrix products, arithmetic and copies ran while one was open for 0% of the time, Pallas kernels for 16%

profile of v6, /device:TPU:0, one launch (start us, length us, event | category | flops | bytes accessed | tf_op | source)
XLA Modules:
  0.0 57.7 jit_solution(5301869969752204329)
XLA Ops:
  0.0 1.6 %shard_map.95 = bf16[112,2048]{1,0:T(8,128)(2,1)S(1)} custom-call(bf16[192,2048]{1,0:T(8,128)(2,1)} %bitcast.1.gate, bf16[192,2048]{1,0:T(8,128)(2,1)} %bitcast.3.up), custom_call_target="tpu_custom_call" | custom-call | tf_op jit(solution)/shard_map/pallas_call | solution.py:110
  1.6 3.0 %collective-permute-start.7 = (bf16[112,2048]{1,0:T(8,128)(2,1)S(1)}, bf16[112,2048]{1,0:T(8,128)(2,1)S(1)}, u32[]{:S(2)}, u32[]{:S(2)}) collective-permute-start(bf16[112,2048]{1,0:T(8,128)(2,1)S(1)} %shard_map.95), channel_id=1, source_target_pairs={{0,2},{2,0},{1,3},{3,1},{4,6},{6,4},{5,7},{7,5},{8,10},{10,8},{9,1... | collective-permute-start | bytes 1376264 | tf_op jit(solution)/shard_map/ppermute | solution.py:267
  5.1 1.6 %collective-permute-start = (bf16[128,2048]{1,0:T(8,128)(2,1)S(1)}, bf16[128,2048]{1,0:T(8,128)(2,1)S(1)}, u32[]{:S(2)}, u32[]{:S(2)}) collective-permute-start(bf16[128,2048]{1,0:T(8,128)(2,1)S(1)} %copy-done), channel_id=1, source_target_pairs={{0,4},{4,0},{8,12},{12,8},{1,5},{5,1},{9,13},{13,9},{2,6},{6,2},{1... | collective-permute-start | bytes 1572872 | tf_op jit(solution)/shard_map/ppermute | solution.py:261
  8.1 2.3 %shard_map.91 = (bf16[16,2048]{1,0:T(8,128)(2,1)S(1)}, bf16[96,2048]{1,0:T(8,128)(2,1)S(1)}, bf16[80,2048]{1,0:T(8,128)(2,1)S(1)}, bf16[192,2048]{1,0:T(8,128)(2...) custom-call(s32[2]{0:T(128)S(1)} %copy-done.6, ...), custom_call_target="tpu_custom_call" | custom-call | tf_op jit(solution)/shard_map/pallas_call | solution.py:110
  10.3 4.8 %collective-permute-done.7.refs_0_ = bf16[112,2048]{1,0:T(8,128)(2,1)S(1)} collective-permute-done((bf16[112,2048]{1,0:T(8,128)(2,1)S(1)}, bf16[112,2048]{1,0:T(8,128)(2,1)S(1)}, u32[]{:S(2)}, u32[]{:S(2)}) %collective-permute-start.7) | collective-permute-done | bytes 458784 | tf_op jit(solution)/shard_map/ppermute | solution.py:267
  15.1 1.7 %collective-permute-start.9 = (bf16[96,2048]{1,0:T(8,128)(2,1)S(1)}, bf16[96,2048]{1,0:T(8,128)(2,1)S(1)}, u32[]{:S(2)}, u32[]{:S(2)}) collective-permute-start(bf16[96,2048]{1,0:T(8,128)(2,1)S(1)} %get-tuple-element.24), channel_id=1, source_target_pairs={{0,2},{2,0},{1,3},{3,1},{4,6},{6,4},{5,7},{7,5},{8,10},{10,8},{9,1... | collective-permute-start | bytes 1179656 | tf_op jit(solution)/shard_map/ppermute | solution.py:283
  16.8 2.1 %collective-permute-done.near.refs_1_ = bf16[128,2048]{1,0:T(8,128)(2,1)S(1)} collective-permute-done((bf16[128,2048]{1,0:T(8,128)(2,1)S(1)}, bf16[128,2048]{1,0:T(8,128)(2,1)S(1)}, u32[]{:S(2)}, u32[]{:S(2)}) %collective-permute-start) | collective-permute-done | bytes 524320 | tf_op jit(solution)/shard_map/ppermute | solution.py:261
  19.6 1.3 %collective-permute-start.2 = (bf16[128,2048]{1,0:T(8,128)(2,1)S(1)}, bf16[128,2048]{1,0:T(8,128)(2,1)S(1)}, u32[]{:S(2)}, u32[]{:S(2)}) collective-permute-start(bf16[128,2048]{1,0:T(8,128)(2,1)S(1)} %collective-permute-done.1.refs_2_.across), channel_id=1, source_target_pairs={{4,0},{8,12},{5,1},{9,13},{6,2},{10,14},{7,3},{11,15},{20,16},{24,... | collective-permute-start | bytes 1572872 | tf_op jit(solution)/shard_map/ppermute | solution.py:282
  21.0 4.4 %collective-permute-done.9.refs_2_.refs_8_ = bf16[96,2048]{1,0:T(8,128)(2,1)S(1)} collective-permute-done((bf16[96,2048]{1,0:T(8,128)(2,1)S(1)}, bf16[96,2048]{1,0:T(8,128)(2,1)S(1)}, u32[]{:S(2)}, u32[]{:S(2)}) %collective-permute-start.9) | collective-permute-done | bytes 393248 | tf_op jit(solution)/shard_map/ppermute | solution.py:283
  25.4 1.4 %collective-permute-start.8 = (bf16[112,2048]{1,0:T(8,128)(2,1)S(1)}, bf16[112,2048]{1,0:T(8,128)(2,1)S(1)}, u32[]{:S(2)}, u32[]{:S(2)}) collective-permute-start(bf16[112,2048]{1,0:T(8,128)(2,1)S(1)} %shard_map.96.refs_0_.refs_6_), channel_id=1, source_target_pairs={{0,16},{16,0},{1,17},{17,1},{2,18},{18,2},{3,19},{19,3},{4,20},{20... | collective-permute-start | bytes 1376264 | tf_op jit(solution)/shard_map/ppermute | solution.py:285
  27.5 1.2 %collective-permute-done.6.refs_5_ = bf16[16,2048]{1,0:T(8,128)(2,1)S(1)} collective-permute-done((bf16[16,2048]{1,0:T(8,128)(2,1)S(1)}, bf16[16,2048]{1,0:T(8,128)(2,1)S(1)}, u32[]{:S(2)}, u32[]{:S(2)}) %collective-permute-start.6) | collective-permute-done | bytes 65568 | tf_op jit(solution)/shard_map/ppermute | solution.py:277
  28.7 1.5 %collective-permute-start.10 = (bf16[80,2048]{1,0:T(8,128)(2,1)S(1)}, bf16[80,2048]{1,0:T(8,128)(2,1)S(1)}, u32[]{:S(2)}, u32[]{:S(2)}) collective-permute-start(bf16[80,2048]{1,0:T(8,128)(2,1)S(1)} %shard_map.97), channel_id=1, source_target_pairs={{0,2},{2,0},{1,3},{3,1},{4,6},{6,4},{5,7},{7,5},{8,10},{10,8},{9,1... | collective-permute-start | bytes 983048 | tf_op jit(solution)/shard_map/ppermute | solution.py:283
  30.2 1.3 %collective-permute-start.17 = (bf16[128,2048]{1,0:T(8,128)(2,1)S(1)}, bf16[128,2048]{1,0:T(8,128)(2,1)S(1)}, u32[]{:S(2)}, u32[]{:S(2)}) collective-permute-start(bf16[128,2048]{1,0:T(8,128)(2,1)S(1)} %collective-permute-done.3.far_inner.refs_3_), channel_id=1, source_target_pairs={{4,0},{8,12},{5,1},{9,13},{6,2},{10,14},{7,3},{11,15},{20,16},{24,... | collective-permute-start | bytes 1572872 | tf_op jit(solution)/shard_map/ppermute | solution.py:288
  31.5 1.2 %shard_map.93.refs_4_.got_own = f32[128,256]{1,0:T(8,128)S(1)} custom-call(bf16[128,2048]{1,0:T(8,128)(2,1)S(1)} %copy-done, bf16[128,2048]{1,0:T(8,128)(2,1)S(1)} %collective-permute-done.near.refs_1_, bf16[192,2048]{1,0:T(8,128)(2,1)S(1)} %get-tuple-element.21.refs_0_, bf16[192,2048]{1,0:T(8,128)(2,1)S(1)} %get-tuple-element.22.refs_1_, ...), custom_call_target="tpu_custom_call" | custom-call | tf_op jit(solution)/shard_map/pallas_call | solution.py:110
  32.7 4.0 %collective-permute-done.2.end_two = bf16[128,2048]{1,0:T(8,128)(2,1)S(1)} collective-permute-done((bf16[128,2048]{1,0:T(8,128)(2,1)S(1)}, bf16[128,2048]{1,0:T(8,128)(2,1)S(1)}, u32[]{:S(2)}, u32[]{:S(2)}) %collective-permute-start.2) | collective-permute-done | bytes 524320 | tf_op jit(solution)/shard_map/ppermute | solution.py:282
  36.7 1.2 %shard_map.94.refs_5_.got_two = f32[128,128]{1,0:T(8,128)S(1)} custom-call(bf16[128,2048]{1,0:T(8,128)(2,1)S(1)} %collective-permute-done.2.end_two, bf16[128,2048]{1,0:T(8,128)(2,1)S(1)} %collective-permute-done.3.far_inner.refs_3_, bf16[192,2048]{1,0:T(8,128)(2,1)S(1)} %get-tuple-element.21.refs_0_, bf16[192,2048]{1,0:T(8,128)(2,1)S(1)} %get-tuple-element.22.refs_1_, ...), custom_call_target="tpu_custom_call" | custom-call | tf_op jit(solution)/shard_map/pallas_call | solution.py:110
  39.2 1.5 %collective-permute-start.19 = (bf16[32,32,128]{2,1,0:T(8,128)(2,1)S(1)}, bf16[32,32,128]{2,1,0:T(8,128)(2,1)S(1)}, u32[]{:S(2)}, u32[]{:S(2)}) collective-permute-start(bf16[32,32,128]{2,1,0:T(8,128)(2,1)S(1)} %copy-done.3), channel_id=1, source_target_pairs={{0,2},{2,0},{1,3},{3,1},{4,6},{6,4},{5,7},{7,5},{8,10},{10,8},{9,1... | collective-permute-start | bytes 786440 | tf_op jit(solution)/shard_map/ppermute | solution.py:293
  41.5 2.0 %shard_map.99 = (f32[256,128]{1,0:T(8,128)S(1)}, bf16[256,128]{1,0:T(8,128)(2,1)S(1)}, bf16[256,128]{1,0:T(8,128)(2,1)S(1)}) custom-call(bf16[128,2048]{1,0:T(8,128)(2,1)S(1)} %copy-done, bf16[128,2048]{1,0:T(8,128)(2,1)S(1)} %collective-permute-done.near.refs_1_, bf16[128,2048]{1,0:T(8,128)(2,1)S(1)} %collective-permute-done.2.end_two, ...), custom_call_target="tpu_custom_call" | custom-call | tf_op jit(solution)/shard_map/pallas_call | solution.py:110
  43.5 1.6 %collective-permute-start.15 = (bf16[256,128]{1,0:T(8,128)(2,1)S(1)}, bf16[256,128]{1,0:T(8,128)(2,1)S(1)}, u32[]{:S(2)}, u32[]{:S(2)}) collective-permute-start(bf16[256,128]{1,0:T(8,128)(2,1)S(1)} %get-tuple-element.30), channel_id=1, source_target_pairs={{0,4},{4,0},{8,12},{12,8},{1,5},{5,1},{9,13},{13,9},{2,6},{6,2},{1... | collective-permute-start | bytes 196616 | tf_op jit(solution)/shard_map/ppermute | solution.py:302
  45.2 2.6 %collective-permute-start.16 = (bf16[256,128]{1,0:T(8,128)(2,1)S(1)}, bf16[256,128]{1,0:T(8,128)(2,1)S(1)}, u32[]{:S(2)}, u32[]{:S(2)}) collective-permute-start(bf16[256,128]{1,0:T(8,128)(2,1)S(1)} %get-tuple-element.31), channel_id=1, source_target_pairs={{0,8},{4,12},{8,0},{12,4},{1,9},{5,13},{9,1},{13,5},{2,10},{6,14},... | collective-permute-start | bytes 196616 | tf_op jit(solution)/shard_map/ppermute | solution.py:302
  48.2 2.2 %shard_map.100 = bf16[256,128]{1,0:T(8,128)(2,1)S(1)} custom-call(bf16[128,2048]{1,0:T(8,128)(2,1)S(1)} %collective-permute-done.17.end_three, bf16[128,2048]{1,0:T(8,128)(2,1)S(1)} %collective-permute-done.1.refs_2_.across, f32[256,128]{1,0:T(8,128)S(1)} %get-tuple-element.29.earlier.here, bf16[192,2048]{1,0:T(8,128)(2,1)S(1)} %get-tuple-element.21.refs_0_, ...), custom_call_target="tpu_custom_call" | custom-call | tf_op jit(solution)/shard_map/pallas_call | solution.py:110
  50.3 1.5 %collective-permute-start.18 = (bf16[256,128]{1,0:T(8,128)(2,1)S(1)}, bf16[256,128]{1,0:T(8,128)(2,1)S(1)}, u32[]{:S(2)}, u32[]{:S(2)}) collective-permute-start(bf16[256,128]{1,0:T(8,128)(2,1)S(1)} %shard_map.100), channel_id=1, source_target_pairs={{0,12},{4,8},{8,4},{12,0},{1,13},{5,9},{9,5},{13,1},{2,14},{6,10},... | collective-permute-start | bytes 196616 | tf_op jit(solution)/shard_map/ppermute | solution.py:302
  51.8 4.6 %collective-permute-done.18.three = bf16[256,128]{1,0:T(8,128)(2,1)S(1)} collective-permute-done((bf16[256,128]{1,0:T(8,128)(2,1)S(1)}, bf16[256,128]{1,0:T(8,128)(2,1)S(1)}, u32[]{:S(2)}, u32[]{:S(2)}) %collective-permute-start.18) | collective-permute-done | bytes 65568 | tf_op jit(solution)/shard_map/ppermute | solution.py:302
  56.5 1.3 %shard_map.101 = f32[2,64]{1,0:T(2,128)} custom-call(f32[128,128]{1,0:T(8,128)S(1)} %get-tuple-element.20.base, f32[256,128]{1,0:T(8,128)S(1)} %get-tuple-element.29.earlier.here, bf16[256,128]{1,0:T(8,128)(2,1)S(1)} %collective-permute-done.15.near, bf16[256,128]{1,0:T(8,128)(2,1)S(1)} %collective-permute-done.16.two, ...), custom_call_target="tpu_custom_call" | custom-call | tf_op jit(solution)/shard_map/pallas_call | solution.py:110
  (41 shorter events, 5.7 us)
Async XLA Ops:
  0.0 5.1 %copy-start = (bf16[128,2048]{1,0:T(8,128)(2,1)S(1)}, bf16[128,2048]{1,0:T(8,128)(2,1)}, u32[]{:S(2)}) copy-start(bf16[128,2048]{1,0:T(8,128)(2,1)} %tokens.5) | copy-start | bytes 1572868
  0.0 7.4 %copy-start.1 = (bf16[1,2048,192]{1,2,0:T(8,128)(2,1)S(1)}, bf16[1,2048,192]{1,2,0:T(8,128)(2,1)}, u32[]{:S(2)}) copy-start(bf16[1,2048,192]{1,2,0:T(8,128)(2,1)} %param.15) | copy-start | bytes 2359300
  0.0 7.4 %copy-start.2 = (bf16[2048,128]{1,0:T(8,128)(2,1)S(1)}, bf16[2048,128]{1,0:T(8,128)(2,1)}, u32[]{:S(2)}) copy-start(bf16[2048,128]{1,0:T(8,128)(2,1)} %proj.1) | copy-start | bytes 1572868
  1.6 13.5 %collective-permute-start.7 = (bf16[112,2048]{1,0:T(8,128)(2,1)S(1)}, bf16[112,2048]{1,0:T(8,128)(2,1)S(1)}, u32[]{:S(2)}, u32[]{:S(2)}) collective-permute-start(bf16[112,2048]{1,0:T(8,128)(2,1)S(1)} %shard_map.95), channel_id=1, source_target_pairs={{0,2},{2,0},{1,3},{3,1},{4,6},{6,4},{5,7},{7,5},{8,10},{10,8},{9,1... | collective-permute-start | bytes 1376264 | tf_op jit(solution)/shard_map/ppermute | solution.py:267
  4.6 22.3 %collective-permute-start.4 = (bf16[192,2048]{1,0:T(8,128)(2,1)}, bf16[192,2048]{1,0:T(8,128)(2,1)S(1)}, u32[]{:S(2)}, u32[]{:S(2)}) collective-permute-start(bf16[192,2048]{1,0:T(8,128)(2,1)} %bitcast.1.gate), channel_id=1, source_target_pairs={{0,1},{1,0},{2,3},{3,2},{4,5},{5,4},{6,7},{7,6},{8,9},{9,8},{10,11... | collective-permute-start | bytes 2359304 | tf_op jit(solution)/shard_map/ppermute | solution.py:276
  4.6 22.3 %collective-permute-start.5 = (bf16[192,2048]{1,0:T(8,128)(2,1)}, bf16[192,2048]{1,0:T(8,128)(2,1)S(1)}, u32[]{:S(2)}, u32[]{:S(2)}) collective-permute-start(bf16[192,2048]{1,0:T(8,128)(2,1)} %bitcast.3.up), channel_id=1, source_target_pairs={{0,1},{1,0},{2,3},{3,2},{4,5},{5,4},{6,7},{7,6},{8,9},{9,8},{10,11... | collective-permute-start | bytes 2359304 | tf_op jit(solution)/shard_map/ppermute | solution.py:276
  5.1 13.8 %collective-permute-start = (bf16[128,2048]{1,0:T(8,128)(2,1)S(1)}, bf16[128,2048]{1,0:T(8,128)(2,1)S(1)}, u32[]{:S(2)}, u32[]{:S(2)}) collective-permute-start(bf16[128,2048]{1,0:T(8,128)(2,1)S(1)} %copy-done), channel_id=1, source_target_pairs={{0,4},{4,0},{8,12},{12,8},{1,5},{5,1},{9,13},{13,9},{2,6},{6,2},{1... | collective-permute-start | bytes 1572872 | tf_op jit(solution)/shard_map/ppermute | solution.py:261
  6.7 12.9 %collective-permute-start.1 = (bf16[128,2048]{1,0:T(8,128)(2,1)S(1)}, bf16[128,2048]{1,0:T(8,128)(2,1)S(1)}, u32[]{:S(2)}, u32[]{:S(2)}) collective-permute-start(bf16[128,2048]{1,0:T(8,128)(2,1)S(1)} %copy-done), channel_id=1, source_target_pairs={{4,8},{8,4},{5,9},{9,5},{6,10},{10,6},{7,11},{11,7},{20,24},{24,20... | collective-permute-start | bytes 1572872 | tf_op jit(solution)/shard_map/ppermute | solution.py:262
  15.1 10.3 %collective-permute-start.9 = (bf16[96,2048]{1,0:T(8,128)(2,1)S(1)}, bf16[96,2048]{1,0:T(8,128)(2,1)S(1)}, u32[]{:S(2)}, u32[]{:S(2)}) collective-permute-start(bf16[96,2048]{1,0:T(8,128)(2,1)S(1)} %get-tuple-element.24), channel_id=1, source_target_pairs={{0,2},{2,0},{1,3},{3,1},{4,6},{6,4},{5,7},{7,5},{8,10},{10,8},{9,1... | collective-permute-start | bytes 1179656 | tf_op jit(solution)/shard_map/ppermute | solution.py:283
  18.9 11.2 %collective-permute-start.3 = (bf16[128,2048]{1,0:T(8,128)(2,1)S(1)}, bf16[128,2048]{1,0:T(8,128)(2,1)S(1)}, u32[]{:S(2)}, u32[]{:S(2)}) collective-permute-start(bf16[128,2048]{1,0:T(8,128)(2,1)S(1)} %collective-permute-done.near.refs_1_), channel_id=1, source_target_pairs={{4,8},{8,4},{5,9},{9,5},{6,10},{10,6},{7,11},{11,7},{20,24},{24,20... | collective-permute-start | bytes 1572872 | tf_op jit(solution)/shard_map/ppermute | solution.py:281
  19.6 17.0 %collective-permute-start.2 = (bf16[128,2048]{1,0:T(8,128)(2,1)S(1)}, bf16[128,2048]{1,0:T(8,128)(2,1)S(1)}, u32[]{:S(2)}, u32[]{:S(2)}) collective-permute-start(bf16[128,2048]{1,0:T(8,128)(2,1)S(1)} %collective-permute-done.1.refs_2_.across), channel_id=1, source_target_pairs={{4,0},{8,12},{5,1},{9,13},{6,2},{10,14},{7,3},{11,15},{20,16},{24,... | collective-permute-start | bytes 1572872 | tf_op jit(solution)/shard_map/ppermute | solution.py:282
  25.4 13.0 %collective-permute-start.8 = (bf16[112,2048]{1,0:T(8,128)(2,1)S(1)}, bf16[112,2048]{1,0:T(8,128)(2,1)S(1)}, u32[]{:S(2)}, u32[]{:S(2)}) collective-permute-start(bf16[112,2048]{1,0:T(8,128)(2,1)S(1)} %shard_map.96.refs_0_.refs_6_), channel_id=1, source_target_pairs={{0,16},{16,0},{1,17},{17,1},{2,18},{18,2},{3,19},{19,3},{4,20},{20... | collective-permute-start | bytes 1376264 | tf_op jit(solution)/shard_map/ppermute | solution.py:285
  26.8 11.0 %collective-permute-start.11 = (bf16[96,2048]{1,0:T(8,128)(2,1)S(1)}, bf16[96,2048]{1,0:T(8,128)(2,1)S(1)}, u32[]{:S(2)}, u32[]{:S(2)}) collective-permute-start(bf16[96,2048]{1,0:T(8,128)(2,1)S(1)} %collective-permute-done.9.refs_2_.refs_8_), channel_id=1, source_target_pairs={{0,1},{1,0},{2,3},{3,2},{4,5},{5,4},{6,7},{7,6},{8,9},{9,8},{10,11... | collective-permute-start | bytes 1179656 | tf_op jit(solution)/shard_map/ppermute | solution.py:290
  26.9 1.8 %collective-permute-start.6 = (bf16[16,2048]{1,0:T(8,128)(2,1)S(1)}, bf16[16,2048]{1,0:T(8,128)(2,1)S(1)}, u32[]{:S(2)}, u32[]{:S(2)}) collective-permute-start(bf16[16,2048]{1,0:T(8,128)(2,1)S(1)} %shard_map.92), channel_id=1, source_target_pairs={{0,1},{1,0},{2,3},{3,2},{4,5},{5,4},{6,7},{7,6},{8,9},{9,8},{10,11... | collective-permute-start | bytes 196616 | tf_op jit(solution)/shard_map/ppermute | solution.py:277
  28.7 9.8 %collective-permute-start.10 = (bf16[80,2048]{1,0:T(8,128)(2,1)S(1)}, bf16[80,2048]{1,0:T(8,128)(2,1)S(1)}, u32[]{:S(2)}, u32[]{:S(2)}) collective-permute-start(bf16[80,2048]{1,0:T(8,128)(2,1)S(1)} %shard_map.97), channel_id=1, source_target_pairs={{0,2},{2,0},{1,3},{3,1},{4,6},{6,4},{5,7},{7,5},{8,10},{10,8},{9,1... | collective-permute-start | bytes 983048 | tf_op jit(solution)/shard_map/ppermute | solution.py:283
  30.2 18.0 %collective-permute-start.17 = (bf16[128,2048]{1,0:T(8,128)(2,1)S(1)}, bf16[128,2048]{1,0:T(8,128)(2,1)S(1)}, u32[]{:S(2)}, u32[]{:S(2)}) collective-permute-start(bf16[128,2048]{1,0:T(8,128)(2,1)S(1)} %collective-permute-done.3.far_inner.refs_3_), channel_id=1, source_target_pairs={{4,0},{8,12},{5,1},{9,13},{6,2},{10,14},{7,3},{11,15},{20,16},{24,... | collective-permute-start | bytes 1572872 | tf_op jit(solution)/shard_map/ppermute | solution.py:288
  37.9 1.3 %copy-start.3 = (bf16[32,32,128]{2,1,0:T(8,128)(2,1)S(1)}, bf16[32,32,128]{2,1,0:T(8,128)(2,1)}, u32[]{:S(2)}) copy-start(bf16[32,32,128]{2,1,0:T(8,128)(2,1)} %param.17) | copy-start | bytes 786436
  38.5 3.0 %collective-permute-start.12 = (bf16[112,2048]{1,0:T(8,128)(2,1)S(1)}, bf16[112,2048]{1,0:T(8,128)(2,1)S(1)}, u32[]{:S(2)}, u32[]{:S(2)}) collective-permute-start(bf16[112,2048]{1,0:T(8,128)(2,1)S(1)} %get-tuple-element.26), channel_id=1, source_target_pairs={{0,1},{1,0},{2,3},{3,2},{4,5},{5,4},{6,7},{7,6},{8,9},{9,8},{10,11... | collective-permute-start | bytes 1376264 | tf_op jit(solution)/shard_map/ppermute | solution.py:292
  38.6 2.9 %collective-permute-start.13 = (bf16[112,2048]{1,0:T(8,128)(2,1)S(1)}, bf16[112,2048]{1,0:T(8,128)(2,1)S(1)}, u32[]{:S(2)}, u32[]{:S(2)}) collective-permute-start(bf16[112,2048]{1,0:T(8,128)(2,1)S(1)} %get-tuple-element.27), channel_id=1, source_target_pairs={{0,1},{1,0},{2,3},{3,2},{4,5},{5,4},{6,7},{7,6},{8,9},{9,8},{10,11... | collective-permute-start | bytes 1376264 | tf_op jit(solution)/shard_map/ppermute | solution.py:292
  39.1 2.4 %collective-permute-start.14 = (bf16[80,2048]{1,0:T(8,128)(2,1)S(1)}, bf16[80,2048]{1,0:T(8,128)(2,1)S(1)}, u32[]{:S(2)}, u32[]{:S(2)}) collective-permute-start(bf16[80,2048]{1,0:T(8,128)(2,1)S(1)} %get-tuple-element.28), channel_id=1, source_target_pairs={{0,1},{1,0},{2,3},{3,2},{4,5},{5,4},{6,7},{7,6},{8,9},{9,8},{10,11... | collective-permute-start | bytes 983048 | tf_op jit(solution)/shard_map/ppermute | solution.py:292
  39.2 12.6 %collective-permute-start.19 = (bf16[32,32,128]{2,1,0:T(8,128)(2,1)S(1)}, bf16[32,32,128]{2,1,0:T(8,128)(2,1)S(1)}, u32[]{:S(2)}, u32[]{:S(2)}) collective-permute-start(bf16[32,32,128]{2,1,0:T(8,128)(2,1)S(1)} %copy-done.3), channel_id=1, source_target_pairs={{0,2},{2,0},{1,3},{3,1},{4,6},{6,4},{5,7},{7,5},{8,10},{10,8},{9,1... | collective-permute-start | bytes 786440 | tf_op jit(solution)/shard_map/ppermute | solution.py:293
  43.5 8.3 %collective-permute-start.15 = (bf16[256,128]{1,0:T(8,128)(2,1)S(1)}, bf16[256,128]{1,0:T(8,128)(2,1)S(1)}, u32[]{:S(2)}, u32[]{:S(2)}) collective-permute-start(bf16[256,128]{1,0:T(8,128)(2,1)S(1)} %get-tuple-element.30), channel_id=1, source_target_pairs={{0,4},{4,0},{8,12},{12,8},{1,5},{5,1},{9,13},{13,9},{2,6},{6,2},{1... | collective-permute-start | bytes 196616 | tf_op jit(solution)/shard_map/ppermute | solution.py:302
  45.2 6.6 %collective-permute-start.16 = (bf16[256,128]{1,0:T(8,128)(2,1)S(1)}, bf16[256,128]{1,0:T(8,128)(2,1)S(1)}, u32[]{:S(2)}, u32[]{:S(2)}) collective-permute-start(bf16[256,128]{1,0:T(8,128)(2,1)S(1)} %get-tuple-element.31), channel_id=1, source_target_pairs={{0,8},{4,12},{8,0},{12,4},{1,9},{5,13},{9,1},{13,5},{2,10},{6,14},... | collective-permute-start | bytes 196616 | tf_op jit(solution)/shard_map/ppermute | solution.py:302
  50.3 6.1 %collective-permute-start.18 = (bf16[256,128]{1,0:T(8,128)(2,1)S(1)}, bf16[256,128]{1,0:T(8,128)(2,1)S(1)}, u32[]{:S(2)}, u32[]{:S(2)}) collective-permute-start(bf16[256,128]{1,0:T(8,128)(2,1)S(1)} %shard_map.100), channel_id=1, source_target_pairs={{0,12},{4,8},{8,4},{12,0},{1,13},{5,9},{9,5},{13,1},{2,14},{6,10},... | collective-permute-start | bytes 196616 | tf_op jit(solution)/shard_map/ppermute | solution.py:302
  (3 other events, 2.1 us)

commit v7 on v6

--- a/solution.py
+++ b/solution.py
@@ -212,7 +212,9 @@
     mine = [got_own[:, :n], got_own[:, n:], got_two[...]]
     for k, to in enumerate((here, back_near, back_two)):
         to[:width, :] = mine[k].astype(to.dtype)
-        to[width:, :] = got[:, k * n : (k + 1) * n].astype(to.dtype)
+        to[width : 2 * width, :] = got[:, k * n : (k + 1) * n].astype(to.dtype)
+        if k:
+            to[2 * width :, :] = jnp.zeros((to.shape[0] - 2 * width, n), to.dtype)
 
 
 def third_body(end_three, across, earlier, *refs):
@@ -257,7 +259,7 @@
     f32, bf16 = jnp.float32, jnp.bfloat16
 
     rows = queries.shape[0] * queries.shape[1]
-    both = (2 * width, n)
+    both, longer = (2 * width, n), (2 * width + FOLD, n)
     near = lax.ppermute(tokens, E, [(i, i ^ 1) for i in range(4)])
     across = lax.ppermute(tokens, E, middle)
     gate, up, down = gate_weight[0].T, up_weight[0].T, down_weight[0].T
@@ -280,7 +282,7 @@
 
     far_inner = lax.ppermute(near, E, middle)
     end_two = lax.ppermute(across, E, ends)
-    rest_x = [lax.ppermute(a, Q, swap) for a in (rest_gate, *tied([rest_up], [near, across], 1))]
+    rest_x = [lax.ppermute(a, Q, swap) for a in (*tied([rest_gate], [pair_gate, pair_up], 1), *tied([rest_up], [near, across], 1))]
     (part_x,) = tied([part_x], [near, across], 1)
     part_y = lax.ppermute(part_x, G, swap)
     (got_two,) = kernel(two_body, [end_two, far_inner, *own], [((width, n), f32)])
@@ -294,7 +296,7 @@
     here, *back = kernel(
         second_body,
         [tokens, near, end_two, far_inner, got_own, got_two, *other],
-        [(both, f32), (both, bf16), (both, bf16)],
+        [(both, f32), (longer, bf16), (longer, bf16)],
         fetched=(0,),
     )
     back += kernel(third_body, [end_three, across, here, *own, *other], [(both, bf16)])

time: 58 us -> 56.7 us (0.978)
  local copies, waits for them, and re-layouts: 0.68 us -> 4.08 us
  Pallas kernels: 11.8 us -> 9.44 us
  waiting for transfers between devices: 23 us -> 21 us
    ppermute x2, waiting for transfers between devices: 4.96 us -> 8.42 us  [by_column(): lax.ppermute(a, Q, swap)]
    unnamed x14 -> x20, local copies, waits for them, and re-layouts: 0.68 us -> 4.08 us
    ppermute x1, waiting for transfers between devices: 4.78 us -> 2.13 us  [by_column(): part_x = lax.ppermute(part, Q, swap)]
    pallas_call x7, Pallas kernels: 11.6 us -> 9.28 us  [kernel(): pl.pallas_call(body, out_shape=[jax.ShapeDtypeStruct(shape, dtype) for sh...]
    ppermute x1, waiting for transfers between devices: 4.01 us -> 2.08 us  [by_column(): end_two = lax.ppermute(across, E, ends)]
    ppermute x1, waiting for transfers between devices: 2.09 us -> 3.79 us  [by_column(): near = lax.ppermute(tokens, E, [(i, i ^ 1) for i in range(4)])]
    ppermute x1, starting transfers between devices: 3.01 us -> 1.56 us  [by_column(): part_x = lax.ppermute(part, Q, swap)]
    ppermute x1, starting transfers between devices: 1.58 us -> 3.02 us  [by_column(): near = lax.ppermute(tokens, E, [(i, i ^ 1) for i in range(4)])]
  transfers between devices with their start and end apart: 20 -> 20, of which waited for: 9 -> 7; matrix products, arithmetic and copies ran while one was open for 0% -> 0% of each run, Pallas kernels for 16% -> 15%
where the time goes in v7:
time: 56.7 us; the launch traced here: 56.4 us
  starting transfers between devices  21.7 us (38%)
  waiting for transfers between devices  21 us (37%)
  Pallas kernels  9.44 us (17%)
  local copies, waits for them, and re-layouts  4.08 us (7%)
    pallas_call x7, Pallas kernels, kernel(): pl.pallas_call(body, out_shape=[jax.ShapeDtypeStruct(shape, dtype) for sh...  9.28 us
    ppermute x2, waiting for transfers between devices, by_column(): lax.ppermute(a, Q, swap)  8.42 us
    ppermute x3, starting transfers between devices, by_column(): lax.ppermute(a, E, [(i, i ^ k) for i in range(4)])  6.65 us
    unnamed x20, local copies, waits for them, and re-layouts  4.08 us
    ppermute x1, waiting for transfers between devices, by_column(): near = lax.ppermute(tokens, E, [(i, i ^ 1) for i in range(4)])  3.79 us
    ppermute x3, waiting for transfers between devices, by_column(): lax.ppermute(a, E, [(i, i ^ k) for i in range(4)])  3.69 us
    ppermute x1, starting transfers between devices, by_column(): near = lax.ppermute(tokens, E, [(i, i ^ 1) for i in range(4)])  3.02 us
    ppermute x2, starting transfers between devices, by_column(): lax.ppermute(a, Q, swap)  2.25 us
  transfers between devices with their start and end apart: 20, of which 7 were waited for; matrix products, arithmetic and copies ran while one was open for 0% of the time, Pallas kernels for 15%

profile of v7, /device:TPU:0, one launch (start us, length us, event | category | flops | bytes accessed | tf_op | source)
XLA Modules:
  0.0 56.4 jit_solution(6385304597639513304)
XLA Ops:
  0.5 3.0 %collective-permute-start = (bf16[128,2048]{1,0:T(8,128)(2,1)}, bf16[128,2048]{1,0:T(8,128)(2,1)S(1)}, u32[]{:S(2)}, u32[]{:S(2)}) collective-permute-start(bf16[128,2048]{1,0:T(8,128)(2,1)} %tokens.5), channel_id=1, source_target_pairs={{0,4},{4,0},{8,12},{12,8},{1,5},{5,1},{9,13},{13,9},{2,6},{6,2},{1... | collective-permute-start | bytes 1572872 | tf_op jit(solution)/shard_map/ppermute | solution.py:263
  4.2 1.1 %copy-done.1 = bf16[1,2048,192]{1,2,0:T(8,128)(2,1)S(1)} copy-done((bf16[1,2048,192]{1,2,0:T(8,128)(2,1)S(1)}, bf16[1,2048,192]{1,2,0:T(8,128)(2,1)}, u32[]{:S(2)}) %copy-start.1) | copy-done | bytes 786456
  5.4 1.1 %copy-done.3 = bf16[1,2048,192]{1,2,0:T(8,128)(2,1)S(1)} copy-done((bf16[1,2048,192]{1,2,0:T(8,128)(2,1)S(1)}, bf16[1,2048,192]{1,2,0:T(8,128)(2,1)}, u32[]{:S(2)}) %copy-start.3) | copy-done | bytes 786456
  6.6 1.6 %collective-permute-start.7 = (bf16[112,2048]{1,0:T(8,128)(2,1)S(1)}, bf16[112,2048]{1,0:T(8,128)(2,1)S(1)}, u32[]{:S(2)}, u32[]{:S(2)}) collective-permute-start(bf16[112,2048]{1,0:T(8,128)(2,1)S(1)} %shard_map.95), channel_id=1, source_target_pairs={{0,2},{2,0},{1,3},{3,1},{4,6},{6,4},{5,7},{7,5},{8,10},{10,8},{9,1... | collective-permute-start | bytes 1376264 | tf_op jit(solution)/shard_map/ppermute | solution.py:269
  8.8 1.1 %copy-done.4 = bf16[1,2048,192]{1,2,0:T(8,128)(2,1)S(1)} copy-done((bf16[1,2048,192]{1,2,0:T(8,128)(2,1)S(1)}, bf16[1,2048,192]{1,2,0:T(8,128)(2,1)}, u32[]{:S(2)}) %copy-start.4) | copy-done | bytes 786456
  9.9 1.4 %shard_map.91 = (bf16[16,2048]{1,0:T(8,128)(2,1)S(1)}, bf16[96,2048]{1,0:T(8,128)(2,1)S(1)}, bf16[80,2048]{1,0:T(8,128)(2,1)S(1)}, bf16[192,2048]{1,0:T(8,128)(2...) custom-call(s32[2]{0:T(128)S(1)} %copy-done.9, ...), custom_call_target="tpu_custom_call" | custom-call | tf_op jit(solution)/shard_map/pallas_call | solution.py:110
  12.1 3.8 %collective-permute-done.near.refs_1_ = bf16[128,2048]{1,0:T(8,128)(2,1)S(1)} collective-permute-done((bf16[128,2048]{1,0:T(8,128)(2,1)}, bf16[128,2048]{1,0:T(8,128)(2,1)S(1)}, u32[]{:S(2)}, u32[]{:S(2)}) %collective-permute-start) | collective-permute-done | bytes 524320 | tf_op jit(solution)/shard_map/ppermute | solution.py:263
  16.6 1.3 %collective-permute-start.2 = (bf16[128,2048]{1,0:T(8,128)(2,1)S(1)}, bf16[128,2048]{1,0:T(8,128)(2,1)S(1)}, u32[]{:S(2)}, u32[]{:S(2)}) collective-permute-start(bf16[128,2048]{1,0:T(8,128)(2,1)S(1)} %collective-permute-done.1.refs_2_.across), channel_id=1, source_target_pairs={{4,0},{8,12},{5,1},{9,13},{6,2},{10,14},{7,3},{11,15},{20,16},{24,... | collective-permute-start | bytes 1572872 | tf_op jit(solution)/shard_map/ppermute | solution.py:284
  17.9 2.1 %collective-permute-done.7.refs_0_ = bf16[112,2048]{1,0:T(8,128)(2,1)S(1)} collective-permute-done((bf16[112,2048]{1,0:T(8,128)(2,1)S(1)}, bf16[112,2048]{1,0:T(8,128)(2,1)S(1)}, u32[]{:S(2)}, u32[]{:S(2)}) %collective-permute-start.7) | collective-permute-done | bytes 458784 | tf_op jit(solution)/shard_map/ppermute | solution.py:269
  20.1 1.6 %collective-permute-start.8 = (bf16[112,2048]{1,0:T(8,128)(2,1)S(1)}, bf16[112,2048]{1,0:T(8,128)(2,1)S(1)}, u32[]{:S(2)}, u32[]{:S(2)}) collective-permute-start(bf16[112,2048]{1,0:T(8,128)(2,1)S(1)} %shard_map.96.refs_0_.refs_6_), channel_id=1, source_target_pairs={{0,16},{16,0},{1,17},{17,1},{2,18},{18,2},{3,19},{19,3},{4,20},{20... | collective-permute-start | bytes 1376264 | tf_op jit(solution)/shard_map/ppermute | solution.py:287
  21.7 5.6 %collective-permute-done.9.refs_2_.refs_8_ = bf16[96,2048]{1,0:T(8,128)(2,1)S(1)} collective-permute-done((bf16[96,2048]{1,0:T(8,128)(2,1)S(1)}, bf16[96,2048]{1,0:T(8,128)(2,1)S(1)}, u32[]{:S(2)}, u32[]{:S(2)}) %collective-permute-start.9) | collective-permute-done | bytes 393248 | tf_op jit(solution)/shard_map/ppermute | solution.py:285
  27.3 1.6 %collective-permute-start.10 = (bf16[80,2048]{1,0:T(8,128)(2,1)S(1)}, bf16[80,2048]{1,0:T(8,128)(2,1)S(1)}, u32[]{:S(2)}, u32[]{:S(2)}) collective-permute-start(bf16[80,2048]{1,0:T(8,128)(2,1)S(1)} %shard_map.98), channel_id=1, source_target_pairs={{0,2},{2,0},{1,3},{3,1},{4,6},{6,4},{5,7},{7,5},{8,10},{10,8},{9,1... | collective-permute-start | bytes 983048 | tf_op jit(solution)/shard_map/ppermute | solution.py:285
  28.9 1.3 %collective-permute-start.17 = (bf16[128,2048]{1,0:T(8,128)(2,1)S(1)}, bf16[128,2048]{1,0:T(8,128)(2,1)S(1)}, u32[]{:S(2)}, u32[]{:S(2)}) collective-permute-start(bf16[128,2048]{1,0:T(8,128)(2,1)S(1)} %collective-permute-done.3.far_inner.refs_3_), channel_id=1, source_target_pairs={{4,0},{8,12},{5,1},{9,13},{6,2},{10,14},{7,3},{11,15},{20,16},{24,... | collective-permute-start | bytes 1572872 | tf_op jit(solution)/shard_map/ppermute | solution.py:290
  30.1 1.2 %shard_map.93.refs_4_.got_own = f32[128,256]{1,0:T(8,128)S(1)} custom-call(bf16[128,2048]{1,0:T(8,128)(2,1)S(1)} %copy-done, bf16[128,2048]{1,0:T(8,128)(2,1)S(1)} %collective-permute-done.near.refs_1_, bf16[192,2048]{1,0:T(8,128)(2,1)S(1)} %get-tuple-element.21.refs_0_, bf16[192,2048]{1,0:T(8,128)(2,1)S(1)} %get-tuple-element.22.refs_1_, ...), custom_call_target="tpu_custom_call" | custom-call | tf_op jit(solution)/shard_map/pallas_call | solution.py:110
  31.4 2.1 %collective-permute-done.2.end_two = bf16[128,2048]{1,0:T(8,128)(2,1)S(1)} collective-permute-done((bf16[128,2048]{1,0:T(8,128)(2,1)S(1)}, bf16[128,2048]{1,0:T(8,128)(2,1)S(1)}, u32[]{:S(2)}, u32[]{:S(2)}) %collective-permute-start.2) | collective-permute-done | bytes 524320 | tf_op jit(solution)/shard_map/ppermute | solution.py:284
  33.4 1.2 %shard_map.94.refs_5_.got_two = f32[128,128]{1,0:T(8,128)S(1)} custom-call(bf16[128,2048]{1,0:T(8,128)(2,1)S(1)} %collective-permute-done.2.end_two, bf16[128,2048]{1,0:T(8,128)(2,1)S(1)} %collective-permute-done.3.far_inner.refs_3_, bf16[192,2048]{1,0:T(8,128)(2,1)S(1)} %get-tuple-element.21.refs_0_, bf16[192,2048]{1,0:T(8,128)(2,1)S(1)} %get-tuple-element.22.refs_1_, ...), custom_call_target="tpu_custom_call" | custom-call | tf_op jit(solution)/shard_map/pallas_call | solution.py:110
  34.6 2.8 %collective-permute-done.10.refs_2_.refs_3_.refs_9_ = bf16[80,2048]{1,0:T(8,128)(2,1)S(1)} collective-permute-done((bf16[80,2048]{1,0:T(8,128)(2,1)S(1)}, bf16[80,2048]{1,0:T(8,128)(2,1)S(1)}, u32[]{:S(2)}, u32[]{:S(2)}) %collective-permute-start.10) | collective-permute-done | bytes 327712 | tf_op jit(solution)/shard_map/ppermute | solution.py:285
  38.2 1.5 %collective-permute-start.19 = (bf16[32,32,128]{2,1,0:T(8,128)(2,1)S(1)}, bf16[32,32,128]{2,1,0:T(8,128)(2,1)S(1)}, u32[]{:S(2)}, u32[]{:S(2)}) collective-permute-start(bf16[32,32,128]{2,1,0:T(8,128)(2,1)S(1)} %copy-done.6), channel_id=1, source_target_pairs={{0,2},{2,0},{1,3},{3,1},{4,6},{6,4},{5,7},{7,5},{8,10},{10,8},{9,1... | collective-permute-start | bytes 786440 | tf_op jit(solution)/shard_map/ppermute | solution.py:295
  40.6 2.0 %shard_map.100 = (f32[256,128]{1,0:T(8,128)S(1)}, bf16[272,128]{1,0:T(8,128)(2,1)S(1)}, bf16[272,128]{1,0:T(8,128)(2,1)S(1)}) custom-call(bf16[128,2048]{1,0:T(8,128)(2,1)S(1)} %copy-done, bf16[128,2048]{1,0:T(8,128)(2,1)S(1)} %collective-permute-done.near.refs_1_, bf16[128,2048]{1,0:T(8,128)(2,1)S(1)} %collective-permute-done.2.end_two, ...), custom_call_target="tpu_custom_call" | custom-call | tf_op jit(solution)/shard_map/pallas_call | solution.py:110
  42.6 4.2 %collective-permute-start.15 = (bf16[272,128]{1,0:T(8,128)(2,1)S(1)}, bf16[272,128]{1,0:T(8,128)(2,1)S(1)}, u32[]{:S(2)}, u32[]{:S(2)}) collective-permute-start(bf16[272,128]{1,0:T(8,128)(2,1)S(1)} %get-tuple-element.30), channel_id=1, source_target_pairs={{0,4},{4,0},{8,12},{12,8},{1,5},{5,1},{9,13},{13,9},{2,6},{6,2},{1... | collective-permute-start | bytes 208904 | tf_op jit(solution)/shard_map/ppermute | solution.py:304
  46.8 2.2 %shard_map.101 = bf16[256,128]{1,0:T(8,128)(2,1)S(1)} custom-call(bf16[128,2048]{1,0:T(8,128)(2,1)S(1)} %collective-permute-done.17.end_three, bf16[128,2048]{1,0:T(8,128)(2,1)S(1)} %collective-permute-done.1.refs_2_.across, f32[256,128]{1,0:T(8,128)S(1)} %get-tuple-element.29.earlier.here, bf16[192,2048]{1,0:T(8,128)(2,1)S(1)} %get-tuple-element.21.refs_0_, ...), custom_call_target="tpu_custom_call" | custom-call | tf_op jit(solution)/shard_map/pallas_call | solution.py:110
  48.9 2.5 %collective-permute-start.18 = (bf16[256,128]{1,0:T(8,128)(2,1)S(1)}, bf16[256,128]{1,0:T(8,128)(2,1)S(1)}, u32[]{:S(2)}, u32[]{:S(2)}) collective-permute-start(bf16[256,128]{1,0:T(8,128)(2,1)S(1)} %shard_map.101), channel_id=1, source_target_pairs={{0,12},{4,8},{8,4},{12,0},{1,13},{5,9},{9,5},{13,1},{2,14},{6,10},... | collective-permute-start | bytes 196616 | tf_op jit(solution)/shard_map/ppermute | solution.py:304
  51.4 3.7 %collective-permute-done.18.three = bf16[256,128]{1,0:T(8,128)(2,1)S(1)} collective-permute-done((bf16[256,128]{1,0:T(8,128)(2,1)S(1)}, bf16[256,128]{1,0:T(8,128)(2,1)S(1)}, u32[]{:S(2)}, u32[]{:S(2)}) %collective-permute-start.18) | collective-permute-done | bytes 65568 | tf_op jit(solution)/shard_map/ppermute | solution.py:304
  55.1 1.3 %shard_map.102 = f32[2,64]{1,0:T(2,128)} custom-call(f32[128,128]{1,0:T(8,128)S(1)} %get-tuple-element.20.base, f32[256,128]{1,0:T(8,128)S(1)} %get-tuple-element.29.earlier.here, bf16[272,128]{1,0:T(8,128)(2,1)S(1)} %collective-permute-done.15.near, bf16[272,128]{1,0:T(8,128)(2,1)S(1)} %collective-permute-done.16.two, ...), custom_call_target="tpu_custom_call" | custom-call | tf_op jit(solution)/shard_map/pallas_call | solution.py:110
  (48 shorter events, 5.0 us)
Async XLA Ops:
  0.0 11.4 %collective-permute-start.4 = (bf16[192,2048]{1,0:T(8,128)(2,1)}, bf16[192,2048]{1,0:T(8,128)(2,1)S(1)}, u32[]{:S(2)}, u32[]{:S(2)}) collective-permute-start(bf16[192,2048]{1,0:T(8,128)(2,1)} %bitcast.13), channel_id=1, source_target_pairs={{0,1},{1,0},{2,3},{3,2},{4,5},{5,4},{6,7},{7,6},{8,9},{9,8},{10,11... | collective-permute-start | bytes 2359304 | tf_op jit(solution)/shard_map/ppermute | solution.py:278
  0.5 7.7 %copy-start = (bf16[128,2048]{1,0:T(8,128)(2,1)S(1)}, bf16[128,2048]{1,0:T(8,128)(2,1)}, u32[]{:S(2)}) copy-start(bf16[128,2048]{1,0:T(8,128)(2,1)} %tokens.5) | copy-start | bytes 1572868
  0.5 10.9 %collective-permute-start.5 = (bf16[192,2048]{1,0:T(8,128)(2,1)}, bf16[192,2048]{1,0:T(8,128)(2,1)S(1)}, u32[]{:S(2)}, u32[]{:S(2)}) collective-permute-start(bf16[192,2048]{1,0:T(8,128)(2,1)} %bitcast.16), channel_id=1, source_target_pairs={{0,1},{1,0},{2,3},{3,2},{4,5},{5,4},{6,7},{7,6},{8,9},{9,8},{10,11... | collective-permute-start | bytes 2359304 | tf_op jit(solution)/shard_map/ppermute | solution.py:278
  0.5 15.4 %collective-permute-start = (bf16[128,2048]{1,0:T(8,128)(2,1)}, bf16[128,2048]{1,0:T(8,128)(2,1)S(1)}, u32[]{:S(2)}, u32[]{:S(2)}) collective-permute-start(bf16[128,2048]{1,0:T(8,128)(2,1)} %tokens.5), channel_id=1, source_target_pairs={{0,4},{4,0},{8,12},{12,8},{1,5},{5,1},{9,13},{13,9},{2,6},{6,2},{1... | collective-permute-start | bytes 1572872 | tf_op jit(solution)/shard_map/ppermute | solution.py:263
  3.5 13.1 %collective-permute-start.1 = (bf16[128,2048]{1,0:T(8,128)(2,1)}, bf16[128,2048]{1,0:T(8,128)(2,1)S(1)}, u32[]{:S(2)}, u32[]{:S(2)}) collective-permute-start(bf16[128,2048]{1,0:T(8,128)(2,1)} %tokens.5), channel_id=1, source_target_pairs={{4,8},{8,4},{5,9},{9,5},{6,10},{10,6},{7,11},{11,7},{20,24},{24,20... | collective-permute-start | bytes 1572872 | tf_op jit(solution)/shard_map/ppermute | solution.py:264
  6.5 1.6 %copy-start.2 = (bf16[1,2048,192]{1,2,0:T(8,128)(2,1)S(1)}, bf16[1,2048,192]{1,2,0:T(8,128)(2,1)}, u32[]{:S(2)}) copy-start(bf16[1,2048,192]{1,2,0:T(8,128)(2,1)} %param.13) | copy-start | bytes 2359300
  6.5 1.6 %copy-start.5 = (bf16[2048,128]{1,0:T(8,128)(2,1)S(1)}, bf16[2048,128]{1,0:T(8,128)(2,1)}, u32[]{:S(2)}) copy-start(bf16[2048,128]{1,0:T(8,128)(2,1)} %proj.1) | copy-start | bytes 1572868
  6.6 13.5 %collective-permute-start.7 = (bf16[112,2048]{1,0:T(8,128)(2,1)S(1)}, bf16[112,2048]{1,0:T(8,128)(2,1)S(1)}, u32[]{:S(2)}, u32[]{:S(2)}) collective-permute-start(bf16[112,2048]{1,0:T(8,128)(2,1)S(1)} %shard_map.95), channel_id=1, source_target_pairs={{0,2},{2,0},{1,3},{3,1},{4,6},{6,4},{5,7},{7,5},{8,10},{10,8},{9,1... | collective-permute-start | bytes 1376264 | tf_op jit(solution)/shard_map/ppermute | solution.py:269
  11.4 15.8 %collective-permute-start.9 = (bf16[96,2048]{1,0:T(8,128)(2,1)S(1)}, bf16[96,2048]{1,0:T(8,128)(2,1)S(1)}, u32[]{:S(2)}, u32[]{:S(2)}) collective-permute-start(bf16[96,2048]{1,0:T(8,128)(2,1)S(1)} %shard_map.97), channel_id=1, source_target_pairs={{0,2},{2,0},{1,3},{3,1},{4,6},{6,4},{5,7},{7,5},{8,10},{10,8},{9,1... | collective-permute-start | bytes 1179656 | tf_op jit(solution)/shard_map/ppermute | solution.py:285
  15.9 12.9 %collective-permute-start.3 = (bf16[128,2048]{1,0:T(8,128)(2,1)S(1)}, bf16[128,2048]{1,0:T(8,128)(2,1)S(1)}, u32[]{:S(2)}, u32[]{:S(2)}) collective-permute-start(bf16[128,2048]{1,0:T(8,128)(2,1)S(1)} %collective-permute-done.near.refs_1_), channel_id=1, source_target_pairs={{4,8},{8,4},{5,9},{9,5},{6,10},{10,6},{7,11},{11,7},{20,24},{24,20... | collective-permute-start | bytes 1572872 | tf_op jit(solution)/shard_map/ppermute | solution.py:283
  16.6 16.8 %collective-permute-start.2 = (bf16[128,2048]{1,0:T(8,128)(2,1)S(1)}, bf16[128,2048]{1,0:T(8,128)(2,1)S(1)}, u32[]{:S(2)}, u32[]{:S(2)}) collective-permute-start(bf16[128,2048]{1,0:T(8,128)(2,1)S(1)} %collective-permute-done.1.refs_2_.across), channel_id=1, source_target_pairs={{4,0},{8,12},{5,1},{9,13},{6,2},{10,14},{7,3},{11,15},{20,16},{24,... | collective-permute-start | bytes 1572872 | tf_op jit(solution)/shard_map/ppermute | solution.py:284
  20.1 17.4 %collective-permute-start.8 = (bf16[112,2048]{1,0:T(8,128)(2,1)S(1)}, bf16[112,2048]{1,0:T(8,128)(2,1)S(1)}, u32[]{:S(2)}, u32[]{:S(2)}) collective-permute-start(bf16[112,2048]{1,0:T(8,128)(2,1)S(1)} %shard_map.96.refs_0_.refs_6_), channel_id=1, source_target_pairs={{0,16},{16,0},{1,17},{17,1},{2,18},{18,2},{3,19},{19,3},{4,20},{20... | collective-permute-start | bytes 1376264 | tf_op jit(solution)/shard_map/ppermute | solution.py:287
  21.7 5.6 %collective-permute-start.6 = (bf16[16,2048]{1,0:T(8,128)(2,1)S(1)}, bf16[16,2048]{1,0:T(8,128)(2,1)S(1)}, u32[]{:S(2)}, u32[]{:S(2)}) collective-permute-start(bf16[16,2048]{1,0:T(8,128)(2,1)S(1)} %shard_map.92), channel_id=1, source_target_pairs={{0,1},{1,0},{2,3},{3,2},{4,5},{5,4},{6,7},{7,6},{8,9},{9,8},{10,11... | collective-permute-start | bytes 196616 | tf_op jit(solution)/shard_map/ppermute | solution.py:279
  27.3 10.2 %collective-permute-start.11 = (bf16[96,2048]{1,0:T(8,128)(2,1)S(1)}, bf16[96,2048]{1,0:T(8,128)(2,1)S(1)}, u32[]{:S(2)}, u32[]{:S(2)}) collective-permute-start(bf16[96,2048]{1,0:T(8,128)(2,1)S(1)} %collective-permute-done.9.refs_2_.refs_8_), channel_id=1, source_target_pairs={{0,1},{1,0},{2,3},{3,2},{4,5},{5,4},{6,7},{7,6},{8,9},{9,8},{10,11... | collective-permute-start | bytes 1179656 | tf_op jit(solution)/shard_map/ppermute | solution.py:292
  27.3 10.2 %collective-permute-start.10 = (bf16[80,2048]{1,0:T(8,128)(2,1)S(1)}, bf16[80,2048]{1,0:T(8,128)(2,1)S(1)}, u32[]{:S(2)}, u32[]{:S(2)}) collective-permute-start(bf16[80,2048]{1,0:T(8,128)(2,1)S(1)} %shard_map.98), channel_id=1, source_target_pairs={{0,2},{2,0},{1,3},{3,1},{4,6},{6,4},{5,7},{7,5},{8,10},{10,8},{9,1... | collective-permute-start | bytes 983048 | tf_op jit(solution)/shard_map/ppermute | solution.py:285
  28.9 17.9 %collective-permute-start.17 = (bf16[128,2048]{1,0:T(8,128)(2,1)S(1)}, bf16[128,2048]{1,0:T(8,128)(2,1)S(1)}, u32[]{:S(2)}, u32[]{:S(2)}) collective-permute-start(bf16[128,2048]{1,0:T(8,128)(2,1)S(1)} %collective-permute-done.3.far_inner.refs_3_), channel_id=1, source_target_pairs={{4,0},{8,12},{5,1},{9,13},{6,2},{10,14},{7,3},{11,15},{20,16},{24,... | collective-permute-start | bytes 1572872 | tf_op jit(solution)/shard_map/ppermute | solution.py:290
  34.6 3.6 %copy-start.6 = (bf16[32,32,128]{2,1,0:T(8,128)(2,1)S(1)}, bf16[32,32,128]{2,1,0:T(8,128)(2,1)}, u32[]{:S(2)}) copy-start(bf16[32,32,128]{2,1,0:T(8,128)(2,1)} %param.17) | copy-start | bytes 786436
  37.6 3.0 %collective-permute-start.12 = (bf16[112,2048]{1,0:T(8,128)(2,1)S(1)}, bf16[112,2048]{1,0:T(8,128)(2,1)S(1)}, u32[]{:S(2)}, u32[]{:S(2)}) collective-permute-start(bf16[112,2048]{1,0:T(8,128)(2,1)S(1)} %get-tuple-element.26), channel_id=1, source_target_pairs={{0,1},{1,0},{2,3},{3,2},{4,5},{5,4},{6,7},{7,6},{8,9},{9,8},{10,11... | collective-permute-start | bytes 1376264 | tf_op jit(solution)/shard_map/ppermute | solution.py:294
  37.7 2.9 %collective-permute-start.13 = (bf16[112,2048]{1,0:T(8,128)(2,1)S(1)}, bf16[112,2048]{1,0:T(8,128)(2,1)S(1)}, u32[]{:S(2)}, u32[]{:S(2)}) collective-permute-start(bf16[112,2048]{1,0:T(8,128)(2,1)S(1)} %get-tuple-element.27), channel_id=1, source_target_pairs={{0,1},{1,0},{2,3},{3,2},{4,5},{5,4},{6,7},{7,6},{8,9},{9,8},{10,11... | collective-permute-start | bytes 1376264 | tf_op jit(solution)/shard_map/ppermute | solution.py:294
  38.2 2.4 %collective-permute-start.14 = (bf16[80,2048]{1,0:T(8,128)(2,1)S(1)}, bf16[80,2048]{1,0:T(8,128)(2,1)S(1)}, u32[]{:S(2)}, u32[]{:S(2)}) collective-permute-start(bf16[80,2048]{1,0:T(8,128)(2,1)S(1)} %get-tuple-element.28), channel_id=1, source_target_pairs={{0,1},{1,0},{2,3},{3,2},{4,5},{5,4},{6,7},{7,6},{8,9},{9,8},{10,11... | collective-permute-start | bytes 983048 | tf_op jit(solution)/shard_map/ppermute | solution.py:294
  38.2 13.2 %collective-permute-start.19 = (bf16[32,32,128]{2,1,0:T(8,128)(2,1)S(1)}, bf16[32,32,128]{2,1,0:T(8,128)(2,1)S(1)}, u32[]{:S(2)}, u32[]{:S(2)}) collective-permute-start(bf16[32,32,128]{2,1,0:T(8,128)(2,1)S(1)} %copy-done.6), channel_id=1, source_target_pairs={{0,2},{2,0},{1,3},{3,1},{4,6},{6,4},{5,7},{7,5},{8,10},{10,8},{9,1... | collective-permute-start | bytes 786440 | tf_op jit(solution)/shard_map/ppermute | solution.py:295
  42.6 12.5 %collective-permute-start.15 = (bf16[272,128]{1,0:T(8,128)(2,1)S(1)}, bf16[272,128]{1,0:T(8,128)(2,1)S(1)}, u32[]{:S(2)}, u32[]{:S(2)}) collective-permute-start(bf16[272,128]{1,0:T(8,128)(2,1)S(1)} %get-tuple-element.30), channel_id=1, source_target_pairs={{0,4},{4,0},{8,12},{12,8},{1,5},{5,1},{9,13},{13,9},{2,6},{6,2},{1... | collective-permute-start | bytes 208904 | tf_op jit(solution)/shard_map/ppermute | solution.py:304
  46.8 8.4 %collective-permute-start.16 = (bf16[272,128]{1,0:T(8,128)(2,1)S(1)}, bf16[272,128]{1,0:T(8,128)(2,1)S(1)}, u32[]{:S(2)}, u32[]{:S(2)}) collective-permute-start(bf16[272,128]{1,0:T(8,128)(2,1)S(1)} %get-tuple-element.31), channel_id=1, source_target_pairs={{0,8},{4,12},{8,0},{12,4},{1,9},{5,13},{9,1},{13,5},{2,10},{6,14},... | collective-permute-start | bytes 208904 | tf_op jit(solution)/shard_map/ppermute | solution.py:304
  48.9 6.2 %collective-permute-start.18 = (bf16[256,128]{1,0:T(8,128)(2,1)S(1)}, bf16[256,128]{1,0:T(8,128)(2,1)S(1)}, u32[]{:S(2)}, u32[]{:S(2)}) collective-permute-start(bf16[256,128]{1,0:T(8,128)(2,1)S(1)} %shard_map.101), channel_id=1, source_target_pairs={{0,12},{4,8},{8,4},{12,0},{1,13},{5,9},{9,5},{13,1},{2,14},{6,10},... | collective-permute-start | bytes 196616 | tf_op jit(solution)/shard_map/ppermute | solution.py:304
  (6 other events, 5.5 us)

commit v8 on v7

--- a/solution.py
+++ b/solution.py
@@ -136,10 +136,10 @@
     fold[...] = jnp.zeros_like(fold)
     for i in range(rows // FOLD):
         fold[:, i * width : (i + 1) * width] = folded[i * FOLD : (i + 1) * FOLD]
-    left = rest_up.shape[0]
-    rest_gate[:left, :] = gate[rows - left :, :]
-    rest_gate[left:, :] = fold[...]
-    rest_up[...] = up[rows - left :, :]
+    left = rest_gate.shape[0]
+    rest_gate[...] = gate[rows - left :, :]
+    rest_up[:left, :] = up[rows - left :, :]
+    rest_up[left:, :] = fold[...]
     held_gate[...] = gate[...]
     held_up[...] = up[...]
     base[...] = dot(tokens[...], proj[...]).T
@@ -182,9 +182,9 @@
     first = lax.axis_index(G) == 0
     cores = []
     for mine, others, rest_gate, rest_up in (refs[:4], refs[4:]):
-        left = rest_up.shape[0]
+        left = rest_gate.shape[0]
         gate, up = jnp.where(first, mine[...], others[...]), jnp.where(first, others[...], mine[...])
-        cores.append(([gate, rest_gate[:left, :], up, rest_up[...]], rest_gate[left:, :]))
+        cores.append(([gate, rest_gate[...], up, rest_up[:left, :]], rest_up[left:, :]))
     return cores
 
 
@@ -270,7 +270,7 @@
     fold, rest_gate, rest_up, held_gate, held_up, base, weights, live, chosen = kernel(
         fold_body,
         [passage_lengths, tokens, gate, up, down, proj_weight, route_ids.T, gate_values.T],
-        [((r, model_width), bf16) for r in (FOLD, left + FOLD, left, hidden_part, hidden_part)]
+        [((r, model_width), bf16) for r in (FOLD, left, left + FOLD, hidden_part, hidden_part)]
         + [((width, n), f32), ((8, n), f32), ((n, width), f32), ((2 * rows, 2 * queries.shape[0]), bf16)],
         smem=(0,),
         fetched=(1,),

time: 56.7 us -> 55.9 us (0.986)
  starting transfers between devices: 21.7 us -> 20.5 us
    ppermute x2, waiting for transfers between devices: 8.42 us -> 3.81 us  [by_column(): lax.ppermute(a, Q, swap)]
    ppermute x1, waiting for transfers between devices: 0.01 us -> 2.31 us  [by_column(): end_three = lax.ppermute(far_inner, E, ends)]
    ppermute x1, waiting for transfers between devices: 2.08 us -> 3.88 us  [by_column(): end_two = lax.ppermute(across, E, ends)]
    ppermute x3, starting transfers between devices: 6.65 us -> 5.38 us  [by_column(): lax.ppermute(a, E, [(i, i ^ k) for i in range(4)])]
    ppermute x3, waiting for transfers between devices: 3.69 us -> 4.5 us  [by_column(): lax.ppermute(a, E, [(i, i ^ k) for i in range(4)])]
where the time goes in v8:
time: 55.9 us; the launch traced here: 55.5 us
  waiting for transfers between devices  21.1 us (38%)
  starting transfers between devices  20.5 us (37%)
  Pallas kernels  9.44 us (17%)
  local copies, waits for them, and re-layouts  4.24 us (8%)
    pallas_call x7, Pallas kernels, kernel(): pl.pallas_call(body, out_shape=[jax.ShapeDtypeStruct(shape, dtype) for sh...  9.27 us
    ppermute x3, starting transfers between devices, by_column(): lax.ppermute(a, E, [(i, i ^ k) for i in range(4)])  5.38 us
    ppermute x3, waiting for transfers between devices, by_column(): lax.ppermute(a, E, [(i, i ^ k) for i in range(4)])  4.5 us
    unnamed x20, local copies, waits for them, and re-layouts  4.24 us
    ppermute x1, waiting for transfers between devices, by_column(): end_two = lax.ppermute(across, E, ends)  3.88 us
    ppermute x2, waiting for transfers between devices, by_column(): lax.ppermute(a, Q, swap)  3.81 us
    ppermute x1, waiting for transfers between devices, by_column(): near = lax.ppermute(tokens, E, [(i, i ^ 1) for i in range(4)])  3.8 us
    ppermute x1, starting transfers between devices, by_column(): near = lax.ppermute(tokens, E, [(i, i ^ 1) for i in range(4)])  3.02 us
  transfers between devices with their start and end apart: 20, of which 7 were waited for; matrix products, arithmetic and copies ran while one was open for 0% of the time, Pallas kernels for 15%

profile of v8, /device:TPU:0, one launch (start us, length us, event | category | flops | bytes accessed | tf_op | source)
XLA Modules:
  0.0 55.5 jit_solution(14963776747789852469)
XLA Ops:
  0.5 3.0 %collective-permute-start = (bf16[128,2048]{1,0:T(8,128)(2,1)}, bf16[128,2048]{1,0:T(8,128)(2,1)S(1)}, u32[]{:S(2)}, u32[]{:S(2)}) collective-permute-start(bf16[128,2048]{1,0:T(8,128)(2,1)} %tokens.5), channel_id=1, source_target_pairs={{0,4},{4,0},{8,12},{12,8},{1,5},{5,1},{9,13},{13,9},{2,6},{6,2},{1... | collective-permute-start | bytes 1572872 | tf_op jit(solution)/shard_map/ppermute | solution.py:263
  4.2 1.1 %copy-done.1 = bf16[1,2048,192]{1,2,0:T(8,128)(2,1)S(1)} copy-done((bf16[1,2048,192]{1,2,0:T(8,128)(2,1)S(1)}, bf16[1,2048,192]{1,2,0:T(8,128)(2,1)}, u32[]{:S(2)}) %copy-start.1) | copy-done | bytes 786456
  5.4 1.1 %copy-done.3 = bf16[1,2048,192]{1,2,0:T(8,128)(2,1)S(1)} copy-done((bf16[1,2048,192]{1,2,0:T(8,128)(2,1)S(1)}, bf16[1,2048,192]{1,2,0:T(8,128)(2,1)}, u32[]{:S(2)}) %copy-start.3) | copy-done | bytes 786456
  6.6 1.6 %collective-permute-start.7 = (bf16[112,2048]{1,0:T(8,128)(2,1)S(1)}, bf16[112,2048]{1,0:T(8,128)(2,1)S(1)}, u32[]{:S(2)}, u32[]{:S(2)}) collective-permute-start(bf16[112,2048]{1,0:T(8,128)(2,1)S(1)} %shard_map.95), channel_id=1, source_target_pairs={{0,2},{2,0},{1,3},{3,1},{4,6},{6,4},{5,7},{7,5},{8,10},{10,8},{9,1... | collective-permute-start | bytes 1376264 | tf_op jit(solution)/shard_map/ppermute | solution.py:269
  8.8 1.1 %copy-done.4 = bf16[1,2048,192]{1,2,0:T(8,128)(2,1)S(1)} copy-done((bf16[1,2048,192]{1,2,0:T(8,128)(2,1)S(1)}, bf16[1,2048,192]{1,2,0:T(8,128)(2,1)}, u32[]{:S(2)}) %copy-start.4) | copy-done | bytes 786456
  9.9 1.4 %shard_map.91 = (bf16[16,2048]{1,0:T(8,128)(2,1)S(1)}, bf16[80,2048]{1,0:T(8,128)(2,1)S(1)}, bf16[96,2048]{1,0:T(8,128)(2,1)S(1)}, bf16[192,2048]{1,0:T(8,128)(2...) custom-call(s32[2]{0:T(128)S(1)} %copy-done.9, ...), custom_call_target="tpu_custom_call" | custom-call | tf_op jit(solution)/shard_map/pallas_call | solution.py:110
  12.1 3.8 %collective-permute-done.near.refs_1_ = bf16[128,2048]{1,0:T(8,128)(2,1)S(1)} collective-permute-done((bf16[128,2048]{1,0:T(8,128)(2,1)}, bf16[128,2048]{1,0:T(8,128)(2,1)S(1)}, u32[]{:S(2)}, u32[]{:S(2)}) %collective-permute-start) | collective-permute-done | bytes 524320 | tf_op jit(solution)/shard_map/ppermute | solution.py:263
  16.6 1.3 %collective-permute-start.2 = (bf16[128,2048]{1,0:T(8,128)(2,1)S(1)}, bf16[128,2048]{1,0:T(8,128)(2,1)S(1)}, u32[]{:S(2)}, u32[]{:S(2)}) collective-permute-start(bf16[128,2048]{1,0:T(8,128)(2,1)S(1)} %collective-permute-done.1.refs_2_.across), channel_id=1, source_target_pairs={{4,0},{8,12},{5,1},{9,13},{6,2},{10,14},{7,3},{11,15},{20,16},{24,... | collective-permute-start | bytes 1572872 | tf_op jit(solution)/shard_map/ppermute | solution.py:284
  18.0 2.0 %collective-permute-done.7.refs_0_ = bf16[112,2048]{1,0:T(8,128)(2,1)S(1)} collective-permute-done((bf16[112,2048]{1,0:T(8,128)(2,1)S(1)}, bf16[112,2048]{1,0:T(8,128)(2,1)S(1)}, u32[]{:S(2)}, u32[]{:S(2)}) %collective-permute-start.7) | collective-permute-done | bytes 458784 | tf_op jit(solution)/shard_map/ppermute | solution.py:269
  20.1 1.6 %collective-permute-start.8 = (bf16[112,2048]{1,0:T(8,128)(2,1)S(1)}, bf16[112,2048]{1,0:T(8,128)(2,1)S(1)}, u32[]{:S(2)}, u32[]{:S(2)}) collective-permute-start(bf16[112,2048]{1,0:T(8,128)(2,1)S(1)} %shard_map.96.refs_0_.refs_6_), channel_id=1, source_target_pairs={{0,16},{16,0},{1,17},{17,1},{2,18},{18,2},{3,19},{19,3},{4,20},{20... | collective-permute-start | bytes 1376264 | tf_op jit(solution)/shard_map/ppermute | solution.py:287
  21.7 1.6 %collective-permute-start.10 = (bf16[96,2048]{1,0:T(8,128)(2,1)S(1)}, bf16[96,2048]{1,0:T(8,128)(2,1)S(1)}, u32[]{:S(2)}, u32[]{:S(2)}) collective-permute-start(bf16[96,2048]{1,0:T(8,128)(2,1)S(1)} %shard_map.98), channel_id=1, source_target_pairs={{0,2},{2,0},{1,3},{3,1},{4,6},{6,4},{5,7},{7,5},{8,10},{10,8},{9,1... | collective-permute-start | bytes 1179656 | tf_op jit(solution)/shard_map/ppermute | solution.py:285
  23.3 3.8 %collective-permute-done.9.refs_2_.refs_8_ = bf16[80,2048]{1,0:T(8,128)(2,1)S(1)} collective-permute-done((bf16[80,2048]{1,0:T(8,128)(2,1)S(1)}, bf16[80,2048]{1,0:T(8,128)(2,1)S(1)}, u32[]{:S(2)}, u32[]{:S(2)}) %collective-permute-start.9) | collective-permute-done | bytes 327712 | tf_op jit(solution)/shard_map/ppermute | solution.py:285
  27.1 1.3 %collective-permute-start.17 = (bf16[128,2048]{1,0:T(8,128)(2,1)S(1)}, bf16[128,2048]{1,0:T(8,128)(2,1)S(1)}, u32[]{:S(2)}, u32[]{:S(2)}) collective-permute-start(bf16[128,2048]{1,0:T(8,128)(2,1)S(1)} %collective-permute-done.3.far_inner.refs_3_), channel_id=1, source_target_pairs={{4,0},{8,12},{5,1},{9,13},{6,2},{10,14},{7,3},{11,15},{20,16},{24,... | collective-permute-start | bytes 1572872 | tf_op jit(solution)/shard_map/ppermute | solution.py:290
  28.4 1.2 %shard_map.93.refs_4_.got_own = f32[128,256]{1,0:T(8,128)S(1)} custom-call(bf16[128,2048]{1,0:T(8,128)(2,1)S(1)} %copy-done, bf16[128,2048]{1,0:T(8,128)(2,1)S(1)} %collective-permute-done.near.refs_1_, bf16[192,2048]{1,0:T(8,128)(2,1)S(1)} %get-tuple-element.21.refs_0_, bf16[192,2048]{1,0:T(8,128)(2,1)S(1)} %get-tuple-element.22.refs_1_, ...), custom_call_target="tpu_custom_call" | custom-call | tf_op jit(solution)/shard_map/pallas_call | solution.py:110
  29.6 3.9 %collective-permute-done.2.end_two = bf16[128,2048]{1,0:T(8,128)(2,1)S(1)} collective-permute-done((bf16[128,2048]{1,0:T(8,128)(2,1)S(1)}, bf16[128,2048]{1,0:T(8,128)(2,1)S(1)}, u32[]{:S(2)}, u32[]{:S(2)}) %collective-permute-start.2) | collective-permute-done | bytes 524320 | tf_op jit(solution)/shard_map/ppermute | solution.py:284
  33.4 1.2 %shard_map.94.refs_5_.got_two = f32[128,128]{1,0:T(8,128)S(1)} custom-call(bf16[128,2048]{1,0:T(8,128)(2,1)S(1)} %collective-permute-done.2.end_two, bf16[128,2048]{1,0:T(8,128)(2,1)S(1)} %collective-permute-done.3.far_inner.refs_3_, bf16[192,2048]{1,0:T(8,128)(2,1)S(1)} %get-tuple-element.21.refs_0_, bf16[192,2048]{1,0:T(8,128)(2,1)S(1)} %get-tuple-element.22.refs_1_, ...), custom_call_target="tpu_custom_call" | custom-call | tf_op jit(solution)/shard_map/pallas_call | solution.py:110
  35.6 1.5 %collective-permute-start.19 = (bf16[32,32,128]{2,1,0:T(8,128)(2,1)S(1)}, bf16[32,32,128]{2,1,0:T(8,128)(2,1)S(1)}, u32[]{:S(2)}, u32[]{:S(2)}) collective-permute-start(bf16[32,32,128]{2,1,0:T(8,128)(2,1)S(1)} %copy-done.6), channel_id=1, source_target_pairs={{0,2},{2,0},{1,3},{3,1},{4,6},{6,4},{5,7},{7,5},{8,10},{10,8},{9,1... | collective-permute-start | bytes 786440 | tf_op jit(solution)/shard_map/ppermute | solution.py:295
  37.9 2.0 %shard_map.100 = (f32[256,128]{1,0:T(8,128)S(1)}, bf16[272,128]{1,0:T(8,128)(2,1)S(1)}, bf16[272,128]{1,0:T(8,128)(2,1)S(1)}) custom-call(bf16[128,2048]{1,0:T(8,128)(2,1)S(1)} %copy-done, bf16[128,2048]{1,0:T(8,128)(2,1)S(1)} %collective-permute-done.near.refs_1_, bf16[128,2048]{1,0:T(8,128)(2,1)S(1)} %collective-permute-done.2.end_two, ...), custom_call_target="tpu_custom_call" | custom-call | tf_op jit(solution)/shard_map/pallas_call | solution.py:110
  39.9 3.7 %collective-permute-start.15 = (bf16[272,128]{1,0:T(8,128)(2,1)S(1)}, bf16[272,128]{1,0:T(8,128)(2,1)S(1)}, u32[]{:S(2)}, u32[]{:S(2)}) collective-permute-start(bf16[272,128]{1,0:T(8,128)(2,1)S(1)} %get-tuple-element.30), channel_id=1, source_target_pairs={{0,4},{4,0},{8,12},{12,8},{1,5},{5,1},{9,13},{13,9},{2,6},{6,2},{1... | collective-permute-start | bytes 208904 | tf_op jit(solution)/shard_map/ppermute | solution.py:304
  43.6 2.3 %collective-permute-done.17.end_three = bf16[128,2048]{1,0:T(8,128)(2,1)S(1)} collective-permute-done((bf16[128,2048]{1,0:T(8,128)(2,1)S(1)}, bf16[128,2048]{1,0:T(8,128)(2,1)S(1)}, u32[]{:S(2)}, u32[]{:S(2)}) %collective-permute-start.17) | collective-permute-done | bytes 524320 | tf_op jit(solution)/shard_map/ppermute | solution.py:290
  46.0 2.2 %shard_map.101 = bf16[256,128]{1,0:T(8,128)(2,1)S(1)} custom-call(bf16[128,2048]{1,0:T(8,128)(2,1)S(1)} %collective-permute-done.17.end_three, bf16[128,2048]{1,0:T(8,128)(2,1)S(1)} %collective-permute-done.1.refs_2_.across, f32[256,128]{1,0:T(8,128)S(1)} %get-tuple-element.29.earlier.here, bf16[192,2048]{1,0:T(8,128)(2,1)S(1)} %get-tuple-element.21.refs_0_, ...), custom_call_target="tpu_custom_call" | custom-call | tf_op jit(solution)/shard_map/pallas_call | solution.py:110
  48.1 1.6 %collective-permute-start.18 = (bf16[256,128]{1,0:T(8,128)(2,1)S(1)}, bf16[256,128]{1,0:T(8,128)(2,1)S(1)}, u32[]{:S(2)}, u32[]{:S(2)}) collective-permute-start(bf16[256,128]{1,0:T(8,128)(2,1)S(1)} %shard_map.101), channel_id=1, source_target_pairs={{0,12},{4,8},{8,4},{12,0},{1,13},{5,9},{9,5},{13,1},{2,14},{6,10},... | collective-permute-start | bytes 196616 | tf_op jit(solution)/shard_map/ppermute | solution.py:304
  49.8 4.5 %collective-permute-done.18.three = bf16[256,128]{1,0:T(8,128)(2,1)S(1)} collective-permute-done((bf16[256,128]{1,0:T(8,128)(2,1)S(1)}, bf16[256,128]{1,0:T(8,128)(2,1)S(1)}, u32[]{:S(2)}, u32[]{:S(2)}) %collective-permute-start.18) | collective-permute-done | bytes 65568 | tf_op jit(solution)/shard_map/ppermute | solution.py:304
  54.3 1.3 %shard_map.102 = f32[2,64]{1,0:T(2,128)} custom-call(f32[128,128]{1,0:T(8,128)S(1)} %get-tuple-element.20.base, f32[256,128]{1,0:T(8,128)S(1)} %get-tuple-element.29.earlier.here, bf16[272,128]{1,0:T(8,128)(2,1)S(1)} %collective-permute-done.15.near, bf16[272,128]{1,0:T(8,128)(2,1)S(1)} %collective-permute-done.16.two, ...), custom_call_target="tpu_custom_call" | custom-call | tf_op jit(solution)/shard_map/pallas_call | solution.py:110
  (48 shorter events, 5.2 us)
Async XLA Ops:
  0.0 11.4 %collective-permute-start.4 = (bf16[192,2048]{1,0:T(8,128)(2,1)}, bf16[192,2048]{1,0:T(8,128)(2,1)S(1)}, u32[]{:S(2)}, u32[]{:S(2)}) collective-permute-start(bf16[192,2048]{1,0:T(8,128)(2,1)} %bitcast.13), channel_id=1, source_target_pairs={{0,1},{1,0},{2,3},{3,2},{4,5},{5,4},{6,7},{7,6},{8,9},{9,8},{10,11... | collective-permute-start | bytes 2359304 | tf_op jit(solution)/shard_map/ppermute | solution.py:278
  0.5 7.7 %copy-start = (bf16[128,2048]{1,0:T(8,128)(2,1)S(1)}, bf16[128,2048]{1,0:T(8,128)(2,1)}, u32[]{:S(2)}) copy-start(bf16[128,2048]{1,0:T(8,128)(2,1)} %tokens.5) | copy-start | bytes 1572868
  0.5 10.9 %collective-permute-start.5 = (bf16[192,2048]{1,0:T(8,128)(2,1)}, bf16[192,2048]{1,0:T(8,128)(2,1)S(1)}, u32[]{:S(2)}, u32[]{:S(2)}) collective-permute-start(bf16[192,2048]{1,0:T(8,128)(2,1)} %bitcast.16), channel_id=1, source_target_pairs={{0,1},{1,0},{2,3},{3,2},{4,5},{5,4},{6,7},{7,6},{8,9},{9,8},{10,11... | collective-permute-start | bytes 2359304 | tf_op jit(solution)/shard_map/ppermute | solution.py:278
  0.5 15.4 %collective-permute-start = (bf16[128,2048]{1,0:T(8,128)(2,1)}, bf16[128,2048]{1,0:T(8,128)(2,1)S(1)}, u32[]{:S(2)}, u32[]{:S(2)}) collective-permute-start(bf16[128,2048]{1,0:T(8,128)(2,1)} %tokens.5), channel_id=1, source_target_pairs={{0,4},{4,0},{8,12},{12,8},{1,5},{5,1},{9,13},{13,9},{2,6},{6,2},{1... | collective-permute-start | bytes 1572872 | tf_op jit(solution)/shard_map/ppermute | solution.py:263
  3.5 13.1 %collective-permute-start.1 = (bf16[128,2048]{1,0:T(8,128)(2,1)}, bf16[128,2048]{1,0:T(8,128)(2,1)S(1)}, u32[]{:S(2)}, u32[]{:S(2)}) collective-permute-start(bf16[128,2048]{1,0:T(8,128)(2,1)} %tokens.5), channel_id=1, source_target_pairs={{4,8},{8,4},{5,9},{9,5},{6,10},{10,6},{7,11},{11,7},{20,24},{24,20... | collective-permute-start | bytes 1572872 | tf_op jit(solution)/shard_map/ppermute | solution.py:264
  4.2 1.1 %copy-start.1 = (bf16[1,2048,192]{1,2,0:T(8,128)(2,1)S(1)}, bf16[1,2048,192]{1,2,0:T(8,128)(2,1)}, u32[]{:S(2)}) copy-start(bf16[1,2048,192]{1,2,0:T(8,128)(2,1)} %param.13) | copy-start | bytes 2359300
  6.5 1.6 %copy-start.2 = (bf16[1,2048,192]{1,2,0:T(8,128)(2,1)S(1)}, bf16[1,2048,192]{1,2,0:T(8,128)(2,1)}, u32[]{:S(2)}) copy-start(bf16[1,2048,192]{1,2,0:T(8,128)(2,1)} %param.13) | copy-start | bytes 2359300
  6.5 1.6 %copy-start.5 = (bf16[2048,128]{1,0:T(8,128)(2,1)S(1)}, bf16[2048,128]{1,0:T(8,128)(2,1)}, u32[]{:S(2)}) copy-start(bf16[2048,128]{1,0:T(8,128)(2,1)} %proj.1) | copy-start | bytes 1572868
  6.6 13.5 %collective-permute-start.7 = (bf16[112,2048]{1,0:T(8,128)(2,1)S(1)}, bf16[112,2048]{1,0:T(8,128)(2,1)S(1)}, u32[]{:S(2)}, u32[]{:S(2)}) collective-permute-start(bf16[112,2048]{1,0:T(8,128)(2,1)S(1)} %shard_map.95), channel_id=1, source_target_pairs={{0,2},{2,0},{1,3},{3,1},{4,6},{6,4},{5,7},{7,5},{8,10},{10,8},{9,1... | collective-permute-start | bytes 1376264 | tf_op jit(solution)/shard_map/ppermute | solution.py:269
  11.4 15.6 %collective-permute-start.9 = (bf16[80,2048]{1,0:T(8,128)(2,1)S(1)}, bf16[80,2048]{1,0:T(8,128)(2,1)S(1)}, u32[]{:S(2)}, u32[]{:S(2)}) collective-permute-start(bf16[80,2048]{1,0:T(8,128)(2,1)S(1)} %shard_map.97), channel_id=1, source_target_pairs={{0,2},{2,0},{1,3},{3,1},{4,6},{6,4},{5,7},{7,5},{8,10},{10,8},{9,1... | collective-permute-start | bytes 983048 | tf_op jit(solution)/shard_map/ppermute | solution.py:285
  15.9 11.2 %collective-permute-start.3 = (bf16[128,2048]{1,0:T(8,128)(2,1)S(1)}, bf16[128,2048]{1,0:T(8,128)(2,1)S(1)}, u32[]{:S(2)}, u32[]{:S(2)}) collective-permute-start(bf16[128,2048]{1,0:T(8,128)(2,1)S(1)} %collective-permute-done.near.refs_1_), channel_id=1, source_target_pairs={{4,8},{8,4},{5,9},{9,5},{6,10},{10,6},{7,11},{11,7},{20,24},{24,20... | collective-permute-start | bytes 1572872 | tf_op jit(solution)/shard_map/ppermute | solution.py:283
  16.6 16.8 %collective-permute-start.2 = (bf16[128,2048]{1,0:T(8,128)(2,1)S(1)}, bf16[128,2048]{1,0:T(8,128)(2,1)S(1)}, u32[]{:S(2)}, u32[]{:S(2)}) collective-permute-start(bf16[128,2048]{1,0:T(8,128)(2,1)S(1)} %collective-permute-done.1.refs_2_.across), channel_id=1, source_target_pairs={{4,0},{8,12},{5,1},{9,13},{6,2},{10,14},{7,3},{11,15},{20,16},{24,... | collective-permute-start | bytes 1572872 | tf_op jit(solution)/shard_map/ppermute | solution.py:284
  17.9 3.8 %collective-permute-start.6 = (bf16[16,2048]{1,0:T(8,128)(2,1)S(1)}, bf16[16,2048]{1,0:T(8,128)(2,1)S(1)}, u32[]{:S(2)}, u32[]{:S(2)}) collective-permute-start(bf16[16,2048]{1,0:T(8,128)(2,1)S(1)} %shard_map.92), channel_id=1, source_target_pairs={{0,1},{1,0},{2,3},{3,2},{4,5},{5,4},{6,7},{7,6},{8,9},{9,8},{10,11... | collective-permute-start | bytes 196616 | tf_op jit(solution)/shard_map/ppermute | solution.py:279
  20.1 14.6 %collective-permute-start.8 = (bf16[112,2048]{1,0:T(8,128)(2,1)S(1)}, bf16[112,2048]{1,0:T(8,128)(2,1)S(1)}, u32[]{:S(2)}, u32[]{:S(2)}) collective-permute-start(bf16[112,2048]{1,0:T(8,128)(2,1)S(1)} %shard_map.96.refs_0_.refs_6_), channel_id=1, source_target_pairs={{0,16},{16,0},{1,17},{17,1},{2,18},{18,2},{3,19},{19,3},{4,20},{20... | collective-permute-start | bytes 1376264 | tf_op jit(solution)/shard_map/ppermute | solution.py:287
  21.7 13.0 %collective-permute-start.10 = (bf16[96,2048]{1,0:T(8,128)(2,1)S(1)}, bf16[96,2048]{1,0:T(8,128)(2,1)S(1)}, u32[]{:S(2)}, u32[]{:S(2)}) collective-permute-start(bf16[96,2048]{1,0:T(8,128)(2,1)S(1)} %shard_map.98), channel_id=1, source_target_pairs={{0,2},{2,0},{1,3},{3,1},{4,6},{6,4},{5,7},{7,5},{8,10},{10,8},{9,1... | collective-permute-start | bytes 1179656 | tf_op jit(solution)/shard_map/ppermute | solution.py:285
  27.1 7.6 %collective-permute-start.11 = (bf16[80,2048]{1,0:T(8,128)(2,1)S(1)}, bf16[80,2048]{1,0:T(8,128)(2,1)S(1)}, u32[]{:S(2)}, u32[]{:S(2)}) collective-permute-start(bf16[80,2048]{1,0:T(8,128)(2,1)S(1)} %collective-permute-done.9.refs_2_.refs_8_), channel_id=1, source_target_pairs={{0,1},{1,0},{2,3},{3,2},{4,5},{5,4},{6,7},{7,6},{8,9},{9,8},{10,11... | collective-permute-start | bytes 983048 | tf_op jit(solution)/shard_map/ppermute | solution.py:292
  27.1 18.9 %collective-permute-start.17 = (bf16[128,2048]{1,0:T(8,128)(2,1)S(1)}, bf16[128,2048]{1,0:T(8,128)(2,1)S(1)}, u32[]{:S(2)}, u32[]{:S(2)}) collective-permute-start(bf16[128,2048]{1,0:T(8,128)(2,1)S(1)} %collective-permute-done.3.far_inner.refs_3_), channel_id=1, source_target_pairs={{4,0},{8,12},{5,1},{9,13},{6,2},{10,14},{7,3},{11,15},{20,16},{24,... | collective-permute-start | bytes 1572872 | tf_op jit(solution)/shard_map/ppermute | solution.py:290
  34.8 3.1 %collective-permute-start.12 = (bf16[112,2048]{1,0:T(8,128)(2,1)S(1)}, bf16[112,2048]{1,0:T(8,128)(2,1)S(1)}, u32[]{:S(2)}, u32[]{:S(2)}) collective-permute-start(bf16[112,2048]{1,0:T(8,128)(2,1)S(1)} %get-tuple-element.26), channel_id=1, source_target_pairs={{0,1},{1,0},{2,3},{3,2},{4,5},{5,4},{6,7},{7,6},{8,9},{9,8},{10,11... | collective-permute-start | bytes 1376264 | tf_op jit(solution)/shard_map/ppermute | solution.py:294
  34.9 3.0 %collective-permute-start.13 = (bf16[112,2048]{1,0:T(8,128)(2,1)S(1)}, bf16[112,2048]{1,0:T(8,128)(2,1)S(1)}, u32[]{:S(2)}, u32[]{:S(2)}) collective-permute-start(bf16[112,2048]{1,0:T(8,128)(2,1)S(1)} %get-tuple-element.27), channel_id=1, source_target_pairs={{0,1},{1,0},{2,3},{3,2},{4,5},{5,4},{6,7},{7,6},{8,9},{9,8},{10,11... | collective-permute-start | bytes 1376264 | tf_op jit(solution)/shard_map/ppermute | solution.py:294
  35.4 2.5 %collective-permute-start.14 = (bf16[96,2048]{1,0:T(8,128)(2,1)S(1)}, bf16[96,2048]{1,0:T(8,128)(2,1)S(1)}, u32[]{:S(2)}, u32[]{:S(2)}) collective-permute-start(bf16[96,2048]{1,0:T(8,128)(2,1)S(1)} %get-tuple-element.28), channel_id=1, source_target_pairs={{0,1},{1,0},{2,3},{3,2},{4,5},{5,4},{6,7},{7,6},{8,9},{9,8},{10,11... | collective-permute-start | bytes 1179656 | tf_op jit(solution)/shard_map/ppermute | solution.py:294
  35.6 14.2 %collective-permute-start.19 = (bf16[32,32,128]{2,1,0:T(8,128)(2,1)S(1)}, bf16[32,32,128]{2,1,0:T(8,128)(2,1)S(1)}, u32[]{:S(2)}, u32[]{:S(2)}) collective-permute-start(bf16[32,32,128]{2,1,0:T(8,128)(2,1)S(1)} %copy-done.6), channel_id=1, source_target_pairs={{0,2},{2,0},{1,3},{3,1},{4,6},{6,4},{5,7},{7,5},{8,10},{10,8},{9,1... | collective-permute-start | bytes 786440 | tf_op jit(solution)/shard_map/ppermute | solution.py:295
  39.9 14.4 %collective-permute-start.15 = (bf16[272,128]{1,0:T(8,128)(2,1)S(1)}, bf16[272,128]{1,0:T(8,128)(2,1)S(1)}, u32[]{:S(2)}, u32[]{:S(2)}) collective-permute-start(bf16[272,128]{1,0:T(8,128)(2,1)S(1)} %get-tuple-element.30), channel_id=1, source_target_pairs={{0,4},{4,0},{8,12},{12,8},{1,5},{5,1},{9,13},{13,9},{2,6},{6,2},{1... | collective-permute-start | bytes 208904 | tf_op jit(solution)/shard_map/ppermute | solution.py:304
  43.6 10.6 %collective-permute-start.16 = (bf16[272,128]{1,0:T(8,128)(2,1)S(1)}, bf16[272,128]{1,0:T(8,128)(2,1)S(1)}, u32[]{:S(2)}, u32[]{:S(2)}) collective-permute-start(bf16[272,128]{1,0:T(8,128)(2,1)S(1)} %get-tuple-element.31), channel_id=1, source_target_pairs={{0,8},{4,12},{8,0},{12,4},{1,9},{5,13},{9,1},{13,5},{2,10},{6,14},... | collective-permute-start | bytes 208904 | tf_op jit(solution)/shard_map/ppermute | solution.py:304
  48.1 6.1 %collective-permute-start.18 = (bf16[256,128]{1,0:T(8,128)(2,1)S(1)}, bf16[256,128]{1,0:T(8,128)(2,1)S(1)}, u32[]{:S(2)}, u32[]{:S(2)}) collective-permute-start(bf16[256,128]{1,0:T(8,128)(2,1)S(1)} %shard_map.101), channel_id=1, source_target_pairs={{0,12},{4,8},{8,4},{12,0},{1,13},{5,9},{9,5},{13,1},{2,14},{6,10},... | collective-permute-start | bytes 196616 | tf_op jit(solution)/shard_map/ppermute | solution.py:304
  (6 other events, 5.3 us)

commit v9 on v8

--- a/solution.py
+++ b/solution.py
@@ -263,7 +263,7 @@
     near = lax.ppermute(tokens, E, [(i, i ^ 1) for i in range(4)])
     across = lax.ppermute(tokens, E, middle)
     gate, up, down = gate_weight[0].T, up_weight[0].T, down_weight[0].T
-    part_rows = min(2 * hidden_part // 3, n - 1) // 16 * 16
+    part_rows = hidden_part // 2 // 16 * 16
     left = hidden_part - part_rows
     (part,) = kernel(part_body, [gate, up], [((part_rows, model_width), bf16)])
     part_x = lax.ppermute(part, Q, swap)

time: 55.9 us -> 55.3 us (0.989)
  waiting for transfers between devices: 21.1 us -> 20 us
  starting transfers between devices: 20.5 us -> 21.3 us
    ppermute x2, waiting for transfers between devices: 3.81 us -> 6.32 us  [by_column(): lax.ppermute(a, Q, swap)]
    ppermute x1, waiting for transfers between devices: 2.31 us -> 0.38 us  [by_column(): end_three = lax.ppermute(far_inner, E, ends)]
    ppermute x1, waiting for transfers between devices: 2.03 us -> 0.58 us  [by_column(): part_x = lax.ppermute(part, Q, swap)]
    ppermute x3, starting transfers between devices: 5.38 us -> 6.27 us  [by_column(): lax.ppermute(a, E, [(i, i ^ k) for i in range(4)])]
  transfers between devices with their start and end apart: 20 -> 20, of which waited for: 7 -> 9; matrix products, arithmetic and copies ran while one was open for 0% -> 0% of each run, Pallas kernels for 15% -> 15%
where the time goes in v9:
time: 55.3 us; the launch traced here: 55 us
  starting transfers between devices  21.3 us (39%)
  waiting for transfers between devices  20 us (36%)
  Pallas kernels  9.45 us (17%)
  local copies, waits for them, and re-layouts  4.08 us (7%)
    pallas_call x7, Pallas kernels, kernel(): pl.pallas_call(body, out_shape=[jax.ShapeDtypeStruct(shape, dtype) for sh...  9.28 us
    ppermute x2, waiting for transfers between devices, by_column(): lax.ppermute(a, Q, swap)  6.32 us
    ppermute x3, starting transfers between devices, by_column(): lax.ppermute(a, E, [(i, i ^ k) for i in range(4)])  6.27 us
    ppermute x3, waiting for transfers between devices, by_column(): lax.ppermute(a, E, [(i, i ^ k) for i in range(4)])  4.12 us
    unnamed x20, local copies, waits for them, and re-layouts  4.08 us
    ppermute x1, waiting for transfers between devices, by_column(): end_two = lax.ppermute(across, E, ends)  3.88 us
    ppermute x1, waiting for transfers between devices, by_column(): near = lax.ppermute(tokens, E, [(i, i ^ 1) for i in range(4)])  3.79 us
    ppermute x1, starting transfers between devices, by_column(): near = lax.ppermute(tokens, E, [(i, i ^ 1) for i in range(4)])  3.02 us
  transfers between devices with their start and end apart: 20, of which 9 were waited for; matrix products, arithmetic and copies ran while one was open for 0% of the time, Pallas kernels for 15%

profile of v9, /device:TPU:0, one launch (start us, length us, event | category | flops | bytes accessed | tf_op | source)
XLA Modules:
  0.0 55.0 jit_solution(6796831958274134305)
XLA Ops:
  0.5 3.0 %collective-permute-start = (bf16[128,2048]{1,0:T(8,128)(2,1)}, bf16[128,2048]{1,0:T(8,128)(2,1)S(1)}, u32[]{:S(2)}, u32[]{:S(2)}) collective-permute-start(bf16[128,2048]{1,0:T(8,128)(2,1)} %tokens.5), channel_id=1, source_target_pairs={{0,4},{4,0},{8,12},{12,8},{1,5},{5,1},{9,13},{13,9},{2,6},{6,2},{1... | collective-permute-start | bytes 1572872 | tf_op jit(solution)/shard_map/ppermute | solution.py:263
  4.2 1.1 %copy-done.1 = bf16[1,2048,192]{1,2,0:T(8,128)(2,1)S(1)} copy-done((bf16[1,2048,192]{1,2,0:T(8,128)(2,1)S(1)}, bf16[1,2048,192]{1,2,0:T(8,128)(2,1)}, u32[]{:S(2)}) %copy-start.1) | copy-done | bytes 786456
  5.4 1.1 %copy-done.3 = bf16[1,2048,192]{1,2,0:T(8,128)(2,1)S(1)} copy-done((bf16[1,2048,192]{1,2,0:T(8,128)(2,1)S(1)}, bf16[1,2048,192]{1,2,0:T(8,128)(2,1)}, u32[]{:S(2)}) %copy-start.3) | copy-done | bytes 786456
  6.5 1.6 %collective-permute-start.7 = (bf16[96,2048]{1,0:T(8,128)(2,1)S(1)}, bf16[96,2048]{1,0:T(8,128)(2,1)S(1)}, u32[]{:S(2)}, u32[]{:S(2)}) collective-permute-start(bf16[96,2048]{1,0:T(8,128)(2,1)S(1)} %shard_map.95), channel_id=1, source_target_pairs={{0,2},{2,0},{1,3},{3,1},{4,6},{6,4},{5,7},{7,5},{8,10},{10,8},{9,1... | collective-permute-start | bytes 1179656 | tf_op jit(solution)/shard_map/ppermute | solution.py:269
  8.8 1.1 %copy-done.4 = bf16[1,2048,192]{1,2,0:T(8,128)(2,1)S(1)} copy-done((bf16[1,2048,192]{1,2,0:T(8,128)(2,1)S(1)}, bf16[1,2048,192]{1,2,0:T(8,128)(2,1)}, u32[]{:S(2)}) %copy-start.4) | copy-done | bytes 786456
  9.9 1.4 %shard_map.91 = (bf16[16,2048]{1,0:T(8,128)(2,1)S(1)}, bf16[96,2048]{1,0:T(8,128)(2,1)S(1)}, bf16[112,2048]{1,0:T(8,128)(2,1)S(1)}, bf16[192,2048]{1,0:T(8,128)(...) custom-call(s32[2]{0:T(128)S(1)} %copy-done.9, ...), custom_call_target="tpu_custom_call" | custom-call | tf_op jit(solution)/shard_map/pallas_call | solution.py:110
  11.4 0.7 %collective-permute-start.9 = (bf16[96,2048]{1,0:T(8,128)(2,1)S(1)}, bf16[96,2048]{1,0:T(8,128)(2,1)S(1)}, u32[]{:S(2)}, u32[]{:S(2)}) collective-permute-start(bf16[96,2048]{1,0:T(8,128)(2,1)S(1)} %shard_map.97), channel_id=1, source_target_pairs={{0,2},{2,0},{1,3},{3,1},{4,6},{6,4},{5,7},{7,5},{8,10},{10,8},{9,1... | collective-permute-start | bytes 1179656 | tf_op jit(solution)/shard_map/ppermute | solution.py:285
  12.1 3.8 %collective-permute-done.near.refs_1_ = bf16[128,2048]{1,0:T(8,128)(2,1)S(1)} collective-permute-done((bf16[128,2048]{1,0:T(8,128)(2,1)}, bf16[128,2048]{1,0:T(8,128)(2,1)S(1)}, u32[]{:S(2)}, u32[]{:S(2)}) %collective-permute-start) | collective-permute-done | bytes 524320 | tf_op jit(solution)/shard_map/ppermute | solution.py:263
  16.6 1.3 %collective-permute-start.2 = (bf16[128,2048]{1,0:T(8,128)(2,1)S(1)}, bf16[128,2048]{1,0:T(8,128)(2,1)S(1)}, u32[]{:S(2)}, u32[]{:S(2)}) collective-permute-start(bf16[128,2048]{1,0:T(8,128)(2,1)S(1)} %collective-permute-done.1.refs_2_.across), channel_id=1, source_target_pairs={{4,0},{8,12},{5,1},{9,13},{6,2},{10,14},{7,3},{11,15},{20,16},{24,... | collective-permute-start | bytes 1572872 | tf_op jit(solution)/shard_map/ppermute | solution.py:284
  18.6 1.5 %collective-permute-start.10 = (bf16[112,2048]{1,0:T(8,128)(2,1)S(1)}, bf16[112,2048]{1,0:T(8,128)(2,1)S(1)}, u32[]{:S(2)}, u32[]{:S(2)}) collective-permute-start(bf16[112,2048]{1,0:T(8,128)(2,1)S(1)} %shard_map.98), channel_id=1, source_target_pairs={{0,2},{2,0},{1,3},{3,1},{4,6},{6,4},{5,7},{7,5},{8,10},{10,8},{9,1... | collective-permute-start | bytes 1376264 | tf_op jit(solution)/shard_map/ppermute | solution.py:285
  20.2 1.6 %collective-permute-start.8 = (bf16[96,2048]{1,0:T(8,128)(2,1)S(1)}, bf16[96,2048]{1,0:T(8,128)(2,1)S(1)}, u32[]{:S(2)}, u32[]{:S(2)}) collective-permute-start(bf16[96,2048]{1,0:T(8,128)(2,1)S(1)} %shard_map.96.refs_0_.refs_6_), channel_id=1, source_target_pairs={{0,16},{16,0},{1,17},{17,1},{2,18},{18,2},{3,19},{19,3},{4,20},{20... | collective-permute-start | bytes 1179656 | tf_op jit(solution)/shard_map/ppermute | solution.py:287
  21.7 5.3 %collective-permute-done.9.refs_2_.refs_8_ = bf16[96,2048]{1,0:T(8,128)(2,1)S(1)} collective-permute-done((bf16[96,2048]{1,0:T(8,128)(2,1)S(1)}, bf16[96,2048]{1,0:T(8,128)(2,1)S(1)}, u32[]{:S(2)}, u32[]{:S(2)}) %collective-permute-start.9) | collective-permute-done | bytes 393248 | tf_op jit(solution)/shard_map/ppermute | solution.py:285
  27.1 1.3 %collective-permute-start.17 = (bf16[128,2048]{1,0:T(8,128)(2,1)S(1)}, bf16[128,2048]{1,0:T(8,128)(2,1)S(1)}, u32[]{:S(2)}, u32[]{:S(2)}) collective-permute-start(bf16[128,2048]{1,0:T(8,128)(2,1)S(1)} %collective-permute-done.3.far_inner.refs_3_), channel_id=1, source_target_pairs={{4,0},{8,12},{5,1},{9,13},{6,2},{10,14},{7,3},{11,15},{20,16},{24,... | collective-permute-start | bytes 1572872 | tf_op jit(solution)/shard_map/ppermute | solution.py:290
  28.3 1.2 %shard_map.93.refs_4_.got_own = f32[128,256]{1,0:T(8,128)S(1)} custom-call(bf16[128,2048]{1,0:T(8,128)(2,1)S(1)} %copy-done, bf16[128,2048]{1,0:T(8,128)(2,1)S(1)} %collective-permute-done.near.refs_1_, bf16[192,2048]{1,0:T(8,128)(2,1)S(1)} %get-tuple-element.21.refs_0_, bf16[192,2048]{1,0:T(8,128)(2,1)S(1)} %get-tuple-element.22.refs_1_, ...), custom_call_target="tpu_custom_call" | custom-call | tf_op jit(solution)/shard_map/pallas_call | solution.py:110
  29.6 3.9 %collective-permute-done.2.end_two = bf16[128,2048]{1,0:T(8,128)(2,1)S(1)} collective-permute-done((bf16[128,2048]{1,0:T(8,128)(2,1)S(1)}, bf16[128,2048]{1,0:T(8,128)(2,1)S(1)}, u32[]{:S(2)}, u32[]{:S(2)}) %collective-permute-start.2) | collective-permute-done | bytes 524320 | tf_op jit(solution)/shard_map/ppermute | solution.py:284
  33.4 1.2 %shard_map.94.refs_5_.got_two = f32[128,128]{1,0:T(8,128)S(1)} custom-call(bf16[128,2048]{1,0:T(8,128)(2,1)S(1)} %collective-permute-done.2.end_two, bf16[128,2048]{1,0:T(8,128)(2,1)S(1)} %collective-permute-done.3.far_inner.refs_3_, bf16[192,2048]{1,0:T(8,128)(2,1)S(1)} %get-tuple-element.21.refs_0_, bf16[192,2048]{1,0:T(8,128)(2,1)S(1)} %get-tuple-element.22.refs_1_, ...), custom_call_target="tpu_custom_call" | custom-call | tf_op jit(solution)/shard_map/pallas_call | solution.py:110
  34.7 1.0 %collective-permute-done.10.refs_2_.refs_3_.refs_9_ = bf16[112,2048]{1,0:T(8,128)(2,1)S(1)} collective-permute-done((bf16[112,2048]{1,0:T(8,128)(2,1)S(1)}, bf16[112,2048]{1,0:T(8,128)(2,1)S(1)}, u32[]{:S(2)}, u32[]{:S(2)}) %collective-permute-start.10) | collective-permute-done | bytes 458784 | tf_op jit(solution)/shard_map/ppermute | solution.py:285
  36.4 1.5 %collective-permute-start.19 = (bf16[32,32,128]{2,1,0:T(8,128)(2,1)S(1)}, bf16[32,32,128]{2,1,0:T(8,128)(2,1)S(1)}, u32[]{:S(2)}, u32[]{:S(2)}) collective-permute-start(bf16[32,32,128]{2,1,0:T(8,128)(2,1)S(1)} %copy-done.6), channel_id=1, source_target_pairs={{0,2},{2,0},{1,3},{3,1},{4,6},{6,4},{5,7},{7,5},{8,10},{10,8},{9,1... | collective-permute-start | bytes 786440 | tf_op jit(solution)/shard_map/ppermute | solution.py:295
  38.8 2.0 %shard_map.100 = (f32[256,128]{1,0:T(8,128)S(1)}, bf16[272,128]{1,0:T(8,128)(2,1)S(1)}, bf16[272,128]{1,0:T(8,128)(2,1)S(1)}) custom-call(bf16[128,2048]{1,0:T(8,128)(2,1)S(1)} %copy-done, bf16[128,2048]{1,0:T(8,128)(2,1)S(1)} %collective-permute-done.near.refs_1_, bf16[128,2048]{1,0:T(8,128)(2,1)S(1)} %collective-permute-done.2.end_two, ...), custom_call_target="tpu_custom_call" | custom-call | tf_op jit(solution)/shard_map/pallas_call | solution.py:110
  40.8 4.2 %collective-permute-start.15 = (bf16[272,128]{1,0:T(8,128)(2,1)S(1)}, bf16[272,128]{1,0:T(8,128)(2,1)S(1)}, u32[]{:S(2)}, u32[]{:S(2)}) collective-permute-start(bf16[272,128]{1,0:T(8,128)(2,1)S(1)} %get-tuple-element.30), channel_id=1, source_target_pairs={{0,4},{4,0},{8,12},{12,8},{1,5},{5,1},{9,13},{13,9},{2,6},{6,2},{1... | collective-permute-start | bytes 208904 | tf_op jit(solution)/shard_map/ppermute | solution.py:304
  45.3 2.2 %shard_map.101 = bf16[256,128]{1,0:T(8,128)(2,1)S(1)} custom-call(bf16[128,2048]{1,0:T(8,128)(2,1)S(1)} %collective-permute-done.17.end_three, bf16[128,2048]{1,0:T(8,128)(2,1)S(1)} %collective-permute-done.1.refs_2_.across, f32[256,128]{1,0:T(8,128)S(1)} %get-tuple-element.29.earlier.here, bf16[192,2048]{1,0:T(8,128)(2,1)S(1)} %get-tuple-element.21.refs_0_, ...), custom_call_target="tpu_custom_call" | custom-call | tf_op jit(solution)/shard_map/pallas_call | solution.py:110
  47.5 2.1 %collective-permute-start.18 = (bf16[256,128]{1,0:T(8,128)(2,1)S(1)}, bf16[256,128]{1,0:T(8,128)(2,1)S(1)}, u32[]{:S(2)}, u32[]{:S(2)}) collective-permute-start(bf16[256,128]{1,0:T(8,128)(2,1)S(1)} %shard_map.101), channel_id=1, source_target_pairs={{0,12},{4,8},{8,4},{12,0},{1,13},{5,9},{9,5},{13,1},{2,14},{6,10},... | collective-permute-start | bytes 196616 | tf_op jit(solution)/shard_map/ppermute | solution.py:304
  49.6 4.1 %collective-permute-done.18.three = bf16[256,128]{1,0:T(8,128)(2,1)S(1)} collective-permute-done((bf16[256,128]{1,0:T(8,128)(2,1)S(1)}, bf16[256,128]{1,0:T(8,128)(2,1)S(1)}, u32[]{:S(2)}, u32[]{:S(2)}) %collective-permute-start.18) | collective-permute-done | bytes 65568 | tf_op jit(solution)/shard_map/ppermute | solution.py:304
  53.7 1.3 %shard_map.102 = f32[2,64]{1,0:T(2,128)} custom-call(f32[128,128]{1,0:T(8,128)S(1)} %get-tuple-element.20.base, f32[256,128]{1,0:T(8,128)S(1)} %get-tuple-element.29.earlier.here, bf16[272,128]{1,0:T(8,128)(2,1)S(1)} %collective-permute-done.15.near, bf16[272,128]{1,0:T(8,128)(2,1)S(1)} %collective-permute-done.16.two, ...), custom_call_target="tpu_custom_call" | custom-call | tf_op jit(solution)/shard_map/pallas_call | solution.py:110
  (48 shorter events, 5.4 us)
Async XLA Ops:
  0.0 11.4 %collective-permute-start.4 = (bf16[192,2048]{1,0:T(8,128)(2,1)}, bf16[192,2048]{1,0:T(8,128)(2,1)S(1)}, u32[]{:S(2)}, u32[]{:S(2)}) collective-permute-start(bf16[192,2048]{1,0:T(8,128)(2,1)} %bitcast.13), channel_id=1, source_target_pairs={{0,1},{1,0},{2,3},{3,2},{4,5},{5,4},{6,7},{7,6},{8,9},{9,8},{10,11... | collective-permute-start | bytes 2359304 | tf_op jit(solution)/shard_map/ppermute | solution.py:278
  0.5 7.7 %copy-start = (bf16[128,2048]{1,0:T(8,128)(2,1)S(1)}, bf16[128,2048]{1,0:T(8,128)(2,1)}, u32[]{:S(2)}) copy-start(bf16[128,2048]{1,0:T(8,128)(2,1)} %tokens.5) | copy-start | bytes 1572868
  0.5 10.9 %collective-permute-start.5 = (bf16[192,2048]{1,0:T(8,128)(2,1)}, bf16[192,2048]{1,0:T(8,128)(2,1)S(1)}, u32[]{:S(2)}, u32[]{:S(2)}) collective-permute-start(bf16[192,2048]{1,0:T(8,128)(2,1)} %bitcast.16), channel_id=1, source_target_pairs={{0,1},{1,0},{2,3},{3,2},{4,5},{5,4},{6,7},{7,6},{8,9},{9,8},{10,11... | collective-permute-start | bytes 2359304 | tf_op jit(solution)/shard_map/ppermute | solution.py:278
  0.5 15.4 %collective-permute-start = (bf16[128,2048]{1,0:T(8,128)(2,1)}, bf16[128,2048]{1,0:T(8,128)(2,1)S(1)}, u32[]{:S(2)}, u32[]{:S(2)}) collective-permute-start(bf16[128,2048]{1,0:T(8,128)(2,1)} %tokens.5), channel_id=1, source_target_pairs={{0,4},{4,0},{8,12},{12,8},{1,5},{5,1},{9,13},{13,9},{2,6},{6,2},{1... | collective-permute-start | bytes 1572872 | tf_op jit(solution)/shard_map/ppermute | solution.py:263
  3.5 13.1 %collective-permute-start.1 = (bf16[128,2048]{1,0:T(8,128)(2,1)}, bf16[128,2048]{1,0:T(8,128)(2,1)S(1)}, u32[]{:S(2)}, u32[]{:S(2)}) collective-permute-start(bf16[128,2048]{1,0:T(8,128)(2,1)} %tokens.5), channel_id=1, source_target_pairs={{4,8},{8,4},{5,9},{9,5},{6,10},{10,6},{7,11},{11,7},{20,24},{24,20... | collective-permute-start | bytes 1572872 | tf_op jit(solution)/shard_map/ppermute | solution.py:264
  6.5 1.6 %copy-start.2 = (bf16[1,2048,192]{1,2,0:T(8,128)(2,1)S(1)}, bf16[1,2048,192]{1,2,0:T(8,128)(2,1)}, u32[]{:S(2)}) copy-start(bf16[1,2048,192]{1,2,0:T(8,128)(2,1)} %param.13) | copy-start | bytes 2359300
  6.5 1.6 %copy-start.5 = (bf16[2048,128]{1,0:T(8,128)(2,1)S(1)}, bf16[2048,128]{1,0:T(8,128)(2,1)}, u32[]{:S(2)}) copy-start(bf16[2048,128]{1,0:T(8,128)(2,1)} %proj.1) | copy-start | bytes 1572868
  6.5 12.1 %collective-permute-start.7 = (bf16[96,2048]{1,0:T(8,128)(2,1)S(1)}, bf16[96,2048]{1,0:T(8,128)(2,1)S(1)}, u32[]{:S(2)}, u32[]{:S(2)}) collective-permute-start(bf16[96,2048]{1,0:T(8,128)(2,1)S(1)} %shard_map.95), channel_id=1, source_target_pairs={{0,2},{2,0},{1,3},{3,1},{4,6},{6,4},{5,7},{7,5},{8,10},{10,8},{9,1... | collective-permute-start | bytes 1179656 | tf_op jit(solution)/shard_map/ppermute | solution.py:269
  11.4 15.6 %collective-permute-start.9 = (bf16[96,2048]{1,0:T(8,128)(2,1)S(1)}, bf16[96,2048]{1,0:T(8,128)(2,1)S(1)}, u32[]{:S(2)}, u32[]{:S(2)}) collective-permute-start(bf16[96,2048]{1,0:T(8,128)(2,1)S(1)} %shard_map.97), channel_id=1, source_target_pairs={{0,2},{2,0},{1,3},{3,1},{4,6},{6,4},{5,7},{7,5},{8,10},{10,8},{9,1... | collective-permute-start | bytes 1179656 | tf_op jit(solution)/shard_map/ppermute | solution.py:285
  15.9 11.2 %collective-permute-start.3 = (bf16[128,2048]{1,0:T(8,128)(2,1)S(1)}, bf16[128,2048]{1,0:T(8,128)(2,1)S(1)}, u32[]{:S(2)}, u32[]{:S(2)}) collective-permute-start(bf16[128,2048]{1,0:T(8,128)(2,1)S(1)} %collective-permute-done.near.refs_1_), channel_id=1, source_target_pairs={{4,8},{8,4},{5,9},{9,5},{6,10},{10,6},{7,11},{11,7},{20,24},{24,20... | collective-permute-start | bytes 1572872 | tf_op jit(solution)/shard_map/ppermute | solution.py:283
  16.6 16.8 %collective-permute-start.2 = (bf16[128,2048]{1,0:T(8,128)(2,1)S(1)}, bf16[128,2048]{1,0:T(8,128)(2,1)S(1)}, u32[]{:S(2)}, u32[]{:S(2)}) collective-permute-start(bf16[128,2048]{1,0:T(8,128)(2,1)S(1)} %collective-permute-done.1.refs_2_.across), channel_id=1, source_target_pairs={{4,0},{8,12},{5,1},{9,13},{6,2},{10,14},{7,3},{11,15},{20,16},{24,... | collective-permute-start | bytes 1572872 | tf_op jit(solution)/shard_map/ppermute | solution.py:284
  18.0 2.2 %collective-permute-start.6 = (bf16[16,2048]{1,0:T(8,128)(2,1)S(1)}, bf16[16,2048]{1,0:T(8,128)(2,1)S(1)}, u32[]{:S(2)}, u32[]{:S(2)}) collective-permute-start(bf16[16,2048]{1,0:T(8,128)(2,1)S(1)} %shard_map.92), channel_id=1, source_target_pairs={{0,1},{1,0},{2,3},{3,2},{4,5},{5,4},{6,7},{7,6},{8,9},{9,8},{10,11... | collective-permute-start | bytes 196616 | tf_op jit(solution)/shard_map/ppermute | solution.py:279
  18.6 17.1 %collective-permute-start.10 = (bf16[112,2048]{1,0:T(8,128)(2,1)S(1)}, bf16[112,2048]{1,0:T(8,128)(2,1)S(1)}, u32[]{:S(2)}, u32[]{:S(2)}) collective-permute-start(bf16[112,2048]{1,0:T(8,128)(2,1)S(1)} %shard_map.98), channel_id=1, source_target_pairs={{0,2},{2,0},{1,3},{3,1},{4,6},{6,4},{5,7},{7,5},{8,10},{10,8},{9,1... | collective-permute-start | bytes 1376264 | tf_op jit(solution)/shard_map/ppermute | solution.py:285
  20.2 14.5 %collective-permute-start.8 = (bf16[96,2048]{1,0:T(8,128)(2,1)S(1)}, bf16[96,2048]{1,0:T(8,128)(2,1)S(1)}, u32[]{:S(2)}, u32[]{:S(2)}) collective-permute-start(bf16[96,2048]{1,0:T(8,128)(2,1)S(1)} %shard_map.96.refs_0_.refs_6_), channel_id=1, source_target_pairs={{0,16},{16,0},{1,17},{17,1},{2,18},{18,2},{3,19},{19,3},{4,20},{20... | collective-permute-start | bytes 1179656 | tf_op jit(solution)/shard_map/ppermute | solution.py:287
  27.1 8.6 %collective-permute-start.11 = (bf16[96,2048]{1,0:T(8,128)(2,1)S(1)}, bf16[96,2048]{1,0:T(8,128)(2,1)S(1)}, u32[]{:S(2)}, u32[]{:S(2)}) collective-permute-start(bf16[96,2048]{1,0:T(8,128)(2,1)S(1)} %collective-permute-done.9.refs_2_.refs_8_), channel_id=1, source_target_pairs={{0,1},{1,0},{2,3},{3,2},{4,5},{5,4},{6,7},{7,6},{8,9},{9,8},{10,11... | collective-permute-start | bytes 1179656 | tf_op jit(solution)/shard_map/ppermute | solution.py:292
  27.1 18.3 %collective-permute-start.17 = (bf16[128,2048]{1,0:T(8,128)(2,1)S(1)}, bf16[128,2048]{1,0:T(8,128)(2,1)S(1)}, u32[]{:S(2)}, u32[]{:S(2)}) collective-permute-start(bf16[128,2048]{1,0:T(8,128)(2,1)S(1)} %collective-permute-done.3.far_inner.refs_3_), channel_id=1, source_target_pairs={{4,0},{8,12},{5,1},{9,13},{6,2},{10,14},{7,3},{11,15},{20,16},{24,... | collective-permute-start | bytes 1572872 | tf_op jit(solution)/shard_map/ppermute | solution.py:290
  34.6 1.8 %copy-start.6 = (bf16[32,32,128]{2,1,0:T(8,128)(2,1)S(1)}, bf16[32,32,128]{2,1,0:T(8,128)(2,1)}, u32[]{:S(2)}) copy-start(bf16[32,32,128]{2,1,0:T(8,128)(2,1)} %param.17) | copy-start | bytes 786436
  35.8 3.0 %collective-permute-start.14 = (bf16[112,2048]{1,0:T(8,128)(2,1)S(1)}, bf16[112,2048]{1,0:T(8,128)(2,1)S(1)}, u32[]{:S(2)}, u32[]{:S(2)}) collective-permute-start(bf16[112,2048]{1,0:T(8,128)(2,1)S(1)} %get-tuple-element.28), channel_id=1, source_target_pairs={{0,1},{1,0},{2,3},{3,2},{4,5},{5,4},{6,7},{7,6},{8,9},{9,8},{10,11... | collective-permute-start | bytes 1376264 | tf_op jit(solution)/shard_map/ppermute | solution.py:294
  35.8 2.4 %collective-permute-start.12 = (bf16[96,2048]{1,0:T(8,128)(2,1)S(1)}, bf16[96,2048]{1,0:T(8,128)(2,1)S(1)}, u32[]{:S(2)}, u32[]{:S(2)}) collective-permute-start(bf16[96,2048]{1,0:T(8,128)(2,1)S(1)} %get-tuple-element.26), channel_id=1, source_target_pairs={{0,1},{1,0},{2,3},{3,2},{4,5},{5,4},{6,7},{7,6},{8,9},{9,8},{10,11... | collective-permute-start | bytes 1179656 | tf_op jit(solution)/shard_map/ppermute | solution.py:294
  36.3 2.4 %collective-permute-start.13 = (bf16[96,2048]{1,0:T(8,128)(2,1)S(1)}, bf16[96,2048]{1,0:T(8,128)(2,1)S(1)}, u32[]{:S(2)}, u32[]{:S(2)}) collective-permute-start(bf16[96,2048]{1,0:T(8,128)(2,1)S(1)} %get-tuple-element.27), channel_id=1, source_target_pairs={{0,1},{1,0},{2,3},{3,2},{4,5},{5,4},{6,7},{7,6},{8,9},{9,8},{10,11... | collective-permute-start | bytes 1179656 | tf_op jit(solution)/shard_map/ppermute | solution.py:294
  36.4 13.2 %collective-permute-start.19 = (bf16[32,32,128]{2,1,0:T(8,128)(2,1)S(1)}, bf16[32,32,128]{2,1,0:T(8,128)(2,1)S(1)}, u32[]{:S(2)}, u32[]{:S(2)}) collective-permute-start(bf16[32,32,128]{2,1,0:T(8,128)(2,1)S(1)} %copy-done.6), channel_id=1, source_target_pairs={{0,2},{2,0},{1,3},{3,1},{4,6},{6,4},{5,7},{7,5},{8,10},{10,8},{9,1... | collective-permute-start | bytes 786440 | tf_op jit(solution)/shard_map/ppermute | solution.py:295
  40.8 12.9 %collective-permute-start.15 = (bf16[272,128]{1,0:T(8,128)(2,1)S(1)}, bf16[272,128]{1,0:T(8,128)(2,1)S(1)}, u32[]{:S(2)}, u32[]{:S(2)}) collective-permute-start(bf16[272,128]{1,0:T(8,128)(2,1)S(1)} %get-tuple-element.30), channel_id=1, source_target_pairs={{0,4},{4,0},{8,12},{12,8},{1,5},{5,1},{9,13},{13,9},{2,6},{6,2},{1... | collective-permute-start | bytes 208904 | tf_op jit(solution)/shard_map/ppermute | solution.py:304
  44.9 8.8 %collective-permute-start.16 = (bf16[272,128]{1,0:T(8,128)(2,1)S(1)}, bf16[272,128]{1,0:T(8,128)(2,1)S(1)}, u32[]{:S(2)}, u32[]{:S(2)}) collective-permute-start(bf16[272,128]{1,0:T(8,128)(2,1)S(1)} %get-tuple-element.31), channel_id=1, source_target_pairs={{0,8},{4,12},{8,0},{12,4},{1,9},{5,13},{9,1},{13,5},{2,10},{6,14},... | collective-permute-start | bytes 208904 | tf_op jit(solution)/shard_map/ppermute | solution.py:304
  47.5 6.2 %collective-permute-start.18 = (bf16[256,128]{1,0:T(8,128)(2,1)S(1)}, bf16[256,128]{1,0:T(8,128)(2,1)S(1)}, u32[]{:S(2)}, u32[]{:S(2)}) collective-permute-start(bf16[256,128]{1,0:T(8,128)(2,1)S(1)} %shard_map.101), channel_id=1, source_target_pairs={{0,12},{4,8},{8,4},{12,0},{1,13},{5,9},{9,5},{13,1},{2,14},{6,10},... | collective-permute-start | bytes 196616 | tf_op jit(solution)/shard_map/ppermute | solution.py:304
  (6 other events, 5.5 us)

commit v10 on v9

--- a/solution.py
+++ b/solution.py
@@ -242,10 +242,11 @@
     left = jnp.concatenate([jnp.concatenate(found, axis=1) for found in best], axis=0)
     thirds = []
     for _ in range(3):
-        thirds.append(left.astype(jnp.bfloat16))
-        left = left - thirds[-1].astype(jnp.float32)
-    sums = [dot(third, chosen[...]) for third in thirds]
-    scores[...] = sums[0] + (sums[1] + sums[2])
+        thirds.append(left.astype(jnp.bfloat16).astype(jnp.float32))
+        left = left - thirds[-1]
+    sums = dot(jnp.concatenate(thirds, axis=0).astype(jnp.bfloat16), chosen[...])
+    count = scores.shape[0]
+    scores[...] = sums[:count] + (sums[count : 2 * count] + sums[2 * count :])
 
 
 def by_column(

time: 55.3 us -> 55.2 us (level)
  no operation moved by 1% of the time
where the time goes in v10:
time: 55.2 us; the launch traced here: 54.9 us
  starting transfers between devices  21.3 us (39%)
  waiting for transfers between devices  20 us (36%)
  Pallas kernels  9.32 us (17%)
  local copies, waits for them, and re-layouts  4.08 us (7%)
    pallas_call x7, Pallas kernels, kernel(): pl.pallas_call(body, out_shape=[jax.ShapeDtypeStruct(shape, dtype) for sh...  9.15 us
    ppermute x2, waiting for transfers between devices, by_column(): lax.ppermute(a, Q, swap)  6.32 us
    ppermute x3, starting transfers between devices, by_column(): lax.ppermute(a, E, [(i, i ^ k) for i in range(4)])  6.27 us
    ppermute x3, waiting for transfers between devices, by_column(): lax.ppermute(a, E, [(i, i ^ k) for i in range(4)])  4.12 us
    unnamed x20, local copies, waits for them, and re-layouts  4.08 us
    ppermute x1, waiting for transfers between devices, by_column(): end_two = lax.ppermute(across, E, ends)  3.88 us
    ppermute x1, waiting for transfers between devices, by_column(): near = lax.ppermute(tokens, E, [(i, i ^ 1) for i in range(4)])  3.79 us
    ppermute x1, starting transfers between devices, by_column(): near = lax.ppermute(tokens, E, [(i, i ^ 1) for i in range(4)])  3.02 us
  transfers between devices with their start and end apart: 20, of which 9 were waited for; matrix products, arithmetic and copies ran while one was open for 0% of the time, Pallas kernels for 15%

profile of v10, /device:TPU:0, one launch (start us, length us, event | category | flops | bytes accessed | tf_op | source)
XLA Modules:
  0.0 54.9 jit_solution(18346333642735930925)
XLA Ops:
  0.5 3.0 %collective-permute-start = (bf16[128,2048]{1,0:T(8,128)(2,1)}, bf16[128,2048]{1,0:T(8,128)(2,1)S(1)}, u32[]{:S(2)}, u32[]{:S(2)}) collective-permute-start(bf16[128,2048]{1,0:T(8,128)(2,1)} %tokens.5), channel_id=1, source_target_pairs={{0,4},{4,0},{8,12},{12,8},{1,5},{5,1},{9,13},{13,9},{2,6},{6,2},{1... | collective-permute-start | bytes 1572872 | tf_op jit(solution)/shard_map/ppermute | solution.py:264
  4.2 1.1 %copy-done.1 = bf16[1,2048,192]{1,2,0:T(8,128)(2,1)S(1)} copy-done((bf16[1,2048,192]{1,2,0:T(8,128)(2,1)S(1)}, bf16[1,2048,192]{1,2,0:T(8,128)(2,1)}, u32[]{:S(2)}) %copy-start.1) | copy-done | bytes 786456
  5.4 1.1 %copy-done.3 = bf16[1,2048,192]{1,2,0:T(8,128)(2,1)S(1)} copy-done((bf16[1,2048,192]{1,2,0:T(8,128)(2,1)S(1)}, bf16[1,2048,192]{1,2,0:T(8,128)(2,1)}, u32[]{:S(2)}) %copy-start.3) | copy-done | bytes 786456
  6.5 1.6 %collective-permute-start.7 = (bf16[96,2048]{1,0:T(8,128)(2,1)S(1)}, bf16[96,2048]{1,0:T(8,128)(2,1)S(1)}, u32[]{:S(2)}, u32[]{:S(2)}) collective-permute-start(bf16[96,2048]{1,0:T(8,128)(2,1)S(1)} %shard_map.95), channel_id=1, source_target_pairs={{0,2},{2,0},{1,3},{3,1},{4,6},{6,4},{5,7},{7,5},{8,10},{10,8},{9,1... | collective-permute-start | bytes 1179656 | tf_op jit(solution)/shard_map/ppermute | solution.py:270
  8.8 1.1 %copy-done.4 = bf16[1,2048,192]{1,2,0:T(8,128)(2,1)S(1)} copy-done((bf16[1,2048,192]{1,2,0:T(8,128)(2,1)S(1)}, bf16[1,2048,192]{1,2,0:T(8,128)(2,1)}, u32[]{:S(2)}) %copy-start.4) | copy-done | bytes 786456
  9.9 1.4 %shard_map.91 = (bf16[16,2048]{1,0:T(8,128)(2,1)S(1)}, bf16[96,2048]{1,0:T(8,128)(2,1)S(1)}, bf16[112,2048]{1,0:T(8,128)(2,1)S(1)}, bf16[192,2048]{1,0:T(8,128)(...) custom-call(s32[2]{0:T(128)S(1)} %copy-done.9, ...), custom_call_target="tpu_custom_call" | custom-call | tf_op jit(solution)/shard_map/pallas_call | solution.py:110
  11.4 0.7 %collective-permute-start.9 = (bf16[96,2048]{1,0:T(8,128)(2,1)S(1)}, bf16[96,2048]{1,0:T(8,128)(2,1)S(1)}, u32[]{:S(2)}, u32[]{:S(2)}) collective-permute-start(bf16[96,2048]{1,0:T(8,128)(2,1)S(1)} %shard_map.97), channel_id=1, source_target_pairs={{0,2},{2,0},{1,3},{3,1},{4,6},{6,4},{5,7},{7,5},{8,10},{10,8},{9,1... | collective-permute-start | bytes 1179656 | tf_op jit(solution)/shard_map/ppermute | solution.py:286
  12.1 3.8 %collective-permute-done.near.refs_1_ = bf16[128,2048]{1,0:T(8,128)(2,1)S(1)} collective-permute-done((bf16[128,2048]{1,0:T(8,128)(2,1)}, bf16[128,2048]{1,0:T(8,128)(2,1)S(1)}, u32[]{:S(2)}, u32[]{:S(2)}) %collective-permute-start) | collective-permute-done | bytes 524320 | tf_op jit(solution)/shard_map/ppermute | solution.py:264
  16.6 1.3 %collective-permute-start.2 = (bf16[128,2048]{1,0:T(8,128)(2,1)S(1)}, bf16[128,2048]{1,0:T(8,128)(2,1)S(1)}, u32[]{:S(2)}, u32[]{:S(2)}) collective-permute-start(bf16[128,2048]{1,0:T(8,128)(2,1)S(1)} %collective-permute-done.1.refs_2_.across), channel_id=1, source_target_pairs={{4,0},{8,12},{5,1},{9,13},{6,2},{10,14},{7,3},{11,15},{20,16},{24,... | collective-permute-start | bytes 1572872 | tf_op jit(solution)/shard_map/ppermute | solution.py:285
  18.6 1.5 %collective-permute-start.10 = (bf16[112,2048]{1,0:T(8,128)(2,1)S(1)}, bf16[112,2048]{1,0:T(8,128)(2,1)S(1)}, u32[]{:S(2)}, u32[]{:S(2)}) collective-permute-start(bf16[112,2048]{1,0:T(8,128)(2,1)S(1)} %shard_map.98), channel_id=1, source_target_pairs={{0,2},{2,0},{1,3},{3,1},{4,6},{6,4},{5,7},{7,5},{8,10},{10,8},{9,1... | collective-permute-start | bytes 1376264 | tf_op jit(solution)/shard_map/ppermute | solution.py:286
  20.2 1.6 %collective-permute-start.8 = (bf16[96,2048]{1,0:T(8,128)(2,1)S(1)}, bf16[96,2048]{1,0:T(8,128)(2,1)S(1)}, u32[]{:S(2)}, u32[]{:S(2)}) collective-permute-start(bf16[96,2048]{1,0:T(8,128)(2,1)S(1)} %shard_map.96.refs_0_.refs_6_), channel_id=1, source_target_pairs={{0,16},{16,0},{1,17},{17,1},{2,18},{18,2},{3,19},{19,3},{4,20},{20... | collective-permute-start | bytes 1179656 | tf_op jit(solution)/shard_map/ppermute | solution.py:288
  21.7 5.3 %collective-permute-done.9.refs_2_.refs_8_ = bf16[96,2048]{1,0:T(8,128)(2,1)S(1)} collective-permute-done((bf16[96,2048]{1,0:T(8,128)(2,1)S(1)}, bf16[96,2048]{1,0:T(8,128)(2,1)S(1)}, u32[]{:S(2)}, u32[]{:S(2)}) %collective-permute-start.9) | collective-permute-done | bytes 393248 | tf_op jit(solution)/shard_map/ppermute | solution.py:286
  27.1 1.3 %collective-permute-start.17 = (bf16[128,2048]{1,0:T(8,128)(2,1)S(1)}, bf16[128,2048]{1,0:T(8,128)(2,1)S(1)}, u32[]{:S(2)}, u32[]{:S(2)}) collective-permute-start(bf16[128,2048]{1,0:T(8,128)(2,1)S(1)} %collective-permute-done.3.far_inner.refs_3_), channel_id=1, source_target_pairs={{4,0},{8,12},{5,1},{9,13},{6,2},{10,14},{7,3},{11,15},{20,16},{24,... | collective-permute-start | bytes 1572872 | tf_op jit(solution)/shard_map/ppermute | solution.py:291
  28.3 1.2 %shard_map.93.refs_4_.got_own = f32[128,256]{1,0:T(8,128)S(1)} custom-call(bf16[128,2048]{1,0:T(8,128)(2,1)S(1)} %copy-done, bf16[128,2048]{1,0:T(8,128)(2,1)S(1)} %collective-permute-done.near.refs_1_, bf16[192,2048]{1,0:T(8,128)(2,1)S(1)} %get-tuple-element.21.refs_0_, bf16[192,2048]{1,0:T(8,128)(2,1)S(1)} %get-tuple-element.22.refs_1_, ...), custom_call_target="tpu_custom_call" | custom-call | tf_op jit(solution)/shard_map/pallas_call | solution.py:110
  29.6 3.9 %collective-permute-done.2.end_two = bf16[128,2048]{1,0:T(8,128)(2,1)S(1)} collective-permute-done((bf16[128,2048]{1,0:T(8,128)(2,1)S(1)}, bf16[128,2048]{1,0:T(8,128)(2,1)S(1)}, u32[]{:S(2)}, u32[]{:S(2)}) %collective-permute-start.2) | collective-permute-done | bytes 524320 | tf_op jit(solution)/shard_map/ppermute | solution.py:285
  33.4 1.2 %shard_map.94.refs_5_.got_two = f32[128,128]{1,0:T(8,128)S(1)} custom-call(bf16[128,2048]{1,0:T(8,128)(2,1)S(1)} %collective-permute-done.2.end_two, bf16[128,2048]{1,0:T(8,128)(2,1)S(1)} %collective-permute-done.3.far_inner.refs_3_, bf16[192,2048]{1,0:T(8,128)(2,1)S(1)} %get-tuple-element.21.refs_0_, bf16[192,2048]{1,0:T(8,128)(2,1)S(1)} %get-tuple-element.22.refs_1_, ...), custom_call_target="tpu_custom_call" | custom-call | tf_op jit(solution)/shard_map/pallas_call | solution.py:110
  34.7 1.0 %collective-permute-done.10.refs_2_.refs_3_.refs_9_ = bf16[112,2048]{1,0:T(8,128)(2,1)S(1)} collective-permute-done((bf16[112,2048]{1,0:T(8,128)(2,1)S(1)}, bf16[112,2048]{1,0:T(8,128)(2,1)S(1)}, u32[]{:S(2)}, u32[]{:S(2)}) %collective-permute-start.10) | collective-permute-done | bytes 458784 | tf_op jit(solution)/shard_map/ppermute | solution.py:286
  36.4 1.5 %collective-permute-start.19 = (bf16[32,32,128]{2,1,0:T(8,128)(2,1)S(1)}, bf16[32,32,128]{2,1,0:T(8,128)(2,1)S(1)}, u32[]{:S(2)}, u32[]{:S(2)}) collective-permute-start(bf16[32,32,128]{2,1,0:T(8,128)(2,1)S(1)} %copy-done.6), channel_id=1, source_target_pairs={{0,2},{2,0},{1,3},{3,1},{4,6},{6,4},{5,7},{7,5},{8,10},{10,8},{9,1... | collective-permute-start | bytes 786440 | tf_op jit(solution)/shard_map/ppermute | solution.py:296
  38.8 2.0 %shard_map.100 = (f32[256,128]{1,0:T(8,128)S(1)}, bf16[272,128]{1,0:T(8,128)(2,1)S(1)}, bf16[272,128]{1,0:T(8,128)(2,1)S(1)}) custom-call(bf16[128,2048]{1,0:T(8,128)(2,1)S(1)} %copy-done, bf16[128,2048]{1,0:T(8,128)(2,1)S(1)} %collective-permute-done.near.refs_1_, bf16[128,2048]{1,0:T(8,128)(2,1)S(1)} %collective-permute-done.2.end_two, ...), custom_call_target="tpu_custom_call" | custom-call | tf_op jit(solution)/shard_map/pallas_call | solution.py:110
  40.8 4.2 %collective-permute-start.15 = (bf16[272,128]{1,0:T(8,128)(2,1)S(1)}, bf16[272,128]{1,0:T(8,128)(2,1)S(1)}, u32[]{:S(2)}, u32[]{:S(2)}) collective-permute-start(bf16[272,128]{1,0:T(8,128)(2,1)S(1)} %get-tuple-element.30), channel_id=1, source_target_pairs={{0,4},{4,0},{8,12},{12,8},{1,5},{5,1},{9,13},{13,9},{2,6},{6,2},{1... | collective-permute-start | bytes 208904 | tf_op jit(solution)/shard_map/ppermute | solution.py:305
  45.3 2.2 %shard_map.101 = bf16[256,128]{1,0:T(8,128)(2,1)S(1)} custom-call(bf16[128,2048]{1,0:T(8,128)(2,1)S(1)} %collective-permute-done.17.end_three, bf16[128,2048]{1,0:T(8,128)(2,1)S(1)} %collective-permute-done.1.refs_2_.across, f32[256,128]{1,0:T(8,128)S(1)} %get-tuple-element.29.earlier.here, bf16[192,2048]{1,0:T(8,128)(2,1)S(1)} %get-tuple-element.21.refs_0_, ...), custom_call_target="tpu_custom_call" | custom-call | tf_op jit(solution)/shard_map/pallas_call | solution.py:110
  47.5 2.1 %collective-permute-start.18 = (bf16[256,128]{1,0:T(8,128)(2,1)S(1)}, bf16[256,128]{1,0:T(8,128)(2,1)S(1)}, u32[]{:S(2)}, u32[]{:S(2)}) collective-permute-start(bf16[256,128]{1,0:T(8,128)(2,1)S(1)} %shard_map.101), channel_id=1, source_target_pairs={{0,12},{4,8},{8,4},{12,0},{1,13},{5,9},{9,5},{13,1},{2,14},{6,10},... | collective-permute-start | bytes 196616 | tf_op jit(solution)/shard_map/ppermute | solution.py:305
  49.6 4.1 %collective-permute-done.18.three = bf16[256,128]{1,0:T(8,128)(2,1)S(1)} collective-permute-done((bf16[256,128]{1,0:T(8,128)(2,1)S(1)}, bf16[256,128]{1,0:T(8,128)(2,1)S(1)}, u32[]{:S(2)}, u32[]{:S(2)}) %collective-permute-start.18) | collective-permute-done | bytes 65568 | tf_op jit(solution)/shard_map/ppermute | solution.py:305
  53.7 1.1 %shard_map.102 = f32[2,64]{1,0:T(2,128)} custom-call(f32[128,128]{1,0:T(8,128)S(1)} %get-tuple-element.20.base, f32[256,128]{1,0:T(8,128)S(1)} %get-tuple-element.29.earlier.here, bf16[272,128]{1,0:T(8,128)(2,1)S(1)} %collective-permute-done.15.near, bf16[272,128]{1,0:T(8,128)(2,1)S(1)} %collective-permute-done.16.two, ...), custom_call_target="tpu_custom_call" | custom-call | tf_op jit(solution)/shard_map/pallas_call | solution.py:110
  (48 shorter events, 5.4 us)
Async XLA Ops:
  0.0 11.4 %collective-permute-start.4 = (bf16[192,2048]{1,0:T(8,128)(2,1)}, bf16[192,2048]{1,0:T(8,128)(2,1)S(1)}, u32[]{:S(2)}, u32[]{:S(2)}) collective-permute-start(bf16[192,2048]{1,0:T(8,128)(2,1)} %bitcast.13), channel_id=1, source_target_pairs={{0,1},{1,0},{2,3},{3,2},{4,5},{5,4},{6,7},{7,6},{8,9},{9,8},{10,11... | collective-permute-start | bytes 2359304 | tf_op jit(solution)/shard_map/ppermute | solution.py:279
  0.5 7.7 %copy-start = (bf16[128,2048]{1,0:T(8,128)(2,1)S(1)}, bf16[128,2048]{1,0:T(8,128)(2,1)}, u32[]{:S(2)}) copy-start(bf16[128,2048]{1,0:T(8,128)(2,1)} %tokens.5) | copy-start | bytes 1572868
  0.5 10.9 %collective-permute-start.5 = (bf16[192,2048]{1,0:T(8,128)(2,1)}, bf16[192,2048]{1,0:T(8,128)(2,1)S(1)}, u32[]{:S(2)}, u32[]{:S(2)}) collective-permute-start(bf16[192,2048]{1,0:T(8,128)(2,1)} %bitcast.16), channel_id=1, source_target_pairs={{0,1},{1,0},{2,3},{3,2},{4,5},{5,4},{6,7},{7,6},{8,9},{9,8},{10,11... | collective-permute-start | bytes 2359304 | tf_op jit(solution)/shard_map/ppermute | solution.py:279
  0.5 15.4 %collective-permute-start = (bf16[128,2048]{1,0:T(8,128)(2,1)}, bf16[128,2048]{1,0:T(8,128)(2,1)S(1)}, u32[]{:S(2)}, u32[]{:S(2)}) collective-permute-start(bf16[128,2048]{1,0:T(8,128)(2,1)} %tokens.5), channel_id=1, source_target_pairs={{0,4},{4,0},{8,12},{12,8},{1,5},{5,1},{9,13},{13,9},{2,6},{6,2},{1... | collective-permute-start | bytes 1572872 | tf_op jit(solution)/shard_map/ppermute | solution.py:264
  3.5 13.1 %collective-permute-start.1 = (bf16[128,2048]{1,0:T(8,128)(2,1)}, bf16[128,2048]{1,0:T(8,128)(2,1)S(1)}, u32[]{:S(2)}, u32[]{:S(2)}) collective-permute-start(bf16[128,2048]{1,0:T(8,128)(2,1)} %tokens.5), channel_id=1, source_target_pairs={{4,8},{8,4},{5,9},{9,5},{6,10},{10,6},{7,11},{11,7},{20,24},{24,20... | collective-permute-start | bytes 1572872 | tf_op jit(solution)/shard_map/ppermute | solution.py:265
  6.5 1.6 %copy-start.2 = (bf16[1,2048,192]{1,2,0:T(8,128)(2,1)S(1)}, bf16[1,2048,192]{1,2,0:T(8,128)(2,1)}, u32[]{:S(2)}) copy-start(bf16[1,2048,192]{1,2,0:T(8,128)(2,1)} %param.13) | copy-start | bytes 2359300
  6.5 1.6 %copy-start.5 = (bf16[2048,128]{1,0:T(8,128)(2,1)S(1)}, bf16[2048,128]{1,0:T(8,128)(2,1)}, u32[]{:S(2)}) copy-start(bf16[2048,128]{1,0:T(8,128)(2,1)} %proj.1) | copy-start | bytes 1572868
  6.5 12.1 %collective-permute-start.7 = (bf16[96,2048]{1,0:T(8,128)(2,1)S(1)}, bf16[96,2048]{1,0:T(8,128)(2,1)S(1)}, u32[]{:S(2)}, u32[]{:S(2)}) collective-permute-start(bf16[96,2048]{1,0:T(8,128)(2,1)S(1)} %shard_map.95), channel_id=1, source_target_pairs={{0,2},{2,0},{1,3},{3,1},{4,6},{6,4},{5,7},{7,5},{8,10},{10,8},{9,1... | collective-permute-start | bytes 1179656 | tf_op jit(solution)/shard_map/ppermute | solution.py:270
  11.4 15.6 %collective-permute-start.9 = (bf16[96,2048]{1,0:T(8,128)(2,1)S(1)}, bf16[96,2048]{1,0:T(8,128)(2,1)S(1)}, u32[]{:S(2)}, u32[]{:S(2)}) collective-permute-start(bf16[96,2048]{1,0:T(8,128)(2,1)S(1)} %shard_map.97), channel_id=1, source_target_pairs={{0,2},{2,0},{1,3},{3,1},{4,6},{6,4},{5,7},{7,5},{8,10},{10,8},{9,1... | collective-permute-start | bytes 1179656 | tf_op jit(solution)/shard_map/ppermute | solution.py:286
  15.9 11.2 %collective-permute-start.3 = (bf16[128,2048]{1,0:T(8,128)(2,1)S(1)}, bf16[128,2048]{1,0:T(8,128)(2,1)S(1)}, u32[]{:S(2)}, u32[]{:S(2)}) collective-permute-start(bf16[128,2048]{1,0:T(8,128)(2,1)S(1)} %collective-permute-done.near.refs_1_), channel_id=1, source_target_pairs={{4,8},{8,4},{5,9},{9,5},{6,10},{10,6},{7,11},{11,7},{20,24},{24,20... | collective-permute-start | bytes 1572872 | tf_op jit(solution)/shard_map/ppermute | solution.py:284
  16.6 16.8 %collective-permute-start.2 = (bf16[128,2048]{1,0:T(8,128)(2,1)S(1)}, bf16[128,2048]{1,0:T(8,128)(2,1)S(1)}, u32[]{:S(2)}, u32[]{:S(2)}) collective-permute-start(bf16[128,2048]{1,0:T(8,128)(2,1)S(1)} %collective-permute-done.1.refs_2_.across), channel_id=1, source_target_pairs={{4,0},{8,12},{5,1},{9,13},{6,2},{10,14},{7,3},{11,15},{20,16},{24,... | collective-permute-start | bytes 1572872 | tf_op jit(solution)/shard_map/ppermute | solution.py:285
  18.0 2.2 %collective-permute-start.6 = (bf16[16,2048]{1,0:T(8,128)(2,1)S(1)}, bf16[16,2048]{1,0:T(8,128)(2,1)S(1)}, u32[]{:S(2)}, u32[]{:S(2)}) collective-permute-start(bf16[16,2048]{1,0:T(8,128)(2,1)S(1)} %shard_map.92), channel_id=1, source_target_pairs={{0,1},{1,0},{2,3},{3,2},{4,5},{5,4},{6,7},{7,6},{8,9},{9,8},{10,11... | collective-permute-start | bytes 196616 | tf_op jit(solution)/shard_map/ppermute | solution.py:280
  18.6 17.1 %collective-permute-start.10 = (bf16[112,2048]{1,0:T(8,128)(2,1)S(1)}, bf16[112,2048]{1,0:T(8,128)(2,1)S(1)}, u32[]{:S(2)}, u32[]{:S(2)}) collective-permute-start(bf16[112,2048]{1,0:T(8,128)(2,1)S(1)} %shard_map.98), channel_id=1, source_target_pairs={{0,2},{2,0},{1,3},{3,1},{4,6},{6,4},{5,7},{7,5},{8,10},{10,8},{9,1... | collective-permute-start | bytes 1376264 | tf_op jit(solution)/shard_map/ppermute | solution.py:286
  20.2 14.5 %collective-permute-start.8 = (bf16[96,2048]{1,0:T(8,128)(2,1)S(1)}, bf16[96,2048]{1,0:T(8,128)(2,1)S(1)}, u32[]{:S(2)}, u32[]{:S(2)}) collective-permute-start(bf16[96,2048]{1,0:T(8,128)(2,1)S(1)} %shard_map.96.refs_0_.refs_6_), channel_id=1, source_target_pairs={{0,16},{16,0},{1,17},{17,1},{2,18},{18,2},{3,19},{19,3},{4,20},{20... | collective-permute-start | bytes 1179656 | tf_op jit(solution)/shard_map/ppermute | solution.py:288
  27.1 8.6 %collective-permute-start.11 = (bf16[96,2048]{1,0:T(8,128)(2,1)S(1)}, bf16[96,2048]{1,0:T(8,128)(2,1)S(1)}, u32[]{:S(2)}, u32[]{:S(2)}) collective-permute-start(bf16[96,2048]{1,0:T(8,128)(2,1)S(1)} %collective-permute-done.9.refs_2_.refs_8_), channel_id=1, source_target_pairs={{0,1},{1,0},{2,3},{3,2},{4,5},{5,4},{6,7},{7,6},{8,9},{9,8},{10,11... | collective-permute-start | bytes 1179656 | tf_op jit(solution)/shard_map/ppermute | solution.py:293
  27.1 18.3 %collective-permute-start.17 = (bf16[128,2048]{1,0:T(8,128)(2,1)S(1)}, bf16[128,2048]{1,0:T(8,128)(2,1)S(1)}, u32[]{:S(2)}, u32[]{:S(2)}) collective-permute-start(bf16[128,2048]{1,0:T(8,128)(2,1)S(1)} %collective-permute-done.3.far_inner.refs_3_), channel_id=1, source_target_pairs={{4,0},{8,12},{5,1},{9,13},{6,2},{10,14},{7,3},{11,15},{20,16},{24,... | collective-permute-start | bytes 1572872 | tf_op jit(solution)/shard_map/ppermute | solution.py:291
  34.6 1.8 %copy-start.6 = (bf16[32,32,128]{2,1,0:T(8,128)(2,1)S(1)}, bf16[32,32,128]{2,1,0:T(8,128)(2,1)}, u32[]{:S(2)}) copy-start(bf16[32,32,128]{2,1,0:T(8,128)(2,1)} %param.17) | copy-start | bytes 786436
  35.8 3.0 %collective-permute-start.14 = (bf16[112,2048]{1,0:T(8,128)(2,1)S(1)}, bf16[112,2048]{1,0:T(8,128)(2,1)S(1)}, u32[]{:S(2)}, u32[]{:S(2)}) collective-permute-start(bf16[112,2048]{1,0:T(8,128)(2,1)S(1)} %get-tuple-element.28), channel_id=1, source_target_pairs={{0,1},{1,0},{2,3},{3,2},{4,5},{5,4},{6,7},{7,6},{8,9},{9,8},{10,11... | collective-permute-start | bytes 1376264 | tf_op jit(solution)/shard_map/ppermute | solution.py:295
  35.8 2.4 %collective-permute-start.12 = (bf16[96,2048]{1,0:T(8,128)(2,1)S(1)}, bf16[96,2048]{1,0:T(8,128)(2,1)S(1)}, u32[]{:S(2)}, u32[]{:S(2)}) collective-permute-start(bf16[96,2048]{1,0:T(8,128)(2,1)S(1)} %get-tuple-element.26), channel_id=1, source_target_pairs={{0,1},{1,0},{2,3},{3,2},{4,5},{5,4},{6,7},{7,6},{8,9},{9,8},{10,11... | collective-permute-start | bytes 1179656 | tf_op jit(solution)/shard_map/ppermute | solution.py:295
  36.3 2.4 %collective-permute-start.13 = (bf16[96,2048]{1,0:T(8,128)(2,1)S(1)}, bf16[96,2048]{1,0:T(8,128)(2,1)S(1)}, u32[]{:S(2)}, u32[]{:S(2)}) collective-permute-start(bf16[96,2048]{1,0:T(8,128)(2,1)S(1)} %get-tuple-element.27), channel_id=1, source_target_pairs={{0,1},{1,0},{2,3},{3,2},{4,5},{5,4},{6,7},{7,6},{8,9},{9,8},{10,11... | collective-permute-start | bytes 1179656 | tf_op jit(solution)/shard_map/ppermute | solution.py:295
  36.4 13.2 %collective-permute-start.19 = (bf16[32,32,128]{2,1,0:T(8,128)(2,1)S(1)}, bf16[32,32,128]{2,1,0:T(8,128)(2,1)S(1)}, u32[]{:S(2)}, u32[]{:S(2)}) collective-permute-start(bf16[32,32,128]{2,1,0:T(8,128)(2,1)S(1)} %copy-done.6), channel_id=1, source_target_pairs={{0,2},{2,0},{1,3},{3,1},{4,6},{6,4},{5,7},{7,5},{8,10},{10,8},{9,1... | collective-permute-start | bytes 786440 | tf_op jit(solution)/shard_map/ppermute | solution.py:296
  40.8 12.9 %collective-permute-start.15 = (bf16[272,128]{1,0:T(8,128)(2,1)S(1)}, bf16[272,128]{1,0:T(8,128)(2,1)S(1)}, u32[]{:S(2)}, u32[]{:S(2)}) collective-permute-start(bf16[272,128]{1,0:T(8,128)(2,1)S(1)} %get-tuple-element.30), channel_id=1, source_target_pairs={{0,4},{4,0},{8,12},{12,8},{1,5},{5,1},{9,13},{13,9},{2,6},{6,2},{1... | collective-permute-start | bytes 208904 | tf_op jit(solution)/shard_map/ppermute | solution.py:305
  44.9 8.8 %collective-permute-start.16 = (bf16[272,128]{1,0:T(8,128)(2,1)S(1)}, bf16[272,128]{1,0:T(8,128)(2,1)S(1)}, u32[]{:S(2)}, u32[]{:S(2)}) collective-permute-start(bf16[272,128]{1,0:T(8,128)(2,1)S(1)} %get-tuple-element.31), channel_id=1, source_target_pairs={{0,8},{4,12},{8,0},{12,4},{1,9},{5,13},{9,1},{13,5},{2,10},{6,14},... | collective-permute-start | bytes 208904 | tf_op jit(solution)/shard_map/ppermute | solution.py:305
  47.5 6.2 %collective-permute-start.18 = (bf16[256,128]{1,0:T(8,128)(2,1)S(1)}, bf16[256,128]{1,0:T(8,128)(2,1)S(1)}, u32[]{:S(2)}, u32[]{:S(2)}) collective-permute-start(bf16[256,128]{1,0:T(8,128)(2,1)S(1)} %shard_map.101), channel_id=1, source_target_pairs={{0,12},{4,8},{8,4},{12,0},{1,13},{5,9},{9,5},{13,1},{2,14},{6,10},... | collective-permute-start | bytes 196616 | tf_op jit(solution)/shard_map/ppermute | solution.py:305
  (6 other events, 5.5 us)

commit v11 on v10

--- a/solution.py
+++ b/solution.py
@@ -232,8 +232,8 @@
         for w in (0, 1):
             part = sent[w * width : (w + 1) * width, :].astype(jnp.float32)
             total = total + weights[2 * k + w : 2 * k + w + 1, :] * part
-    norm = jnp.sqrt(jnp.sum(total * total, axis=0, keepdims=True) + 1e-06)
-    embedding = (total / norm).T.astype(jnp.bfloat16)
+    scale = lax.rsqrt(jnp.sum(total * total, axis=0, keepdims=True) + 1e-06)
+    embedding = (total * scale).T.astype(jnp.bfloat16)
     best = [[] for _ in range(tokens // PLEN)]
     for block in (queries, others):
         raw = dot(embedding, block[...], NT) + live[:, :1]

time: 55.2 us -> 55.2 us (level)
  no operation moved by 1% of the time
where the time goes in v11:
time: 55.2 us; the launch traced here: 54.9 us
  starting transfers between devices  21.3 us (39%)
  waiting for transfers between devices  20 us (36%)
  Pallas kernels  9.31 us (17%)
  local copies, waits for them, and re-layouts  4.08 us (7%)
    pallas_call x7, Pallas kernels, kernel(): pl.pallas_call(body, out_shape=[jax.ShapeDtypeStruct(shape, dtype) for sh...  9.14 us
    ppermute x2, waiting for transfers between devices, by_column(): lax.ppermute(a, Q, swap)  6.32 us
    ppermute x3, starting transfers between devices, by_column(): lax.ppermute(a, E, [(i, i ^ k) for i in range(4)])  6.27 us
    ppermute x3, waiting for transfers between devices, by_column(): lax.ppermute(a, E, [(i, i ^ k) for i in range(4)])  4.12 us
    unnamed x20, local copies, waits for them, and re-layouts  4.08 us
    ppermute x1, waiting for transfers between devices, by_column(): end_two = lax.ppermute(across, E, ends)  3.88 us
    ppermute x1, waiting for transfers between devices, by_column(): near = lax.ppermute(tokens, E, [(i, i ^ 1) for i in range(4)])  3.79 us
    ppermute x1, starting transfers between devices, by_column(): near = lax.ppermute(tokens, E, [(i, i ^ 1) for i in range(4)])  3.02 us
  transfers between devices with their start and end apart: 20, of which 9 were waited for; matrix products, arithmetic and copies ran while one was open for 0% of the time, Pallas kernels for 15%

profile of v11, /device:TPU:0, one launch (start us, length us, event | category | flops | bytes accessed | tf_op | source)
XLA Modules:
  0.0 54.9 jit_solution(11674321368135870788)
XLA Ops:
  0.5 3.0 %collective-permute-start = (bf16[128,2048]{1,0:T(8,128)(2,1)}, bf16[128,2048]{1,0:T(8,128)(2,1)S(1)}, u32[]{:S(2)}, u32[]{:S(2)}) collective-permute-start(bf16[128,2048]{1,0:T(8,128)(2,1)} %tokens.5), channel_id=1, source_target_pairs={{0,4},{4,0},{8,12},{12,8},{1,5},{5,1},{9,13},{13,9},{2,6},{6,2},{1... | collective-permute-start | bytes 1572872 | tf_op jit(solution)/shard_map/ppermute | solution.py:264
  4.2 1.1 %copy-done.1 = bf16[1,2048,192]{1,2,0:T(8,128)(2,1)S(1)} copy-done((bf16[1,2048,192]{1,2,0:T(8,128)(2,1)S(1)}, bf16[1,2048,192]{1,2,0:T(8,128)(2,1)}, u32[]{:S(2)}) %copy-start.1) | copy-done | bytes 786456
  5.4 1.1 %copy-done.3 = bf16[1,2048,192]{1,2,0:T(8,128)(2,1)S(1)} copy-done((bf16[1,2048,192]{1,2,0:T(8,128)(2,1)S(1)}, bf16[1,2048,192]{1,2,0:T(8,128)(2,1)}, u32[]{:S(2)}) %copy-start.3) | copy-done | bytes 786456
  6.5 1.6 %collective-permute-start.7 = (bf16[96,2048]{1,0:T(8,128)(2,1)S(1)}, bf16[96,2048]{1,0:T(8,128)(2,1)S(1)}, u32[]{:S(2)}, u32[]{:S(2)}) collective-permute-start(bf16[96,2048]{1,0:T(8,128)(2,1)S(1)} %shard_map.95), channel_id=1, source_target_pairs={{0,2},{2,0},{1,3},{3,1},{4,6},{6,4},{5,7},{7,5},{8,10},{10,8},{9,1... | collective-permute-start | bytes 1179656 | tf_op jit(solution)/shard_map/ppermute | solution.py:270
  8.8 1.1 %copy-done.4 = bf16[1,2048,192]{1,2,0:T(8,128)(2,1)S(1)} copy-done((bf16[1,2048,192]{1,2,0:T(8,128)(2,1)S(1)}, bf16[1,2048,192]{1,2,0:T(8,128)(2,1)}, u32[]{:S(2)}) %copy-start.4) | copy-done | bytes 786456
  9.9 1.4 %shard_map.91 = (bf16[16,2048]{1,0:T(8,128)(2,1)S(1)}, bf16[96,2048]{1,0:T(8,128)(2,1)S(1)}, bf16[112,2048]{1,0:T(8,128)(2,1)S(1)}, bf16[192,2048]{1,0:T(8,128)(...) custom-call(s32[2]{0:T(128)S(1)} %copy-done.9, ...), custom_call_target="tpu_custom_call" | custom-call | tf_op jit(solution)/shard_map/pallas_call | solution.py:110
  11.4 0.7 %collective-permute-start.9 = (bf16[96,2048]{1,0:T(8,128)(2,1)S(1)}, bf16[96,2048]{1,0:T(8,128)(2,1)S(1)}, u32[]{:S(2)}, u32[]{:S(2)}) collective-permute-start(bf16[96,2048]{1,0:T(8,128)(2,1)S(1)} %shard_map.97), channel_id=1, source_target_pairs={{0,2},{2,0},{1,3},{3,1},{4,6},{6,4},{5,7},{7,5},{8,10},{10,8},{9,1... | collective-permute-start | bytes 1179656 | tf_op jit(solution)/shard_map/ppermute | solution.py:286
  12.1 3.8 %collective-permute-done.near.refs_1_ = bf16[128,2048]{1,0:T(8,128)(2,1)S(1)} collective-permute-done((bf16[128,2048]{1,0:T(8,128)(2,1)}, bf16[128,2048]{1,0:T(8,128)(2,1)S(1)}, u32[]{:S(2)}, u32[]{:S(2)}) %collective-permute-start) | collective-permute-done | bytes 524320 | tf_op jit(solution)/shard_map/ppermute | solution.py:264
  16.6 1.3 %collective-permute-start.2 = (bf16[128,2048]{1,0:T(8,128)(2,1)S(1)}, bf16[128,2048]{1,0:T(8,128)(2,1)S(1)}, u32[]{:S(2)}, u32[]{:S(2)}) collective-permute-start(bf16[128,2048]{1,0:T(8,128)(2,1)S(1)} %collective-permute-done.1.refs_2_.across), channel_id=1, source_target_pairs={{4,0},{8,12},{5,1},{9,13},{6,2},{10,14},{7,3},{11,15},{20,16},{24,... | collective-permute-start | bytes 1572872 | tf_op jit(solution)/shard_map/ppermute | solution.py:285
  18.6 1.5 %collective-permute-start.10 = (bf16[112,2048]{1,0:T(8,128)(2,1)S(1)}, bf16[112,2048]{1,0:T(8,128)(2,1)S(1)}, u32[]{:S(2)}, u32[]{:S(2)}) collective-permute-start(bf16[112,2048]{1,0:T(8,128)(2,1)S(1)} %shard_map.98), channel_id=1, source_target_pairs={{0,2},{2,0},{1,3},{3,1},{4,6},{6,4},{5,7},{7,5},{8,10},{10,8},{9,1... | collective-permute-start | bytes 1376264 | tf_op jit(solution)/shard_map/ppermute | solution.py:286
  20.2 1.6 %collective-permute-start.8 = (bf16[96,2048]{1,0:T(8,128)(2,1)S(1)}, bf16[96,2048]{1,0:T(8,128)(2,1)S(1)}, u32[]{:S(2)}, u32[]{:S(2)}) collective-permute-start(bf16[96,2048]{1,0:T(8,128)(2,1)S(1)} %shard_map.96.refs_0_.refs_6_), channel_id=1, source_target_pairs={{0,16},{16,0},{1,17},{17,1},{2,18},{18,2},{3,19},{19,3},{4,20},{20... | collective-permute-start | bytes 1179656 | tf_op jit(solution)/shard_map/ppermute | solution.py:288
  21.7 5.3 %collective-permute-done.9.refs_2_.refs_8_ = bf16[96,2048]{1,0:T(8,128)(2,1)S(1)} collective-permute-done((bf16[96,2048]{1,0:T(8,128)(2,1)S(1)}, bf16[96,2048]{1,0:T(8,128)(2,1)S(1)}, u32[]{:S(2)}, u32[]{:S(2)}) %collective-permute-start.9) | collective-permute-done | bytes 393248 | tf_op jit(solution)/shard_map/ppermute | solution.py:286
  27.1 1.3 %collective-permute-start.17 = (bf16[128,2048]{1,0:T(8,128)(2,1)S(1)}, bf16[128,2048]{1,0:T(8,128)(2,1)S(1)}, u32[]{:S(2)}, u32[]{:S(2)}) collective-permute-start(bf16[128,2048]{1,0:T(8,128)(2,1)S(1)} %collective-permute-done.3.far_inner.refs_3_), channel_id=1, source_target_pairs={{4,0},{8,12},{5,1},{9,13},{6,2},{10,14},{7,3},{11,15},{20,16},{24,... | collective-permute-start | bytes 1572872 | tf_op jit(solution)/shard_map/ppermute | solution.py:291
  28.3 1.2 %shard_map.93.refs_4_.got_own = f32[128,256]{1,0:T(8,128)S(1)} custom-call(bf16[128,2048]{1,0:T(8,128)(2,1)S(1)} %copy-done, bf16[128,2048]{1,0:T(8,128)(2,1)S(1)} %collective-permute-done.near.refs_1_, bf16[192,2048]{1,0:T(8,128)(2,1)S(1)} %get-tuple-element.21.refs_0_, bf16[192,2048]{1,0:T(8,128)(2,1)S(1)} %get-tuple-element.22.refs_1_, ...), custom_call_target="tpu_custom_call" | custom-call | tf_op jit(solution)/shard_map/pallas_call | solution.py:110
  29.6 3.9 %collective-permute-done.2.end_two = bf16[128,2048]{1,0:T(8,128)(2,1)S(1)} collective-permute-done((bf16[128,2048]{1,0:T(8,128)(2,1)S(1)}, bf16[128,2048]{1,0:T(8,128)(2,1)S(1)}, u32[]{:S(2)}, u32[]{:S(2)}) %collective-permute-start.2) | collective-permute-done | bytes 524320 | tf_op jit(solution)/shard_map/ppermute | solution.py:285
  33.4 1.2 %shard_map.94.refs_5_.got_two = f32[128,128]{1,0:T(8,128)S(1)} custom-call(bf16[128,2048]{1,0:T(8,128)(2,1)S(1)} %collective-permute-done.2.end_two, bf16[128,2048]{1,0:T(8,128)(2,1)S(1)} %collective-permute-done.3.far_inner.refs_3_, bf16[192,2048]{1,0:T(8,128)(2,1)S(1)} %get-tuple-element.21.refs_0_, bf16[192,2048]{1,0:T(8,128)(2,1)S(1)} %get-tuple-element.22.refs_1_, ...), custom_call_target="tpu_custom_call" | custom-call | tf_op jit(solution)/shard_map/pallas_call | solution.py:110
  34.7 1.0 %collective-permute-done.10.refs_2_.refs_3_.refs_9_ = bf16[112,2048]{1,0:T(8,128)(2,1)S(1)} collective-permute-done((bf16[112,2048]{1,0:T(8,128)(2,1)S(1)}, bf16[112,2048]{1,0:T(8,128)(2,1)S(1)}, u32[]{:S(2)}, u32[]{:S(2)}) %collective-permute-start.10) | collective-permute-done | bytes 458784 | tf_op jit(solution)/shard_map/ppermute | solution.py:286
  36.4 1.5 %collective-permute-start.19 = (bf16[32,32,128]{2,1,0:T(8,128)(2,1)S(1)}, bf16[32,32,128]{2,1,0:T(8,128)(2,1)S(1)}, u32[]{:S(2)}, u32[]{:S(2)}) collective-permute-start(bf16[32,32,128]{2,1,0:T(8,128)(2,1)S(1)} %copy-done.6), channel_id=1, source_target_pairs={{0,2},{2,0},{1,3},{3,1},{4,6},{6,4},{5,7},{7,5},{8,10},{10,8},{9,1... | collective-permute-start | bytes 786440 | tf_op jit(solution)/shard_map/ppermute | solution.py:296
  38.8 2.0 %shard_map.100 = (f32[256,128]{1,0:T(8,128)S(1)}, bf16[272,128]{1,0:T(8,128)(2,1)S(1)}, bf16[272,128]{1,0:T(8,128)(2,1)S(1)}) custom-call(bf16[128,2048]{1,0:T(8,128)(2,1)S(1)} %copy-done, bf16[128,2048]{1,0:T(8,128)(2,1)S(1)} %collective-permute-done.near.refs_1_, bf16[128,2048]{1,0:T(8,128)(2,1)S(1)} %collective-permute-done.2.end_two, ...), custom_call_target="tpu_custom_call" | custom-call | tf_op jit(solution)/shard_map/pallas_call | solution.py:110
  40.8 4.2 %collective-permute-start.15 = (bf16[272,128]{1,0:T(8,128)(2,1)S(1)}, bf16[272,128]{1,0:T(8,128)(2,1)S(1)}, u32[]{:S(2)}, u32[]{:S(2)}) collective-permute-start(bf16[272,128]{1,0:T(8,128)(2,1)S(1)} %get-tuple-element.30), channel_id=1, source_target_pairs={{0,4},{4,0},{8,12},{12,8},{1,5},{5,1},{9,13},{13,9},{2,6},{6,2},{1... | collective-permute-start | bytes 208904 | tf_op jit(solution)/shard_map/ppermute | solution.py:305
  45.3 2.2 %shard_map.101 = bf16[256,128]{1,0:T(8,128)(2,1)S(1)} custom-call(bf16[128,2048]{1,0:T(8,128)(2,1)S(1)} %collective-permute-done.17.end_three, bf16[128,2048]{1,0:T(8,128)(2,1)S(1)} %collective-permute-done.1.refs_2_.across, f32[256,128]{1,0:T(8,128)S(1)} %get-tuple-element.29.earlier.here, bf16[192,2048]{1,0:T(8,128)(2,1)S(1)} %get-tuple-element.21.refs_0_, ...), custom_call_target="tpu_custom_call" | custom-call | tf_op jit(solution)/shard_map/pallas_call | solution.py:110
  47.5 2.1 %collective-permute-start.18 = (bf16[256,128]{1,0:T(8,128)(2,1)S(1)}, bf16[256,128]{1,0:T(8,128)(2,1)S(1)}, u32[]{:S(2)}, u32[]{:S(2)}) collective-permute-start(bf16[256,128]{1,0:T(8,128)(2,1)S(1)} %shard_map.101), channel_id=1, source_target_pairs={{0,12},{4,8},{8,4},{12,0},{1,13},{5,9},{9,5},{13,1},{2,14},{6,10},... | collective-permute-start | bytes 196616 | tf_op jit(solution)/shard_map/ppermute | solution.py:305
  49.6 4.1 %collective-permute-done.18.three = bf16[256,128]{1,0:T(8,128)(2,1)S(1)} collective-permute-done((bf16[256,128]{1,0:T(8,128)(2,1)S(1)}, bf16[256,128]{1,0:T(8,128)(2,1)S(1)}, u32[]{:S(2)}, u32[]{:S(2)}) %collective-permute-start.18) | collective-permute-done | bytes 65568 | tf_op jit(solution)/shard_map/ppermute | solution.py:305
  53.7 1.1 %shard_map.102 = f32[2,64]{1,0:T(2,128)} custom-call(f32[128,128]{1,0:T(8,128)S(1)} %get-tuple-element.20.base, f32[256,128]{1,0:T(8,128)S(1)} %get-tuple-element.29.earlier.here, bf16[272,128]{1,0:T(8,128)(2,1)S(1)} %collective-permute-done.15.near, bf16[272,128]{1,0:T(8,128)(2,1)S(1)} %collective-permute-done.16.two, ...), custom_call_target="tpu_custom_call" | custom-call | tf_op jit(solution)/shard_map/pallas_call | solution.py:110
  (48 shorter events, 5.4 us)
Async XLA Ops:
  0.0 11.4 %collective-permute-start.4 = (bf16[192,2048]{1,0:T(8,128)(2,1)}, bf16[192,2048]{1,0:T(8,128)(2,1)S(1)}, u32[]{:S(2)}, u32[]{:S(2)}) collective-permute-start(bf16[192,2048]{1,0:T(8,128)(2,1)} %bitcast.13), channel_id=1, source_target_pairs={{0,1},{1,0},{2,3},{3,2},{4,5},{5,4},{6,7},{7,6},{8,9},{9,8},{10,11... | collective-permute-start | bytes 2359304 | tf_op jit(solution)/shard_map/ppermute | solution.py:279
  0.5 7.7 %copy-start = (bf16[128,2048]{1,0:T(8,128)(2,1)S(1)}, bf16[128,2048]{1,0:T(8,128)(2,1)}, u32[]{:S(2)}) copy-start(bf16[128,2048]{1,0:T(8,128)(2,1)} %tokens.5) | copy-start | bytes 1572868
  0.5 10.9 %collective-permute-start.5 = (bf16[192,2048]{1,0:T(8,128)(2,1)}, bf16[192,2048]{1,0:T(8,128)(2,1)S(1)}, u32[]{:S(2)}, u32[]{:S(2)}) collective-permute-start(bf16[192,2048]{1,0:T(8,128)(2,1)} %bitcast.16), channel_id=1, source_target_pairs={{0,1},{1,0},{2,3},{3,2},{4,5},{5,4},{6,7},{7,6},{8,9},{9,8},{10,11... | collective-permute-start | bytes 2359304 | tf_op jit(solution)/shard_map/ppermute | solution.py:279
  0.5 15.4 %collective-permute-start = (bf16[128,2048]{1,0:T(8,128)(2,1)}, bf16[128,2048]{1,0:T(8,128)(2,1)S(1)}, u32[]{:S(2)}, u32[]{:S(2)}) collective-permute-start(bf16[128,2048]{1,0:T(8,128)(2,1)} %tokens.5), channel_id=1, source_target_pairs={{0,4},{4,0},{8,12},{12,8},{1,5},{5,1},{9,13},{13,9},{2,6},{6,2},{1... | collective-permute-start | bytes 1572872 | tf_op jit(solution)/shard_map/ppermute | solution.py:264
  3.5 13.1 %collective-permute-start.1 = (bf16[128,2048]{1,0:T(8,128)(2,1)}, bf16[128,2048]{1,0:T(8,128)(2,1)S(1)}, u32[]{:S(2)}, u32[]{:S(2)}) collective-permute-start(bf16[128,2048]{1,0:T(8,128)(2,1)} %tokens.5), channel_id=1, source_target_pairs={{4,8},{8,4},{5,9},{9,5},{6,10},{10,6},{7,11},{11,7},{20,24},{24,20... | collective-permute-start | bytes 1572872 | tf_op jit(solution)/shard_map/ppermute | solution.py:265
  6.5 1.6 %copy-start.2 = (bf16[1,2048,192]{1,2,0:T(8,128)(2,1)S(1)}, bf16[1,2048,192]{1,2,0:T(8,128)(2,1)}, u32[]{:S(2)}) copy-start(bf16[1,2048,192]{1,2,0:T(8,128)(2,1)} %param.13) | copy-start | bytes 2359300
  6.5 1.6 %copy-start.5 = (bf16[2048,128]{1,0:T(8,128)(2,1)S(1)}, bf16[2048,128]{1,0:T(8,128)(2,1)}, u32[]{:S(2)}) copy-start(bf16[2048,128]{1,0:T(8,128)(2,1)} %proj.1) | copy-start | bytes 1572868
  6.5 12.1 %collective-permute-start.7 = (bf16[96,2048]{1,0:T(8,128)(2,1)S(1)}, bf16[96,2048]{1,0:T(8,128)(2,1)S(1)}, u32[]{:S(2)}, u32[]{:S(2)}) collective-permute-start(bf16[96,2048]{1,0:T(8,128)(2,1)S(1)} %shard_map.95), channel_id=1, source_target_pairs={{0,2},{2,0},{1,3},{3,1},{4,6},{6,4},{5,7},{7,5},{8,10},{10,8},{9,1... | collective-permute-start | bytes 1179656 | tf_op jit(solution)/shard_map/ppermute | solution.py:270
  11.4 15.6 %collective-permute-start.9 = (bf16[96,2048]{1,0:T(8,128)(2,1)S(1)}, bf16[96,2048]{1,0:T(8,128)(2,1)S(1)}, u32[]{:S(2)}, u32[]{:S(2)}) collective-permute-start(bf16[96,2048]{1,0:T(8,128)(2,1)S(1)} %shard_map.97), channel_id=1, source_target_pairs={{0,2},{2,0},{1,3},{3,1},{4,6},{6,4},{5,7},{7,5},{8,10},{10,8},{9,1... | collective-permute-start | bytes 1179656 | tf_op jit(solution)/shard_map/ppermute | solution.py:286
  15.9 11.2 %collective-permute-start.3 = (bf16[128,2048]{1,0:T(8,128)(2,1)S(1)}, bf16[128,2048]{1,0:T(8,128)(2,1)S(1)}, u32[]{:S(2)}, u32[]{:S(2)}) collective-permute-start(bf16[128,2048]{1,0:T(8,128)(2,1)S(1)} %collective-permute-done.near.refs_1_), channel_id=1, source_target_pairs={{4,8},{8,4},{5,9},{9,5},{6,10},{10,6},{7,11},{11,7},{20,24},{24,20... | collective-permute-start | bytes 1572872 | tf_op jit(solution)/shard_map/ppermute | solution.py:284
  16.6 16.8 %collective-permute-start.2 = (bf16[128,2048]{1,0:T(8,128)(2,1)S(1)}, bf16[128,2048]{1,0:T(8,128)(2,1)S(1)}, u32[]{:S(2)}, u32[]{:S(2)}) collective-permute-start(bf16[128,2048]{1,0:T(8,128)(2,1)S(1)} %collective-permute-done.1.refs_2_.across), channel_id=1, source_target_pairs={{4,0},{8,12},{5,1},{9,13},{6,2},{10,14},{7,3},{11,15},{20,16},{24,... | collective-permute-start | bytes 1572872 | tf_op jit(solution)/shard_map/ppermute | solution.py:285
  18.0 2.2 %collective-permute-start.6 = (bf16[16,2048]{1,0:T(8,128)(2,1)S(1)}, bf16[16,2048]{1,0:T(8,128)(2,1)S(1)}, u32[]{:S(2)}, u32[]{:S(2)}) collective-permute-start(bf16[16,2048]{1,0:T(8,128)(2,1)S(1)} %shard_map.92), channel_id=1, source_target_pairs={{0,1},{1,0},{2,3},{3,2},{4,5},{5,4},{6,7},{7,6},{8,9},{9,8},{10,11... | collective-permute-start | bytes 196616 | tf_op jit(solution)/shard_map/ppermute | solution.py:280
  18.6 17.1 %collective-permute-start.10 = (bf16[112,2048]{1,0:T(8,128)(2,1)S(1)}, bf16[112,2048]{1,0:T(8,128)(2,1)S(1)}, u32[]{:S(2)}, u32[]{:S(2)}) collective-permute-start(bf16[112,2048]{1,0:T(8,128)(2,1)S(1)} %shard_map.98), channel_id=1, source_target_pairs={{0,2},{2,0},{1,3},{3,1},{4,6},{6,4},{5,7},{7,5},{8,10},{10,8},{9,1... | collective-permute-start | bytes 1376264 | tf_op jit(solution)/shard_map/ppermute | solution.py:286
  20.2 14.5 %collective-permute-start.8 = (bf16[96,2048]{1,0:T(8,128)(2,1)S(1)}, bf16[96,2048]{1,0:T(8,128)(2,1)S(1)}, u32[]{:S(2)}, u32[]{:S(2)}) collective-permute-start(bf16[96,2048]{1,0:T(8,128)(2,1)S(1)} %shard_map.96.refs_0_.refs_6_), channel_id=1, source_target_pairs={{0,16},{16,0},{1,17},{17,1},{2,18},{18,2},{3,19},{19,3},{4,20},{20... | collective-permute-start | bytes 1179656 | tf_op jit(solution)/shard_map/ppermute | solution.py:288
  27.1 8.6 %collective-permute-start.11 = (bf16[96,2048]{1,0:T(8,128)(2,1)S(1)}, bf16[96,2048]{1,0:T(8,128)(2,1)S(1)}, u32[]{:S(2)}, u32[]{:S(2)}) collective-permute-start(bf16[96,2048]{1,0:T(8,128)(2,1)S(1)} %collective-permute-done.9.refs_2_.refs_8_), channel_id=1, source_target_pairs={{0,1},{1,0},{2,3},{3,2},{4,5},{5,4},{6,7},{7,6},{8,9},{9,8},{10,11... | collective-permute-start | bytes 1179656 | tf_op jit(solution)/shard_map/ppermute | solution.py:293
  27.1 18.3 %collective-permute-start.17 = (bf16[128,2048]{1,0:T(8,128)(2,1)S(1)}, bf16[128,2048]{1,0:T(8,128)(2,1)S(1)}, u32[]{:S(2)}, u32[]{:S(2)}) collective-permute-start(bf16[128,2048]{1,0:T(8,128)(2,1)S(1)} %collective-permute-done.3.far_inner.refs_3_), channel_id=1, source_target_pairs={{4,0},{8,12},{5,1},{9,13},{6,2},{10,14},{7,3},{11,15},{20,16},{24,... | collective-permute-start | bytes 1572872 | tf_op jit(solution)/shard_map/ppermute | solution.py:291
  34.6 1.8 %copy-start.6 = (bf16[32,32,128]{2,1,0:T(8,128)(2,1)S(1)}, bf16[32,32,128]{2,1,0:T(8,128)(2,1)}, u32[]{:S(2)}) copy-start(bf16[32,32,128]{2,1,0:T(8,128)(2,1)} %param.17) | copy-start | bytes 786436
  35.8 3.0 %collective-permute-start.14 = (bf16[112,2048]{1,0:T(8,128)(2,1)S(1)}, bf16[112,2048]{1,0:T(8,128)(2,1)S(1)}, u32[]{:S(2)}, u32[]{:S(2)}) collective-permute-start(bf16[112,2048]{1,0:T(8,128)(2,1)S(1)} %get-tuple-element.28), channel_id=1, source_target_pairs={{0,1},{1,0},{2,3},{3,2},{4,5},{5,4},{6,7},{7,6},{8,9},{9,8},{10,11... | collective-permute-start | bytes 1376264 | tf_op jit(solution)/shard_map/ppermute | solution.py:295
  35.8 2.4 %collective-permute-start.12 = (bf16[96,2048]{1,0:T(8,128)(2,1)S(1)}, bf16[96,2048]{1,0:T(8,128)(2,1)S(1)}, u32[]{:S(2)}, u32[]{:S(2)}) collective-permute-start(bf16[96,2048]{1,0:T(8,128)(2,1)S(1)} %get-tuple-element.26), channel_id=1, source_target_pairs={{0,1},{1,0},{2,3},{3,2},{4,5},{5,4},{6,7},{7,6},{8,9},{9,8},{10,11... | collective-permute-start | bytes 1179656 | tf_op jit(solution)/shard_map/ppermute | solution.py:295
  36.3 2.4 %collective-permute-start.13 = (bf16[96,2048]{1,0:T(8,128)(2,1)S(1)}, bf16[96,2048]{1,0:T(8,128)(2,1)S(1)}, u32[]{:S(2)}, u32[]{:S(2)}) collective-permute-start(bf16[96,2048]{1,0:T(8,128)(2,1)S(1)} %get-tuple-element.27), channel_id=1, source_target_pairs={{0,1},{1,0},{2,3},{3,2},{4,5},{5,4},{6,7},{7,6},{8,9},{9,8},{10,11... | collective-permute-start | bytes 1179656 | tf_op jit(solution)/shard_map/ppermute | solution.py:295
  36.4 13.2 %collective-permute-start.19 = (bf16[32,32,128]{2,1,0:T(8,128)(2,1)S(1)}, bf16[32,32,128]{2,1,0:T(8,128)(2,1)S(1)}, u32[]{:S(2)}, u32[]{:S(2)}) collective-permute-start(bf16[32,32,128]{2,1,0:T(8,128)(2,1)S(1)} %copy-done.6), channel_id=1, source_target_pairs={{0,2},{2,0},{1,3},{3,1},{4,6},{6,4},{5,7},{7,5},{8,10},{10,8},{9,1... | collective-permute-start | bytes 786440 | tf_op jit(solution)/shard_map/ppermute | solution.py:296
  40.8 12.9 %collective-permute-start.15 = (bf16[272,128]{1,0:T(8,128)(2,1)S(1)}, bf16[272,128]{1,0:T(8,128)(2,1)S(1)}, u32[]{:S(2)}, u32[]{:S(2)}) collective-permute-start(bf16[272,128]{1,0:T(8,128)(2,1)S(1)} %get-tuple-element.30), channel_id=1, source_target_pairs={{0,4},{4,0},{8,12},{12,8},{1,5},{5,1},{9,13},{13,9},{2,6},{6,2},{1... | collective-permute-start | bytes 208904 | tf_op jit(solution)/shard_map/ppermute | solution.py:305
  44.9 8.8 %collective-permute-start.16 = (bf16[272,128]{1,0:T(8,128)(2,1)S(1)}, bf16[272,128]{1,0:T(8,128)(2,1)S(1)}, u32[]{:S(2)}, u32[]{:S(2)}) collective-permute-start(bf16[272,128]{1,0:T(8,128)(2,1)S(1)} %get-tuple-element.31), channel_id=1, source_target_pairs={{0,8},{4,12},{8,0},{12,4},{1,9},{5,13},{9,1},{13,5},{2,10},{6,14},... | collective-permute-start | bytes 208904 | tf_op jit(solution)/shard_map/ppermute | solution.py:305
  47.5 6.2 %collective-permute-start.18 = (bf16[256,128]{1,0:T(8,128)(2,1)S(1)}, bf16[256,128]{1,0:T(8,128)(2,1)S(1)}, u32[]{:S(2)}, u32[]{:S(2)}) collective-permute-start(bf16[256,128]{1,0:T(8,128)(2,1)S(1)} %shard_map.101), channel_id=1, source_target_pairs={{0,12},{4,8},{8,4},{12,0},{1,13},{5,9},{9,5},{13,1},{2,14},{6,10},... | collective-permute-start | bytes 196616 | tf_op jit(solution)/shard_map/ppermute | solution.py:305
  (6 other events, 5.5 us)
